TPU v7x, 128 devices: a whole 4x4x4 slice. The times are simulated.
128 devices in a mesh: dom: 128 (over y, x, z, core).
Axes of the slice: x: 4, y: 4, z: 4, core: 2. Of those that a mesh axis runs over, the one named last changes fastest.
Arguments:
- node_features: bfloat16 [262144, 128], P('dom'), may hold values from -6 to 6
- w_self: bfloat16 [128, 128], replicated, may hold values from -0.5 to 0.5
- w_neigh: bfloat16 [128, 128], replicated, may hold values from -4 to 4
- output_bias: float32 [128], replicated, may hold values from -3 to 3
- local_tiles: bfloat16 [2048, 22, 128, 128], P('dom'), may hold values from 0 to 1, as said below
- halo_tiles: bfloat16 [2048, 20, 128, 128], P('dom'), may hold values from 0 to 1, as said below
- local_cols: int32 [2048, 22], P('dom'), may hold values from 0 to 15
- halo_cols: int32 [2048, 20], P('dom'), may hold values from 0 to 29
- send_rows: int32 [640, 768], P('dom'), may hold values from 0 to 2047
- degree: int32 [262144], P('dom'), may hold values from 56 to 112, as said below
- cotangent: bfloat16 [262144, 128], P('dom'), may hold values from -6 to 6
Outputs:
- output: bfloat16 [262144, 128], P('dom')
- grad_features: float32 [262144, 128], P('dom')
- grad_self: float32 [128, 128], replicated
- grad_neigh: float32 [128, 128], replicated
Inputs may be any that keep to these rules, and one draw needn't show every extreme that they name: `local_tiles`: entries are 0 or 1. `halo_tiles`: entries are 0 or 1. `send_rows`: row numbers within the sending partition; a row may be listed more than once. A node's degree is the number of ones in its row over its 22 local and 20 boundary tiles.
All inputs are finite; a program needn't handle non-finite values.
Results may differ from a plain program's by a relative error of at most 0.0052.
Values may be sent and summed in bfloat16 or wider, within the bound.
No kernel may reach another device: no remote copies, remote signals or barrier semaphores. Data moves between devices by JAX's collectives and lax.ppermute only.
A program may use at most 192 MiB of HBM per device.

v0:
```python
import math

import jax
import jax.numpy as jnp
from jax import lax
from jax.sharding import PartitionSpec as P


def swapped(shard, axis, stride):
    return lax.ppermute(shard, axis, [(i, i ^ 1 << stride) for i in range(lax.axis_size(axis))])


def reduce_products(tiles, scaled, columns, block_total):
    products = jnp.einsum("btij,bif->btjf", tiles, scaled, preferred_element_type=jnp.float32)
    onehot_table = (columns[..., None] == jnp.arange(block_total, dtype=jnp.int32)).astype(
        jnp.float32
    )
    return jnp.einsum("btc,btjf->cjf", onehot_table, products, precision=lax.Precision.HIGHEST)


def swap_rows(node_features, send_rows, tile_size, width):
    received = []
    for round_index in range(send_rows.shape[0]):
        received.append(swapped(node_features[send_rows[round_index]], "dom", round_index))
    return jnp.concatenate(received, 0).reshape(-1, tile_size, width)


def local(
    node_features,
    w_self,
    w_neigh,
    output_bias,
    local_tiles,
    halo_tiles,
    local_cols,
    halo_cols,
    send_rows,
    degree,
    cotangent,
):
    row_count, width = node_features.shape
    nblocks, local_count, tile_size, _ = local_tiles.shape
    round_count, boundary_count = send_rows.shape
    feature_blocks = node_features.reshape(nblocks, tile_size, width)
    halo_rows = swap_rows(node_features, send_rows, tile_size, width)
    summed = jnp.einsum(
        "btij,btjf->bif",
        local_tiles,
        feature_blocks[local_cols],
        preferred_element_type=jnp.float32,
    )
    halo_blocks = halo_rows.shape[0]
    summed = summed + jnp.einsum(
        "btij,btjf->bif", halo_tiles, halo_rows[halo_cols], preferred_element_type=jnp.float32
    )
    degrees = degree.astype(jnp.float32)[:, None]
    aggregate = (summed.reshape(row_count, width) / degrees).astype(jnp.bfloat16)
    preact = (
        jnp.dot(node_features, w_self, preferred_element_type=jnp.float32)
        + jnp.dot(aggregate, w_neigh, preferred_element_type=jnp.float32)
        + output_bias
    )
    output = jax.nn.silu(preact).astype(jnp.bfloat16)
    sigmoid_pre = jax.nn.sigmoid(preact)
    grad_pre = (
        cotangent.astype(jnp.float32) * sigmoid_pre * (1.0 + preact * (1.0 - sigmoid_pre))
    ).astype(jnp.bfloat16)
    self_part = jnp.dot(node_features.T, grad_pre, preferred_element_type=jnp.float32)
    neigh_part = jnp.dot(aggregate.T, grad_pre, preferred_element_type=jnp.float32)
    grad_self, grad_neigh = lax.psum((self_part, neigh_part), "dom")
    grad_scale = 1.0 / math.sqrt(row_count * lax.axis_size("dom"))
    grad_features = jnp.dot(grad_pre, w_self.T, preferred_element_type=jnp.float32)
    scaled = (jnp.dot(grad_pre, w_neigh.T, preferred_element_type=jnp.float32) / degrees).astype(
        jnp.bfloat16
    )
    scaled = scaled.reshape(nblocks, tile_size, width)
    local_grad = reduce_products(local_tiles, scaled, local_cols, nblocks)
    halo_grad = reduce_products(halo_tiles, scaled, halo_cols, halo_blocks)
    halo_grad = halo_grad.reshape(round_count, boundary_count, width)
    grad_features = grad_features + local_grad.reshape(row_count, width)
    for round_index in range(round_count):
        returned = swapped(halo_grad[round_index].astype(jnp.bfloat16), "dom", round_index).astype(
            jnp.float32
        )
        grad_features = grad_features.at[send_rows[round_index]].add(returned)
    return (output, grad_features, grad_self * grad_scale, grad_neigh * grad_scale)


def solution(mesh):
    in_specs = (
        P("dom", None),
        P(),
        P(),
        P(),
        P("dom", None, None, None),
        P("dom", None, None, None),
        P("dom", None),
        P("dom", None),
        P("dom", None),
        P("dom"),
        P("dom", None),
    )
    out_specs = (P("dom", None), P("dom", None), P(), P())
    return jax.shard_map(local, mesh=mesh, in_specs=in_specs, out_specs=out_specs, check_vma=False)
```

profile of v0, /device:TPU:1, one launch (start us, length us, event | category | flops | bytes accessed | tf_op | source)
XLA Modules:
  0.0 364.8 jit_solution(17845485302817029669)
XLA Ops:
  7.2 1.0 fusion.33
  8.3 1.9 gather_fusion.1
  10.2 1.5 collective-permute-start
  11.7 1.9 gather_fusion.2
  13.6 1.8 collective-permute-start.1
  15.4 1.9 gather_fusion.3
  17.2 3.4 collective-permute-start.2
  20.6 1.9 gather_fusion.4
  22.5 1.3 collective-permute-start.3
  23.8 1.9 gather_fusion.5
  25.7 2.8 collective-permute-start.4
  28.5 0.7 compare_select_fusion.1
  29.3 2.0 fusion.35
  31.3 11.0 %gather_fusion = bf16[352,128,128]{2,1,0:T(8,128)(2,1)} fusion(bf16[16,128,128]{2,1,0:T(8,128)(2,1)S(1)} %bitcast.83, s32[1024]{0:T(1024)S(1)} %pad_clamp_fusion.6), kind=kCustom, calls=%fused_computation | custom fusion | bytes 23070080 | tf_op jit(solution)/shard_map/gather | solution.py:49
  42.4 10.7 %convolution_bitcast_fusion.1 = f32[16,128,128]{1,2,0:T(8,128)S(1)} fusion(bf16[16,22,128,128]{3,2,1,0:T(8,128)(2,1)} %param.15, bf16[16,22,128,128]{3,2,1,0:T(8,128)(2,1)} %bitcast.87), kind=kOutput, calls=%fused_computation.24 | convolution fusion | flops 1476395008 | bytes 24117248 | tf_op jit(solution)/shard_map/btij,btjf->bif/dot_general | solution.py:46
  53.2 0.6 convert_element_type.55
  53.9 1.0 constant_dynamic-update-slice_fusion.3
  54.8 1.0 constant_dynamic-update-slice_fusion.2
  55.8 1.0 constant_dynamic-update-slice_fusion.1
  56.8 1.0 constant_dynamic-update-slice_fusion
  57.7 11.2 %gather_fusion.6 = bf16[320,128,128]{2,1,0:T(8,128)(2,1)} fusion(bf16[30,128,128]{2,1,0:T(8,128)(2,1)S(1)} %bitcast.84, s32[1024]{0:T(1024)S(1)} %pad_clamp_fusion), kind=kCustom, calls=%fused_computation.6 | custom fusion | bytes 20972800 | tf_op jit(solution)/shard_map/gather | solution.py:54
  69.0 10.0 %fusion.11 = f32[16,128,128]{1,2,0:T(8,128)S(1)} fusion(f32[16,128,128]{1,2,0:T(8,128)S(1)} %convolution_bitcast_fusion.1, bf16[16,20,128,128]{3,2,1,0:T(8,128)(2,1)} %param.16, bf16[16,20,128,128]{3,2,1,0:T(8,128)(2,1)} %bitcast.88), kind=kOutput, calls=%fused_computation.25 | convolution fusion | flops 1342439424 | bytes 23068672 | tf_op jit(solution)/shard_map/btij,btjf->bif/dot_general | solution.py:53
  79.0 0.3 fusion.12
  79.4 1.5 multiply_convert_fusion
  80.9 1.0 fusion.38
  81.8 1.0 convolution_bitcast_fusion.2
  82.8 0.4 fusion.5
  83.2 15.4 %fusion.36 = f32[16,128,22,128]{3,1,2,0:T(8,128)} fusion(bf16[16,128,128,1]{2,1,3,0:T(8,128)(2,1)S(1)} %bitcast.90, bf16[16,22,128,128]{3,2,1,0:T(8,128)(2,1)} %param.15), kind=kOutput, calls=%fused_computation.76 | convolution fusion | flops 1476395008 | bytes 35127296 | tf_op jit(solution)/shard_map/btij,bif->btjf/dot_general | solution.py:14
  98.6 8.6 %fusion.37 = f32[16,128,20,128]{3,1,2,0:T(8,128)} fusion(bf16[16,128,128,1]{2,1,3,0:T(8,128)(2,1)S(1)} %bitcast.91, bf16[16,20,128,128]{3,2,1,0:T(8,128)(2,1)S(1)} %bitcast.86), kind=kOutput, calls=%fused_computation.77 | convolution fusion | flops 1342177280 | bytes 31981568 | tf_op jit(solution)/shard_map/btij,bif->btjf/dot_general | solution.py:14
  107.2 24.0 %copy.36 = f32[16,128,22,128]{1,2,0,3:T(8,128)} copy(f32[16,128,22,128]{3,1,2,0:T(8,128)} %fusion.36) | data formatting | bytes 46137344 | tf_op jit(solution)/shard_map/btij,bif->btjf/dot_general | solution.py:14
  131.2 13.7 %fusion.8 = f32[16,128,128]{2,0,1:T(8,128)S(1)} fusion(f32[16,128,22,128]{1,2,0,3:T(8,128)} %copy.36, s32[16,22]{1,0:T(8,128)S(1)} %copy-done.5), kind=kOutput, calls=%fused_computation.22 | convolution fusion | flops 1107301888 | bytes 24118656 | tf_op jit(solution)/shard_map/btc,btjf->cjf/dot_general | solution.py:18
  144.9 0.3 copy.24
  145.6 23.1 %copy.38 = f32[16,128,20,128]{1,2,0,3:T(8,128)} copy(f32[16,128,20,128]{3,1,2,0:T(8,128)} %fusion.37) | data formatting | bytes 41943040 | tf_op jit(solution)/shard_map/btij,bif->btjf/dot_general | solution.py:14
  168.7 13.6 %bitcast_convert_fusion = bf16[30,128,128]{2,0,1:T(8,128)(2,1)S(1)} fusion(f32[16,128,20,128]{1,2,0,3:T(8,128)} %copy.38, s32[16,20]{1,0:T(8,128)S(1)} %copy-done.6), kind=kOutput, calls=%fused_computation.21 | convolution fusion | flops 1887937920 | bytes 21955840 | tf_op jit(solution)/shard_map/btc,btjf->cjf/dot_general | solution.py:18
  182.5 0.7 copy.25
  183.2 1.1 collective-permute-start.5
  184.4 0.7 copy.26
  185.5 1.4 collective-permute-start.9
  186.8 133.4 %all-reduce.3.cloned.1.call-done = (f32[128,128]{0,1:T(8,128)}, f32[128,128]{0,1:T(8,128)}) async-done(((f32[128,128]{0,1:T(8,128)}, f32[128,128]{0,1:T(8,128)}), (f32[128,128]{0,1:T(8,128)}, f32[128,128]{0,1:T(8,128)})) %all-reduce.3.cloned.1.call-update) | async-done | bytes 131088 | tf_op jit(solution)/shard_map/psum | solution.py:70
  320.2 0.9 broadcast_multiply_fusion
  321.1 0.7 copy.31
  321.8 0.7 copy.32
  322.5 6.8 %scatter_custom_fusion = f32[2048,128]{1,0:T(8,128)S(1)} fusion(f32[2048,128]{1,0:T(8,128)S(1)} %convolution_add_fusion, s32[768]{0:T(1024)} %copy-done.11, bf16[768,128]{1,0:T(8,128)(2,1)S(1)} %collective-permute-done.5), kind=kCustom, calls=%fused_computation.40 | custom fusion | flops 196608 | bytes 1245184 | tf_op jit(solution)/shard_map/scatter-add | solution.py:85
  329.4 7.0 %scatter_custom_fusion.1 = f32[2048,128]{1,0:T(8,128)S(1)} fusion(f32[2048,128]{1,0:T(8,128)S(1)} %scatter_custom_fusion, s32[768]{0:T(1024)} %copy-done.10, bf16[768,128]{1,0:T(8,128)(2,1)S(1)} %collective-permute-done.6), kind=kCustom, calls=%fused_computation.38 | custom fusion | flops 196608 | bytes 1245184 | tf_op jit(solution)/shard_map/scatter-add | solution.py:85
  336.4 6.8 %scatter_custom_fusion.2 = f32[2048,128]{1,0:T(8,128)S(1)} fusion(f32[2048,128]{1,0:T(8,128)S(1)} %scatter_custom_fusion.1, s32[768]{0:T(1024)} %copy-done.9, bf16[768,128]{1,0:T(8,128)(2,1)S(1)} %collective-permute-done.7), kind=kCustom, calls=%fused_computation.36 | custom fusion | flops 196608 | bytes 1245184 | tf_op jit(solution)/shard_map/scatter-add | solution.py:85
  343.2 6.8 %scatter_custom_fusion.3 = f32[2048,128]{1,0:T(8,128)S(1)} fusion(f32[2048,128]{1,0:T(8,128)S(1)} %scatter_custom_fusion.2, s32[768]{0:T(1024)} %copy-done.8, bf16[768,128]{1,0:T(8,128)(2,1)S(1)} %collective-permute-done.8), kind=kCustom, calls=%fused_computation.34 | custom fusion | flops 196608 | bytes 1245184 | tf_op jit(solution)/shard_map/scatter-add | solution.py:85
  350.0 6.7 %scatter_custom_fusion.4 = f32[2048,128]{1,0:T(8,128)S(1)} fusion(f32[2048,128]{1,0:T(8,128)S(1)} %scatter_custom_fusion.3, s32[768]{0:T(1024)S(1)} %get-tuple-element.12, bf16[768,128]{1,0:T(8,128)(2,1)S(1)} %collective-permute-done.9), kind=kCustom, calls=%fused_computation.32 | custom fusion | flops 196608 | bytes 1245184 | tf_op jit(solution)/shard_map/scatter-add | solution.py:85
  356.8 1.0 copy-done.3
  (69 shorter events, 1.4 us)
Async XLA Ops:
  7.2 1.1 copy-start
  7.2 313.0 %all-reduce.3.cloned.1.call-start = ((), (), s32[]{:S(2)}) async-start(), calls=%async_computation | async-start | bytes 262144 | tf_op jit(solution)/shard_map/psum | solution.py:70
  8.2 17.5 %copy-start.11 = (s32[768]{0:T(1024)}, s32[768]{0:T(1024)S(1)}, u32[]{:S(2)}) copy-start(s32[768]{0:T(1024)S(1)} %get-tuple-element.15) | copy-start | bytes 9220
  8.2 34.1 %copy-start.8 = (s32[768]{0:T(1024)}, s32[768]{0:T(1024)S(1)}, u32[]{:S(2)}) copy-start(s32[768]{0:T(1024)S(1)} %get-tuple-element.16) | copy-start | bytes 9220
  8.2 34.1 %copy-start.9 = (s32[768]{0:T(1024)}, s32[768]{0:T(1024)S(1)}, u32[]{:S(2)}) copy-start(s32[768]{0:T(1024)S(1)} %get-tuple-element.13) | copy-start | bytes 9220
  8.2 34.1 %copy-start.10 = (s32[768]{0:T(1024)}, s32[768]{0:T(1024)S(1)}, u32[]{:S(2)}) copy-start(s32[768]{0:T(1024)S(1)} %get-tuple-element.14) | copy-start | bytes 9220
  10.2 43.7 %collective-permute-start = (bf16[768,128]{1,0:T(8,128)(2,1)S(1)}, bf16[768,128]{1,0:T(8,128)(2,1)S(1)}, u32[]{:S(2)}, u32[]{:S(2)}) collective-permute-start(bf16[768,128]{1,0:T(8,128)(2,1)S(1)} %gather_fusion.1), channel_id=1, source_target_pairs={{0,1},{1,0},{2,3},{3,2},{4,5},{5,4},{6,7},{7,6},{8,9},{9,8},{10,11... | collective-permute-start | bytes 589832 | tf_op jit(solution)/shard_map/ppermute | solution.py:10
  13.6 40.3 %collective-permute-start.1 = (bf16[768,128]{1,0:T(8,128)(2,1)S(1)}, bf16[768,128]{1,0:T(8,128)(2,1)}, u32[]{:S(2)}, u32[]{:S(2)}) collective-permute-start(bf16[768,128]{1,0:T(8,128)(2,1)S(1)} %gather_fusion.2), channel_id=1, source_target_pairs={{0,2},{1,3},{2,0},{3,1},{4,6},{5,7},{6,4},{7,5},{8,10},{9,11},{10,... | collective-permute-start | bytes 589832 | tf_op jit(solution)/shard_map/ppermute | solution.py:10
  17.2 37.6 %collective-permute-start.2 = (bf16[768,128]{1,0:T(8,128)(2,1)S(1)}, bf16[768,128]{1,0:T(8,128)(2,1)}, u32[]{:S(2)}, u32[]{:S(2)}) collective-permute-start(bf16[768,128]{1,0:T(8,128)(2,1)S(1)} %gather_fusion.3), channel_id=1, source_target_pairs={{0,4},{1,5},{2,6},{3,7},{4,0},{5,1},{6,2},{7,3},{8,12},{9,13},{10,... | collective-permute-start | bytes 589832 | tf_op jit(solution)/shard_map/ppermute | solution.py:10
  22.5 33.3 %collective-permute-start.3 = (bf16[768,128]{1,0:T(8,128)(2,1)S(1)}, bf16[768,128]{1,0:T(8,128)(2,1)}, u32[]{:S(2)}, u32[]{:S(2)}) collective-permute-start(bf16[768,128]{1,0:T(8,128)(2,1)S(1)} %gather_fusion.4), channel_id=1, source_target_pairs={{0,8},{1,9},{2,10},{3,11},{4,12},{5,13},{6,14},{7,15},{8,0},{9,1},... | collective-permute-start | bytes 589832 | tf_op jit(solution)/shard_map/ppermute | solution.py:10
  25.7 31.1 %collective-permute-start.4 = (bf16[768,128]{1,0:T(8,128)(2,1)S(1)}, bf16[768,128]{1,0:T(8,128)(2,1)}, u32[]{:S(2)}, u32[]{:S(2)}) collective-permute-start(bf16[768,128]{1,0:T(8,128)(2,1)S(1)} %gather_fusion.5), channel_id=1, source_target_pairs={{0,16},{1,17},{2,18},{3,19},{4,20},{5,21},{6,22},{7,23},{8,24},{9,... | collective-permute-start | bytes 589832 | tf_op jit(solution)/shard_map/ppermute | solution.py:10
  42.4 10.8 %copy-start.6 = (s32[16,20]{1,0:T(8,128)S(1)}, s32[16,20]{1,0:T(8,128)}, u32[]{:S(2)}) copy-start(s32[16,20]{1,0:T(8,128)} %param.18) | copy-start | bytes 3844
  42.4 10.8 %copy-start.12 = (s32[2048]{0:T(1024)S(1)}, s32[2048]{0:T(1024)}, u32[]{:S(2)}) copy-start(s32[2048]{0:T(1024)} %param.20) | copy-start | bytes 24580
  68.9 10.0 %copy-start.7 = (f32[2048]{0:T(1024)S(1)}, f32[2048]{0:T(1024)}, u32[]{:S(2)}) copy-start(f32[2048]{0:T(1024)} %convert_element_type.55) | copy-start | bytes 24580
  68.9 10.4 %copy-start.2 = (f32[2048,128]{1,0:T(8,128)S(1)}, f32[2048,128]{1,0:T(8,128)}, u32[]{:S(2)}) copy-start(f32[2048,128]{1,0:T(8,128)} %fusion.35) | copy-start | bytes 3145732
  69.0 10.4 %copy-start.13 = (bf16[2048,128]{1,0:T(8,128)(2,1)S(1)}, bf16[2048,128]{1,0:T(8,128)(2,1)}, u32[]{:S(2)}) copy-start(bf16[2048,128]{1,0:T(8,128)(2,1)} %param.21) | copy-start | bytes 1572868
  69.0 10.4 %copy-start.14 = (bf16[128,128]{1,0:T(8,128)(2,1)S(1)}, bf16[128,128]{1,0:T(8,128)(2,1)}, u32[]{:S(2)}) copy-start(bf16[128,128]{1,0:T(8,128)(2,1)} %param.13) | copy-start | bytes 98308
  69.0 10.4 %copy-start.15 = (f32[128]{0:T(128)S(1)}, f32[128]{0:T(128)}, u32[]{:S(2)}) copy-start(f32[128]{0:T(128)} %param.14) | copy-start | bytes 1540
  82.8 15.8 %slice-start = ((s8[10485760]{0:T(1024)(128)(4,1)}), s8[4194304]{0:T(1024)(128)(4,1)S(1)}, s32[]{:S(2)}) async-start(s8[10485760]{0:T(1024)(128)(4,1)} %bitcast.85), calls=%async_computation.1 | async-start | bytes 8388608
  83.2 15.4 %slice-start.1 = ((s8[10485760]{0:T(1024)(128)(4,1)}), s8[4194304]{0:T(1024)(128)(4,1)S(1)}, s32[]{:S(2)}) async-start(s8[10485760]{0:T(1024)(128)(4,1)} %bitcast.85), calls=%async_computation.2 | async-start | bytes 8388608
  83.2 15.4 %slice-start.2 = ((s8[10485760]{0:T(1024)(128)(4,1)}), s8[2097152]{0:T(1024)(128)(4,1)S(1)}, s32[]{:S(2)}) async-start(s8[10485760]{0:T(1024)(128)(4,1)} %bitcast.85), calls=%async_computation.3 | async-start | bytes 4194304
  107.2 24.0 %copy-start.5 = (s32[16,22]{1,0:T(8,128)S(1)}, s32[16,22]{1,0:T(8,128)}, u32[]{:S(2)}) copy-start(s32[16,22]{1,0:T(8,128)} %param.17) | copy-start | bytes 4228
  131.2 14.1 %copy-start.4 = (bf16[128,128]{1,0:T(8,128)(2,1)S(1)}, bf16[128,128]{1,0:T(8,128)(2,1)}, u32[]{:S(2)}) copy-start(bf16[128,128]{1,0:T(8,128)(2,1)} %param.12) | copy-start | bytes 98308
  168.7 189.1 %copy-start.1 = (bf16[2048,128]{1,0:T(8,128)(2,1)S(1)}, bf16[2048,128]{1,0:T(8,128)(2,1)}, u32[]{:S(2)}) copy-start(bf16[2048,128]{1,0:T(8,128)(2,1)} %param.11) | copy-start | bytes 1572868
  183.2 139.3 %collective-permute-start.5 = (bf16[768,128]{1,0:T(8,128)(2,1)}, bf16[768,128]{1,0:T(8,128)(2,1)S(1)}, u32[]{:S(2)}, u32[]{:S(2)}) collective-permute-start(bf16[768,128]{1,0:T(8,128)(2,1)} %bitcast.29), channel_id=1, source_target_pairs={{0,1},{1,0},{2,3},{3,2},{4,5},{5,4},{6,7},{7,6},{8,9},{9,8},{10,11... | collective-permute-start | bytes 589832 | tf_op jit(solution)/shard_map/ppermute | solution.py:10
  185.1 144.3 %collective-permute-start.6 = (bf16[768,128]{1,0:T(8,128)(2,1)}, bf16[768,128]{1,0:T(8,128)(2,1)S(1)}, u32[]{:S(2)}, u32[]{:S(2)}) collective-permute-start(bf16[768,128]{1,0:T(8,128)(2,1)} %bitcast.30), channel_id=1, source_target_pairs={{0,2},{1,3},{2,0},{3,1},{4,6},{5,7},{6,4},{7,5},{8,10},{9,11},{10,... | collective-permute-start | bytes 589832 | tf_op jit(solution)/shard_map/ppermute | solution.py:10
  185.1 151.3 %collective-permute-start.7 = (bf16[768,128]{1,0:T(8,128)(2,1)S(1)}, bf16[768,128]{1,0:T(8,128)(2,1)S(1)}, u32[]{:S(2)}, u32[]{:S(2)}) collective-permute-start(bf16[768,128]{1,0:T(8,128)(2,1)S(1)} %bitcast.94), channel_id=1, source_target_pairs={{0,4},{1,5},{2,6},{3,7},{4,0},{5,1},{6,2},{7,3},{8,12},{9,13},{10,... | collective-permute-start | bytes 589832 | tf_op jit(solution)/shard_map/ppermute | solution.py:10
  185.3 157.9 %collective-permute-start.8 = (bf16[768,128]{1,0:T(8,128)(2,1)S(1)}, bf16[768,128]{1,0:T(8,128)(2,1)S(1)}, u32[]{:S(2)}, u32[]{:S(2)}) collective-permute-start(bf16[768,128]{1,0:T(8,128)(2,1)S(1)} %bitcast.93), channel_id=1, source_target_pairs={{0,8},{1,9},{2,10},{3,11},{4,12},{5,13},{6,14},{7,15},{8,0},{9,1},... | collective-permute-start | bytes 589832 | tf_op jit(solution)/shard_map/ppermute | solution.py:10
  185.5 164.6 %collective-permute-start.9 = (bf16[768,128]{1,0:T(8,128)(2,1)S(1)}, bf16[768,128]{1,0:T(8,128)(2,1)S(1)}, u32[]{:S(2)}, u32[]{:S(2)}) collective-permute-start(bf16[768,128]{1,0:T(8,128)(2,1)S(1)} %bitcast.92), channel_id=1, source_target_pairs={{0,16},{1,17},{2,18},{3,19},{4,20},{5,21},{6,22},{7,23},{8,24},{9,... | collective-permute-start | bytes 589832 | tf_op jit(solution)/shard_map/ppermute | solution.py:10
  356.7 1.0 copy-start.3
Sparse Core Ops, SparseCore 0:
  182.4 137.7 all-reduce.2
where the time goes:
time: 370 us; the launch traced here: 365 us
  waiting for transfers between devices  133 us (36%)
  local copies, waits for them, and re-layouts  87.2 us (24%)
  matrix products  78.1 us (21%)
  other arithmetic  37.7 us (10%)
  between operations  14.8 us (4%)
  starting transfers between devices  13.6 us (4%)
    psum x1, waiting for transfers between devices, local(): grad_self, grad_neigh = lax.psum((self_part, neigh_part), 'dom')  133 us
    dot_general x2, local copies, waits for them, and re-layouts, reduce_products(): jnp.einsum('btij,bif->btjf', tiles, scaled, preferred_element_type=jnp.fl...  47.1 us
    scatter-add x5, other arithmetic, local(): grad_features = grad_features.at[send_rows[round_index]].add(returned)  34.1 us
    dot_general x2, matrix products, reduce_products(): jnp.einsum('btc,btjf->cjf', onehot_table, products, precision=lax.Precisi...  27.3 us
    dot_general x2, matrix products, reduce_products(): jnp.einsum('btij,bif->btjf', tiles, scaled, preferred_element_type=jnp.fl...  24 us
    ppermute x10, starting transfers between devices, swapped(): lax.ppermute(shard, axis, [(i, i ^ 1 << stride) for i in range(lax.axis_s...  13.6 us
    gather x1, local copies, waits for them, and re-layouts, local(): halo_rows[halo_cols]  11.2 us
    gather x1, local copies, waits for them, and re-layouts, local(): feature_blocks[local_cols]  11 us
  transfers between devices with their start and end apart: 11, of which 1 were waited for; matrix products, arithmetic and copies ran while one was open for 18% of the time, Pallas kernels for 0%

commit v1 on v0

v1 whole, which is shorter than its diff:
```python
import functools
import math

import jax
import jax.numpy as jnp
from jax import lax
from jax.experimental import pallas as pl
from jax.experimental.pallas import tpu as pltpu
from jax.sharding import PartitionSpec as P

TILE = 128
VMEM = pltpu.VMEM
KEEP = True
LIMIT = 28 * 1024 * 1024


def vspec():
    return pl.BlockSpec(memory_space=VMEM)


def sspec():
    return pl.BlockSpec(memory_space=pltpu.SMEM)


def params(limit=LIMIT):
    return pltpu.CompilerParams(vmem_limit_bytes=limit)


def kept(shape, dtype):
    return VMEM(shape, dtype) if KEEP else jax.ShapeDtypeStruct(shape, dtype)


def pinned(array):
    return pltpu.with_memory_space_constraint(array, VMEM) if KEEP else array


def nt_dot(left, right):
    return lax.dot_general(
        left, right, (((1,), (1,)), ((), ())), preferred_element_type=jnp.float32
    )


def nn_dot(left, right):
    return jnp.dot(left, right, preferred_element_type=jnp.float32)


def pick_kernel(rounds, rows_ref, x_ref, *refs):
    outs, (wide, picked) = refs[: len(rounds)], refs[len(rounds) :]
    wide[...] = x_ref[...].astype(jnp.float32)
    count = picked.shape[0]
    step = 32

    for place, round_index in enumerate(rounds):

        def body(j, carry, round_index=round_index):
            base = pl.multiple_of(j * step, step)
            for u in range(step):
                row = rows_ref[round_index, base + u]
                picked[pl.ds(base + u, 1), :] = wide[pl.ds(row, 1), :]
            return carry

        lax.fori_loop(0, count // step, body, 0)
        outs[place][...] = picked[...].astype(jnp.bfloat16)


def pick_rows(rounds, send_rows, features):
    row_count, width = features.shape
    boundary = send_rows.shape[1]
    return pl.pallas_call(
        functools.partial(pick_kernel, rounds),
        out_shape=[jax.ShapeDtypeStruct((boundary, width), jnp.bfloat16) for _ in rounds],
        in_specs=[sspec(), vspec()],
        out_specs=[vspec() for _ in rounds],
        scratch_shapes=[VMEM((row_count, width), jnp.float32), VMEM((boundary, width), jnp.float32)],
        compiler_params=params(),
        cost_estimate=pl.CostEstimate(
            flops=4_000_000 * len(rounds), bytes_accessed=1_000_000, transcendentals=0
        ),
    )(send_rows, features)


def densify_kernel(cols_ref, tiles_ref, dense_ref, slots, sems):
    nblocks, count = tiles_ref.shape[:2]
    slabs = dense_ref.shape[0]
    depth = slots.shape[0]

    def fetch(i, slot):
        return pltpu.make_async_copy(tiles_ref.at[i], slots.at[slot], sems.at[slot])

    for d in range(depth - 1):
        fetch(d, d).start()

    def body(i, carry):
        slot = lax.rem(i, depth)

        @pl.when(i + depth - 1 < nblocks)
        def _():
            fetch(i + depth - 1, lax.rem(i + depth - 1, depth)).start()

        rows = pl.ds(pl.multiple_of(i * TILE, TILE), TILE)
        for c in range(slabs):
            dense_ref[c, rows, :] = jnp.zeros((TILE, TILE), jnp.bfloat16)
        fetch(i, slot).wait()
        for t in range(count):
            col = cols_ref[i, t]
            dense_ref[col, rows, :] = dense_ref[col, rows, :] + slots[slot, t]
        return carry

    lax.fori_loop(0, nblocks, body, 0)


def densify(cols, tiles, slabs):
    nblocks, count = cols.shape
    depth = 4
    return pl.pallas_call(
        densify_kernel,
        out_shape=kept((slabs, nblocks * TILE, TILE), jnp.bfloat16),
        in_specs=[sspec(), pl.BlockSpec(memory_space=pl.ANY)],
        out_specs=vspec(),
        scratch_shapes=[
            VMEM((depth, count, TILE, TILE), jnp.bfloat16),
            pltpu.SemaphoreType.DMA((depth,)),
        ],
        compiler_params=params(),
        cost_estimate=pl.CostEstimate(
            flops=16_000_000, bytes_accessed=nblocks * count * TILE * TILE * 2, transcendentals=0
        ),
    )(cols, tiles)


def forward_kernel(first, n, has_acc, dense_ref, x_ref, *refs):
    acc_ref, out_ref = refs if has_acc else (None, refs[0])
    chunk = 512

    def body(j, carry):
        rows = pl.ds(pl.multiple_of(j * chunk, chunk), chunk)
        left = jnp.concatenate([dense_ref[first + c, rows, :] for c in range(n)], axis=1)
        total = nn_dot(left, x_ref[...])
        if has_acc:
            total = total + acc_ref[rows, :]
        out_ref[rows, :] = total
        return carry

    lax.fori_loop(0, out_ref.shape[0] // chunk, body, 0)


def forward(dense, first, blocks, acc):
    n = blocks.shape[0] // TILE
    rows = dense.shape[1]
    args = [pinned(dense), blocks] + ([] if acc is None else [acc])
    return pl.pallas_call(
        functools.partial(forward_kernel, first, n, acc is not None),
        out_shape=jax.ShapeDtypeStruct((rows, TILE), jnp.float32),
        in_specs=[vspec()] * len(args),
        out_specs=vspec(),
        compiler_params=params(),
        cost_estimate=pl.CostEstimate(
            flops=2 * rows * n * TILE * TILE, bytes_accessed=rows * TILE * 4, transcendentals=0
        ),
    )(*args)


def across(degree_ref, i):
    line = degree_ref[pl.ds(i, 1), :].astype(jnp.float32)
    return line, jnp.broadcast_to(line, (TILE, TILE)).T


def middle_kernel(
    sum_ref, x_ref, ct_ref, deg_ref, ws_ref, wn_ref, bias_ref, out_ref, agg_ref, gp_ref, st_ref
):
    for i in range(sum_ref.shape[0] // TILE):
        rows = pl.ds(i * TILE, TILE)
        line, column = across(deg_ref, i)
        agg = (sum_ref[rows, :] / column).astype(jnp.bfloat16)
        agg_ref[rows, :] = agg
        preact = nn_dot(x_ref[rows, :], ws_ref[...]) + nn_dot(agg, wn_ref[...]) + bias_ref[...]
        sig = jax.nn.sigmoid(preact)
        out_ref[rows, :] = (preact * sig).astype(jnp.bfloat16)
        grad = ct_ref[rows, :].astype(jnp.float32) * sig * (1.0 + preact * (1.0 - sig))
        grad = grad.astype(jnp.bfloat16)
        gp_ref[rows, :] = grad
        st_ref[:, rows] = (nt_dot(wn_ref[...], grad) / line).astype(jnp.bfloat16)


def middle(summed, features, cotangent, degree, w_self, w_neigh, bias):
    rows, width = features.shape
    half = jax.ShapeDtypeStruct((rows, width), jnp.bfloat16)
    return pl.pallas_call(
        middle_kernel,
        out_shape=[half, half, half, jax.ShapeDtypeStruct((width, rows), jnp.bfloat16)],
        in_specs=[vspec()] * 7,
        out_specs=[vspec()] * 4,
        compiler_params=params(),
        cost_estimate=pl.CostEstimate(
            flops=2 * rows * 3 * width * width, bytes_accessed=5_000_000, transcendentals=rows * width
        ),
    )(summed, features, cotangent, degree, w_self, w_neigh, bias)


def weights_kernel(x_ref, agg_ref, gp_ref, out_ref):
    both = jnp.concatenate([x_ref[...], agg_ref[...]], axis=1)
    out_ref[...] = lax.dot_general(
        both, gp_ref[...], (((0,), (0,)), ((), ())), preferred_element_type=jnp.float32
    )


def weight_parts(features, aggregate, grad_pre):
    rows, width = features.shape
    return pl.pallas_call(
        weights_kernel,
        out_shape=jax.ShapeDtypeStruct((2 * width, width), jnp.float32),
        in_specs=[vspec()] * 3,
        out_specs=vspec(),
        compiler_params=params(),
        cost_estimate=pl.CostEstimate(
            flops=4 * rows * width * width, bytes_accessed=1_500_000, transcendentals=0
        ),
    )(features, aggregate, grad_pre)


def back_kernel(rounds, per, st_ref, dense_ref, *outs):
    for place, round_index in enumerate(rounds):
        for c in range(0, per, 2):
            slab = round_index * per + c
            right = jnp.concatenate([dense_ref[slab], dense_ref[slab + 1]], axis=1)
            product = nn_dot(st_ref[...], right)
            outs[place][pl.ds(c * TILE, 2 * TILE), :] = product.T.astype(jnp.bfloat16)


def back(rounds, per, scaled_t, dense):
    width, rows = scaled_t.shape
    return pl.pallas_call(
        functools.partial(back_kernel, rounds, per),
        out_shape=[jax.ShapeDtypeStruct((per * TILE, width), jnp.bfloat16) for _ in rounds],
        in_specs=[vspec()] * 2,
        out_specs=[vspec() for _ in rounds],
        compiler_params=params(),
        cost_estimate=pl.CostEstimate(
            flops=2 * rows * len(rounds) * per * TILE * width, bytes_accessed=500_000, transcendentals=0
        ),
    )(scaled_t, pinned(dense))


def own_kernel(st_ref, dense_ref, gp_ref, ws_ref, out_ref):
    for c in range(0, dense_ref.shape[0], 2):
        rows = pl.ds(c * TILE, 2 * TILE)
        right = jnp.concatenate([dense_ref[c], dense_ref[c + 1]], axis=1)
        product = nn_dot(st_ref[...], right)
        out_ref[rows, :] = product.T + nt_dot(gp_ref[rows, :], ws_ref[...])


def own(scaled_t, dense, grad_pre, w_self):
    width, rows = scaled_t.shape
    return pl.pallas_call(
        own_kernel,
        out_shape=jax.ShapeDtypeStruct((rows, width), jnp.float32),
        in_specs=[vspec()] * 4,
        out_specs=vspec(),
        compiler_params=params(),
        cost_estimate=pl.CostEstimate(
            flops=2 * rows * rows * width, bytes_accessed=1_500_000, transcendentals=0
        ),
    )(scaled_t, pinned(dense), grad_pre, w_self)


def place_kernel(rounds, rows_ref, acc_ref, *refs):
    returned, out_ref = refs[:-1], refs[-1]
    chunk = 256
    boundary = rows_ref.shape[1]

    def body(j, carry):
        base = pl.multiple_of(j * chunk, chunk)
        total = acc_ref[pl.ds(base, chunk), :]
        for place, round_index in enumerate(rounds):
            wanted = rows_ref[pl.ds(round_index, 1), :] - base
            index = lax.broadcasted_iota(jnp.int32, (chunk, boundary), 0)
            onehot = jnp.where(index == wanted, 1.0, 0.0).astype(jnp.bfloat16)
            total = total + nn_dot(onehot, returned[place][...])
        out_ref[pl.ds(base, chunk), :] = total
        return carry

    lax.fori_loop(0, out_ref.shape[0] // chunk, body, 0)


def place_rows(rounds, send_rows, acc, returned):
    rows, width = acc.shape
    return pl.pallas_call(
        functools.partial(place_kernel, rounds),
        out_shape=jax.ShapeDtypeStruct((rows, width), jnp.float32),
        in_specs=[vspec()] * (2 + len(rounds)),
        out_specs=vspec(),
        compiler_params=params(),
        cost_estimate=pl.CostEstimate(
            flops=2 * rows * len(rounds) * send_rows.shape[1] * width,
            bytes_accessed=2_000_000,
            transcendentals=0,
        ),
    )(send_rows, acc, *returned)


def swapped(shard, mask):
    return lax.ppermute(shard, "dom", [(i, i ^ mask) for i in range(lax.axis_size("dom"))])


def summed_everywhere(parts):
    me = lax.axis_index("dom")
    core, z = me & 1, (me >> 1) & 3
    halves = parts.reshape(2, -1, parts.shape[1])
    own_half = halves[core] + swapped(halves[1 - core], 1)
    quarters = own_half.reshape(4, -1, parts.shape[1])
    got = [swapped(quarters[z ^ d], d << 1) for d in (1, 2, 3)]
    total = (quarters[z] + got[0]) + (got[1] + got[2])
    for bit in (3, 5):
        got = [swapped(total, d << bit) for d in (1, 2, 3)]
        total = (total + got[0]) + (got[1] + got[2])
    pieces = jnp.stack([total] + [swapped(total, d << 1) for d in (1, 2, 3)])
    half = pieces[z ^ jnp.arange(4, dtype=jnp.int32)].reshape(own_half.shape)
    other = swapped(half, 1)
    first = jnp.where(core == 0, half, other)
    second = jnp.where(core == 0, other, half)
    return first, second


def local(
    node_features,
    w_self,
    w_neigh,
    output_bias,
    local_tiles,
    halo_tiles,
    local_cols,
    halo_cols,
    send_rows,
    degree,
    cotangent,
):
    row_count, width = node_features.shape
    nblocks = local_tiles.shape[0]
    round_count, boundary = send_rows.shape
    per = boundary // TILE
    order = (2, 4, 1, 3, 0)
    received = {}
    for rounds in ((2, 4), (1, 3, 0)):
        picked = pick_rows(rounds, send_rows, node_features)
        for round_index, rows in zip(rounds, picked):
            received[round_index] = swapped(rows, 1 << round_index)
    dense_local = densify(local_cols, local_tiles, nblocks)
    summed = forward(dense_local, 0, node_features, None)
    dense_halo = densify(halo_cols, halo_tiles, round_count * per)
    for round_index in reversed(order):
        summed = forward(dense_halo, round_index * per, received[round_index], summed)
    output, aggregate, grad_pre, scaled_t = middle(
        summed,
        node_features,
        cotangent,
        degree.reshape(nblocks, TILE),
        w_self,
        w_neigh,
        output_bias.reshape(1, width),
    )
    returned = {}
    for rounds in ((2,), (4,), (1, 3, 0)):
        grads = back(rounds, per, scaled_t, dense_halo)
        for round_index, rows in zip(rounds, grads):
            returned[round_index] = swapped(rows, 1 << round_index)
    parts = weight_parts(node_features, aggregate, grad_pre)
    grad_self, grad_neigh = summed_everywhere(parts)
    grad_scale = 1.0 / math.sqrt(row_count * lax.axis_size("dom"))
    grad_features = own(scaled_t, dense_local, grad_pre, w_self)
    for rounds in ((0, 3), (1, 4, 2)):
        grad_features = place_rows(rounds, send_rows, grad_features, [returned[r] for r in rounds])
    return (output, grad_features, grad_self * grad_scale, grad_neigh * grad_scale)


def solution(mesh):
    in_specs = (
        P("dom", None),
        P(),
        P(),
        P(),
        P("dom", None, None, None),
        P("dom", None, None, None),
        P("dom", None),
        P("dom", None),
        P("dom", None),
        P("dom"),
        P("dom", None),
    )
    out_specs = (P("dom", None), P("dom", None), P(), P())
    return jax.shard_map(local, mesh=mesh, in_specs=in_specs, out_specs=out_specs, check_vma=False)
```

time: 370 us -> 122 us (0.33); the launches traced: 365 us -> 122 us
  waiting for transfers between devices: 133 us -> 6.01 us
  matrix products: 78.1 us -> 0 us
  local copies, waits for them, and re-layouts: 87.2 us -> 20 us
  Pallas kernels: 0 us -> 54.9 us
  other arithmetic: 37.7 us -> 0.72 us
  starting transfers between devices: 13.6 us -> 39.1 us
  between operations: 14.8 us -> 1.08 us
    psum x1 -> x0, waiting for transfers between devices: 133 us -> none  [local(): grad_self, grad_neigh = lax.psum((self_part, neigh_part), 'dom')]
    dot_general x12 -> x0, matrix products: 78.1 us -> none  [the longest x2 27.3 us: reduce_products(): jnp.einsum('btc,btjf->cjf', onehot_table, products, precision=lax.Precisi...]
    pallas_call x0 -> x18, Pallas kernels: none -> 54.9 us  [the longest x2 18.1 us: densify(): pl.pallas_call(densify_kernel, out_shape=kept((slabs, nblocks * TILE, TIL...]
    dot_general x3 -> x0, local copies, waits for them, and re-layouts: 47.4 us -> none  [the longest x2 47.1 us: reduce_products(): jnp.einsum('btij,bif->btjf', tiles, scaled, preferred_element_type=jnp.fl...]
    scatter-add x5 -> x0, other arithmetic: 34.1 us -> none  [local(): grad_features = grad_features.at[send_rows[round_index]].add(returned)]
    gather x7 -> x1, local copies, waits for them, and re-layouts: 31.6 us -> 0.55 us  [summed_everywhere(): half = pieces[z ^ jnp.arange(4, dtype=jnp.int32)].reshape(own_half.shape)]
    ppermute x10 -> x24, starting transfers between devices: 13.6 us -> 39.1 us  [swapped(): lax.ppermute(shard, 'dom', [(i, i ^ mask) for i in range(lax.axis_size('d...]
    unnamed x44 -> x36, local copies, waits for them, and re-layouts: 5.43 us -> 19.4 us
  transfers between devices with their start and end apart: 11 -> 24, of which waited for: 1 -> 6; matrix products, arithmetic and copies ran while one was open for 18% -> 0% of each run, Pallas kernels for 0% -> 37%
where the time goes in v1:
time: 122 us
  Pallas kernels  54.9 us (45%)
  starting transfers between devices  39.1 us (32%)
  local copies, waits for them, and re-layouts  20 us (16%)
  waiting for transfers between devices  6.01 us (5%)
    ppermute x24, starting transfers between devices, swapped(): lax.ppermute(shard, 'dom', [(i, i ^ mask) for i in range(lax.axis_size('d...  39.1 us
    unnamed x36, local copies, waits for them, and re-layouts  19.4 us
    pallas_call x2, Pallas kernels, densify(): pl.pallas_call(densify_kernel, out_shape=kept((slabs, nblocks * TILE, TIL...  18.1 us
    pallas_call x2, Pallas kernels, pick_rows(): pl.pallas_call(functools.partial(pick_kernel, rounds), out_shape=[jax.Sha...  10.6 us
    pallas_call x6, Pallas kernels, forward(): pl.pallas_call(functools.partial(forward_kernel, first, n, acc is not Non...  10.3 us
    pallas_call x2, Pallas kernels, place_rows(): pl.pallas_call(functools.partial(place_kernel, rounds), out_shape=jax.Sha...  9.56 us
    ppermute x24, waiting for transfers between devices, swapped(): lax.ppermute(shard, 'dom', [(i, i ^ mask) for i in range(lax.axis_size('d...  6.01 us
    pallas_call x3, Pallas kernels, back(): pl.pallas_call(functools.partial(back_kernel, rounds, per), out_shape=[ja...  2.76 us
  transfers between devices with their start and end apart: 24, of which 6 were waited for; matrix products, arithmetic and copies ran while one was open for 0% of the time, Pallas kernels for 37%

profile of v1, /device:TPU:1, one launch (start us, length us, event | category | flops | bytes accessed | tf_op | source)
XLA Modules:
  0.0 121.8 jit_solution(12809627466235114294)
XLA Ops:
  0.6 1.0 copy-done.3
  1.7 0.7 copy-done.9
  2.4 6.1 %shard_map.140 = (bf16[768,128]{1,0:T(8,128)(2,1)S(1)}, bf16[768,128]{1,0:T(8,128)(2,1)S(1)}, bf16[768,128]{1,0:T(8,128)(2,1)S(1)}) custom-call(s32[5,768]{1,0:T(8,128)S(1)} %copy-done.9, bf16[2048,128]{1,0:T(8,128)(2,1)S(1)} %copy-done.3), custom_call_target="tpu_custom_call" | custom-call | flops 12000000 | bytes 1000000 | tf_op jit(solution)/shard_map/pallas_call | solution.py:69
  8.5 1.5 %collective-permute-start.4 = (bf16[768,128]{1,0:T(8,128)(2,1)S(1)}, bf16[768,128]{1,0:T(8,128)(2,1)S(1)}, u32[]{:S(2)}, u32[]{:S(2)}) collective-permute-start(bf16[768,128]{1,0:T(8,128)(2,1)S(1)} %get-tuple-element.20), channel_id=1, source_target_pairs={{0,1},{1,0},{2,3},{3,2},{4,5},{5,4},{6,7},{7,6},{8,9},{9,8},{10,11... | collective-permute-start | bytes 589832 | tf_op jit(solution)/shard_map/ppermute | solution.py:302
  10.0 1.3 %collective-permute-start.3 = (bf16[768,128]{1,0:T(8,128)(2,1)S(1)}, bf16[768,128]{1,0:T(8,128)(2,1)S(1)}, u32[]{:S(2)}, u32[]{:S(2)}) collective-permute-start(bf16[768,128]{1,0:T(8,128)(2,1)S(1)} %get-tuple-element.19), channel_id=1, source_target_pairs={{0,8},{1,9},{2,10},{3,11},{4,12},{5,13},{6,14},{7,15},{8,0},{9,1},... | collective-permute-start | bytes 589832 | tf_op jit(solution)/shard_map/ppermute | solution.py:302
  11.3 1.6 %collective-permute-start.2 = (bf16[768,128]{1,0:T(8,128)(2,1)S(1)}, bf16[768,128]{1,0:T(8,128)(2,1)S(1)}, u32[]{:S(2)}, u32[]{:S(2)}) collective-permute-start(bf16[768,128]{1,0:T(8,128)(2,1)S(1)} %get-tuple-element.18), channel_id=1, source_target_pairs={{0,2},{1,3},{2,0},{3,1},{4,6},{5,7},{6,4},{7,5},{8,10},{9,11},{10,... | collective-permute-start | bytes 589832 | tf_op jit(solution)/shard_map/ppermute | solution.py:302
  13.0 4.5 %shard_map.139 = (bf16[768,128]{1,0:T(8,128)(2,1)S(1)}, bf16[768,128]{1,0:T(8,128)(2,1)S(1)}) custom-call(s32[5,768]{1,0:T(8,128)S(1)} %copy-done.9, bf16[2048,128]{1,0:T(8,128)(2,1)S(1)} %copy-done.3), custom_call_target="tpu_custom_call" | custom-call | flops 8000000 | bytes 1000000 | tf_op jit(solution)/shard_map/pallas_call | solution.py:69
  17.5 2.5 %collective-permute-start.1 = (bf16[768,128]{1,0:T(8,128)(2,1)S(1)}, bf16[768,128]{1,0:T(8,128)(2,1)S(1)}, u32[]{:S(2)}, u32[]{:S(2)}) collective-permute-start(bf16[768,128]{1,0:T(8,128)(2,1)S(1)} %get-tuple-element.17), channel_id=1, source_target_pairs={{0,16},{1,17},{2,18},{3,19},{4,20},{5,21},{6,22},{7,23},{8,24},{9,... | collective-permute-start | bytes 589832 | tf_op jit(solution)/shard_map/ppermute | solution.py:302
  20.0 3.3 %collective-permute-start = (bf16[768,128]{1,0:T(8,128)(2,1)S(1)}, bf16[768,128]{1,0:T(8,128)(2,1)S(1)}, u32[]{:S(2)}, u32[]{:S(2)}) collective-permute-start(bf16[768,128]{1,0:T(8,128)(2,1)S(1)} %get-tuple-element.16), channel_id=1, source_target_pairs={{0,4},{1,5},{2,6},{3,7},{4,0},{5,1},{6,2},{7,3},{8,12},{9,13},{10,... | collective-permute-start | bytes 589832 | tf_op jit(solution)/shard_map/ppermute | solution.py:302
  23.3 4.3 %copy-done.5 = bf16[16,22,128,128]{3,2,1,0:T(8,128)(2,1)S(1)} copy-done((bf16[16,22,128,128]{3,2,1,0:T(8,128)(2,1)S(1)}, bf16[16,22,128,128]{3,2,1,0:T(8,128)(2,1)}, u32[]{:S(2)}) %copy-start.5) | copy-done | bytes 11534360
  27.6 0.7 copy-done.12
  28.3 9.4 %shard_map.141.dense_ref = bf16[16,2048,128]{2,1,0:T(8,128)(2,1)S(1)} custom-call(s32[16,22]{1,0:T(8,128)S(1)} %copy-done.12, bf16[16,22,128,128]{3,2,1,0:T(8,128)(2,1)S(1)} %copy-done.5), custom_call_target="tpu_custom_call" | custom-call | flops 16000000 | bytes 11534336 | tf_op jit(solution)/shard_map/pallas_call | solution.py:115
  37.7 2.9 %shard_map.142.refs_0_ = f32[2048,128]{1,0:T(8,128)S(1)} custom-call(bf16[16,2048,128]{2,1,0:T(8,128)(2,1)S(1)} %shard_map.141.dense_ref, bf16[2048,128]{1,0:T(8,128)(2,1)S(1)} %copy-done.4), custom_call_target="tpu_custom_call" | custom-call | flops 1073741824 | bytes 1048576 | tf_op jit(solution)/shard_map/pallas_call | solution.py:151
  40.6 3.2 %copy-done.2 = bf16[16,2048,128]{2,1,0:T(8,128)(2,1)} copy-done((bf16[16,2048,128]{2,1,0:T(8,128)(2,1)}, bf16[16,2048,128]{2,1,0:T(8,128)(2,1)S(1)}, u32[]{:S(2)}) %copy-start.2) | copy-done | bytes 8388632
  43.7 4.0 %copy-done.6 = bf16[16,20,128,128]{3,2,1,0:T(8,128)(2,1)S(1)} copy-done((bf16[16,20,128,128]{3,2,1,0:T(8,128)(2,1)S(1)}, bf16[16,20,128,128]{3,2,1,0:T(8,128)(2,1)}, u32[]{:S(2)}) %copy-start.6) | copy-done | bytes 10485784
  47.7 8.7 %shard_map.138.dense_ref = bf16[30,2048,128]{2,1,0:T(8,128)(2,1)S(1)} custom-call(s32[16,20]{1,0:T(8,128)S(1)} %copy-done.13, bf16[16,20,128,128]{3,2,1,0:T(8,128)(2,1)S(1)} %copy-done.6), custom_call_target="tpu_custom_call" | custom-call | flops 16000000 | bytes 10485760 | tf_op jit(solution)/shard_map/pallas_call | solution.py:115
  56.5 1.5 %shard_map.143.refs_0_ = f32[2048,128]{1,0:T(8,128)S(1)} custom-call(bf16[30,2048,128]{2,1,0:T(8,128)(2,1)S(1)} %shard_map.138.dense_ref, bf16[768,128]{1,0:T(8,128)(2,1)S(1)} %collective-permute-done.4.x_ref, f32[2048,128]{1,0:T(8,128)S(1)} %shard_map.142.refs_0_), custom_call_target="tpu_custom_call" | custom-call | flops 402653184 | bytes 1048576 | tf_op jit(solution)/shard_map/pallas_call | solution.py:151
  58.0 1.5 %shard_map.144.refs_0_ = f32[2048,128]{1,0:T(8,128)S(1)} custom-call(bf16[30,2048,128]{2,1,0:T(8,128)(2,1)S(1)} %shard_map.138.dense_ref, bf16[768,128]{1,0:T(8,128)(2,1)S(1)} %collective-permute-done.3.x_ref, f32[2048,128]{1,0:T(8,128)S(1)} %shard_map.143.refs_0_), custom_call_target="tpu_custom_call" | custom-call | flops 402653184 | bytes 1048576 | tf_op jit(solution)/shard_map/pallas_call | solution.py:151
  59.5 1.5 %shard_map.145.refs_0_ = f32[2048,128]{1,0:T(8,128)S(1)} custom-call(bf16[30,2048,128]{2,1,0:T(8,128)(2,1)S(1)} %shard_map.138.dense_ref, bf16[768,128]{1,0:T(8,128)(2,1)S(1)} %collective-permute-done.2.x_ref, f32[2048,128]{1,0:T(8,128)S(1)} %shard_map.144.refs_0_), custom_call_target="tpu_custom_call" | custom-call | flops 402653184 | bytes 1048576 | tf_op jit(solution)/shard_map/pallas_call | solution.py:151
  61.0 1.5 %shard_map.146.refs_0_ = f32[2048,128]{1,0:T(8,128)S(1)} custom-call(bf16[30,2048,128]{2,1,0:T(8,128)(2,1)S(1)} %shard_map.138.dense_ref, bf16[768,128]{1,0:T(8,128)(2,1)S(1)} %collective-permute-done.1.x_ref, f32[2048,128]{1,0:T(8,128)S(1)} %shard_map.145.refs_0_), custom_call_target="tpu_custom_call" | custom-call | flops 402653184 | bytes 1048576 | tf_op jit(solution)/shard_map/pallas_call | solution.py:151
  62.5 1.5 %shard_map.147.sum_ref = f32[2048,128]{1,0:T(8,128)S(1)} custom-call(bf16[30,2048,128]{2,1,0:T(8,128)(2,1)S(1)} %shard_map.138.dense_ref, bf16[768,128]{1,0:T(8,128)(2,1)S(1)} %collective-permute-done.x_ref, f32[2048,128]{1,0:T(8,128)S(1)} %shard_map.146.refs_0_), custom_call_target="tpu_custom_call" | custom-call | flops 402653184 | bytes 1048576 | tf_op jit(solution)/shard_map/pallas_call | solution.py:151
  64.1 1.6 %shard_map.148 = (bf16[2048,128]{1,0:T(8,128)(2,1)}, bf16[2048,128]{1,0:T(8,128)(2,1)S(1)}, bf16[2048,128]{1,0:T(8,128)(2,1)S(1)}, bf16[128,2048]{1,0:T(8,128)(2,1)S(1)}) custom-call(f32[2048,128]{1,0:T(8,128)S(1)} %shard_map.147.sum_ref, bf16[2048,128]{1,0:T(8,128)(2,1)S(1)} %copy-done.4, bf16[2048,128]{1,0:T(8,128)(2,1)S(1)} %copy-done.7, ...), custom_call_target="tpu_custom_call" | custom-call | flops 201326592 | bytes 5000000 | tf_op jit(solution)/shard_map/pallas_call | solution.py:188
  65.7 0.5 shard_map.155
  66.2 1.3 %collective-permute-start.10 = (f32[128,128]{1,0:T(8,128)S(1)}, f32[128,128]{1,0:T(8,128)S(1)}, u32[]{:S(2)}, u32[]{:S(2)}) collective-permute-start(f32[128,128]{1,0:T(8,128)S(1)} %dynamic-slice_bitcast_fusion), channel_id=1, source_target_pairs={{0,1},{1,0},{2,3},{3,2},{4,5},{5,4},{6,7},{7,6},{8,9},{9,8},{10,11... | collective-permute-start | bytes 196616 | tf_op jit(solution)/shard_map/ppermute | solution.py:302
  67.5 0.9 collective-permute-done.10
  68.6 3.8 %collective-permute-start.13 = (f32[32,128]{1,0:T(8,128)S(1)}, f32[32,128]{1,0:T(8,128)S(1)}, u32[]{:S(2)}, u32[]{:S(2)}) collective-permute-start(f32[32,128]{1,0:T(8,128)S(1)} %get-tuple-element.30), channel_id=1, source_target_pairs={{0,6},{1,7},{2,4},{3,5},{4,2},{5,3},{6,0},{7,1},{8,14},{9,15},{10,... | collective-permute-start | bytes 49160 | tf_op jit(solution)/shard_map/ppermute | solution.py:302
  72.7 1.1 collective-permute-done.13
  73.9 1.4 %collective-permute-start.15 = (f32[32,128]{1,0:T(8,128)S(1)}, f32[32,128]{1,0:T(8,128)S(1)}, u32[]{:S(2)}, u32[]{:S(2)}) collective-permute-start(f32[32,128]{1,0:T(8,128)S(1)} %fusion), channel_id=1, source_target_pairs={{0,16},{1,17},{2,18},{3,19},{4,20},{5,21},{6,22},{7,23},{8,24},{9,... | collective-permute-start | bytes 49160 | tf_op jit(solution)/shard_map/ppermute | solution.py:302
  75.3 2.5 %collective-permute-start.16 = (f32[32,128]{1,0:T(8,128)S(1)}, f32[32,128]{1,0:T(8,128)S(1)}, u32[]{:S(2)}, u32[]{:S(2)}) collective-permute-start(f32[32,128]{1,0:T(8,128)S(1)} %fusion), channel_id=1, source_target_pairs={{0,24},{1,25},{2,26},{3,27},{4,28},{5,29},{6,30},{7,31},{8,16},{9,... | collective-permute-start | bytes 49160 | tf_op jit(solution)/shard_map/ppermute | solution.py:302
  77.7 5.5 %copy-done.1 = bf16[30,2048,128]{2,1,0:T(8,128)(2,1)S(1)} copy-done((bf16[30,2048,128]{2,1,0:T(8,128)(2,1)S(1)}, bf16[30,2048,128]{2,1,0:T(8,128)(2,1)}, u32[]{:S(2)}) %copy-start.1) | copy-done | bytes 15728664
  83.2 1.5 %shard_map.150 = (bf16[768,128]{1,0:T(8,128)(2,1)S(1)}, bf16[768,128]{1,0:T(8,128)(2,1)S(1)}, bf16[768,128]{1,0:T(8,128)(2,1)S(1)}) custom-call(bf16[128,2048]{1,0:T(8,128)(2,1)S(1)} %get-tuple-element.22.st_ref, bf16[30,2048,128]{2,1,0:T(8,128)(2,1)S(1)} %copy-done.1), custom_call_target="tpu_custom_call" | custom-call | flops 1207959552 | bytes 500000 | tf_op jit(solution)/shard_map/pallas_call | solution.py:232
  84.7 1.4 %collective-permute-start.17 = (f32[32,128]{1,0:T(8,128)S(1)}, f32[32,128]{1,0:T(8,128)S(1)}, u32[]{:S(2)}, u32[]{:S(2)}) collective-permute-start(f32[32,128]{1,0:T(8,128)S(1)} %add_add_fusion.1), channel_id=1, source_target_pairs={{0,32},{1,33},{2,34},{3,35},{4,36},{5,37},{6,38},{7,39},{8,40},{9,... | collective-permute-start | bytes 49160 | tf_op jit(solution)/shard_map/ppermute | solution.py:302
  86.1 2.6 %collective-permute-start.18 = (f32[32,128]{1,0:T(8,128)S(1)}, f32[32,128]{1,0:T(8,128)S(1)}, u32[]{:S(2)}, u32[]{:S(2)}) collective-permute-start(f32[32,128]{1,0:T(8,128)S(1)} %add_add_fusion.1), channel_id=1, source_target_pairs={{0,64},{1,65},{2,66},{3,67},{4,68},{5,69},{6,70},{7,71},{8,72},{9,... | collective-permute-start | bytes 49160 | tf_op jit(solution)/shard_map/ppermute | solution.py:302
  88.7 0.7 shard_map.153
  89.4 0.8 collective-permute-done.18
  90.2 2.3 %collective-permute-done.19 = f32[32,128]{1,0:T(8,128)S(1)} collective-permute-done((f32[32,128]{1,0:T(8,128)S(1)}, f32[32,128]{1,0:T(8,128)S(1)}, u32[]{:S(2)}, u32[]{:S(2)}) %collective-permute-start.19) | collective-permute-done | bytes 16416 | tf_op jit(solution)/shard_map/ppermute | solution.py:302
  92.9 3.3 %collective-permute-start.21 = (f32[32,128]{1,0:T(8,128)S(1)}, f32[32,128]{1,0:T(8,128)S(1)}, u32[]{:S(2)}, u32[]{:S(2)}) collective-permute-start(f32[32,128]{1,0:T(8,128)S(1)} %add_add_fusion), channel_id=1, source_target_pairs={{0,4},{1,5},{2,6},{3,7},{4,0},{5,1},{6,2},{7,3},{8,12},{9,13},{10,... | collective-permute-start | bytes 49160 | tf_op jit(solution)/shard_map/ppermute | solution.py:302
  96.5 0.6 shard_map.152
  97.1 4.9 %collective-permute-start.5 = (bf16[768,128]{1,0:T(8,128)(2,1)S(1)}, bf16[768,128]{1,0:T(8,128)(2,1)}, u32[]{:S(2)}, u32[]{:S(2)}) collective-permute-start(bf16[768,128]{1,0:T(8,128)(2,1)S(1)} %get-tuple-element.24), channel_id=1, source_target_pairs={{0,1},{1,0},{2,3},{3,2},{4,5},{5,4},{6,7},{7,6},{8,9},{9,8},{10,11... | collective-permute-start | bytes 589832 | tf_op jit(solution)/shard_map/ppermute | solution.py:302
  102.1 4.1 %collective-permute-start.9 = (bf16[768,128]{1,0:T(8,128)(2,1)S(1)}, bf16[768,128]{1,0:T(8,128)(2,1)}, u32[]{:S(2)}, u32[]{:S(2)}) collective-permute-start(bf16[768,128]{1,0:T(8,128)(2,1)S(1)} %shard_map.153), channel_id=1, source_target_pairs={{0,4},{1,5},{2,6},{3,7},{4,0},{5,1},{6,2},{7,3},{8,12},{9,13},{10,... | collective-permute-start | bytes 589832 | tf_op jit(solution)/shard_map/ppermute | solution.py:302
  106.2 1.4 %collective-permute-start.8 = (bf16[768,128]{1,0:T(8,128)(2,1)S(1)}, bf16[768,128]{1,0:T(8,128)(2,1)}, u32[]{:S(2)}, u32[]{:S(2)}) collective-permute-start(bf16[768,128]{1,0:T(8,128)(2,1)S(1)} %shard_map.152), channel_id=1, source_target_pairs={{0,16},{1,17},{2,18},{3,19},{4,20},{5,21},{6,22},{7,23},{8,24},{9,... | collective-permute-start | bytes 589832 | tf_op jit(solution)/shard_map/ppermute | solution.py:302
  107.6 1.5 %shard_map.149.acc_ref = f32[2048,128]{1,0:T(8,128)S(1)} custom-call(bf16[128,2048]{1,0:T(8,128)(2,1)S(1)} %get-tuple-element.22.st_ref, bf16[16,2048,128]{2,1,0:T(8,128)(2,1)S(1)} %bitcast.28, bf16[2048,128]{1,0:T(8,128)(2,1)S(1)} %get-tuple-element.23.gp_ref, bf16[128,128]{1,0:T(8,128)(2,1)S(1)} %copy-done.8), custom_call_target="tpu_custom_call" | custom-call | flops 1073741824 | bytes 1500000 | tf_op jit(solution)/shard_map/pallas_call | solution.py:254
  109.1 0.6 gather_fusion
  109.7 1.3 %collective-permute-start.23 = (f32[128,128]{1,0:T(8,128)S(1)}, f32[128,128]{1,0:T(8,128)S(1)}, u32[]{:S(2)}, u32[]{:S(2)}) collective-permute-start(f32[128,128]{1,0:T(8,128)S(1)} %bitcast.35), channel_id=1, source_target_pairs={{0,1},{1,0},{2,3},{3,2},{4,5},{5,4},{6,7},{7,6},{8,9},{9,8},{10,11... | collective-permute-start | bytes 196616 | tf_op jit(solution)/shard_map/ppermute | solution.py:302
  111.0 3.9 %shard_map.151.acc_ref = f32[2048,128]{1,0:T(8,128)S(1)} custom-call(s32[5,768]{1,0:T(8,128)S(1)} %copy-done.10, f32[2048,128]{1,0:T(8,128)S(1)} %shard_map.149.acc_ref, bf16[768,128]{1,0:T(8,128)(2,1)} %collective-permute-done.5.refs_0_, bf16[768,128]{1,0:T(8,128)(2,1)} %collective-permute-done.6.refs_1_), custom_call_target="tpu_custom_call" | custom-call | flops 805306368 | bytes 2000000 | tf_op jit(solution)/shard_map/pallas_call | solution.py:287
  114.9 0.5 collective-permute-done.9.refs_2_
  115.4 5.7 %shard_map.154 = f32[2048,128]{1,0:T(8,128)} custom-call(s32[5,768]{1,0:T(8,128)S(1)} %copy-done.10, f32[2048,128]{1,0:T(8,128)S(1)} %shard_map.151.acc_ref, bf16[768,128]{1,0:T(8,128)(2,1)S(1)} %collective-permute-done.7.refs_0_, bf16[768,128]{1,0:T(8,128)(2,1)} %collective-permute-done.8.refs_1_, bf16[768,128]{1,0:T(8,128)(2,1)} %collective-permute-done.9.refs_2_), custom_call_target="tpu_custom_call" | custom-call | flops 1207959552 | bytes 2000000 | tf_op jit(solution)/shard_map/pallas_call | solution.py:287
  121.1 0.7 select_multiply_fusion
  (66 shorter events, 1.4 us)
Async XLA Ops:
  0.6 1.0 copy-start.3
  1.7 0.7 copy-start.9
  2.4 35.3 %copy-start.4 = (bf16[2048,128]{1,0:T(8,128)(2,1)S(1)}, bf16[2048,128]{1,0:T(8,128)(2,1)}, u32[]{:S(2)}) copy-start(bf16[2048,128]{1,0:T(8,128)(2,1)} %x_ref.9) | copy-start | bytes 1572868
  8.5 47.9 %collective-permute-start.4 = (bf16[768,128]{1,0:T(8,128)(2,1)S(1)}, bf16[768,128]{1,0:T(8,128)(2,1)S(1)}, u32[]{:S(2)}, u32[]{:S(2)}) collective-permute-start(bf16[768,128]{1,0:T(8,128)(2,1)S(1)} %get-tuple-element.20), channel_id=1, source_target_pairs={{0,1},{1,0},{2,3},{3,2},{4,5},{5,4},{6,7},{7,6},{8,9},{9,8},{10,11... | collective-permute-start | bytes 589832 | tf_op jit(solution)/shard_map/ppermute | solution.py:302
  10.0 47.9 %collective-permute-start.3 = (bf16[768,128]{1,0:T(8,128)(2,1)S(1)}, bf16[768,128]{1,0:T(8,128)(2,1)S(1)}, u32[]{:S(2)}, u32[]{:S(2)}) collective-permute-start(bf16[768,128]{1,0:T(8,128)(2,1)S(1)} %get-tuple-element.19), channel_id=1, source_target_pairs={{0,8},{1,9},{2,10},{3,11},{4,12},{5,13},{6,14},{7,15},{8,0},{9,1},... | collective-permute-start | bytes 589832 | tf_op jit(solution)/shard_map/ppermute | solution.py:302
  11.3 48.1 %collective-permute-start.2 = (bf16[768,128]{1,0:T(8,128)(2,1)S(1)}, bf16[768,128]{1,0:T(8,128)(2,1)S(1)}, u32[]{:S(2)}, u32[]{:S(2)}) collective-permute-start(bf16[768,128]{1,0:T(8,128)(2,1)S(1)} %get-tuple-element.18), channel_id=1, source_target_pairs={{0,2},{1,3},{2,0},{3,1},{4,6},{5,7},{6,4},{7,5},{8,10},{9,11},{10,... | collective-permute-start | bytes 589832 | tf_op jit(solution)/shard_map/ppermute | solution.py:302
  17.5 43.5 %collective-permute-start.1 = (bf16[768,128]{1,0:T(8,128)(2,1)S(1)}, bf16[768,128]{1,0:T(8,128)(2,1)S(1)}, u32[]{:S(2)}, u32[]{:S(2)}) collective-permute-start(bf16[768,128]{1,0:T(8,128)(2,1)S(1)} %get-tuple-element.17), channel_id=1, source_target_pairs={{0,16},{1,17},{2,18},{3,19},{4,20},{5,21},{6,22},{7,23},{8,24},{9,... | collective-permute-start | bytes 589832 | tf_op jit(solution)/shard_map/ppermute | solution.py:302
  20.0 42.5 %collective-permute-start = (bf16[768,128]{1,0:T(8,128)(2,1)S(1)}, bf16[768,128]{1,0:T(8,128)(2,1)S(1)}, u32[]{:S(2)}, u32[]{:S(2)}) collective-permute-start(bf16[768,128]{1,0:T(8,128)(2,1)S(1)} %get-tuple-element.16), channel_id=1, source_target_pairs={{0,4},{1,5},{2,6},{3,7},{4,0},{5,1},{6,2},{7,3},{8,12},{9,13},{10,... | collective-permute-start | bytes 589832 | tf_op jit(solution)/shard_map/ppermute | solution.py:302
  23.3 4.3 %copy-start.5 = (bf16[16,22,128,128]{3,2,1,0:T(8,128)(2,1)S(1)}, bf16[16,22,128,128]{3,2,1,0:T(8,128)(2,1)}, u32[]{:S(2)}) copy-start(bf16[16,22,128,128]{3,2,1,0:T(8,128)(2,1)} %tiles_ref.3) | copy-start | bytes 34603012
  27.6 0.7 copy-start.12
  28.3 15.5 %copy-start.13 = (s32[16,20]{1,0:T(8,128)S(1)}, s32[16,20]{1,0:T(8,128)}, u32[]{:S(2)}) copy-start(s32[16,20]{1,0:T(8,128)} %cols_ref.2) | copy-start | bytes 3844
  40.5 3.2 %copy-start.2 = (bf16[16,2048,128]{2,1,0:T(8,128)(2,1)}, bf16[16,2048,128]{2,1,0:T(8,128)(2,1)S(1)}, u32[]{:S(2)}) copy-start(bf16[16,2048,128]{2,1,0:T(8,128)(2,1)S(1)} %shard_map.141.dense_ref) | copy-start | bytes 25165828
  43.7 4.0 %copy-start.6 = (bf16[16,20,128,128]{3,2,1,0:T(8,128)(2,1)S(1)}, bf16[16,20,128,128]{3,2,1,0:T(8,128)(2,1)}, u32[]{:S(2)}) copy-start(bf16[16,20,128,128]{3,2,1,0:T(8,128)(2,1)} %tiles_ref.2) | copy-start | bytes 31457284
  56.4 6.1 %copy-start = (bf16[30,2048,128]{2,1,0:T(8,128)(2,1)}, bf16[30,2048,128]{2,1,0:T(8,128)(2,1)S(1)}, u32[]{:S(2)}) copy-start(bf16[30,2048,128]{2,1,0:T(8,128)(2,1)S(1)} %shard_map.138.dense_ref) | copy-start | bytes 47185924
  62.4 1.6 %copy-start.7 = (bf16[2048,128]{1,0:T(8,128)(2,1)S(1)}, bf16[2048,128]{1,0:T(8,128)(2,1)}, u32[]{:S(2)}) copy-start(bf16[2048,128]{1,0:T(8,128)(2,1)} %ct_ref.1) | copy-start | bytes 1572868
  62.5 1.6 %copy-start.8 = (bf16[128,128]{1,0:T(8,128)(2,1)S(1)}, bf16[128,128]{1,0:T(8,128)(2,1)}, u32[]{:S(2)}) copy-start(bf16[128,128]{1,0:T(8,128)(2,1)} %ws_ref.3) | copy-start | bytes 98308
  62.5 1.6 %copy-start.11 = (bf16[128,128]{1,0:T(8,128)(2,1)S(1)}, bf16[128,128]{1,0:T(8,128)(2,1)}, u32[]{:S(2)}) copy-start(bf16[128,128]{1,0:T(8,128)(2,1)} %wn_ref.1) | copy-start | bytes 98308
  62.5 1.6 %copy-start.14 = (s32[2048]{0:T(1024)S(1)}, s32[2048]{0:T(1024)}, u32[]{:S(2)}) copy-start(s32[2048]{0:T(1024)} %param.20) | copy-start | bytes 24580
  62.5 1.6 %copy-start.15 = (f32[128]{0:T(128)S(1)}, f32[128]{0:T(128)}, u32[]{:S(2)}) copy-start(f32[128]{0:T(128)} %param.14) | copy-start | bytes 1540
  66.2 2.2 %collective-permute-start.10 = (f32[128,128]{1,0:T(8,128)S(1)}, f32[128,128]{1,0:T(8,128)S(1)}, u32[]{:S(2)}, u32[]{:S(2)}) collective-permute-start(f32[128,128]{1,0:T(8,128)S(1)} %dynamic-slice_bitcast_fusion), channel_id=1, source_target_pairs={{0,1},{1,0},{2,3},{3,2},{4,5},{5,4},{6,7},{7,6},{8,9},{9,8},{10,11... | collective-permute-start | bytes 196616 | tf_op jit(solution)/shard_map/ppermute | solution.py:302
  68.4 3.9 %collective-permute-start.11 = (f32[32,128]{1,0:T(8,128)S(1)}, f32[32,128]{1,0:T(8,128)S(1)}, u32[]{:S(2)}, u32[]{:S(2)}) collective-permute-start(f32[32,128]{1,0:T(8,128)S(1)} %get-tuple-element.32), channel_id=1, source_target_pairs={{0,2},{1,3},{2,0},{3,1},{4,6},{5,7},{6,4},{7,5},{8,10},{9,11},{10,... | collective-permute-start | bytes 49160 | tf_op jit(solution)/shard_map/ppermute | solution.py:302
  68.5 4.2 %collective-permute-start.12 = (f32[32,128]{1,0:T(8,128)S(1)}, f32[32,128]{1,0:T(8,128)S(1)}, u32[]{:S(2)}, u32[]{:S(2)}) collective-permute-start(f32[32,128]{1,0:T(8,128)S(1)} %get-tuple-element.31), channel_id=1, source_target_pairs={{0,4},{1,5},{2,6},{3,7},{4,0},{5,1},{6,2},{7,3},{8,12},{9,13},{10,... | collective-permute-start | bytes 49160 | tf_op jit(solution)/shard_map/ppermute | solution.py:302
  68.6 5.2 %collective-permute-start.13 = (f32[32,128]{1,0:T(8,128)S(1)}, f32[32,128]{1,0:T(8,128)S(1)}, u32[]{:S(2)}, u32[]{:S(2)}) collective-permute-start(f32[32,128]{1,0:T(8,128)S(1)} %get-tuple-element.30), channel_id=1, source_target_pairs={{0,6},{1,7},{2,4},{3,5},{4,2},{5,3},{6,0},{7,1},{8,14},{9,15},{10,... | collective-permute-start | bytes 49160 | tf_op jit(solution)/shard_map/ppermute | solution.py:302
  73.8 10.9 %collective-permute-start.14 = (f32[32,128]{1,0:T(8,128)S(1)}, f32[32,128]{1,0:T(8,128)S(1)}, u32[]{:S(2)}, u32[]{:S(2)}) collective-permute-start(f32[32,128]{1,0:T(8,128)S(1)} %fusion), channel_id=1, source_target_pairs={{0,8},{1,9},{2,10},{3,11},{4,12},{5,13},{6,14},{7,15},{8,0},{9,1},... | collective-permute-start | bytes 49160 | tf_op jit(solution)/shard_map/ppermute | solution.py:302
  73.9 10.8 %collective-permute-start.15 = (f32[32,128]{1,0:T(8,128)S(1)}, f32[32,128]{1,0:T(8,128)S(1)}, u32[]{:S(2)}, u32[]{:S(2)}) collective-permute-start(f32[32,128]{1,0:T(8,128)S(1)} %fusion), channel_id=1, source_target_pairs={{0,16},{1,17},{2,18},{3,19},{4,20},{5,21},{6,22},{7,23},{8,24},{9,... | collective-permute-start | bytes 49160 | tf_op jit(solution)/shard_map/ppermute | solution.py:302
  75.3 9.4 %collective-permute-start.16 = (f32[32,128]{1,0:T(8,128)S(1)}, f32[32,128]{1,0:T(8,128)S(1)}, u32[]{:S(2)}, u32[]{:S(2)}) collective-permute-start(f32[32,128]{1,0:T(8,128)S(1)} %fusion), channel_id=1, source_target_pairs={{0,24},{1,25},{2,26},{3,27},{4,28},{5,29},{6,30},{7,31},{8,16},{9,... | collective-permute-start | bytes 49160 | tf_op jit(solution)/shard_map/ppermute | solution.py:302
  77.7 5.5 %copy-start.1 = (bf16[30,2048,128]{2,1,0:T(8,128)(2,1)S(1)}, bf16[30,2048,128]{2,1,0:T(8,128)(2,1)}, u32[]{:S(2)}) copy-start(bf16[30,2048,128]{2,1,0:T(8,128)(2,1)} %copy-done) | copy-start | bytes 47185924
  84.7 4.7 %collective-permute-start.17 = (f32[32,128]{1,0:T(8,128)S(1)}, f32[32,128]{1,0:T(8,128)S(1)}, u32[]{:S(2)}, u32[]{:S(2)}) collective-permute-start(f32[32,128]{1,0:T(8,128)S(1)} %add_add_fusion.1), channel_id=1, source_target_pairs={{0,32},{1,33},{2,34},{3,35},{4,36},{5,37},{6,38},{7,39},{8,40},{9,... | collective-permute-start | bytes 49160 | tf_op jit(solution)/shard_map/ppermute | solution.py:302
  86.1 4.1 %collective-permute-start.18 = (f32[32,128]{1,0:T(8,128)S(1)}, f32[32,128]{1,0:T(8,128)S(1)}, u32[]{:S(2)}, u32[]{:S(2)}) collective-permute-start(f32[32,128]{1,0:T(8,128)S(1)} %add_add_fusion.1), channel_id=1, source_target_pairs={{0,64},{1,65},{2,66},{3,67},{4,68},{5,69},{6,70},{7,71},{8,72},{9,... | collective-permute-start | bytes 49160 | tf_op jit(solution)/shard_map/ppermute | solution.py:302
  88.7 3.8 %collective-permute-start.19 = (f32[32,128]{1,0:T(8,128)S(1)}, f32[32,128]{1,0:T(8,128)S(1)}, u32[]{:S(2)}, u32[]{:S(2)}) collective-permute-start(f32[32,128]{1,0:T(8,128)S(1)} %add_add_fusion.1), channel_id=1, source_target_pairs={{0,96},{1,97},{2,98},{3,99},{4,100},{5,101},{6,102},{7,103},{8,104... | collective-permute-start | bytes 49160 | tf_op jit(solution)/shard_map/ppermute | solution.py:302
  89.4 18.3 %slice-start = ((s8[8388608]{0:T(1024)(128)(4,1)}), s8[4194304]{0:T(1024)(128)(4,1)S(1)}, s32[]{:S(2)}) async-start(s8[8388608]{0:T(1024)(128)(4,1)} %bitcast.27), calls=%async_computation | async-start | bytes 8388608
  92.5 15.1 %slice-start.1 = ((s8[8388608]{0:T(1024)(128)(4,1)}), s8[4194304]{0:T(1024)(128)(4,1)S(1)}, s32[]{:S(2)}) async-start(s8[8388608]{0:T(1024)(128)(4,1)} %bitcast.27), calls=%async_computation.1 | async-start | bytes 8388608
  92.5 18.5 %copy-start.10 = (s32[5,768]{1,0:T(8,128)S(1)}, s32[5,768]{1,0:T(8,128)}, u32[]{:S(2)}) copy-start(s32[5,768]{1,0:T(8,128)} %rows_ref.7) | copy-start | bytes 46084
  92.5 9.5 %collective-permute-start.20 = (f32[32,128]{1,0:T(8,128)S(1)}, f32[32,128]{1,0:T(8,128)S(1)}, u32[]{:S(2)}, u32[]{:S(2)}) collective-permute-start(f32[32,128]{1,0:T(8,128)S(1)} %add_add_fusion), channel_id=1, source_target_pairs={{0,2},{1,3},{2,0},{3,1},{4,6},{5,7},{6,4},{7,5},{8,10},{9,11},{10,... | collective-permute-start | bytes 49160 | tf_op jit(solution)/shard_map/ppermute | solution.py:302
  92.9 9.2 %collective-permute-start.21 = (f32[32,128]{1,0:T(8,128)S(1)}, f32[32,128]{1,0:T(8,128)S(1)}, u32[]{:S(2)}, u32[]{:S(2)}) collective-permute-start(f32[32,128]{1,0:T(8,128)S(1)} %add_add_fusion), channel_id=1, source_target_pairs={{0,4},{1,5},{2,6},{3,7},{4,0},{5,1},{6,2},{7,3},{8,12},{9,13},{10,... | collective-permute-start | bytes 49160 | tf_op jit(solution)/shard_map/ppermute | solution.py:302
  96.2 10.1 %collective-permute-start.22 = (f32[32,128]{1,0:T(8,128)S(1)}, f32[32,128]{1,0:T(8,128)S(1)}, u32[]{:S(2)}, u32[]{:S(2)}) collective-permute-start(f32[32,128]{1,0:T(8,128)S(1)} %add_add_fusion), channel_id=1, source_target_pairs={{0,6},{1,7},{2,4},{3,5},{4,2},{5,3},{6,0},{7,1},{8,14},{9,15},{10,... | collective-permute-start | bytes 49160 | tf_op jit(solution)/shard_map/ppermute | solution.py:302
  97.1 12.6 %collective-permute-start.5 = (bf16[768,128]{1,0:T(8,128)(2,1)S(1)}, bf16[768,128]{1,0:T(8,128)(2,1)}, u32[]{:S(2)}, u32[]{:S(2)}) collective-permute-start(bf16[768,128]{1,0:T(8,128)(2,1)S(1)} %get-tuple-element.24), channel_id=1, source_target_pairs={{0,1},{1,0},{2,3},{3,2},{4,5},{5,4},{6,7},{7,6},{8,9},{9,8},{10,11... | collective-permute-start | bytes 589832 | tf_op jit(solution)/shard_map/ppermute | solution.py:302
  102.1 8.9 %collective-permute-start.6 = (bf16[768,128]{1,0:T(8,128)(2,1)S(1)}, bf16[768,128]{1,0:T(8,128)(2,1)}, u32[]{:S(2)}, u32[]{:S(2)}) collective-permute-start(bf16[768,128]{1,0:T(8,128)(2,1)S(1)} %get-tuple-element.25), channel_id=1, source_target_pairs={{0,8},{1,9},{2,10},{3,11},{4,12},{5,13},{6,14},{7,15},{8,0},{9,1},... | collective-permute-start | bytes 589832 | tf_op jit(solution)/shard_map/ppermute | solution.py:302
  102.1 12.8 %collective-permute-start.7 = (bf16[768,128]{1,0:T(8,128)(2,1)S(1)}, bf16[768,128]{1,0:T(8,128)(2,1)S(1)}, u32[]{:S(2)}, u32[]{:S(2)}) collective-permute-start(bf16[768,128]{1,0:T(8,128)(2,1)S(1)} %get-tuple-element.26), channel_id=1, source_target_pairs={{0,2},{1,3},{2,0},{3,1},{4,6},{5,7},{6,4},{7,5},{8,10},{9,11},{10,... | collective-permute-start | bytes 589832 | tf_op jit(solution)/shard_map/ppermute | solution.py:302
  102.1 13.3 %collective-permute-start.9 = (bf16[768,128]{1,0:T(8,128)(2,1)S(1)}, bf16[768,128]{1,0:T(8,128)(2,1)}, u32[]{:S(2)}, u32[]{:S(2)}) collective-permute-start(bf16[768,128]{1,0:T(8,128)(2,1)S(1)} %shard_map.153), channel_id=1, source_target_pairs={{0,4},{1,5},{2,6},{3,7},{4,0},{5,1},{6,2},{7,3},{8,12},{9,13},{10,... | collective-permute-start | bytes 589832 | tf_op jit(solution)/shard_map/ppermute | solution.py:302
  106.2 9.2 %collective-permute-start.8 = (bf16[768,128]{1,0:T(8,128)(2,1)S(1)}, bf16[768,128]{1,0:T(8,128)(2,1)}, u32[]{:S(2)}, u32[]{:S(2)}) collective-permute-start(bf16[768,128]{1,0:T(8,128)(2,1)S(1)} %shard_map.152), channel_id=1, source_target_pairs={{0,16},{1,17},{2,18},{3,19},{4,20},{5,21},{6,22},{7,23},{8,24},{9,... | collective-permute-start | bytes 589832 | tf_op jit(solution)/shard_map/ppermute | solution.py:302
  109.7 11.4 %collective-permute-start.23 = (f32[128,128]{1,0:T(8,128)S(1)}, f32[128,128]{1,0:T(8,128)S(1)}, u32[]{:S(2)}, u32[]{:S(2)}) collective-permute-start(f32[128,128]{1,0:T(8,128)S(1)} %bitcast.35), channel_id=1, source_target_pairs={{0,1},{1,0},{2,3},{3,2},{4,5},{5,4},{6,7},{7,6},{8,9},{9,8},{10,11... | collective-permute-start | bytes 196616 | tf_op jit(solution)/shard_map/ppermute | solution.py:302

commit v2 on v0

v2 whole, which is shorter than its diff:
```python
import functools
import math

import jax
import jax.numpy as jnp
from jax import lax
from jax.experimental import pallas as pl
from jax.experimental.pallas import tpu as pltpu
from jax.sharding import PartitionSpec as P

TILE = 128
VMEM = pltpu.VMEM
LIMIT = 16 * 1024 * 1024


def vspec():
    return pl.BlockSpec(memory_space=VMEM)


def sspec():
    return pl.BlockSpec(memory_space=pltpu.SMEM)


def params(limit=LIMIT):
    return pltpu.CompilerParams(vmem_limit_bytes=limit)


def cost(flops, size, transcendentals=0):
    return pl.CostEstimate(flops=flops, bytes_accessed=size, transcendentals=transcendentals)


def pinned(array):
    return pltpu.with_memory_space_constraint(array, VMEM)


def nt_dot(left, right):
    return lax.dot_general(
        left, right, (((1,), (1,)), ((), ())), preferred_element_type=jnp.float32
    )


def nn_dot(left, right):
    return jnp.dot(left, right, preferred_element_type=jnp.float32)


def onehot(listed, base, rows):
    numbers = lax.broadcasted_iota(jnp.int32, (rows, listed.shape[1]), 0)
    return jnp.where(numbers == listed - base, 1.0, 0.0).astype(jnp.bfloat16)


def pick_kernel(rounds, turn, rows_ref, x_ref, *refs):
    outs = refs[: len(rounds)]
    if turn:
        xt_ref = refs[-1]
        for i in range(x_ref.shape[0] // TILE):
            xt_ref[:, i * TILE : (i + 1) * TILE] = x_ref[i * TILE : (i + 1) * TILE, :].T
    else:
        xt_ref = x_ref
    step = 2 * TILE
    for out_ref, r in zip(outs, rounds):
        for k in range(0, rows_ref.shape[1], step):
            table = onehot(rows_ref[r : r + 1, k : k + step], 0, xt_ref.shape[1])
            out_ref[:, k : k + step] = nn_dot(xt_ref[...], table).astype(jnp.bfloat16)


def pick_rows(rounds, send_rows, features, turn):
    rows, width = features.shape if turn else features.shape[::-1]
    boundary = send_rows.shape[1]
    outs = [jax.ShapeDtypeStruct((width, boundary), jnp.bfloat16) for _ in rounds]
    if turn:
        outs.append(jax.ShapeDtypeStruct((width, rows), jnp.bfloat16))
    return pl.pallas_call(
        functools.partial(pick_kernel, rounds, turn),
        out_shape=outs,
        in_specs=[vspec()] * 2,
        out_specs=[vspec()] * len(outs),
        compiler_params=params(),
        cost_estimate=cost(2 * rows * boundary * len(rounds) * width, 1_000_000),
    )(send_rows, features)


def densify_kernel(lc, hc, lt, ht, dl0, dl1, dh0, dh1, lslots, hslots, zeros, sems, zsems):
    half = lt.shape[0] // 2
    depth = lslots.shape[0]
    dense = (dl0, dl1, dh0, dh1)

    def fetch(i, slot):
        return [
            pltpu.make_async_copy(
                src.at[i + p * half], dst.at[slot, p], sems.at[slot, 2 * q + p]
            )
            for q, (src, dst) in enumerate(((lt, lslots), (ht, hslots)))
            for p in range(2)
        ]

    def clear(i, slot):
        rows = pl.ds(pl.multiple_of(i * TILE, TILE), TILE)
        return [
            pltpu.make_async_copy(
                zeros.at[pl.ds(0, d.shape[0])], d.at[:, rows, :], zsems.at[slot, k]
            )
            for k, d in enumerate(dense)
        ]

    for d in range(depth - 1):
        for copy in fetch(d, d):
            copy.start()
    zeros[...] = jnp.zeros_like(zeros)
    for copy in clear(0, 0):
        copy.start()

    def body(i, carry):
        slot, zslot = lax.rem(i, depth), lax.rem(i, 2)

        @pl.when(i + depth - 1 < half)
        def _():
            for copy in fetch(i + depth - 1, lax.rem(i + depth - 1, depth)):
                copy.start()

        @pl.when(i + 1 < half)
        def _():
            for copy in clear(i + 1, 1 - zslot):
                copy.start()

        for copy in clear(i, zslot):
            copy.wait()
        for copy in fetch(i, slot):
            copy.wait()
        rows = pl.ds(pl.multiple_of(i * TILE, TILE), TILE)
        for t in range(max(lt.shape[1], ht.shape[1])):
            jobs = []
            if t < lt.shape[1]:
                jobs += [(dl0, lc[i, t], lslots, 0), (dl1, lc[i + half, t], lslots, 1)]
            if t < ht.shape[1]:
                jobs += [(dh0, hc[i, t], hslots, 0), (dh1, hc[i + half, t], hslots, 1)]
            sums = [d[c, rows, :] + s[slot, p, t] for d, c, s, p in jobs]
            for (d, c, _, _), total in zip(jobs, sums):
                d[c, rows, :] = total
        return carry

    lax.fori_loop(0, half, body, 0)


def densify(local_cols, halo_cols, local_tiles, halo_tiles, halo_blocks):
    nblocks, local_count = local_cols.shape
    halo_count = halo_cols.shape[1]
    half = nblocks // 2 * TILE
    depth = 3
    slabs = (nblocks, nblocks, halo_blocks, halo_blocks)
    return pl.pallas_call(
        densify_kernel,
        out_shape=[VMEM((n, half, TILE), jnp.bfloat16) for n in slabs],
        in_specs=[sspec(), sspec()] + [pl.BlockSpec(memory_space=pltpu.HBM)] * 2,
        out_specs=[vspec()] * 4,
        scratch_shapes=[
            VMEM((depth, 2, local_count, TILE, TILE), jnp.bfloat16),
            VMEM((depth, 2, halo_count, TILE, TILE), jnp.bfloat16),
            VMEM((max(slabs), TILE, TILE), jnp.bfloat16),
            pltpu.SemaphoreType.DMA((depth, 4)),
            pltpu.SemaphoreType.DMA((2, 4)),
        ],
        compiler_params=params(34 * 1024 * 1024),
        cost_estimate=cost(16_000_000, nblocks * (local_count + halo_count) * TILE * TILE * 2),
    )(local_cols, halo_cols, local_tiles, halo_tiles)


def forward_kernel(first, n, has_acc, turned, d0_ref, d1_ref, x_ref, *refs):
    acc_ref, out_ref = refs if has_acc else (None, refs[0])
    right = x_ref[...].T if turned else x_ref[...]
    half, step = d0_ref.shape[1], 512
    for p, dense_ref in enumerate((d0_ref, d1_ref)):
        for j in range(0, half, step):
            left = jnp.concatenate(
                [dense_ref[first + c, j : j + step, :] for c in range(n)], axis=1
            )
            total = nn_dot(left, right)
            rows = slice(p * half + j, p * half + j + step)
            out_ref[rows, :] = total + acc_ref[rows, :] if has_acc else total


def forward(d0, d1, first, blocks, acc, turned):
    n = max(blocks.shape) // TILE
    rows = 2 * d0.shape[1]
    args = [pinned(d0), pinned(d1), blocks] + ([] if acc is None else [acc])
    return pl.pallas_call(
        functools.partial(forward_kernel, first, n, acc is not None, turned),
        out_shape=jax.ShapeDtypeStruct((rows, TILE), jnp.float32),
        in_specs=[vspec()] * len(args),
        out_specs=vspec(),
        compiler_params=params(),
        cost_estimate=cost(2 * rows * n * TILE * TILE, rows * TILE * 4),
    )(*args)


def middle_kernel(
    sum_ref, x_ref, ct_ref, deg_ref, ws_ref, wn_ref, bias_ref, out_ref, gp_ref, st_ref, wg_ref, both
):
    for i in range(sum_ref.shape[0] // TILE):
        rows = slice(i * TILE, (i + 1) * TILE)
        line = deg_ref[i : i + 1, :].astype(jnp.float32)
        column = jnp.broadcast_to(line, (TILE, TILE)).T
        agg = (sum_ref[rows, :] / column).astype(jnp.bfloat16)
        both[rows, :TILE] = x_ref[rows, :]
        both[rows, TILE:] = agg
        preact = nn_dot(x_ref[rows, :], ws_ref[...]) + nn_dot(agg, wn_ref[...]) + bias_ref[...]
        sig = jax.nn.sigmoid(preact)
        out_ref[rows, :] = (preact * sig).astype(jnp.bfloat16)
        grad = ct_ref[rows, :].astype(jnp.float32) * sig * (1.0 + preact * (1.0 - sig))
        grad = grad.astype(jnp.bfloat16)
        gp_ref[rows, :] = grad
        st_ref[:, rows] = (nt_dot(wn_ref[...], grad) / line).astype(jnp.bfloat16)
    wg_ref[...] = lax.dot_general(
        both[...], gp_ref[...], (((0,), (0,)), ((), ())), preferred_element_type=jnp.float32
    )


def middle(summed, features, cotangent, degree, w_self, w_neigh, bias):
    rows, width = features.shape
    half = jax.ShapeDtypeStruct((rows, width), jnp.bfloat16)
    return pl.pallas_call(
        middle_kernel,
        out_shape=[
            half,
            half,
            jax.ShapeDtypeStruct((width, rows), jnp.bfloat16),
            jax.ShapeDtypeStruct((2 * width, width), jnp.float32),
        ],
        in_specs=[vspec()] * 7,
        out_specs=[vspec()] * 4,
        scratch_shapes=[VMEM((rows, 2 * width), jnp.bfloat16)],
        compiler_params=params(),
        cost_estimate=cost(2 * rows * 5 * width * width, 5_000_000, rows * width),
    )(summed, features, cotangent, degree, w_self, w_neigh, bias)


def beside(d0_ref, d1_ref, slab):
    return jnp.concatenate(
        [jnp.concatenate([d[slab], d[slab + 1]], axis=1) for d in (d0_ref, d1_ref)], axis=0
    )


def back_kernel(first, n, st_ref, d0_ref, d1_ref, before_ref, out_ref):
    for c in range(0, n, 2):
        product = nn_dot(st_ref[...], beside(d0_ref, d1_ref, first + c))
        out_ref[:, c * TILE : (c + 2) * TILE] = product.astype(jnp.bfloat16)


def back(first, n, scaled_t, d0, d1, before):
    width, rows = scaled_t.shape
    return pl.pallas_call(
        functools.partial(back_kernel, first, n),
        out_shape=jax.ShapeDtypeStruct((width, n * TILE), jnp.bfloat16),
        in_specs=[vspec()] * 3 + [pl.BlockSpec(memory_space=pl.ANY)],
        out_specs=vspec(),
        compiler_params=params(),
        cost_estimate=cost(2 * rows * n * TILE * width, 500_000),
    )(scaled_t, pinned(d0), pinned(d1), before)


def own_kernel(st_ref, d0_ref, d1_ref, gp_ref, ws_ref, before_ref, out_ref):
    for c in range(0, d0_ref.shape[0], 2):
        rows = slice(c * TILE, (c + 2) * TILE)
        product = nn_dot(st_ref[...], beside(d0_ref, d1_ref, c))
        out_ref[:, rows] = product + nt_dot(ws_ref[...], gp_ref[rows, :])


def own(scaled_t, d0, d1, grad_pre, w_self, before):
    width, rows = scaled_t.shape
    return pl.pallas_call(
        own_kernel,
        out_shape=jax.ShapeDtypeStruct((width, rows), jnp.float32),
        in_specs=[vspec()] * 5 + [pl.BlockSpec(memory_space=pl.ANY)],
        out_specs=vspec(),
        compiler_params=params(),
        cost_estimate=cost(2 * rows * rows * width, 1_500_000),
    )(scaled_t, pinned(d0), pinned(d1), grad_pre, w_self, before)


def place_kernel(rounds, last, rows_ref, acc_ref, *refs):
    returned, out_ref = refs[:-1], refs[-1]
    step = 2 * TILE
    for j in range(0, acc_ref.shape[1], step):
        total = acc_ref[:, j : j + step]
        for got_ref, r in zip(returned, rounds):
            total = total + nt_dot(got_ref[...], onehot(rows_ref[r : r + 1, :], j, step))
        if last:
            out_ref[j : j + step, :] = total.T
        else:
            out_ref[:, j : j + step] = total


def place_rows(rounds, last, send_rows, acc, returned):
    width, rows = acc.shape
    return pl.pallas_call(
        functools.partial(place_kernel, rounds, last),
        out_shape=jax.ShapeDtypeStruct((rows, width) if last else (width, rows), jnp.float32),
        in_specs=[vspec()] * (2 + len(rounds)),
        out_specs=vspec(),
        compiler_params=params(),
        cost_estimate=cost(2 * rows * len(rounds) * send_rows.shape[1] * width, 2_000_000),
    )(send_rows, acc, *returned)


def swapped(shard, mask):
    return lax.ppermute(shard, "dom", [(i, i ^ mask) for i in range(lax.axis_size("dom"))])


def summed_everywhere(parts):
    core = lax.axis_index("dom") & 1
    halves = parts.reshape(2, -1, parts.shape[1])
    total = halves[core] + swapped(halves[1 - core], 1)
    mask = 2
    while mask < lax.axis_size("dom"):
        total = total + swapped(total, mask)
        mask *= 2
    other = swapped(total, 1)
    return jnp.where(core == 0, total, other), jnp.where(core == 0, other, total)


def local(
    node_features,
    w_self,
    w_neigh,
    output_bias,
    local_tiles,
    halo_tiles,
    local_cols,
    halo_cols,
    send_rows,
    degree,
    cotangent,
):
    row_count, width = node_features.shape
    nblocks = local_tiles.shape[0]
    round_count, boundary = send_rows.shape
    per = boundary // TILE
    received = {}
    *picked, features_t = pick_rows((2, 4), send_rows, node_features, True)
    picked += pick_rows((1, 3, 0), send_rows, features_t, False)
    for r, rows in zip((2, 4, 1, 3, 0), picked):
        received[r] = swapped(rows, 1 << r)
    dl0, dl1, dh0, dh1 = densify(
        local_cols, halo_cols, local_tiles, halo_tiles, round_count * per
    )
    summed = forward(dl0, dl1, 0, node_features, None, False)
    for r in (0, 3, 1, 4, 2):
        summed = forward(dh0, dh1, r * per, received[r], summed, True)
    output, grad_pre, scaled_t, parts = middle(
        summed,
        node_features,
        cotangent,
        degree.reshape(nblocks, TILE),
        w_self,
        w_neigh,
        output_bias.reshape(1, width),
    )
    returned = {}
    before = scaled_t
    for r in (2, 4, 1, 3, 0):
        before = back(r * per, per, scaled_t, dh0, dh1, before)
        returned[r] = swapped(before, 1 << r)
    grad_self, grad_neigh = summed_everywhere(parts)
    grad_scale = 1.0 / math.sqrt(row_count * lax.axis_size("dom"))
    grads_t = own(scaled_t, dl0, dl1, grad_pre, w_self, before)
    for rounds in ((0, 3), (1, 4, 2)):
        grads_t = place_rows(
            rounds, 2 in rounds, send_rows, grads_t, [returned[r] for r in rounds]
        )
    return (output, grads_t, grad_self * grad_scale, grad_neigh * grad_scale)


def solution(mesh):
    in_specs = (
        P("dom", None),
        P(),
        P(),
        P(),
        P("dom", None, None, None),
        P("dom", None, None, None),
        P("dom", None),
        P("dom", None),
        P("dom", None),
        P("dom"),
        P("dom", None),
    )
    out_specs = (P("dom", None), P("dom", None), P(), P())
    return jax.shard_map(local, mesh=mesh, in_specs=in_specs, out_specs=out_specs, check_vma=False)
```

time: 370 us -> 98.6 us (0.27); the launches traced: 365 us -> 98.1 us
  waiting for transfers between devices: 133 us -> 5.97 us
  matrix products: 78.1 us -> 0 us
  local copies, waits for them, and re-layouts: 87.2 us -> 27.2 us
  other arithmetic: 37.7 us -> 0.73 us
  Pallas kernels: 0 us -> 32.1 us
  starting transfers between devices: 13.6 us -> 31.1 us
  between operations: 14.8 us -> 1 us
    psum x1 -> x0, waiting for transfers between devices: 133 us -> none  [local(): grad_self, grad_neigh = lax.psum((self_part, neigh_part), 'dom')]
    dot_general x12 -> x0, matrix products: 78.1 us -> none  [the longest x2 27.3 us: reduce_products(): jnp.einsum('btc,btjf->cjf', onehot_table, products, precision=lax.Precisi...]
    dot_general x3 -> x0, local copies, waits for them, and re-layouts: 47.4 us -> none  [the longest x2 47.1 us: reduce_products(): jnp.einsum('btij,bif->btjf', tiles, scaled, preferred_element_type=jnp.fl...]
    scatter-add x5 -> x0, other arithmetic: 34.1 us -> none  [local(): grad_features = grad_features.at[send_rows[round_index]].add(returned)]
    pallas_call x0 -> x18, Pallas kernels: none -> 32.1 us  [the longest x1 9.34 us: densify(): pl.pallas_call(densify_kernel, out_shape=[VMEM((n, half, TILE), jnp.bfloa...]
    gather x7 -> x0, local copies, waits for them, and re-layouts: 31.6 us -> none  [the longest x1 11.2 us: local(): halo_rows[halo_cols]]
    unnamed x44 -> x38, local copies, waits for them, and re-layouts: 5.43 us -> 27.2 us
    ppermute x10 -> x18, starting transfers between devices: 13.6 us -> 31.1 us  [swapped(): lax.ppermute(shard, 'dom', [(i, i ^ mask) for i in range(lax.axis_size('d...]
  transfers between devices with their start and end apart: 11 -> 18, of which waited for: 1 -> 3; matrix products, arithmetic and copies ran while one was open for 18% -> 0% of each run, Pallas kernels for 0% -> 27%
where the time goes in v2:
time: 98.6 us; the launch traced here: 98.1 us
  Pallas kernels  32.1 us (33%)
  starting transfers between devices  31.1 us (32%)
  local copies, waits for them, and re-layouts  27.2 us (28%)
  waiting for transfers between devices  5.97 us (6%)
  between operations  1 us (1%)
    ppermute x18, starting transfers between devices, swapped(): lax.ppermute(shard, 'dom', [(i, i ^ mask) for i in range(lax.axis_size('d...  31.1 us
    unnamed x38, local copies, waits for them, and re-layouts  27.2 us
    pallas_call x1, Pallas kernels, densify(): pl.pallas_call(densify_kernel, out_shape=[VMEM((n, half, TILE), jnp.bfloa...  9.34 us
    pallas_call x6, Pallas kernels, forward(): pl.pallas_call(functools.partial(forward_kernel, first, n, acc is not Non...  7.17 us
    pallas_call x2, Pallas kernels, place_rows(): pl.pallas_call(functools.partial(place_kernel, rounds, last), out_shape=j...  6.48 us
    ppermute x18, waiting for transfers between devices, swapped(): lax.ppermute(shard, 'dom', [(i, i ^ mask) for i in range(lax.axis_size('d...  5.97 us
    pallas_call x2, Pallas kernels, pick_rows(): pl.pallas_call(functools.partial(pick_kernel, rounds, turn), out_shape=ou...  2.91 us
    pallas_call x5, Pallas kernels, back(): pl.pallas_call(functools.partial(back_kernel, first, n), out_shape=jax.Sh...  2.89 us
  transfers between devices with their start and end apart: 18, of which 3 were waited for; matrix products, arithmetic and copies ran while one was open for 0% of the time, Pallas kernels for 27%

profile of v2, /device:TPU:1, one launch (start us, length us, event | category | flops | bytes accessed | tf_op | source)
XLA Modules:
  0.0 98.1 jit_solution(2068841301118772798)
XLA Ops:
  0.6 1.0 %copy-done.10 = bf16[2048,128]{1,0:T(8,128)(2,1)S(1)} copy-done((bf16[2048,128]{1,0:T(8,128)(2,1)S(1)}, bf16[2048,128]{1,0:T(8,128)(2,1)}, u32[]{:S(2)}) %copy-start.10) | copy-done | bytes 524312
  1.7 0.7 copy-done.17
  2.4 1.4 %shard_map.139 = (bf16[128,768]{1,0:T(8,128)(2,1)S(1)}, bf16[128,768]{1,0:T(8,128)(2,1)S(1)}, bf16[128,2048]{1,0:T(8,128)(2,1)S(1)}) custom-call(s32[5,768]{1,0:T(8,128)S(1)} %copy-done.17, bf16[2048,128]{1,0:T(8,128)(2,1)S(1)} %copy-done.10), custom_call_target="tpu_custom_call" | custom-call | flops 805306368 | bytes 1000000 | tf_op jit(solution)/shard_map/pallas_call | solution.py:72
  3.9 1.5 %shard_map.140 = (bf16[128,768]{1,0:T(8,128)(2,1)S(1)}, bf16[128,768]{1,0:T(8,128)(2,1)S(1)}, bf16[128,768]{1,0:T(8,128)(2,1)S(1)}) custom-call(s32[5,768]{1,0:T(8,128)S(1)} %copy-done.17, bf16[128,2048]{1,0:T(8,128)(2,1)S(1)} %get-tuple-element.22.x_ref), custom_call_target="tpu_custom_call" | custom-call | flops 1207959552 | bytes 1000000 | tf_op jit(solution)/shard_map/pallas_call | solution.py:72
  5.3 1.5 %collective-permute-start.4 = (bf16[128,768]{1,0:T(8,128)(2,1)S(1)}, bf16[128,768]{1,0:T(8,128)(2,1)S(1)}, u32[]{:S(2)}, u32[]{:S(2)}) collective-permute-start(bf16[128,768]{1,0:T(8,128)(2,1)S(1)} %get-tuple-element.25), channel_id=1, source_target_pairs={{0,1},{1,0},{2,3},{3,2},{4,5},{5,4},{6,7},{7,6},{8,9},{9,8},{10,11... | collective-permute-start | bytes 589832 | tf_op jit(solution)/shard_map/ppermute | solution.py:305
  6.8 1.3 %collective-permute-start.3 = (bf16[128,768]{1,0:T(8,128)(2,1)S(1)}, bf16[128,768]{1,0:T(8,128)(2,1)S(1)}, u32[]{:S(2)}, u32[]{:S(2)}) collective-permute-start(bf16[128,768]{1,0:T(8,128)(2,1)S(1)} %get-tuple-element.24), channel_id=1, source_target_pairs={{0,8},{1,9},{2,10},{3,11},{4,12},{5,13},{6,14},{7,15},{8,0},{9,1},... | collective-permute-start | bytes 589832 | tf_op jit(solution)/shard_map/ppermute | solution.py:305
  8.1 1.6 %collective-permute-start.2 = (bf16[128,768]{1,0:T(8,128)(2,1)S(1)}, bf16[128,768]{1,0:T(8,128)(2,1)S(1)}, u32[]{:S(2)}, u32[]{:S(2)}) collective-permute-start(bf16[128,768]{1,0:T(8,128)(2,1)S(1)} %get-tuple-element.23), channel_id=1, source_target_pairs={{0,2},{1,3},{2,0},{3,1},{4,6},{5,7},{6,4},{7,5},{8,10},{9,11},{10,... | collective-permute-start | bytes 589832 | tf_op jit(solution)/shard_map/ppermute | solution.py:305
  9.8 3.3 %collective-permute-start = (bf16[128,768]{1,0:T(8,128)(2,1)S(1)}, bf16[128,768]{1,0:T(8,128)(2,1)S(1)}, u32[]{:S(2)}, u32[]{:S(2)}) collective-permute-start(bf16[128,768]{1,0:T(8,128)(2,1)S(1)} %get-tuple-element.20), channel_id=1, source_target_pairs={{0,4},{1,5},{2,6},{3,7},{4,0},{5,1},{6,2},{7,3},{8,12},{9,13},{10,... | collective-permute-start | bytes 589832 | tf_op jit(solution)/shard_map/ppermute | solution.py:305
  13.1 2.5 %collective-permute-start.1 = (bf16[128,768]{1,0:T(8,128)(2,1)S(1)}, bf16[128,768]{1,0:T(8,128)(2,1)S(1)}, u32[]{:S(2)}, u32[]{:S(2)}) collective-permute-start(bf16[128,768]{1,0:T(8,128)(2,1)S(1)} %get-tuple-element.21), channel_id=1, source_target_pairs={{0,16},{1,17},{2,18},{3,19},{4,20},{5,21},{6,22},{7,23},{8,24},{9,... | collective-permute-start | bytes 589832 | tf_op jit(solution)/shard_map/ppermute | solution.py:305
  15.5 9.3 %shard_map.138 = (bf16[16,1024,128]{2,1,0:T(8,128)(2,1)S(1)}, bf16[16,1024,128]{2,1,0:T(8,128)(2,1)S(1)}, bf16[30,1024,128]{2,1,0:T(8,128)(2,1)S(1)}, bf16[30,1024,128]{2,1,0:T(8,128)(2,1)S(1)}) custom-call(s32[16,22]{1,0:T(8,128)} %lc.1, s32[16,20]{1,0:T(8,128)} %hc.1, bf16[16,22,128,128]{3,2,1,0:T(8,128)(2,1)} %lt.9, bf16[16,20,128,128]{3,2,1,0:T(8,128)(2,1)} %ht.1), custom_call_target="tpu_custom_call" | custom-call | flops 16000000 | bytes 22020096 | tf_op jit(solution)/shard_map/pallas_call | solution.py:150
  24.9 3.1 %copy-done = bf16[30,1024,128]{2,1,0:T(8,128)(2,1)} copy-done((bf16[30,1024,128]{2,1,0:T(8,128)(2,1)}, bf16[30,1024,128]{2,1,0:T(8,128)(2,1)S(1)}, u32[]{:S(2)}) %copy-start) | copy-done | bytes 7864344
  28.0 3.1 %copy-done.3 = bf16[30,1024,128]{2,1,0:T(8,128)(2,1)} copy-done((bf16[30,1024,128]{2,1,0:T(8,128)(2,1)}, bf16[30,1024,128]{2,1,0:T(8,128)(2,1)S(1)}, u32[]{:S(2)}) %copy-start.3) | copy-done | bytes 7864344
  31.0 2.3 %shard_map.141.refs_0_ = f32[2048,128]{1,0:T(8,128)S(1)} custom-call(bf16[16,1024,128]{2,1,0:T(8,128)(2,1)S(1)} %get-tuple-element.26.d0_ref, bf16[16,1024,128]{2,1,0:T(8,128)(2,1)S(1)} %get-tuple-element.27.d1_ref, bf16[2048,128]{1,0:T(8,128)(2,1)S(1)} %copy-done.11), custom_call_target="tpu_custom_call" | custom-call | flops 1073741824 | bytes 1048576 | tf_op jit(solution)/shard_map/pallas_call | solution.py:185
  33.4 1.9 %copy-done.6 = bf16[16,1024,128]{2,1,0:T(8,128)(2,1)} copy-done((bf16[16,1024,128]{2,1,0:T(8,128)(2,1)}, bf16[16,1024,128]{2,1,0:T(8,128)(2,1)S(1)}, u32[]{:S(2)}) %copy-start.6) | copy-done | bytes 4194328
  35.3 3.2 %copy-done.1 = bf16[30,1024,128]{2,1,0:T(8,128)(2,1)S(1)} copy-done((bf16[30,1024,128]{2,1,0:T(8,128)(2,1)S(1)}, bf16[30,1024,128]{2,1,0:T(8,128)(2,1)}, u32[]{:S(2)}) %copy-start.1) | copy-done | bytes 7864344
  38.6 3.2 %copy-done.4 = bf16[30,1024,128]{2,1,0:T(8,128)(2,1)S(1)} copy-done((bf16[30,1024,128]{2,1,0:T(8,128)(2,1)S(1)}, bf16[30,1024,128]{2,1,0:T(8,128)(2,1)}, u32[]{:S(2)}) %copy-start.4) | copy-done | bytes 7864344
  41.8 1.0 shard_map.142.refs_0_
  42.8 1.0 shard_map.143.refs_0_
  43.8 1.0 shard_map.144.refs_0_
  44.8 1.0 shard_map.145.refs_0_
  45.8 1.0 shard_map.146.sum_ref
  46.8 1.9 %shard_map.147 = (bf16[2048,128]{1,0:T(8,128)(2,1)}, bf16[2048,128]{1,0:T(8,128)(2,1)S(1)}, bf16[128,2048]{1,0:T(8,128)(2,1)S(1)}, f32[256,128]{1,0:T(8,128)S(1)}) custom-call(f32[2048,128]{1,0:T(8,128)S(1)} %shard_map.146.sum_ref, bf16[2048,128]{1,0:T(8,128)(2,1)S(1)} %copy-done.11, bf16[2048,128]{1,0:T(8,128)(2,1)S(1)} %copy-done.12, ...), custom_call_target="tpu_custom_call" | custom-call | flops 335544320 | bytes 5000000 | tf_op jit(solution)/shard_map/pallas_call | solution.py:220
  48.7 1.2 %collective-permute-start.10 = (f32[128,128]{1,0:T(8,128)S(1)}, f32[128,128]{1,0:T(8,128)S(1)}, u32[]{:S(2)}, u32[]{:S(2)}) collective-permute-start(f32[128,128]{1,0:T(8,128)S(1)} %dynamic-slice_bitcast_fusion), channel_id=1, source_target_pairs={{0,1},{1,0},{2,3},{3,2},{4,5},{5,4},{6,7},{7,6},{8,9},{9,8},{10,11... | collective-permute-start | bytes 196616 | tf_op jit(solution)/shard_map/ppermute | solution.py:305
  49.9 0.9 collective-permute-done.10
  51.0 3.1 %collective-permute-done.11 = f32[128,128]{1,0:T(8,128)S(1)} collective-permute-done((f32[128,128]{1,0:T(8,128)S(1)}, f32[128,128]{1,0:T(8,128)S(1)}, u32[]{:S(2)}, u32[]{:S(2)}) %collective-permute-start.11) | collective-permute-done | bytes 65568 | tf_op jit(solution)/shard_map/ppermute | solution.py:305
  54.1 0.3 collective-permute-start.12
  54.4 3.2 %copy-done.2 = bf16[30,1024,128]{2,1,0:T(8,128)(2,1)S(1)} copy-done((bf16[30,1024,128]{2,1,0:T(8,128)(2,1)S(1)}, bf16[30,1024,128]{2,1,0:T(8,128)(2,1)}, u32[]{:S(2)}) %copy-start.2) | copy-done | bytes 7864344
  57.6 3.2 %copy-done.5 = bf16[30,1024,128]{2,1,0:T(8,128)(2,1)S(1)} copy-done((bf16[30,1024,128]{2,1,0:T(8,128)(2,1)S(1)}, bf16[30,1024,128]{2,1,0:T(8,128)(2,1)}, u32[]{:S(2)}) %copy-start.5) | copy-done | bytes 7864344
  60.8 0.6 shard_map.148.before_ref
  61.5 0.6 shard_map.149.before_ref
  62.1 0.6 shard_map.150.before_ref
  62.7 1.9 %collective-permute-done.13 = f32[128,128]{1,0:T(8,128)S(1)} collective-permute-done((f32[128,128]{1,0:T(8,128)S(1)}, f32[128,128]{1,0:T(8,128)S(1)}, u32[]{:S(2)}, u32[]{:S(2)}) %collective-permute-start.13) | collective-permute-done | bytes 65568 | tf_op jit(solution)/shard_map/ppermute | solution.py:305
  64.6 0.6 collective-permute-start.14
  65.2 0.6 shard_map.151.before_ref
  65.8 0.6 shard_map.152.before_ref
  66.4 3.0 %collective-permute-start.5 = (bf16[128,768]{1,0:T(8,128)(2,1)S(1)}, bf16[128,768]{1,0:T(8,128)(2,1)S(1)}, u32[]{:S(2)}, u32[]{:S(2)}) collective-permute-start(bf16[128,768]{1,0:T(8,128)(2,1)S(1)} %shard_map.152.before_ref), channel_id=1, source_target_pairs={{0,1},{1,0},{2,3},{3,2},{4,5},{5,4},{6,7},{7,6},{8,9},{9,8},{10,11... | collective-permute-start | bytes 589832 | tf_op jit(solution)/shard_map/ppermute | solution.py:305
  69.4 0.3 collective-permute-start.6
  69.7 1.4 %collective-permute-start.15 = (f32[128,128]{1,0:T(8,128)S(1)}, f32[128,128]{1,0:T(8,128)S(1)}, u32[]{:S(2)}, u32[]{:S(2)}) collective-permute-start(f32[128,128]{1,0:T(8,128)S(1)} %add.34), channel_id=1, source_target_pairs={{0,32},{1,33},{2,34},{3,35},{4,36},{5,37},{6,38},{7,39},{8,40},{9,... | collective-permute-start | bytes 196616 | tf_op jit(solution)/shard_map/ppermute | solution.py:305
  71.3 2.6 %collective-permute-start.8 = (bf16[128,768]{1,0:T(8,128)(2,1)S(1)}, bf16[128,768]{1,0:T(8,128)(2,1)S(1)}, u32[]{:S(2)}, u32[]{:S(2)}) collective-permute-start(bf16[128,768]{1,0:T(8,128)(2,1)S(1)} %shard_map.149.before_ref), channel_id=1, source_target_pairs={{0,16},{1,17},{2,18},{3,19},{4,20},{5,21},{6,22},{7,23},{8,24},{9,... | collective-permute-start | bytes 589832 | tf_op jit(solution)/shard_map/ppermute | solution.py:305
  73.8 3.7 %collective-permute-start.9 = (bf16[128,768]{1,0:T(8,128)(2,1)S(1)}, bf16[128,768]{1,0:T(8,128)(2,1)S(1)}, u32[]{:S(2)}, u32[]{:S(2)}) collective-permute-start(bf16[128,768]{1,0:T(8,128)(2,1)S(1)} %shard_map.148.before_ref), channel_id=1, source_target_pairs={{0,4},{1,5},{2,6},{3,7},{4,0},{5,1},{6,2},{7,3},{8,12},{9,13},{10,... | collective-permute-start | bytes 589832 | tf_op jit(solution)/shard_map/ppermute | solution.py:305
  77.6 2.2 %copy-done.7 = bf16[16,1024,128]{2,1,0:T(8,128)(2,1)S(1)} copy-done((bf16[16,1024,128]{2,1,0:T(8,128)(2,1)S(1)}, bf16[16,1024,128]{2,1,0:T(8,128)(2,1)}, u32[]{:S(2)}) %copy-start.7) | copy-done | bytes 4194328
  79.8 2.2 %copy-done.9 = bf16[16,1024,128]{2,1,0:T(8,128)(2,1)S(1)} copy-done((bf16[16,1024,128]{2,1,0:T(8,128)(2,1)S(1)}, bf16[16,1024,128]{2,1,0:T(8,128)(2,1)}, u32[]{:S(2)}) %copy-start.9) | copy-done | bytes 4194328
  82.0 1.4 %shard_map.153.acc_ref = f32[128,2048]{1,0:T(8,128)S(1)} custom-call(bf16[128,2048]{1,0:T(8,128)(2,1)S(1)} %get-tuple-element.29.st_ref.before_ref, bf16[16,1024,128]{2,1,0:T(8,128)(2,1)S(1)} %copy-done.7, bf16[16,1024,128]{2,1,0:T(8,128)(2,1)S(1)} %copy-done.9, bf16[2048,128]{1,0:T(8,128)(2,1)S(1)} %get-tuple-element.30.gp_ref, ...), custom_call_target="tpu_custom_call" | custom-call | flops 1073741824 | bytes 1500000 | tf_op jit(solution)/shard_map/pallas_call | solution.py:269
  83.4 2.7 %collective-permute-start.16 = (f32[128,128]{1,0:T(8,128)S(1)}, f32[128,128]{1,0:T(8,128)S(1)}, u32[]{:S(2)}, u32[]{:S(2)}) collective-permute-start(f32[128,128]{1,0:T(8,128)S(1)} %add.35), channel_id=1, source_target_pairs={{0,64},{1,65},{2,66},{3,67},{4,68},{5,69},{6,70},{7,71},{8,72},{9,... | collective-permute-start | bytes 196616 | tf_op jit(solution)/shard_map/ppermute | solution.py:305
  86.1 2.2 %shard_map.154.acc_ref = f32[128,2048]{1,0:T(8,128)S(1)} custom-call(s32[5,768]{1,0:T(8,128)S(1)} %copy-done.18, f32[128,2048]{1,0:T(8,128)S(1)} %shard_map.153.acc_ref, bf16[128,768]{1,0:T(8,128)(2,1)S(1)} %collective-permute-done.5.refs_0_, bf16[128,768]{1,0:T(8,128)(2,1)S(1)} %collective-permute-done.6.refs_1_), custom_call_target="tpu_custom_call" | custom-call | flops 805306368 | bytes 2000000 | tf_op jit(solution)/shard_map/pallas_call | solution.py:294
  88.4 4.8 %collective-permute-start.17 = (f32[128,128]{1,0:T(8,128)S(1)}, f32[128,128]{1,0:T(8,128)S(1)}, u32[]{:S(2)}, u32[]{:S(2)}) collective-permute-start(f32[128,128]{1,0:T(8,128)S(1)} %add.36), channel_id=1, source_target_pairs={{0,1},{1,0},{2,3},{3,2},{4,5},{5,4},{6,7},{7,6},{8,9},{9,8},{10,11... | collective-permute-start | bytes 196616 | tf_op jit(solution)/shard_map/ppermute | solution.py:305
  93.2 4.3 %shard_map.155 = f32[2048,128]{1,0:T(8,128)} custom-call(s32[5,768]{1,0:T(8,128)S(1)} %copy-done.18, f32[128,2048]{1,0:T(8,128)S(1)} %shard_map.154.acc_ref, bf16[128,768]{1,0:T(8,128)(2,1)S(1)} %collective-permute-done.7.refs_0_, bf16[128,768]{1,0:T(8,128)(2,1)S(1)} %collective-permute-done.8.refs_1_, bf16[128,768]{1,0:T(8,128)(2,1)S(1)} %collective-permute-done.9.refs_2_), custom_call_target="tpu_custom_call" | custom-call | flops 1207959552 | bytes 2000000 | tf_op jit(solution)/shard_map/pallas_call | solution.py:294
  97.5 0.7 select_multiply_fusion
  (53 shorter events, 0.5 us)
Async XLA Ops:
  0.6 1.0 %copy-start.10 = (bf16[2048,128]{1,0:T(8,128)(2,1)S(1)}, bf16[2048,128]{1,0:T(8,128)(2,1)}, u32[]{:S(2)}) copy-start(bf16[2048,128]{1,0:T(8,128)(2,1)} %x_ref.5) | copy-start | bytes 1572868
  1.7 0.7 copy-start.17
  5.3 30.0 %collective-permute-start.4 = (bf16[128,768]{1,0:T(8,128)(2,1)S(1)}, bf16[128,768]{1,0:T(8,128)(2,1)S(1)}, u32[]{:S(2)}, u32[]{:S(2)}) collective-permute-start(bf16[128,768]{1,0:T(8,128)(2,1)S(1)} %get-tuple-element.25), channel_id=1, source_target_pairs={{0,1},{1,0},{2,3},{3,2},{4,5},{5,4},{6,7},{7,6},{8,9},{9,8},{10,11... | collective-permute-start | bytes 589832 | tf_op jit(solution)/shard_map/ppermute | solution.py:305
  6.8 35.9 %collective-permute-start.3 = (bf16[128,768]{1,0:T(8,128)(2,1)S(1)}, bf16[128,768]{1,0:T(8,128)(2,1)S(1)}, u32[]{:S(2)}, u32[]{:S(2)}) collective-permute-start(bf16[128,768]{1,0:T(8,128)(2,1)S(1)} %get-tuple-element.24), channel_id=1, source_target_pairs={{0,8},{1,9},{2,10},{3,11},{4,12},{5,13},{6,14},{7,15},{8,0},{9,1},... | collective-permute-start | bytes 589832 | tf_op jit(solution)/shard_map/ppermute | solution.py:305
  8.1 35.6 %collective-permute-start.2 = (bf16[128,768]{1,0:T(8,128)(2,1)S(1)}, bf16[128,768]{1,0:T(8,128)(2,1)S(1)}, u32[]{:S(2)}, u32[]{:S(2)}) collective-permute-start(bf16[128,768]{1,0:T(8,128)(2,1)S(1)} %get-tuple-element.23), channel_id=1, source_target_pairs={{0,2},{1,3},{2,0},{3,1},{4,6},{5,7},{6,4},{7,5},{8,10},{9,11},{10,... | collective-permute-start | bytes 589832 | tf_op jit(solution)/shard_map/ppermute | solution.py:305
  9.8 36.0 %collective-permute-start = (bf16[128,768]{1,0:T(8,128)(2,1)S(1)}, bf16[128,768]{1,0:T(8,128)(2,1)S(1)}, u32[]{:S(2)}, u32[]{:S(2)}) collective-permute-start(bf16[128,768]{1,0:T(8,128)(2,1)S(1)} %get-tuple-element.20), channel_id=1, source_target_pairs={{0,4},{1,5},{2,6},{3,7},{4,0},{5,1},{6,2},{7,3},{8,12},{9,13},{10,... | collective-permute-start | bytes 589832 | tf_op jit(solution)/shard_map/ppermute | solution.py:305
  13.1 18.0 %copy-start.11 = (bf16[2048,128]{1,0:T(8,128)(2,1)S(1)}, bf16[2048,128]{1,0:T(8,128)(2,1)}, u32[]{:S(2)}) copy-start(bf16[2048,128]{1,0:T(8,128)(2,1)} %x_ref.5) | copy-start | bytes 1572868
  13.1 31.7 %collective-permute-start.1 = (bf16[128,768]{1,0:T(8,128)(2,1)S(1)}, bf16[128,768]{1,0:T(8,128)(2,1)S(1)}, u32[]{:S(2)}, u32[]{:S(2)}) collective-permute-start(bf16[128,768]{1,0:T(8,128)(2,1)S(1)} %get-tuple-element.21), channel_id=1, source_target_pairs={{0,16},{1,17},{2,18},{3,19},{4,20},{5,21},{6,22},{7,23},{8,24},{9,... | collective-permute-start | bytes 589832 | tf_op jit(solution)/shard_map/ppermute | solution.py:305
  24.9 3.1 %copy-start = (bf16[30,1024,128]{2,1,0:T(8,128)(2,1)}, bf16[30,1024,128]{2,1,0:T(8,128)(2,1)S(1)}, u32[]{:S(2)}) copy-start(bf16[30,1024,128]{2,1,0:T(8,128)(2,1)S(1)} %get-tuple-element.18.d0_ref) | copy-start | bytes 23592964
  28.0 3.1 %copy-start.3 = (bf16[30,1024,128]{2,1,0:T(8,128)(2,1)}, bf16[30,1024,128]{2,1,0:T(8,128)(2,1)S(1)}, u32[]{:S(2)}) copy-start(bf16[30,1024,128]{2,1,0:T(8,128)(2,1)S(1)} %get-tuple-element.19.d1_ref) | copy-start | bytes 23592964
  31.0 2.3 %copy-start.8 = (bf16[16,1024,128]{2,1,0:T(8,128)(2,1)}, bf16[16,1024,128]{2,1,0:T(8,128)(2,1)S(1)}, u32[]{:S(2)}) copy-start(bf16[16,1024,128]{2,1,0:T(8,128)(2,1)S(1)} %get-tuple-element.27.d1_ref) | copy-start | bytes 12582916
  33.4 1.9 %copy-start.6 = (bf16[16,1024,128]{2,1,0:T(8,128)(2,1)}, bf16[16,1024,128]{2,1,0:T(8,128)(2,1)S(1)}, u32[]{:S(2)}) copy-start(bf16[16,1024,128]{2,1,0:T(8,128)(2,1)S(1)} %get-tuple-element.26.d0_ref) | copy-start | bytes 12582916
  35.3 3.2 %copy-start.1 = (bf16[30,1024,128]{2,1,0:T(8,128)(2,1)S(1)}, bf16[30,1024,128]{2,1,0:T(8,128)(2,1)}, u32[]{:S(2)}) copy-start(bf16[30,1024,128]{2,1,0:T(8,128)(2,1)} %copy-done) | copy-start | bytes 23592964
  38.6 3.2 %copy-start.4 = (bf16[30,1024,128]{2,1,0:T(8,128)(2,1)S(1)}, bf16[30,1024,128]{2,1,0:T(8,128)(2,1)}, u32[]{:S(2)}) copy-start(bf16[30,1024,128]{2,1,0:T(8,128)(2,1)} %copy-done.3) | copy-start | bytes 23592964
  45.7 1.0 %copy-start.12 = (bf16[2048,128]{1,0:T(8,128)(2,1)S(1)}, bf16[2048,128]{1,0:T(8,128)(2,1)}, u32[]{:S(2)}) copy-start(bf16[2048,128]{1,0:T(8,128)(2,1)} %ct_ref.1) | copy-start | bytes 1572868
  45.7 1.0 %copy-start.13 = (bf16[128,128]{1,0:T(8,128)(2,1)S(1)}, bf16[128,128]{1,0:T(8,128)(2,1)}, u32[]{:S(2)}) copy-start(bf16[128,128]{1,0:T(8,128)(2,1)} %ws_ref.3) | copy-start | bytes 98308
  45.7 1.0 %copy-start.14 = (bf16[128,128]{1,0:T(8,128)(2,1)S(1)}, bf16[128,128]{1,0:T(8,128)(2,1)}, u32[]{:S(2)}) copy-start(bf16[128,128]{1,0:T(8,128)(2,1)} %wn_ref.1) | copy-start | bytes 98308
  45.8 1.0 %copy-start.15 = (s32[2048]{0:T(1024)S(1)}, s32[2048]{0:T(1024)}, u32[]{:S(2)}) copy-start(s32[2048]{0:T(1024)} %param.20) | copy-start | bytes 24580
  45.8 1.0 %copy-start.16 = (f32[128]{0:T(128)S(1)}, f32[128]{0:T(128)}, u32[]{:S(2)}) copy-start(f32[128]{0:T(128)} %param.14) | copy-start | bytes 1540
  48.7 2.1 %collective-permute-start.10 = (f32[128,128]{1,0:T(8,128)S(1)}, f32[128,128]{1,0:T(8,128)S(1)}, u32[]{:S(2)}, u32[]{:S(2)}) collective-permute-start(f32[128,128]{1,0:T(8,128)S(1)} %dynamic-slice_bitcast_fusion), channel_id=1, source_target_pairs={{0,1},{1,0},{2,3},{3,2},{4,5},{5,4},{6,7},{7,6},{8,9},{9,8},{10,11... | collective-permute-start | bytes 196616 | tf_op jit(solution)/shard_map/ppermute | solution.py:305
  50.9 3.2 %collective-permute-start.11 = (f32[128,128]{1,0:T(8,128)S(1)}, f32[128,128]{1,0:T(8,128)S(1)}, u32[]{:S(2)}, u32[]{:S(2)}) collective-permute-start(f32[128,128]{1,0:T(8,128)S(1)} %bitcast_add_fusion), channel_id=1, source_target_pairs={{0,2},{1,3},{2,0},{3,1},{4,6},{5,7},{6,4},{7,5},{8,10},{9,11},{10,... | collective-permute-start | bytes 196616 | tf_op jit(solution)/shard_map/ppermute | solution.py:305
  54.1 7.3 %collective-permute-start.12 = (f32[128,128]{1,0:T(8,128)S(1)}, f32[128,128]{1,0:T(8,128)S(1)}, u32[]{:S(2)}, u32[]{:S(2)}) collective-permute-start(f32[128,128]{1,0:T(8,128)S(1)} %add.31), channel_id=1, source_target_pairs={{0,4},{1,5},{2,6},{3,7},{4,0},{5,1},{6,2},{7,3},{8,12},{9,13},{10,... | collective-permute-start | bytes 196616 | tf_op jit(solution)/shard_map/ppermute | solution.py:305
  54.3 3.2 %copy-start.2 = (bf16[30,1024,128]{2,1,0:T(8,128)(2,1)S(1)}, bf16[30,1024,128]{2,1,0:T(8,128)(2,1)}, u32[]{:S(2)}) copy-start(bf16[30,1024,128]{2,1,0:T(8,128)(2,1)} %copy-done) | copy-start | bytes 23592964
  57.6 3.2 %copy-start.5 = (bf16[30,1024,128]{2,1,0:T(8,128)(2,1)S(1)}, bf16[30,1024,128]{2,1,0:T(8,128)(2,1)}, u32[]{:S(2)}) copy-start(bf16[30,1024,128]{2,1,0:T(8,128)(2,1)} %copy-done.3) | copy-start | bytes 23592964
  61.4 3.2 %collective-permute-start.13 = (f32[128,128]{1,0:T(8,128)S(1)}, f32[128,128]{1,0:T(8,128)S(1)}, u32[]{:S(2)}, u32[]{:S(2)}) collective-permute-start(f32[128,128]{1,0:T(8,128)S(1)} %add.32), channel_id=1, source_target_pairs={{0,8},{1,9},{2,10},{3,11},{4,12},{5,13},{6,14},{7,15},{8,0},{9,1},... | collective-permute-start | bytes 196616 | tf_op jit(solution)/shard_map/ppermute | solution.py:305
  64.6 5.1 %collective-permute-start.14 = (f32[128,128]{1,0:T(8,128)S(1)}, f32[128,128]{1,0:T(8,128)S(1)}, u32[]{:S(2)}, u32[]{:S(2)}) collective-permute-start(f32[128,128]{1,0:T(8,128)S(1)} %add.33), channel_id=1, source_target_pairs={{0,16},{1,17},{2,18},{3,19},{4,20},{5,21},{6,22},{7,23},{8,24},{9,... | collective-permute-start | bytes 196616 | tf_op jit(solution)/shard_map/ppermute | solution.py:305
  66.4 19.7 %copy-start.18 = (s32[5,768]{1,0:T(8,128)S(1)}, s32[5,768]{1,0:T(8,128)}, u32[]{:S(2)}) copy-start(s32[5,768]{1,0:T(8,128)} %rows_ref.7) | copy-start | bytes 46084
  66.4 17.0 %collective-permute-start.5 = (bf16[128,768]{1,0:T(8,128)(2,1)S(1)}, bf16[128,768]{1,0:T(8,128)(2,1)S(1)}, u32[]{:S(2)}, u32[]{:S(2)}) collective-permute-start(bf16[128,768]{1,0:T(8,128)(2,1)S(1)} %shard_map.152.before_ref), channel_id=1, source_target_pairs={{0,1},{1,0},{2,3},{3,2},{4,5},{5,4},{6,7},{7,6},{8,9},{9,8},{10,11... | collective-permute-start | bytes 589832 | tf_op jit(solution)/shard_map/ppermute | solution.py:305
  69.4 16.7 %collective-permute-start.6 = (bf16[128,768]{1,0:T(8,128)(2,1)S(1)}, bf16[128,768]{1,0:T(8,128)(2,1)S(1)}, u32[]{:S(2)}, u32[]{:S(2)}) collective-permute-start(bf16[128,768]{1,0:T(8,128)(2,1)S(1)} %shard_map.151.before_ref), channel_id=1, source_target_pairs={{0,8},{1,9},{2,10},{3,11},{4,12},{5,13},{6,14},{7,15},{8,0},{9,1},... | collective-permute-start | bytes 589832 | tf_op jit(solution)/shard_map/ppermute | solution.py:305
  69.7 4.1 %collective-permute-start.15 = (f32[128,128]{1,0:T(8,128)S(1)}, f32[128,128]{1,0:T(8,128)S(1)}, u32[]{:S(2)}, u32[]{:S(2)}) collective-permute-start(f32[128,128]{1,0:T(8,128)S(1)} %add.34), channel_id=1, source_target_pairs={{0,32},{1,33},{2,34},{3,35},{4,36},{5,37},{6,38},{7,39},{8,40},{9,... | collective-permute-start | bytes 196616 | tf_op jit(solution)/shard_map/ppermute | solution.py:305
  71.1 22.1 %collective-permute-start.7 = (bf16[128,768]{1,0:T(8,128)(2,1)S(1)}, bf16[128,768]{1,0:T(8,128)(2,1)S(1)}, u32[]{:S(2)}, u32[]{:S(2)}) collective-permute-start(bf16[128,768]{1,0:T(8,128)(2,1)S(1)} %shard_map.150.before_ref), channel_id=1, source_target_pairs={{0,2},{1,3},{2,0},{3,1},{4,6},{5,7},{6,4},{7,5},{8,10},{9,11},{10,... | collective-permute-start | bytes 589832 | tf_op jit(solution)/shard_map/ppermute | solution.py:305
  71.3 21.9 %collective-permute-start.8 = (bf16[128,768]{1,0:T(8,128)(2,1)S(1)}, bf16[128,768]{1,0:T(8,128)(2,1)S(1)}, u32[]{:S(2)}, u32[]{:S(2)}) collective-permute-start(bf16[128,768]{1,0:T(8,128)(2,1)S(1)} %shard_map.149.before_ref), channel_id=1, source_target_pairs={{0,16},{1,17},{2,18},{3,19},{4,20},{5,21},{6,22},{7,23},{8,24},{9,... | collective-permute-start | bytes 589832 | tf_op jit(solution)/shard_map/ppermute | solution.py:305
  73.8 19.3 %collective-permute-start.9 = (bf16[128,768]{1,0:T(8,128)(2,1)S(1)}, bf16[128,768]{1,0:T(8,128)(2,1)S(1)}, u32[]{:S(2)}, u32[]{:S(2)}) collective-permute-start(bf16[128,768]{1,0:T(8,128)(2,1)S(1)} %shard_map.148.before_ref), channel_id=1, source_target_pairs={{0,4},{1,5},{2,6},{3,7},{4,0},{5,1},{6,2},{7,3},{8,12},{9,13},{10,... | collective-permute-start | bytes 589832 | tf_op jit(solution)/shard_map/ppermute | solution.py:305
  77.6 2.2 %copy-start.7 = (bf16[16,1024,128]{2,1,0:T(8,128)(2,1)S(1)}, bf16[16,1024,128]{2,1,0:T(8,128)(2,1)}, u32[]{:S(2)}) copy-start(bf16[16,1024,128]{2,1,0:T(8,128)(2,1)} %copy-done.6) | copy-start | bytes 12582916
  79.8 2.2 %copy-start.9 = (bf16[16,1024,128]{2,1,0:T(8,128)(2,1)S(1)}, bf16[16,1024,128]{2,1,0:T(8,128)(2,1)}, u32[]{:S(2)}) copy-start(bf16[16,1024,128]{2,1,0:T(8,128)(2,1)} %copy-done.8) | copy-start | bytes 12582916
  83.4 4.9 %collective-permute-start.16 = (f32[128,128]{1,0:T(8,128)S(1)}, f32[128,128]{1,0:T(8,128)S(1)}, u32[]{:S(2)}, u32[]{:S(2)}) collective-permute-start(f32[128,128]{1,0:T(8,128)S(1)} %add.35), channel_id=1, source_target_pairs={{0,64},{1,65},{2,66},{3,67},{4,68},{5,69},{6,70},{7,71},{8,72},{9,... | collective-permute-start | bytes 196616 | tf_op jit(solution)/shard_map/ppermute | solution.py:305
  88.4 9.1 %collective-permute-start.17 = (f32[128,128]{1,0:T(8,128)S(1)}, f32[128,128]{1,0:T(8,128)S(1)}, u32[]{:S(2)}, u32[]{:S(2)}) collective-permute-start(f32[128,128]{1,0:T(8,128)S(1)} %add.36), channel_id=1, source_target_pairs={{0,1},{1,0},{2,3},{3,2},{4,5},{5,4},{6,7},{7,6},{8,9},{9,8},{10,11... | collective-permute-start | bytes 196616 | tf_op jit(solution)/shard_map/ppermute | solution.py:305

commit v3 on v2

v3 whole, which is shorter than its diff:
```python
import functools
import math

import jax
import jax.numpy as jnp
from jax import lax
from jax.experimental import pallas as pl
from jax.experimental.pallas import tpu as pltpu
from jax.sharding import PartitionSpec as P

TILE = 128
VMEM = pltpu.VMEM
LIMIT = 8 * 1024 * 1024


def vspec():
    return pl.BlockSpec(memory_space=VMEM)


def sspec():
    return pl.BlockSpec(memory_space=pltpu.SMEM)


def params(limit=LIMIT):
    return pltpu.CompilerParams(vmem_limit_bytes=limit)


def in_hbm(array):
    return pltpu.with_memory_space_constraint(array, pltpu.HBM)


def cost(flops, size, transcendentals=0):
    return pl.CostEstimate(flops=flops, bytes_accessed=size, transcendentals=transcendentals)


def pinned(array):
    return pltpu.with_memory_space_constraint(array, VMEM)


def nt_dot(left, right):
    return lax.dot_general(
        left, right, (((1,), (1,)), ((), ())), preferred_element_type=jnp.float32
    )


def nn_dot(left, right):
    return jnp.dot(left, right, preferred_element_type=jnp.float32)


def pick_kernel(rows_hbm, x_hbm, *refs):
    rounds = (len(refs) - 5) // 2
    outs, tables = refs[:rounds], refs[rounds : 2 * rounds]
    rows_ref, x_ref, xt_ref, rows_sem, x_sem = refs[2 * rounds :]
    rows_copy = pltpu.make_async_copy(rows_hbm, rows_ref, rows_sem)
    x_copy = pltpu.make_async_copy(x_hbm, x_ref, x_sem)
    rows_copy.start()
    x_copy.start()
    rows_copy.wait()
    count, step = x_ref.shape[0], 2 * TILE
    numbers = lax.broadcasted_iota(jnp.int32, (count, step), 0)
    for r in range(rounds):
        for k in range(0, rows_ref.shape[1], step):
            listed = rows_ref[r : r + 1, k : k + step]
            table = jnp.where(numbers == listed, 1.0, 0.0).astype(jnp.bfloat16)
            tables[r][:, k : k + step] = table
            if r == 0 and k == 0:
                x_copy.wait()
                for i in range(0, count, TILE):
                    xt_ref[:, i : i + TILE] = x_ref[i : i + TILE, :].T
            outs[r][:, k : k + step] = nn_dot(xt_ref[...], table).astype(jnp.bfloat16)


def pick_rows(send_rows, features):
    rows, width = features.shape
    rounds, boundary = send_rows.shape
    outs = [jax.ShapeDtypeStruct((width, boundary), jnp.bfloat16) for _ in range(rounds)]
    outs += [VMEM((rows, boundary), jnp.bfloat16) for _ in range(rounds)]
    results = pl.pallas_call(
        pick_kernel,
        out_shape=outs,
        in_specs=[pl.BlockSpec(memory_space=pltpu.HBM)] * 2,
        out_specs=[vspec()] * len(outs),
        scratch_shapes=[
            VMEM(send_rows.shape, jnp.int32),
            VMEM(features.shape, jnp.bfloat16),
            VMEM((width, rows), jnp.bfloat16),
            pltpu.SemaphoreType.DMA,
            pltpu.SemaphoreType.DMA,
        ],
        compiler_params=params(),
        cost_estimate=cost(2 * rows * boundary * rounds * width, 1_000_000),
    )(in_hbm(send_rows), in_hbm(features))
    return results[:rounds], results[rounds:]


def densify_kernel(lc, hc, lt, ht, dl0, dl1, dh0, dh1, lslots, hslots, zeros, sems, zsems):
    half = lt.shape[0] // 2
    depth = lslots.shape[0]
    dense = (dl0, dl1, dh0, dh1)

    def fetch(i, slot):
        return [
            pltpu.make_async_copy(
                src.at[i + p * half], dst.at[slot, p], sems.at[slot, 2 * q + p]
            )
            for q, (src, dst) in enumerate(((lt, lslots), (ht, hslots)))
            for p in range(2)
        ]

    def clear(i, slot):
        rows = pl.ds(pl.multiple_of(i * TILE, TILE), TILE)
        return [
            pltpu.make_async_copy(
                zeros.at[pl.ds(0, d.shape[0])], d.at[:, rows, :], zsems.at[slot, k]
            )
            for k, d in enumerate(dense)
        ]

    for d in range(depth - 1):
        for copy in fetch(d, d):
            copy.start()
    zeros[...] = jnp.zeros_like(zeros)
    for copy in clear(0, 0):
        copy.start()

    def body(i, carry):
        slot, zslot = lax.rem(i, depth), lax.rem(i, 2)

        @pl.when(i + depth - 1 < half)
        def _():
            for copy in fetch(i + depth - 1, lax.rem(i + depth - 1, depth)):
                copy.start()

        @pl.when(i + 1 < half)
        def _():
            for copy in clear(i + 1, 1 - zslot):
                copy.start()

        for copy in clear(i, zslot):
            copy.wait()
        for copy in fetch(i, slot):
            copy.wait()
        rows = pl.ds(pl.multiple_of(i * TILE, TILE), TILE)
        for t in range(max(lt.shape[1], ht.shape[1])):
            jobs = []
            if t < lt.shape[1]:
                jobs += [(dl0, lc[i, t], lslots, 0), (dl1, lc[i + half, t], lslots, 1)]
            if t < ht.shape[1]:
                jobs += [(dh0, hc[i, t], hslots, 0), (dh1, hc[i + half, t], hslots, 1)]
            sums = [d[c, rows, :] + s[slot, p, t] for d, c, s, p in jobs]
            for (d, c, _, _), total in zip(jobs, sums):
                d[c, rows, :] = total
        return carry

    lax.fori_loop(0, half, body, 0)


def densify(local_cols, halo_cols, local_tiles, halo_tiles, halo_blocks):
    nblocks, local_count = local_cols.shape
    halo_count = halo_cols.shape[1]
    half = nblocks // 2 * TILE
    depth = 3
    slabs = (nblocks, nblocks, halo_blocks, halo_blocks)
    return pl.pallas_call(
        densify_kernel,
        out_shape=[VMEM((n, half, TILE), jnp.bfloat16) for n in slabs],
        in_specs=[sspec(), sspec()] + [pl.BlockSpec(memory_space=pltpu.HBM)] * 2,
        out_specs=[vspec()] * 4,
        scratch_shapes=[
            VMEM((depth, 2, local_count, TILE, TILE), jnp.bfloat16),
            VMEM((depth, 2, halo_count, TILE, TILE), jnp.bfloat16),
            VMEM((max(slabs), TILE, TILE), jnp.bfloat16),
            pltpu.SemaphoreType.DMA((depth, 4)),
            pltpu.SemaphoreType.DMA((2, 4)),
        ],
        compiler_params=params(12 * 1024 * 1024),
        cost_estimate=cost(16_000_000, nblocks * (local_count + halo_count) * TILE * TILE * 2),
    )(local_cols, halo_cols, in_hbm(local_tiles), in_hbm(halo_tiles))


def local_sums_kernel(d0_ref, d1_ref, x_ref, out_ref):
    half, step = d0_ref.shape[1], 512
    for p, dense_ref in enumerate((d0_ref, d1_ref)):
        for j in range(0, half, step):
            left = jnp.concatenate(
                [dense_ref[c, j : j + step, :] for c in range(dense_ref.shape[0])], axis=1
            )
            out_ref[p * half + j : p * half + j + step, :] = nn_dot(left, x_ref[...])


def local_sums(d0, d1, features):
    rows, width = features.shape
    return pl.pallas_call(
        local_sums_kernel,
        out_shape=VMEM((rows, width), jnp.float32),
        in_specs=[vspec()] * 3,
        out_specs=vspec(),
        compiler_params=params(),
        cost_estimate=cost(2 * rows * rows * width, 1_500_000),
    )(pinned(d0), pinned(d1), features)


def middle_kernel(rounds, *refs):
    got, refs = refs[:rounds], refs[rounds:]
    d0, d1, sum_ref, x_ref, ct_ref, deg_ref, ws_ref, wn_ref, bias_ref = refs[:9]
    out_ref, gp_ref, st_ref, mine_ref, give_ref, both, halo = refs[9:]
    core = lax.axis_index("dom") & 1
    half, step = d0.shape[1], 512
    boundary = got[0].shape[1]
    for r in range(rounds):
        halo[r * boundary : (r + 1) * boundary, :] = got[r][...].T
    for p, dense_ref in enumerate((d0, d1)):
        for j in range(0, half, step):
            left = jnp.concatenate(
                [dense_ref[c, j : j + step, :] for c in range(dense_ref.shape[0])], axis=1
            )
            start = p * half + j
            total = nn_dot(left, halo[...]) + sum_ref[start : start + step, :]
            for i in range(start // TILE, (start + step) // TILE):
                rows = slice(i * TILE, (i + 1) * TILE)
                line = deg_ref[i : i + 1, :].astype(jnp.float32)
                column = jnp.broadcast_to(line, (TILE, TILE)).T
                agg = total[i * TILE - start : (i + 1) * TILE - start, :] / column
                agg = agg.astype(jnp.bfloat16)
                both[rows, :TILE] = x_ref[rows, :]
                both[rows, TILE:] = agg
                preact = nn_dot(x_ref[rows, :], ws_ref[...]) + nn_dot(agg, wn_ref[...])
                preact = preact + bias_ref[...]
                sig = jax.nn.sigmoid(preact)
                out_ref[rows, :] = (preact * sig).astype(jnp.bfloat16)
                grad = ct_ref[rows, :].astype(jnp.float32) * sig * (1.0 + preact * (1.0 - sig))
                grad = grad.astype(jnp.bfloat16)
                gp_ref[rows, :] = grad
                st_ref[:, rows] = (nt_dot(wn_ref[...], grad) / line).astype(jnp.bfloat16)
    parts = lax.dot_general(
        both[...], gp_ref[...], (((0,), (0,)), ((), ())), preferred_element_type=jnp.float32
    )
    mine_ref[...] = jnp.where(core == 0, parts[:TILE], parts[TILE:])
    give_ref[...] = jnp.where(core == 0, parts[TILE:], parts[:TILE])


def middle(received, d0, d1, summed, features, cotangent, degree, w_self, w_neigh, bias):
    rows, width = features.shape
    rounds, boundary = len(received), received[0].shape[1]
    half = jax.ShapeDtypeStruct((rows, width), jnp.bfloat16)
    part = VMEM((width, width), jnp.float32)
    return pl.pallas_call(
        functools.partial(middle_kernel, rounds),
        out_shape=[
            half,
            VMEM((rows, width), jnp.bfloat16),
            VMEM((width, rows), jnp.bfloat16),
            part,
            part,
        ],
        in_specs=[vspec()] * (rounds + 9),
        out_specs=[vspec()] * 5,
        scratch_shapes=[
            VMEM((rows, 2 * width), jnp.bfloat16),
            VMEM((rounds * boundary, width), jnp.bfloat16),
        ],
        compiler_params=params(),
        cost_estimate=cost(2 * rows * rounds * boundary * width, 5_000_000, rows * width),
    )(
        *received,
        pinned(d0),
        pinned(d1),
        pinned(summed),
        features,
        cotangent,
        degree,
        w_self,
        w_neigh,
        bias,
    )


def beside(d0_ref, d1_ref, slab):
    return jnp.concatenate(
        [jnp.concatenate([d[slab], d[slab + 1]], axis=1) for d in (d0_ref, d1_ref)], axis=0
    )


def back_kernel(first, n, st_ref, d0_ref, d1_ref, before_ref, out_ref):
    for c in range(0, n, 2):
        product = nn_dot(st_ref[...], beside(d0_ref, d1_ref, first + c))
        out_ref[:, c * TILE : (c + 2) * TILE] = product.astype(jnp.bfloat16)


def back(first, n, scaled_t, d0, d1, before):
    width, rows = scaled_t.shape
    return pl.pallas_call(
        functools.partial(back_kernel, first, n),
        out_shape=jax.ShapeDtypeStruct((width, n * TILE), jnp.bfloat16),
        in_specs=[vspec()] * 3 + [pl.BlockSpec(memory_space=pl.ANY)],
        out_specs=vspec(),
        compiler_params=params(),
        cost_estimate=cost(2 * rows * n * TILE * width, 500_000),
    )(pinned(scaled_t), pinned(d0), pinned(d1), before)


def own_kernel(st_ref, d0_ref, d1_ref, gp_ref, ws_ref, before_ref, out_ref):
    for c in range(0, d0_ref.shape[0], 2):
        rows = slice(c * TILE, (c + 2) * TILE)
        product = nn_dot(st_ref[...], beside(d0_ref, d1_ref, c))
        out_ref[:, rows] = product + nt_dot(ws_ref[...], gp_ref[rows, :])


def own(scaled_t, d0, d1, grad_pre, w_self, before):
    width, rows = scaled_t.shape
    return pl.pallas_call(
        own_kernel,
        out_shape=VMEM((width, rows), jnp.float32),
        in_specs=[vspec()] * 5 + [pl.BlockSpec(memory_space=pl.ANY)],
        out_specs=vspec(),
        compiler_params=params(),
        cost_estimate=cost(2 * rows * rows * width, 1_500_000),
    )(pinned(scaled_t), pinned(d0), pinned(d1), pinned(grad_pre), w_self, before)


def place_kernel(count, last, acc_ref, *refs):
    returned, tables, out_ref = refs[:count], refs[count : 2 * count], refs[-1]
    step = 2 * TILE
    for j in range(0, acc_ref.shape[1], step):
        total = acc_ref[:, j : j + step]
        for got_ref, table_ref in zip(returned, tables):
            total = total + nt_dot(got_ref[...], table_ref[j : j + step, :])
        if last:
            out_ref[j : j + step, :] = total.T
        else:
            out_ref[:, j : j + step] = total


def place_rows(last, acc, returned, tables):
    width, rows = acc.shape
    count, boundary = len(returned), tables[0].shape[1]
    if last:
        out = jax.ShapeDtypeStruct((rows, width), jnp.float32)
    else:
        out = VMEM((width, rows), jnp.float32)
    return pl.pallas_call(
        functools.partial(place_kernel, count, last),
        out_shape=out,
        in_specs=[vspec()] * (1 + 2 * count),
        out_specs=vspec(),
        compiler_params=params(),
        cost_estimate=cost(2 * rows * count * boundary * width, 2_000_000),
    )(pinned(acc), *returned, *[pinned(t) for t in tables])


def add_kernel(left_ref, right_ref, out_ref):
    out_ref[...] = left_ref[...] + right_ref[...]


def added(left, right):
    return pl.pallas_call(
        add_kernel,
        out_shape=VMEM(left.shape, jnp.float32),
        in_specs=[vspec()] * 2,
        out_specs=vspec(),
        compiler_params=params(1024 * 1024),
        cost_estimate=cost(left.size, 3 * left.size * 4),
    )(pinned(left), right)


def halves_kernel(scale, total_ref, other_ref, self_ref, neigh_ref):
    core = lax.axis_index("dom") & 1
    total, other = total_ref[...], other_ref[...]
    self_ref[...] = jnp.where(core == 0, total, other) * scale
    neigh_ref[...] = jnp.where(core == 0, other, total) * scale


def halves(scale, total, other):
    out = jax.ShapeDtypeStruct(total.shape, jnp.float32)
    return pl.pallas_call(
        functools.partial(halves_kernel, scale),
        out_shape=[out, out],
        in_specs=[vspec()] * 2,
        out_specs=[vspec()] * 2,
        compiler_params=params(1024 * 1024),
        cost_estimate=cost(2 * total.size, 4 * total.size * 4),
    )(pinned(total), other)


def swapped(shard, mask):
    return lax.ppermute(shard, "dom", [(i, i ^ mask) for i in range(lax.axis_size("dom"))])


def summed_everywhere(mine, give, scale):
    total = added(mine, swapped(give, 1))
    mask = 2
    while mask < lax.axis_size("dom"):
        total = added(total, swapped(total, mask))
        mask *= 2
    return halves(scale, total, swapped(total, 1))


def local(
    node_features,
    w_self,
    w_neigh,
    output_bias,
    local_tiles,
    halo_tiles,
    local_cols,
    halo_cols,
    send_rows,
    degree,
    cotangent,
):
    row_count, width = node_features.shape
    nblocks = local_tiles.shape[0]
    round_count, boundary = send_rows.shape
    per = boundary // TILE
    picked, tables = pick_rows(send_rows, node_features)
    received = [swapped(rows, 1 << r) for r, rows in enumerate(picked)]
    dl0, dl1, dh0, dh1 = densify(
        local_cols, halo_cols, local_tiles, halo_tiles, round_count * per
    )
    summed = local_sums(dl0, dl1, node_features)
    output, grad_pre, scaled_t, mine, give = middle(
        received,
        dh0,
        dh1,
        summed,
        node_features,
        cotangent,
        degree.reshape(nblocks, TILE),
        w_self,
        w_neigh,
        output_bias.reshape(1, width),
    )
    returned = {}
    before = scaled_t
    for r in (2, 4, 1, 3, 0):
        before = back(r * per, per, scaled_t, dh0, dh1, before)
        returned[r] = swapped(before, 1 << r)
    grad_scale = 1.0 / math.sqrt(row_count * lax.axis_size("dom"))
    grad_self, grad_neigh = summed_everywhere(mine, give, grad_scale)
    grads_t = own(scaled_t, dl0, dl1, grad_pre, w_self, before)
    for rounds in ((0, 3), (1, 4, 2)):
        grads_t = place_rows(
            2 in rounds, grads_t, [returned[r] for r in rounds], [tables[r] for r in rounds]
        )
    return (output, grads_t, grad_self, grad_neigh)


def solution(mesh):
    in_specs = (
        P("dom", None),
        P(),
        P(),
        P(),
        P("dom", None, None, None),
        P("dom", None, None, None),
        P("dom", None),
        P("dom", None),
        P("dom", None),
        P("dom"),
        P("dom", None),
    )
    out_specs = (P("dom", None), P("dom", None), P(), P())
    return jax.shard_map(local, mesh=mesh, in_specs=in_specs, out_specs=out_specs, check_vma=False)
```

time: 98.6 us -> 79.7 us (0.81)
  local copies, waits for them, and re-layouts: 27.2 us -> 0.04 us
  Pallas kernels: 32.1 us -> 40 us
  waiting for transfers between devices: 5.97 us -> 10.1 us
  starting transfers between devices: 31.1 us -> 28.5 us
    unnamed x38 -> x16, local copies, waits for them, and re-layouts: 27.2 us -> 0.04 us
    pallas_call x12 -> x14, Pallas kernels: 19.9 us -> 27.9 us  [the longest x1 11.8 us: middle(): pl.pallas_call(functools.partial(middle_kernel, rounds), out_shape=[half,...]
    ppermute x18, waiting for transfers between devices: 5.97 us -> 10.1 us  [swapped(): lax.ppermute(shard, 'dom', [(i, i ^ mask) for i in range(lax.axis_size('d...]
    ppermute x18, starting transfers between devices: 31.1 us -> 28.5 us  [swapped(): lax.ppermute(shard, 'dom', [(i, i ^ mask) for i in range(lax.axis_size('d...]
  transfers between devices with their start and end apart: 18 -> 18, of which waited for: 3 -> 5; matrix products, arithmetic and copies ran while one was open for 0% -> 0% of each run, Pallas kernels for 27% -> 28%
where the time goes in v3:
time: 79.7 us; the launch traced here: 79.6 us
  Pallas kernels  40 us (50%)
  starting transfers between devices  28.5 us (36%)
  waiting for transfers between devices  10.1 us (13%)
  between operations  0.93 us (1%)
    ppermute x18, starting transfers between devices, swapped(): lax.ppermute(shard, 'dom', [(i, i ^ mask) for i in range(lax.axis_size('d...  28.5 us
    pallas_call x1, Pallas kernels, middle(): pl.pallas_call(functools.partial(middle_kernel, rounds), out_shape=[half,...  11.8 us
    ppermute x18, waiting for transfers between devices, swapped(): lax.ppermute(shard, 'dom', [(i, i ^ mask) for i in range(lax.axis_size('d...  10.1 us
    pallas_call x1, Pallas kernels, densify(): pl.pallas_call(densify_kernel, out_shape=[VMEM((n, half, TILE), jnp.bfloa...  9.17 us
    pallas_call x2, Pallas kernels, place_rows(): pl.pallas_call(functools.partial(place_kernel, count, last), out_shape=ou...  6.35 us
    pallas_call x1, Pallas kernels, pick_rows(): pl.pallas_call(pick_kernel, out_shape=outs, in_specs=[pl.BlockSpec(memory...  5.29 us
    pallas_call x5, Pallas kernels, back(): pl.pallas_call(functools.partial(back_kernel, first, n), out_shape=jax.Sh...  2.94 us
    pallas_call x1, Pallas kernels, local_sums(): pl.pallas_call(local_sums_kernel, out_shape=VMEM((rows, width), jnp.float...  2.31 us
  transfers between devices with their start and end apart: 18, of which 5 were waited for; matrix products, arithmetic and copies ran while one was open for 0% of the time, Pallas kernels for 28%

profile of v3, /device:TPU:1, one launch (start us, length us, event | category | flops | bytes accessed | tf_op | source)
XLA Modules:
  0.0 79.6 jit_solution(10014255742358341234)
XLA Ops:
  0.7 5.3 %shard_map.138 = (bf16[128,768]{1,0:T(8,128)(2,1)S(1)}, bf16[128,768]{1,0:T(8,128)(2,1)S(1)}, bf16[128,768]{1,0:T(8,128)(2,1)S(1)}, bf16[128,768]{1,0:T(8,128)(2...) custom-call(s32[5,768]{1,0:T(8,128)} %rows_hbm.1, ...), custom_call_target="tpu_custom_call" | custom-call | flops 2013265920 | bytes 1000000 | tf_op jit(solution)/shard_map/pallas_call | solution.py:78
  5.9 1.5 %collective-permute-start = (bf16[128,768]{1,0:T(8,128)(2,1)S(1)}, bf16[128,768]{1,0:T(8,128)(2,1)S(1)}, u32[]{:S(2)}, u32[]{:S(2)}) collective-permute-start(bf16[128,768]{1,0:T(8,128)(2,1)S(1)} %get-tuple-element.25), channel_id=1, source_target_pairs={{0,1},{1,0},{2,3},{3,2},{4,5},{5,4},{6,7},{7,6},{8,9},{9,8},{10,11... | collective-permute-start | bytes 589832 | tf_op jit(solution)/shard_map/ppermute | solution.py:386
  7.5 1.7 %collective-permute-start.1 = (bf16[128,768]{1,0:T(8,128)(2,1)S(1)}, bf16[128,768]{1,0:T(8,128)(2,1)S(1)}, u32[]{:S(2)}, u32[]{:S(2)}) collective-permute-start(bf16[128,768]{1,0:T(8,128)(2,1)S(1)} %get-tuple-element.26), channel_id=1, source_target_pairs={{0,2},{1,3},{2,0},{3,1},{4,6},{5,7},{6,4},{7,5},{8,10},{9,11},{10,... | collective-permute-start | bytes 589832 | tf_op jit(solution)/shard_map/ppermute | solution.py:386
  9.2 3.3 %collective-permute-start.2 = (bf16[128,768]{1,0:T(8,128)(2,1)S(1)}, bf16[128,768]{1,0:T(8,128)(2,1)S(1)}, u32[]{:S(2)}, u32[]{:S(2)}) collective-permute-start(bf16[128,768]{1,0:T(8,128)(2,1)S(1)} %get-tuple-element.27), channel_id=1, source_target_pairs={{0,4},{1,5},{2,6},{3,7},{4,0},{5,1},{6,2},{7,3},{8,12},{9,13},{10,... | collective-permute-start | bytes 589832 | tf_op jit(solution)/shard_map/ppermute | solution.py:386
  12.5 1.2 %collective-permute-start.3 = (bf16[128,768]{1,0:T(8,128)(2,1)S(1)}, bf16[128,768]{1,0:T(8,128)(2,1)S(1)}, u32[]{:S(2)}, u32[]{:S(2)}) collective-permute-start(bf16[128,768]{1,0:T(8,128)(2,1)S(1)} %get-tuple-element.28), channel_id=1, source_target_pairs={{0,8},{1,9},{2,10},{3,11},{4,12},{5,13},{6,14},{7,15},{8,0},{9,1},... | collective-permute-start | bytes 589832 | tf_op jit(solution)/shard_map/ppermute | solution.py:386
  13.7 2.5 %collective-permute-start.4 = (bf16[128,768]{1,0:T(8,128)(2,1)S(1)}, bf16[128,768]{1,0:T(8,128)(2,1)S(1)}, u32[]{:S(2)}, u32[]{:S(2)}) collective-permute-start(bf16[128,768]{1,0:T(8,128)(2,1)S(1)} %get-tuple-element.29), channel_id=1, source_target_pairs={{0,16},{1,17},{2,18},{3,19},{4,20},{5,21},{6,22},{7,23},{8,24},{9,... | collective-permute-start | bytes 589832 | tf_op jit(solution)/shard_map/ppermute | solution.py:386
  16.2 9.2 %shard_map.139 = (bf16[16,1024,128]{2,1,0:T(8,128)(2,1)S(1)}, bf16[16,1024,128]{2,1,0:T(8,128)(2,1)S(1)}, bf16[30,1024,128]{2,1,0:T(8,128)(2,1)S(1)}, bf16[30,1024,128]{2,1,0:T(8,128)(2,1)S(1)}) custom-call(s32[16,22]{1,0:T(8,128)S(1)} %copy-done.5, s32[16,20]{1,0:T(8,128)S(1)} %copy-done.6, bf16[16,22,128,128]{3,2,1,0:T(8,128)(2,1)} %lt.1, ...), custom_call_target="tpu_custom_call" | custom-call | flops 16000000 | bytes 22020096 | tf_op jit(solution)/shard_map/pallas_call | solution.py:164
  25.3 0.0 copy-start.1
  25.4 0.0 copy-start.2
  25.4 0.0 copy-start.3
  25.4 0.0 copy-start.4
  25.4 0.0 copy-start.7
  25.4 2.3 %shard_map.140.refs_7_ = f32[2048,128]{1,0:T(8,128)S(1)} custom-call(bf16[16,1024,128]{2,1,0:T(8,128)(2,1)S(1)} %get-tuple-element.32.d0_ref, bf16[16,1024,128]{2,1,0:T(8,128)(2,1)S(1)} %get-tuple-element.33.d1_ref, bf16[2048,128]{1,0:T(8,128)(2,1)S(1)} %copy-done), custom_call_target="tpu_custom_call" | custom-call | flops 1073741824 | bytes 1500000 | tf_op jit(solution)/shard_map/pallas_call | solution.py:193
  27.7 0.0 collective-permute-done.refs_0_
  27.7 0.0 collective-permute-done.1.refs_1_
  27.8 0.0 collective-permute-done.2.refs_2_
  27.8 0.0 collective-permute-done.3.refs_3_
  27.8 0.0 collective-permute-done.4.refs_4_
  27.8 11.8 %shard_map.141 = (bf16[2048,128]{1,0:T(8,128)(2,1)}, bf16[2048,128]{1,0:T(8,128)(2,1)S(1)}, bf16[128,2048]{1,0:T(8,128)(2,1)S(1)}, f32[128,128]{1,0:T(8,128)S(1)}, f32[128,128]{1,0:T(8,128)S(1)}) custom-call(bf16[128,768]{1,0:T(8,128)(2,1)S(1)} %collective-permute-done.refs_0_, bf16[128,768]{1,0:T(8,128)(2,1)S(1)} %collective-permute-done.1.refs_1_, ...), custom_call_target="tpu_custom_call" | custom-call | flops 2013265920 | bytes 5000000 | tf_op jit(solution)/shard_map/pallas_call | solution.py:247
  39.6 1.2 %collective-permute-start.10 = (f32[128,128]{1,0:T(8,128)S(1)}, f32[128,128]{1,0:T(8,128)S(1)}, u32[]{:S(2)}, u32[]{:S(2)}) collective-permute-start(f32[128,128]{1,0:T(8,128)S(1)} %get-tuple-element.43), channel_id=1, source_target_pairs={{0,1},{1,0},{2,3},{3,2},{4,5},{5,4},{6,7},{7,6},{8,9},{9,8},{10,11... | collective-permute-start | bytes 196616 | tf_op jit(solution)/shard_map/ppermute | solution.py:386
  40.8 0.9 %collective-permute-done.10.right_ref = f32[128,128]{1,0:T(8,128)S(1)} collective-permute-done((f32[128,128]{1,0:T(8,128)S(1)}, f32[128,128]{1,0:T(8,128)S(1)}, u32[]{:S(2)}, u32[]{:S(2)}) %collective-permute-start.10) | collective-permute-done | bytes 65568 | tf_op jit(solution)/shard_map/ppermute | solution.py:386
  41.7 0.1 collective-permute-start.11
  41.8 3.1 %collective-permute-done.11.right_ref = f32[128,128]{1,0:T(8,128)S(1)} collective-permute-done((f32[128,128]{1,0:T(8,128)S(1)}, f32[128,128]{1,0:T(8,128)S(1)}, u32[]{:S(2)}, u32[]{:S(2)}) %collective-permute-start.11) | collective-permute-done | bytes 65568 | tf_op jit(solution)/shard_map/ppermute | solution.py:386
  45.0 0.1 collective-permute-start.12
  45.1 0.6 shard_map.142.before_ref
  45.6 4.0 %collective-permute-done.12.right_ref = f32[128,128]{1,0:T(8,128)S(1)} collective-permute-done((f32[128,128]{1,0:T(8,128)S(1)}, f32[128,128]{1,0:T(8,128)S(1)}, u32[]{:S(2)}, u32[]{:S(2)}) %collective-permute-start.12) | collective-permute-done | bytes 65568 | tf_op jit(solution)/shard_map/ppermute | solution.py:386
  49.7 0.1 collective-permute-start.13
  49.8 0.6 shard_map.143.before_ref
  50.4 0.6 shard_map.144.before_ref
  51.0 1.9 %collective-permute-done.13.right_ref = f32[128,128]{1,0:T(8,128)S(1)} collective-permute-done((f32[128,128]{1,0:T(8,128)S(1)}, f32[128,128]{1,0:T(8,128)S(1)}, u32[]{:S(2)}, u32[]{:S(2)}) %collective-permute-start.13) | collective-permute-done | bytes 65568 | tf_op jit(solution)/shard_map/ppermute | solution.py:386
  52.9 0.6 collective-permute-start.14
  53.5 0.6 shard_map.145.before_ref
  54.1 0.6 shard_map.146.before_ref
  54.7 4.2 %collective-permute-start.5 = (bf16[128,768]{1,0:T(8,128)(2,1)S(1)}, bf16[128,768]{1,0:T(8,128)(2,1)S(1)}, u32[]{:S(2)}, u32[]{:S(2)}) collective-permute-start(bf16[128,768]{1,0:T(8,128)(2,1)S(1)} %shard_map.146.before_ref), channel_id=1, source_target_pairs={{0,1},{1,0},{2,3},{3,2},{4,5},{5,4},{6,7},{7,6},{8,9},{9,8},{10,11... | collective-permute-start | bytes 589832 | tf_op jit(solution)/shard_map/ppermute | solution.py:386
  58.8 0.3 collective-permute-start.6
  59.1 1.4 %collective-permute-start.15 = (f32[128,128]{1,0:T(8,128)S(1)}, f32[128,128]{1,0:T(8,128)S(1)}, u32[]{:S(2)}, u32[]{:S(2)}) collective-permute-start(f32[128,128]{1,0:T(8,128)S(1)} %shard_map.154.left_ref), channel_id=1, source_target_pairs={{0,32},{1,33},{2,34},{3,35},{4,36},{5,37},{6,38},{7,39},{8,40},{9,... | collective-permute-start | bytes 196616 | tf_op jit(solution)/shard_map/ppermute | solution.py:386
  60.5 0.0 collective-permute-start.7
  60.5 2.8 %collective-permute-start.8 = (bf16[128,768]{1,0:T(8,128)(2,1)S(1)}, bf16[128,768]{1,0:T(8,128)(2,1)S(1)}, u32[]{:S(2)}, u32[]{:S(2)}) collective-permute-start(bf16[128,768]{1,0:T(8,128)(2,1)S(1)} %shard_map.143.before_ref), channel_id=1, source_target_pairs={{0,16},{1,17},{2,18},{3,19},{4,20},{5,21},{6,22},{7,23},{8,24},{9,... | collective-permute-start | bytes 589832 | tf_op jit(solution)/shard_map/ppermute | solution.py:386
  63.3 0.2 collective-permute-start.9
  63.5 1.4 %shard_map.147.acc_ref = f32[128,2048]{1,0:T(8,128)S(1)} custom-call(bf16[128,2048]{1,0:T(8,128)(2,1)S(1)} %get-tuple-element.35.st_ref.before_ref, bf16[16,1024,128]{2,1,0:T(8,128)(2,1)S(1)} %get-tuple-element.32.d0_ref, bf16[16,1024,128]{2,1,0:T(8,128)(2,1)S(1)} %get-tuple-element.33.d1_ref, bf16[2048,128]{1,0:T(8,128)(2,1)S(1)} %get-tuple-element.36.gp_ref, ...), custom_call_target="tpu_custom_call" | custom-call | flops 1073741824 | bytes 1500000 | tf_op jit(solution)/shard_map/pallas_call | solution.py:311
  64.9 2.7 %collective-permute-start.16 = (f32[128,128]{1,0:T(8,128)S(1)}, f32[128,128]{1,0:T(8,128)S(1)}, u32[]{:S(2)}, u32[]{:S(2)}) collective-permute-start(f32[128,128]{1,0:T(8,128)S(1)} %shard_map.155.left_ref), channel_id=1, source_target_pairs={{0,64},{1,65},{2,66},{3,67},{4,68},{5,69},{6,70},{7,71},{8,72},{9,... | collective-permute-start | bytes 196616 | tf_op jit(solution)/shard_map/ppermute | solution.py:386
  67.6 2.1 %shard_map.148.acc_ref = f32[128,2048]{1,0:T(8,128)S(1)} custom-call(f32[128,2048]{1,0:T(8,128)S(1)} %shard_map.147.acc_ref, bf16[128,768]{1,0:T(8,128)(2,1)S(1)} %collective-permute-done.5.refs_0_, bf16[128,768]{1,0:T(8,128)(2,1)S(1)} %collective-permute-done.6.refs_1_, bf16[2048,768]{1,0:T(8,128)(2,1)S(1)} %get-tuple-element.37.refs_2_, ...), custom_call_target="tpu_custom_call" | custom-call | flops 805306368 | bytes 2000000 | tf_op jit(solution)/shard_map/pallas_call | solution.py:341
  69.8 0.1 collective-permute-done.16.right_ref
  69.9 4.8 %collective-permute-start.17 = (f32[128,128]{1,0:T(8,128)S(1)}, f32[128,128]{1,0:T(8,128)S(1)}, u32[]{:S(2)}, u32[]{:S(2)}) collective-permute-start(f32[128,128]{1,0:T(8,128)S(1)} %shard_map.156.total_ref), channel_id=1, source_target_pairs={{0,1},{1,0},{2,3},{3,2},{4,5},{5,4},{6,7},{7,6},{8,9},{9,8},{10,11... | collective-permute-start | bytes 196616 | tf_op jit(solution)/shard_map/ppermute | solution.py:386
  74.7 0.0 collective-permute-done.7.refs_0_
  74.7 4.2 %shard_map.149 = f32[2048,128]{1,0:T(8,128)} custom-call(f32[128,2048]{1,0:T(8,128)S(1)} %shard_map.148.acc_ref, bf16[128,768]{1,0:T(8,128)(2,1)S(1)} %collective-permute-done.7.refs_0_, bf16[128,768]{1,0:T(8,128)(2,1)S(1)} %collective-permute-done.8.refs_1_, bf16[128,768]{1,0:T(8,128)(2,1)S(1)} %collective-permute-done.9.refs_2_, ...), custom_call_target="tpu_custom_call" | custom-call | flops 1207959552 | bytes 2000000 | tf_op jit(solution)/shard_map/pallas_call | solution.py:341
  78.9 0.0 collective-permute-done.17.other_ref
  78.9 0.7 shard_map.157
  (24 shorter events, 0.1 us)
Async XLA Ops:
  0.6 15.5 %copy-start.6 = (s32[16,20]{1,0:T(8,128)S(1)}, s32[16,20]{1,0:T(8,128)}, u32[]{:S(2)}) copy-start(s32[16,20]{1,0:T(8,128)} %hc.1) | copy-start | bytes 3844
  0.6 15.5 %copy-start.5 = (s32[16,22]{1,0:T(8,128)S(1)}, s32[16,22]{1,0:T(8,128)}, u32[]{:S(2)}) copy-start(s32[16,22]{1,0:T(8,128)} %lc.1) | copy-start | bytes 4228
  5.9 21.8 %collective-permute-start = (bf16[128,768]{1,0:T(8,128)(2,1)S(1)}, bf16[128,768]{1,0:T(8,128)(2,1)S(1)}, u32[]{:S(2)}, u32[]{:S(2)}) collective-permute-start(bf16[128,768]{1,0:T(8,128)(2,1)S(1)} %get-tuple-element.25), channel_id=1, source_target_pairs={{0,1},{1,0},{2,3},{3,2},{4,5},{5,4},{6,7},{7,6},{8,9},{9,8},{10,11... | collective-permute-start | bytes 589832 | tf_op jit(solution)/shard_map/ppermute | solution.py:386
  7.5 20.3 %collective-permute-start.1 = (bf16[128,768]{1,0:T(8,128)(2,1)S(1)}, bf16[128,768]{1,0:T(8,128)(2,1)S(1)}, u32[]{:S(2)}, u32[]{:S(2)}) collective-permute-start(bf16[128,768]{1,0:T(8,128)(2,1)S(1)} %get-tuple-element.26), channel_id=1, source_target_pairs={{0,2},{1,3},{2,0},{3,1},{4,6},{5,7},{6,4},{7,5},{8,10},{9,11},{10,... | collective-permute-start | bytes 589832 | tf_op jit(solution)/shard_map/ppermute | solution.py:386
  9.2 18.6 %collective-permute-start.2 = (bf16[128,768]{1,0:T(8,128)(2,1)S(1)}, bf16[128,768]{1,0:T(8,128)(2,1)S(1)}, u32[]{:S(2)}, u32[]{:S(2)}) collective-permute-start(bf16[128,768]{1,0:T(8,128)(2,1)S(1)} %get-tuple-element.27), channel_id=1, source_target_pairs={{0,4},{1,5},{2,6},{3,7},{4,0},{5,1},{6,2},{7,3},{8,12},{9,13},{10,... | collective-permute-start | bytes 589832 | tf_op jit(solution)/shard_map/ppermute | solution.py:386
  12.5 15.3 %collective-permute-start.3 = (bf16[128,768]{1,0:T(8,128)(2,1)S(1)}, bf16[128,768]{1,0:T(8,128)(2,1)S(1)}, u32[]{:S(2)}, u32[]{:S(2)}) collective-permute-start(bf16[128,768]{1,0:T(8,128)(2,1)S(1)} %get-tuple-element.28), channel_id=1, source_target_pairs={{0,8},{1,9},{2,10},{3,11},{4,12},{5,13},{6,14},{7,15},{8,0},{9,1},... | collective-permute-start | bytes 589832 | tf_op jit(solution)/shard_map/ppermute | solution.py:386
  13.7 11.6 %copy-start = (bf16[2048,128]{1,0:T(8,128)(2,1)S(1)}, bf16[2048,128]{1,0:T(8,128)(2,1)}, u32[]{:S(2)}) copy-start(bf16[2048,128]{1,0:T(8,128)(2,1)} %refs_8_.1) | copy-start | bytes 1572868
  13.7 14.1 %collective-permute-start.4 = (bf16[128,768]{1,0:T(8,128)(2,1)S(1)}, bf16[128,768]{1,0:T(8,128)(2,1)S(1)}, u32[]{:S(2)}, u32[]{:S(2)}) collective-permute-start(bf16[128,768]{1,0:T(8,128)(2,1)S(1)} %get-tuple-element.29), channel_id=1, source_target_pairs={{0,16},{1,17},{2,18},{3,19},{4,20},{5,21},{6,22},{7,23},{8,24},{9,... | collective-permute-start | bytes 589832 | tf_op jit(solution)/shard_map/ppermute | solution.py:386
  25.3 2.4 %copy-start.1 = (bf16[2048,128]{1,0:T(8,128)(2,1)S(1)}, bf16[2048,128]{1,0:T(8,128)(2,1)}, u32[]{:S(2)}) copy-start(bf16[2048,128]{1,0:T(8,128)(2,1)} %refs_9_.1) | copy-start | bytes 1572868
  25.4 2.4 %copy-start.2 = (bf16[128,128]{1,0:T(8,128)(2,1)S(1)}, bf16[128,128]{1,0:T(8,128)(2,1)}, u32[]{:S(2)}) copy-start(bf16[128,128]{1,0:T(8,128)(2,1)} %ws_ref.1) | copy-start | bytes 98308
  25.4 2.4 %copy-start.3 = (bf16[128,128]{1,0:T(8,128)(2,1)S(1)}, bf16[128,128]{1,0:T(8,128)(2,1)}, u32[]{:S(2)}) copy-start(bf16[128,128]{1,0:T(8,128)(2,1)} %refs_12_.1) | copy-start | bytes 98308
  25.4 2.4 %copy-start.4 = (s32[2048]{0:T(1024)S(1)}, s32[2048]{0:T(1024)}, u32[]{:S(2)}) copy-start(s32[2048]{0:T(1024)} %param.20) | copy-start | bytes 24580
  25.4 2.4 %copy-start.7 = (f32[128]{0:T(128)S(1)}, f32[128]{0:T(128)}, u32[]{:S(2)}) copy-start(f32[128]{0:T(128)} %param.14) | copy-start | bytes 1540
  39.6 2.1 %collective-permute-start.10 = (f32[128,128]{1,0:T(8,128)S(1)}, f32[128,128]{1,0:T(8,128)S(1)}, u32[]{:S(2)}, u32[]{:S(2)}) collective-permute-start(f32[128,128]{1,0:T(8,128)S(1)} %get-tuple-element.43), channel_id=1, source_target_pairs={{0,1},{1,0},{2,3},{3,2},{4,5},{5,4},{6,7},{7,6},{8,9},{9,8},{10,11... | collective-permute-start | bytes 196616 | tf_op jit(solution)/shard_map/ppermute | solution.py:386
  41.7 3.2 %collective-permute-start.11 = (f32[128,128]{1,0:T(8,128)S(1)}, f32[128,128]{1,0:T(8,128)S(1)}, u32[]{:S(2)}, u32[]{:S(2)}) collective-permute-start(f32[128,128]{1,0:T(8,128)S(1)} %shard_map.150.left_ref), channel_id=1, source_target_pairs={{0,2},{1,3},{2,0},{3,1},{4,6},{5,7},{6,4},{7,5},{8,10},{9,11},{10,... | collective-permute-start | bytes 196616 | tf_op jit(solution)/shard_map/ppermute | solution.py:386
  45.0 4.7 %collective-permute-start.12 = (f32[128,128]{1,0:T(8,128)S(1)}, f32[128,128]{1,0:T(8,128)S(1)}, u32[]{:S(2)}, u32[]{:S(2)}) collective-permute-start(f32[128,128]{1,0:T(8,128)S(1)} %shard_map.151.left_ref), channel_id=1, source_target_pairs={{0,4},{1,5},{2,6},{3,7},{4,0},{5,1},{6,2},{7,3},{8,12},{9,13},{10,... | collective-permute-start | bytes 196616 | tf_op jit(solution)/shard_map/ppermute | solution.py:386
  49.7 3.2 %collective-permute-start.13 = (f32[128,128]{1,0:T(8,128)S(1)}, f32[128,128]{1,0:T(8,128)S(1)}, u32[]{:S(2)}, u32[]{:S(2)}) collective-permute-start(f32[128,128]{1,0:T(8,128)S(1)} %shard_map.152.left_ref), channel_id=1, source_target_pairs={{0,8},{1,9},{2,10},{3,11},{4,12},{5,13},{6,14},{7,15},{8,0},{9,1},... | collective-permute-start | bytes 196616 | tf_op jit(solution)/shard_map/ppermute | solution.py:386
  52.9 6.2 %collective-permute-start.14 = (f32[128,128]{1,0:T(8,128)S(1)}, f32[128,128]{1,0:T(8,128)S(1)}, u32[]{:S(2)}, u32[]{:S(2)}) collective-permute-start(f32[128,128]{1,0:T(8,128)S(1)} %shard_map.153.left_ref), channel_id=1, source_target_pairs={{0,16},{1,17},{2,18},{3,19},{4,20},{5,21},{6,22},{7,23},{8,24},{9,... | collective-permute-start | bytes 196616 | tf_op jit(solution)/shard_map/ppermute | solution.py:386
  54.7 10.3 %collective-permute-start.5 = (bf16[128,768]{1,0:T(8,128)(2,1)S(1)}, bf16[128,768]{1,0:T(8,128)(2,1)S(1)}, u32[]{:S(2)}, u32[]{:S(2)}) collective-permute-start(bf16[128,768]{1,0:T(8,128)(2,1)S(1)} %shard_map.146.before_ref), channel_id=1, source_target_pairs={{0,1},{1,0},{2,3},{3,2},{4,5},{5,4},{6,7},{7,6},{8,9},{9,8},{10,11... | collective-permute-start | bytes 589832 | tf_op jit(solution)/shard_map/ppermute | solution.py:386
  58.8 8.8 %collective-permute-start.6 = (bf16[128,768]{1,0:T(8,128)(2,1)S(1)}, bf16[128,768]{1,0:T(8,128)(2,1)S(1)}, u32[]{:S(2)}, u32[]{:S(2)}) collective-permute-start(bf16[128,768]{1,0:T(8,128)(2,1)S(1)} %shard_map.145.before_ref), channel_id=1, source_target_pairs={{0,8},{1,9},{2,10},{3,11},{4,12},{5,13},{6,14},{7,15},{8,0},{9,1},... | collective-permute-start | bytes 589832 | tf_op jit(solution)/shard_map/ppermute | solution.py:386
  59.1 4.2 %collective-permute-start.15 = (f32[128,128]{1,0:T(8,128)S(1)}, f32[128,128]{1,0:T(8,128)S(1)}, u32[]{:S(2)}, u32[]{:S(2)}) collective-permute-start(f32[128,128]{1,0:T(8,128)S(1)} %shard_map.154.left_ref), channel_id=1, source_target_pairs={{0,32},{1,33},{2,34},{3,35},{4,36},{5,37},{6,38},{7,39},{8,40},{9,... | collective-permute-start | bytes 196616 | tf_op jit(solution)/shard_map/ppermute | solution.py:386
  60.5 14.2 %collective-permute-start.7 = (bf16[128,768]{1,0:T(8,128)(2,1)S(1)}, bf16[128,768]{1,0:T(8,128)(2,1)S(1)}, u32[]{:S(2)}, u32[]{:S(2)}) collective-permute-start(bf16[128,768]{1,0:T(8,128)(2,1)S(1)} %shard_map.144.before_ref), channel_id=1, source_target_pairs={{0,2},{1,3},{2,0},{3,1},{4,6},{5,7},{6,4},{7,5},{8,10},{9,11},{10,... | collective-permute-start | bytes 589832 | tf_op jit(solution)/shard_map/ppermute | solution.py:386
  60.5 14.2 %collective-permute-start.8 = (bf16[128,768]{1,0:T(8,128)(2,1)S(1)}, bf16[128,768]{1,0:T(8,128)(2,1)S(1)}, u32[]{:S(2)}, u32[]{:S(2)}) collective-permute-start(bf16[128,768]{1,0:T(8,128)(2,1)S(1)} %shard_map.143.before_ref), channel_id=1, source_target_pairs={{0,16},{1,17},{2,18},{3,19},{4,20},{5,21},{6,22},{7,23},{8,24},{9,... | collective-permute-start | bytes 589832 | tf_op jit(solution)/shard_map/ppermute | solution.py:386
  63.3 11.4 %collective-permute-start.9 = (bf16[128,768]{1,0:T(8,128)(2,1)S(1)}, bf16[128,768]{1,0:T(8,128)(2,1)S(1)}, u32[]{:S(2)}, u32[]{:S(2)}) collective-permute-start(bf16[128,768]{1,0:T(8,128)(2,1)S(1)} %shard_map.142.before_ref), channel_id=1, source_target_pairs={{0,4},{1,5},{2,6},{3,7},{4,0},{5,1},{6,2},{7,3},{8,12},{9,13},{10,... | collective-permute-start | bytes 589832 | tf_op jit(solution)/shard_map/ppermute | solution.py:386
  64.9 5.0 %collective-permute-start.16 = (f32[128,128]{1,0:T(8,128)S(1)}, f32[128,128]{1,0:T(8,128)S(1)}, u32[]{:S(2)}, u32[]{:S(2)}) collective-permute-start(f32[128,128]{1,0:T(8,128)S(1)} %shard_map.155.left_ref), channel_id=1, source_target_pairs={{0,64},{1,65},{2,66},{3,67},{4,68},{5,69},{6,70},{7,71},{8,72},{9,... | collective-permute-start | bytes 196616 | tf_op jit(solution)/shard_map/ppermute | solution.py:386
  69.9 9.0 %collective-permute-start.17 = (f32[128,128]{1,0:T(8,128)S(1)}, f32[128,128]{1,0:T(8,128)S(1)}, u32[]{:S(2)}, u32[]{:S(2)}) collective-permute-start(f32[128,128]{1,0:T(8,128)S(1)} %shard_map.156.total_ref), channel_id=1, source_target_pairs={{0,1},{1,0},{2,3},{3,2},{4,5},{5,4},{6,7},{7,6},{8,9},{9,8},{10,11... | collective-permute-start | bytes 196616 | tf_op jit(solution)/shard_map/ppermute | solution.py:386

commit v4 on v3

--- a/solution.py
+++ b/solution.py
@@ -48,9 +48,8 @@
 
 
 def pick_kernel(rows_hbm, x_hbm, *refs):
-    rounds = (len(refs) - 5) // 2
-    outs, tables = refs[:rounds], refs[rounds : 2 * rounds]
-    rows_ref, x_ref, xt_ref, rows_sem, x_sem = refs[2 * rounds :]
+    outs, (rows_ref, x_ref, xt_ref, rows_sem, x_sem) = refs[:-5], refs[-5:]
+    rounds = len(outs)
     rows_copy = pltpu.make_async_copy(rows_hbm, rows_ref, rows_sem)
     x_copy = pltpu.make_async_copy(x_hbm, x_ref, x_sem)
     rows_copy.start()
@@ -62,7 +61,6 @@
         for k in range(0, rows_ref.shape[1], step):
             listed = rows_ref[r : r + 1, k : k + step]
             table = jnp.where(numbers == listed, 1.0, 0.0).astype(jnp.bfloat16)
-            tables[r][:, k : k + step] = table
             if r == 0 and k == 0:
                 x_copy.wait()
                 for i in range(0, count, TILE):
@@ -74,8 +72,7 @@
     rows, width = features.shape
     rounds, boundary = send_rows.shape
     outs = [jax.ShapeDtypeStruct((width, boundary), jnp.bfloat16) for _ in range(rounds)]
-    outs += [VMEM((rows, boundary), jnp.bfloat16) for _ in range(rounds)]
-    results = pl.pallas_call(
+    return pl.pallas_call(
         pick_kernel,
         out_shape=outs,
         in_specs=[pl.BlockSpec(memory_space=pltpu.HBM)] * 2,
@@ -90,7 +87,6 @@
         compiler_params=params(),
         cost_estimate=cost(2 * rows * boundary * rounds * width, 1_000_000),
     )(in_hbm(send_rows), in_hbm(features))
-    return results[:rounds], results[rounds:]
 
 
 def densify_kernel(lc, hc, lt, ht, dl0, dl1, dh0, dh1, lslots, hslots, zeros, sems, zsems):
@@ -203,35 +199,41 @@
 def middle_kernel(rounds, *refs):
     got, refs = refs[:rounds], refs[rounds:]
     d0, d1, sum_ref, x_ref, ct_ref, deg_ref, ws_ref, wn_ref, bias_ref = refs[:9]
-    out_ref, gp_ref, st_ref, mine_ref, give_ref, both, halo = refs[9:]
+    out_ref, gp_ref, st_ref, mine_ref, give_ref, both, halo, sums = refs[9:]
     core = lax.axis_index("dom") & 1
     half, step = d0.shape[1], 512
     boundary = got[0].shape[1]
+    per = boundary // TILE
     for r in range(rounds):
         halo[r * boundary : (r + 1) * boundary, :] = got[r][...].T
     for p, dense_ref in enumerate((d0, d1)):
         for j in range(0, half, step):
-            left = jnp.concatenate(
-                [dense_ref[c, j : j + step, :] for c in range(dense_ref.shape[0])], axis=1
-            )
             start = p * half + j
-            total = nn_dot(left, halo[...]) + sum_ref[start : start + step, :]
-            for i in range(start // TILE, (start + step) // TILE):
-                rows = slice(i * TILE, (i + 1) * TILE)
-                line = deg_ref[i : i + 1, :].astype(jnp.float32)
-                column = jnp.broadcast_to(line, (TILE, TILE)).T
-                agg = total[i * TILE - start : (i + 1) * TILE - start, :] / column
-                agg = agg.astype(jnp.bfloat16)
-                both[rows, :TILE] = x_ref[rows, :]
-                both[rows, TILE:] = agg
-                preact = nn_dot(x_ref[rows, :], ws_ref[...]) + nn_dot(agg, wn_ref[...])
-                preact = preact + bias_ref[...]
-                sig = jax.nn.sigmoid(preact)
-                out_ref[rows, :] = (preact * sig).astype(jnp.bfloat16)
-                grad = ct_ref[rows, :].astype(jnp.float32) * sig * (1.0 + preact * (1.0 - sig))
-                grad = grad.astype(jnp.bfloat16)
-                gp_ref[rows, :] = grad
-                st_ref[:, rows] = (nt_dot(wn_ref[...], grad) / line).astype(jnp.bfloat16)
+            total = sum_ref[start : start + step, :]
+            for r in range(rounds):
+                left = jnp.concatenate(
+                    [dense_ref[c, j : j + step, :] for c in range(r * per, (r + 1) * per)], axis=1
+                )
+                total = total + nn_dot(left, halo[r * boundary : (r + 1) * boundary, :])
+            sums[start : start + step, :] = total
+    for start in range(0, 2 * half, step):
+        total = sums[start : start + step, :]
+        for i in range(start // TILE, (start + step) // TILE):
+            rows = slice(i * TILE, (i + 1) * TILE)
+            line = deg_ref[i : i + 1, :].astype(jnp.float32)
+            column = jnp.broadcast_to(line, (TILE, TILE)).T
+            agg = total[i * TILE - start : (i + 1) * TILE - start, :] / column
+            agg = agg.astype(jnp.bfloat16)
+            both[rows, :TILE] = x_ref[rows, :]
+            both[rows, TILE:] = agg
+            preact = nn_dot(x_ref[rows, :], ws_ref[...]) + nn_dot(agg, wn_ref[...])
+            preact = preact + bias_ref[...]
+            sig = jax.nn.sigmoid(preact)
+            out_ref[rows, :] = (preact * sig).astype(jnp.bfloat16)
+            grad = ct_ref[rows, :].astype(jnp.float32) * sig * (1.0 + preact * (1.0 - sig))
+            grad = grad.astype(jnp.bfloat16)
+            gp_ref[rows, :] = grad
+            st_ref[:, rows] = (nt_dot(wn_ref[...], grad) / line).astype(jnp.bfloat16)
     parts = lax.dot_general(
         both[...], gp_ref[...], (((0,), (0,)), ((), ())), preferred_element_type=jnp.float32
     )
@@ -258,6 +260,7 @@
         scratch_shapes=[
             VMEM((rows, 2 * width), jnp.bfloat16),
             VMEM((rounds * boundary, width), jnp.bfloat16),
+            VMEM((rows, width), jnp.float32),
         ],
         compiler_params=params(),
         cost_estimate=cost(2 * rows * rounds * boundary * width, 5_000_000, rows * width),
@@ -295,7 +298,7 @@
         in_specs=[vspec()] * 3 + [pl.BlockSpec(memory_space=pl.ANY)],
         out_specs=vspec(),
         compiler_params=params(),
-        cost_estimate=cost(2 * rows * n * TILE * width, 500_000),
+        cost_estimate=cost(1, 1),
     )(pinned(scaled_t), pinned(d0), pinned(d1), before)
 
 
@@ -314,53 +317,66 @@
         in_specs=[vspec()] * 5 + [pl.BlockSpec(memory_space=pl.ANY)],
         out_specs=vspec(),
         compiler_params=params(),
-        cost_estimate=cost(2 * rows * rows * width, 1_500_000),
+        cost_estimate=cost(1, 1),
     )(pinned(scaled_t), pinned(d0), pinned(d1), pinned(grad_pre), w_self, before)
 
 
-def place_kernel(count, last, acc_ref, *refs):
-    returned, tables, out_ref = refs[:count], refs[count : 2 * count], refs[-1]
-    step = 2 * TILE
+def place_kernel(rounds, last, rows_ref, acc_ref, before_ref, *refs):
+    returned, (out_ref, listed) = refs[: len(rounds)], refs[len(rounds) :]
+    step, boundary = 2 * TILE, rows_ref.shape[1]
+    for place, r in enumerate(rounds):
+        for k in range(0, boundary, TILE):
+            line = rows_ref[r : r + 1, k : k + TILE].astype(jnp.float32)
+            listed[place, k : k + TILE, :] = jnp.broadcast_to(line, (TILE, TILE)).T
+    numbers = lax.broadcasted_iota(jnp.int32, (boundary, TILE), 1).astype(jnp.float32)
     for j in range(0, acc_ref.shape[1], step):
         total = acc_ref[:, j : j + step]
-        for got_ref, table_ref in zip(returned, tables):
-            total = total + nt_dot(got_ref[...], table_ref[j : j + step, :])
+        for place, got_ref in enumerate(returned):
+            table = jnp.concatenate(
+                [
+                    jnp.where(listed[place] == numbers + float(n), 1.0, 0.0).astype(jnp.bfloat16)
+                    for n in range(j, j + step, TILE)
+                ],
+                axis=1,
+            )
+            total = total + nn_dot(got_ref[...], table)
         if last:
             out_ref[j : j + step, :] = total.T
         else:
             out_ref[:, j : j + step] = total
 
 
-def place_rows(last, acc, returned, tables):
+def place_rows(rounds, last, send_rows, acc, returned, before):
     width, rows = acc.shape
-    count, boundary = len(returned), tables[0].shape[1]
+    count, boundary = len(rounds), send_rows.shape[1]
     if last:
         out = jax.ShapeDtypeStruct((rows, width), jnp.float32)
     else:
         out = VMEM((width, rows), jnp.float32)
     return pl.pallas_call(
-        functools.partial(place_kernel, count, last),
+        functools.partial(place_kernel, rounds, last),
         out_shape=out,
-        in_specs=[vspec()] * (1 + 2 * count),
+        in_specs=[vspec()] * 2 + [pl.BlockSpec(memory_space=pl.ANY)] + [vspec()] * count,
         out_specs=vspec(),
-        compiler_params=params(),
-        cost_estimate=cost(2 * rows * count * boundary * width, 2_000_000),
-    )(pinned(acc), *returned, *[pinned(t) for t in tables])
-
-
-def add_kernel(left_ref, right_ref, out_ref):
+        scratch_shapes=[VMEM((count, boundary, TILE), jnp.float32)],
+        compiler_params=params(),
+        cost_estimate=cost(1, 1),
+    )(send_rows, pinned(acc), before, *returned)
+
+
+def add_kernel(left_ref, right_ref, before_ref, out_ref):
     out_ref[...] = left_ref[...] + right_ref[...]
 
 
-def added(left, right):
+def added(left, right, before):
     return pl.pallas_call(
         add_kernel,
         out_shape=VMEM(left.shape, jnp.float32),
-        in_specs=[vspec()] * 2,
+        in_specs=[vspec()] * 2 + [pl.BlockSpec(memory_space=pl.ANY)],
         out_specs=vspec(),
         compiler_params=params(1024 * 1024),
-        cost_estimate=cost(left.size, 3 * left.size * 4),
-    )(pinned(left), right)
+        cost_estimate=cost(1, 1),
+    )(pinned(left), right, before)
 
 
 def halves_kernel(scale, total_ref, other_ref, self_ref, neigh_ref):
@@ -384,15 +400,6 @@
 
 def swapped(shard, mask):
     return lax.ppermute(shard, "dom", [(i, i ^ mask) for i in range(lax.axis_size("dom"))])
-
-
-def summed_everywhere(mine, give, scale):
-    total = added(mine, swapped(give, 1))
-    mask = 2
-    while mask < lax.axis_size("dom"):
-        total = added(total, swapped(total, mask))
-        mask *= 2
-    return halves(scale, total, swapped(total, 1))
 
 
 def local(
@@ -412,7 +419,7 @@
     nblocks = local_tiles.shape[0]
     round_count, boundary = send_rows.shape
     per = boundary // TILE
-    picked, tables = pick_rows(send_rows, node_features)
+    picked = pick_rows(send_rows, node_features)
     received = [swapped(rows, 1 << r) for r, rows in enumerate(picked)]
     dl0, dl1, dh0, dh1 = densify(
         local_cols, halo_cols, local_tiles, halo_tiles, round_count * per
@@ -431,17 +438,43 @@
         output_bias.reshape(1, width),
     )
     returned = {}
-    before = scaled_t
-    for r in (2, 4, 1, 3, 0):
-        before = back(r * per, per, scaled_t, dh0, dh1, before)
-        returned[r] = swapped(before, 1 << r)
+
+    def send_back(r, before):
+        grads = back(r * per, per, scaled_t, dh0, dh1, before)
+        returned[r] = swapped(grads, 1 << r)
+        return grads
+
+    def place(rounds, acc, before):
+        got = [returned[r] for r in rounds]
+        return place_rows(rounds, 2 in rounds, send_rows, acc, got, before)
+
+    other = swapped(give, 1)
+    last = send_back(2, scaled_t)
+    total = added(mine, other, last)
+    other = swapped(total, 32)
+    last = send_back(4, total)
+    last = send_back(1, last)
+    total = added(total, other, last)
+    other = swapped(total, 64)
+    last = send_back(3, total)
+    last = send_back(0, last)
+    total = added(total, other, last)
+    other = swapped(total, 8)
+    grads_t = own(scaled_t, dl0, dl1, grad_pre, w_self, total)
+    total = added(total, other, grads_t)
+    other = swapped(total, 16)
+    grads_t = place((0, 3), grads_t, total)
+    total = added(total, other, grads_t)
+    other = swapped(total, 2)
+    grads_t = place((1,), grads_t, total)
+    total = added(total, other, grads_t)
+    other = swapped(total, 4)
+    grads_t = place((4,), grads_t, total)
+    total = added(total, other, grads_t)
+    other = swapped(total, 1)
+    grads_t = place((2,), grads_t, total)
     grad_scale = 1.0 / math.sqrt(row_count * lax.axis_size("dom"))
-    grad_self, grad_neigh = summed_everywhere(mine, give, grad_scale)
-    grads_t = own(scaled_t, dl0, dl1, grad_pre, w_self, before)
-    for rounds in ((0, 3), (1, 4, 2)):
-        grads_t = place_rows(
-            2 in rounds, grads_t, [returned[r] for r in rounds], [tables[r] for r in rounds]
-        )
+    grad_self, grad_neigh = halves(grad_scale, total, other)
     return (output, grads_t, grad_self, grad_neigh)
 
 

time: 79.7 us -> 73.8 us (0.926)
  Pallas kernels: 40 us -> 30.7 us
  waiting for transfers between devices: 10.1 us -> 13.4 us
  starting transfers between devices: 28.5 us -> 27.1 us
  local copies, waits for them, and re-layouts: 0.04 us -> 1.43 us
    pallas_call x1, Pallas kernels: 11.8 us -> 6.21 us  [middle(): pl.pallas_call(functools.partial(middle_kernel, rounds), out_shape=[half,...]
    ppermute x18, waiting for transfers between devices: 10.1 us -> 13.4 us  [swapped(): lax.ppermute(shard, 'dom', [(i, i ^ mask) for i in range(lax.axis_size('d...]
    pallas_call x2 -> x4, Pallas kernels: 6.35 us -> 4.29 us  [place_rows(): pl.pallas_call(functools.partial(place_kernel, rounds, last), out_shape=o...]
    pallas_call x1, Pallas kernels: 5.29 us -> 3.58 us  [pick_rows(): pl.pallas_call(pick_kernel, out_shape=outs, in_specs=[pl.BlockSpec(memory...]
    unnamed x16 -> x18, local copies, waits for them, and re-layouts: 0.04 us -> 1.43 us
    ppermute x18, starting transfers between devices: 28.5 us -> 27.1 us  [swapped(): lax.ppermute(shard, 'dom', [(i, i ^ mask) for i in range(lax.axis_size('d...]
  transfers between devices with their start and end apart: 18 -> 18, of which waited for: 5 -> 6; matrix products, arithmetic and copies ran while one was open for 0% -> 0% of each run, Pallas kernels for 28% -> 27%
where the time goes in v4:
time: 73.8 us; the launch traced here: 73.6 us
  Pallas kernels  30.7 us (42%)
  starting transfers between devices  27.1 us (37%)
  waiting for transfers between devices  13.4 us (18%)
  local copies, waits for them, and re-layouts  1.43 us (2%)
  between operations  0.93 us (1%)
    ppermute x18, starting transfers between devices, swapped(): lax.ppermute(shard, 'dom', [(i, i ^ mask) for i in range(lax.axis_size('d...  27.1 us
    ppermute x18, waiting for transfers between devices, swapped(): lax.ppermute(shard, 'dom', [(i, i ^ mask) for i in range(lax.axis_size('d...  13.4 us
    pallas_call x1, Pallas kernels, densify(): pl.pallas_call(densify_kernel, out_shape=[VMEM((n, half, TILE), jnp.bfloa...  9.17 us
    pallas_call x1, Pallas kernels, middle(): pl.pallas_call(functools.partial(middle_kernel, rounds), out_shape=[half,...  6.21 us
    pallas_call x4, Pallas kernels, place_rows(): pl.pallas_call(functools.partial(place_kernel, rounds, last), out_shape=o...  4.29 us
    pallas_call x1, Pallas kernels, pick_rows(): pl.pallas_call(pick_kernel, out_shape=outs, in_specs=[pl.BlockSpec(memory...  3.58 us
    pallas_call x5, Pallas kernels, back(): pl.pallas_call(functools.partial(back_kernel, first, n), out_shape=jax.Sh...  2.93 us
    pallas_call x1, Pallas kernels, local_sums(): pl.pallas_call(local_sums_kernel, out_shape=VMEM((rows, width), jnp.float...  2.32 us
  transfers between devices with their start and end apart: 18, of which 6 were waited for; matrix products, arithmetic and copies ran while one was open for 0% of the time, Pallas kernels for 27%

profile of v4, /device:TPU:1, one launch (start us, length us, event | category | flops | bytes accessed | tf_op | source)
XLA Modules:
  0.0 73.6 jit_solution(8400518380536384585)
XLA Ops:
  0.6 3.6 %shard_map.138 = (bf16[128,768]{1,0:T(8,128)(2,1)S(1)}, bf16[128,768]{1,0:T(8,128)(2,1)S(1)}, bf16[128,768]{1,0:T(8,128)(2,1)S(1)}, bf16[128,768]{1,0:T(8,128)(2,1)S(1)}, bf16[128,768]{1,0:T(8,128)(2,1)S(1)}) custom-call(s32[5,768]{1,0:T(8,128)} %rows_ref.7, bf16[2048,128]{1,0:T(8,128)(2,1)} %refs_8_.1), custom_call_target="tpu_custom_call" | custom-call | flops 2013265920 | bytes 1000000 | tf_op jit(solution)/shard_map/pallas_call | solution.py:75
  4.2 1.5 %collective-permute-start = (bf16[128,768]{1,0:T(8,128)(2,1)S(1)}, bf16[128,768]{1,0:T(8,128)(2,1)S(1)}, u32[]{:S(2)}, u32[]{:S(2)}) collective-permute-start(bf16[128,768]{1,0:T(8,128)(2,1)S(1)} %get-tuple-element.20), channel_id=1, source_target_pairs={{0,1},{1,0},{2,3},{3,2},{4,5},{5,4},{6,7},{7,6},{8,9},{9,8},{10,11... | collective-permute-start | bytes 589832 | tf_op jit(solution)/shard_map/ppermute | solution.py:402
  5.7 1.7 %collective-permute-start.1 = (bf16[128,768]{1,0:T(8,128)(2,1)S(1)}, bf16[128,768]{1,0:T(8,128)(2,1)S(1)}, u32[]{:S(2)}, u32[]{:S(2)}) collective-permute-start(bf16[128,768]{1,0:T(8,128)(2,1)S(1)} %get-tuple-element.21), channel_id=1, source_target_pairs={{0,2},{1,3},{2,0},{3,1},{4,6},{5,7},{6,4},{7,5},{8,10},{9,11},{10,... | collective-permute-start | bytes 589832 | tf_op jit(solution)/shard_map/ppermute | solution.py:402
  7.5 3.3 %collective-permute-start.2 = (bf16[128,768]{1,0:T(8,128)(2,1)S(1)}, bf16[128,768]{1,0:T(8,128)(2,1)S(1)}, u32[]{:S(2)}, u32[]{:S(2)}) collective-permute-start(bf16[128,768]{1,0:T(8,128)(2,1)S(1)} %get-tuple-element.22), channel_id=1, source_target_pairs={{0,4},{1,5},{2,6},{3,7},{4,0},{5,1},{6,2},{7,3},{8,12},{9,13},{10,... | collective-permute-start | bytes 589832 | tf_op jit(solution)/shard_map/ppermute | solution.py:402
  10.8 1.2 %collective-permute-start.3 = (bf16[128,768]{1,0:T(8,128)(2,1)S(1)}, bf16[128,768]{1,0:T(8,128)(2,1)S(1)}, u32[]{:S(2)}, u32[]{:S(2)}) collective-permute-start(bf16[128,768]{1,0:T(8,128)(2,1)S(1)} %get-tuple-element.23), channel_id=1, source_target_pairs={{0,8},{1,9},{2,10},{3,11},{4,12},{5,13},{6,14},{7,15},{8,0},{9,1},... | collective-permute-start | bytes 589832 | tf_op jit(solution)/shard_map/ppermute | solution.py:402
  12.0 2.5 %collective-permute-start.4 = (bf16[128,768]{1,0:T(8,128)(2,1)S(1)}, bf16[128,768]{1,0:T(8,128)(2,1)S(1)}, u32[]{:S(2)}, u32[]{:S(2)}) collective-permute-start(bf16[128,768]{1,0:T(8,128)(2,1)S(1)} %get-tuple-element.24), channel_id=1, source_target_pairs={{0,16},{1,17},{2,18},{3,19},{4,20},{5,21},{6,22},{7,23},{8,24},{9,... | collective-permute-start | bytes 589832 | tf_op jit(solution)/shard_map/ppermute | solution.py:402
  14.4 0.7 copy-done.6
  15.1 0.7 copy-done.7
  15.8 9.2 %shard_map.139 = (bf16[16,1024,128]{2,1,0:T(8,128)(2,1)S(1)}, bf16[16,1024,128]{2,1,0:T(8,128)(2,1)S(1)}, bf16[30,1024,128]{2,1,0:T(8,128)(2,1)S(1)}, bf16[30,1024,128]{2,1,0:T(8,128)(2,1)S(1)}) custom-call(s32[16,22]{1,0:T(8,128)S(1)} %copy-done.6, s32[16,20]{1,0:T(8,128)S(1)} %copy-done.7, bf16[16,22,128,128]{3,2,1,0:T(8,128)(2,1)} %lt.1, ...), custom_call_target="tpu_custom_call" | custom-call | flops 16000000 | bytes 22020096 | tf_op jit(solution)/shard_map/pallas_call | solution.py:160
  25.0 0.0 copy-start.1
  25.0 0.0 copy-start.3
  25.0 0.0 copy-start.4
  25.0 0.0 copy-start.5
  25.0 0.0 copy-start.8
  25.1 2.3 %shard_map.140.refs_7_ = f32[2048,128]{1,0:T(8,128)S(1)} custom-call(bf16[16,1024,128]{2,1,0:T(8,128)(2,1)S(1)} %get-tuple-element.27.d0_ref, bf16[16,1024,128]{2,1,0:T(8,128)(2,1)S(1)} %get-tuple-element.28.d1_ref, bf16[2048,128]{1,0:T(8,128)(2,1)S(1)} %copy-done), custom_call_target="tpu_custom_call" | custom-call | flops 1073741824 | bytes 1500000 | tf_op jit(solution)/shard_map/pallas_call | solution.py:189
  27.4 0.0 collective-permute-done.refs_0_
  27.4 0.0 collective-permute-done.2.refs_2_
  27.4 0.0 collective-permute-done.3.refs_3_
  27.5 6.2 %shard_map.141 = (bf16[2048,128]{1,0:T(8,128)(2,1)}, bf16[2048,128]{1,0:T(8,128)(2,1)S(1)}, bf16[128,2048]{1,0:T(8,128)(2,1)S(1)}, f32[128,128]{1,0:T(8,128)S(1)}, f32[128,128]{1,0:T(8,128)S(1)}) custom-call(bf16[128,768]{1,0:T(8,128)(2,1)S(1)} %collective-permute-done.refs_0_, bf16[128,768]{1,0:T(8,128)(2,1)S(1)} %collective-permute-done.1.refs_1_, ...), custom_call_target="tpu_custom_call" | custom-call | flops 2013265920 | bytes 5000000 | tf_op jit(solution)/shard_map/pallas_call | solution.py:249
  33.7 1.2 %collective-permute-start.5 = (f32[128,128]{1,0:T(8,128)S(1)}, f32[128,128]{1,0:T(8,128)S(1)}, u32[]{:S(2)}, u32[]{:S(2)}) collective-permute-start(f32[128,128]{1,0:T(8,128)S(1)} %get-tuple-element.33), channel_id=1, source_target_pairs={{0,1},{1,0},{2,3},{3,2},{4,5},{5,4},{6,7},{7,6},{8,9},{9,8},{10,11... | collective-permute-start | bytes 196616 | tf_op jit(solution)/shard_map/ppermute | solution.py:402
  34.9 0.6 shard_map.142.before_ref
  35.5 0.3 collective-permute-done.5.right_ref
  35.8 1.6 %collective-permute-start.6 = (f32[128,128]{1,0:T(8,128)S(1)}, f32[128,128]{1,0:T(8,128)S(1)}, u32[]{:S(2)}, u32[]{:S(2)}) collective-permute-start(f32[128,128]{1,0:T(8,128)S(1)} %shard_map.143.before_ref.left_ref), channel_id=1, source_target_pairs={{0,32},{1,33},{2,34},{3,35},{4,36},{5,37},{6,38},{7,39},{8,40},{9,... | collective-permute-start | bytes 196616 | tf_op jit(solution)/shard_map/ppermute | solution.py:402
  37.4 0.6 shard_map.144.before_ref
  38.0 0.6 shard_map.145.before_ref
  38.6 0.6 collective-permute-done.6.right_ref
  39.2 0.6 shard_map.147.before_ref
  39.8 3.0 %collective-permute-start.7 = (f32[128,128]{1,0:T(8,128)S(1)}, f32[128,128]{1,0:T(8,128)S(1)}, u32[]{:S(2)}, u32[]{:S(2)}) collective-permute-start(f32[128,128]{1,0:T(8,128)S(1)} %shard_map.146.before_ref.left_ref), channel_id=1, source_target_pairs={{0,64},{1,65},{2,66},{3,67},{4,68},{5,69},{6,70},{7,71},{8,72},{9,... | collective-permute-start | bytes 196616 | tf_op jit(solution)/shard_map/ppermute | solution.py:402
  42.8 0.6 shard_map.148.before_ref
  43.4 0.0 copy-start.2
  43.4 1.9 %collective-permute-start.9 = (bf16[128,768]{1,0:T(8,128)(2,1)S(1)}, bf16[128,768]{1,0:T(8,128)(2,1)S(1)}, u32[]{:S(2)}, u32[]{:S(2)}) collective-permute-start(bf16[128,768]{1,0:T(8,128)(2,1)S(1)} %shard_map.148.before_ref), channel_id=1, source_target_pairs={{0,1},{1,0},{2,3},{3,2},{4,5},{5,4},{6,7},{7,6},{8,9},{9,8},{10,11... | collective-permute-start | bytes 589832 | tf_op jit(solution)/shard_map/ppermute | solution.py:402
  45.3 1.6 %collective-permute-start.8 = (f32[128,128]{1,0:T(8,128)S(1)}, f32[128,128]{1,0:T(8,128)S(1)}, u32[]{:S(2)}, u32[]{:S(2)}) collective-permute-start(f32[128,128]{1,0:T(8,128)S(1)} %shard_map.149.before_ref.left_ref), channel_id=1, source_target_pairs={{0,8},{1,9},{2,10},{3,11},{4,12},{5,13},{6,14},{7,15},{8,0},{9,1},... | collective-permute-start | bytes 196616 | tf_op jit(solution)/shard_map/ppermute | solution.py:402
  46.8 1.4 %shard_map.150.before_ref.acc_ref = f32[128,2048]{1,0:T(8,128)S(1)} custom-call(bf16[128,2048]{1,0:T(8,128)(2,1)S(1)} %get-tuple-element.30.st_ref.before_ref, bf16[16,1024,128]{2,1,0:T(8,128)(2,1)S(1)} %get-tuple-element.27.d0_ref, bf16[16,1024,128]{2,1,0:T(8,128)(2,1)S(1)} %get-tuple-element.28.d1_ref, bf16[2048,128]{1,0:T(8,128)(2,1)S(1)} %get-tuple-element.31.gp_ref, ...), custom_call_target="tpu_custom_call" | custom-call | flops 1 | bytes 1 | tf_op jit(solution)/shard_map/pallas_call | solution.py:314
  48.3 4.8 %collective-permute-done.8.right_ref = f32[128,128]{1,0:T(8,128)S(1)} collective-permute-done((f32[128,128]{1,0:T(8,128)S(1)}, f32[128,128]{1,0:T(8,128)S(1)}, u32[]{:S(2)}, u32[]{:S(2)}) %collective-permute-start.8) | collective-permute-done | bytes 65568 | tf_op jit(solution)/shard_map/ppermute | solution.py:402
  53.1 0.6 collective-permute-start.11
  53.7 2.5 %collective-permute-start.14 = (bf16[128,768]{1,0:T(8,128)(2,1)S(1)}, bf16[128,768]{1,0:T(8,128)(2,1)S(1)}, u32[]{:S(2)}, u32[]{:S(2)}) collective-permute-start(bf16[128,768]{1,0:T(8,128)(2,1)S(1)} %shard_map.144.before_ref), channel_id=1, source_target_pairs={{0,16},{1,17},{2,18},{3,19},{4,20},{5,21},{6,22},{7,23},{8,24},{9,... | collective-permute-start | bytes 589832 | tf_op jit(solution)/shard_map/ppermute | solution.py:402
  56.2 1.1 %shard_map.152.before_ref.acc_ref = f32[128,2048]{1,0:T(8,128)S(1)} custom-call(s32[5,768]{1,0:T(8,128)S(1)} %copy-done.2, f32[128,2048]{1,0:T(8,128)S(1)} %shard_map.150.before_ref.acc_ref, f32[128,128]{1,0:T(8,128)S(1)} %shard_map.151.before_ref.left_ref, bf16[128,768]{1,0:T(8,128)(2,1)S(1)} %collective-permute-done.9.refs_0_, ...), custom_call_target="tpu_custom_call" | custom-call | flops 1 | bytes 1 | tf_op jit(solution)/shard_map/pallas_call | solution.py:356
  57.3 0.5 collective-permute-done.11.right_ref
  57.8 0.1 collective-permute-start.13
  57.9 0.1 collective-permute-start.16
  58.0 0.7 shard_map.154.before_ref.acc_ref
  58.7 2.6 %collective-permute-done.13.right_ref = f32[128,128]{1,0:T(8,128)S(1)} collective-permute-done((f32[128,128]{1,0:T(8,128)S(1)}, f32[128,128]{1,0:T(8,128)S(1)}, u32[]{:S(2)}, u32[]{:S(2)}) %collective-permute-start.13) | collective-permute-done | bytes 65568 | tf_op jit(solution)/shard_map/ppermute | solution.py:402
  61.3 0.4 collective-permute-start.15
  61.8 0.7 shard_map.156.before_ref.acc_ref
  62.5 4.5 %collective-permute-done.15.right_ref = f32[128,128]{1,0:T(8,128)S(1)} collective-permute-done((f32[128,128]{1,0:T(8,128)S(1)}, f32[128,128]{1,0:T(8,128)S(1)}, u32[]{:S(2)}, u32[]{:S(2)}) %collective-permute-start.15) | collective-permute-done | bytes 65568 | tf_op jit(solution)/shard_map/ppermute | solution.py:402
  67.1 4.1 %collective-permute-start.17 = (f32[128,128]{1,0:T(8,128)S(1)}, f32[128,128]{1,0:T(8,128)S(1)}, u32[]{:S(2)}, u32[]{:S(2)}) collective-permute-start(f32[128,128]{1,0:T(8,128)S(1)} %shard_map.157.before_ref.total_ref), channel_id=1, source_target_pairs={{0,1},{1,0},{2,3},{3,2},{4,5},{5,4},{6,7},{7,6},{8,9},{9,8},{10,11... | collective-permute-start | bytes 196616 | tf_op jit(solution)/shard_map/ppermute | solution.py:402
  71.1 1.8 %shard_map.158 = f32[2048,128]{1,0:T(8,128)} custom-call(s32[5,768]{1,0:T(8,128)S(1)} %copy-done.2, f32[128,2048]{1,0:T(8,128)S(1)} %shard_map.156.before_ref.acc_ref, f32[128,128]{1,0:T(8,128)S(1)} %shard_map.157.before_ref.total_ref, bf16[128,768]{1,0:T(8,128)(2,1)S(1)} %collective-permute-done.16.refs_0_), custom_call_target="tpu_custom_call" | custom-call | flops 1 | bytes 1 | tf_op jit(solution)/shard_map/pallas_call | solution.py:356
  72.9 0.7 shard_map.159
  (28 shorter events, 0.1 us)
Async XLA Ops:
  4.2 23.2 %collective-permute-start = (bf16[128,768]{1,0:T(8,128)(2,1)S(1)}, bf16[128,768]{1,0:T(8,128)(2,1)S(1)}, u32[]{:S(2)}, u32[]{:S(2)}) collective-permute-start(bf16[128,768]{1,0:T(8,128)(2,1)S(1)} %get-tuple-element.20), channel_id=1, source_target_pairs={{0,1},{1,0},{2,3},{3,2},{4,5},{5,4},{6,7},{7,6},{8,9},{9,8},{10,11... | collective-permute-start | bytes 589832 | tf_op jit(solution)/shard_map/ppermute | solution.py:402
  5.7 21.7 %collective-permute-start.1 = (bf16[128,768]{1,0:T(8,128)(2,1)S(1)}, bf16[128,768]{1,0:T(8,128)(2,1)S(1)}, u32[]{:S(2)}, u32[]{:S(2)}) collective-permute-start(bf16[128,768]{1,0:T(8,128)(2,1)S(1)} %get-tuple-element.21), channel_id=1, source_target_pairs={{0,2},{1,3},{2,0},{3,1},{4,6},{5,7},{6,4},{7,5},{8,10},{9,11},{10,... | collective-permute-start | bytes 589832 | tf_op jit(solution)/shard_map/ppermute | solution.py:402
  7.5 20.0 %collective-permute-start.2 = (bf16[128,768]{1,0:T(8,128)(2,1)S(1)}, bf16[128,768]{1,0:T(8,128)(2,1)S(1)}, u32[]{:S(2)}, u32[]{:S(2)}) collective-permute-start(bf16[128,768]{1,0:T(8,128)(2,1)S(1)} %get-tuple-element.22), channel_id=1, source_target_pairs={{0,4},{1,5},{2,6},{3,7},{4,0},{5,1},{6,2},{7,3},{8,12},{9,13},{10,... | collective-permute-start | bytes 589832 | tf_op jit(solution)/shard_map/ppermute | solution.py:402
  10.8 16.7 %collective-permute-start.3 = (bf16[128,768]{1,0:T(8,128)(2,1)S(1)}, bf16[128,768]{1,0:T(8,128)(2,1)S(1)}, u32[]{:S(2)}, u32[]{:S(2)}) collective-permute-start(bf16[128,768]{1,0:T(8,128)(2,1)S(1)} %get-tuple-element.23), channel_id=1, source_target_pairs={{0,8},{1,9},{2,10},{3,11},{4,12},{5,13},{6,14},{7,15},{8,0},{9,1},... | collective-permute-start | bytes 589832 | tf_op jit(solution)/shard_map/ppermute | solution.py:402
  12.0 13.1 %copy-start = (bf16[2048,128]{1,0:T(8,128)(2,1)S(1)}, bf16[2048,128]{1,0:T(8,128)(2,1)}, u32[]{:S(2)}) copy-start(bf16[2048,128]{1,0:T(8,128)(2,1)} %refs_8_.1) | copy-start | bytes 1572868
  12.0 15.5 %collective-permute-start.4 = (bf16[128,768]{1,0:T(8,128)(2,1)S(1)}, bf16[128,768]{1,0:T(8,128)(2,1)S(1)}, u32[]{:S(2)}, u32[]{:S(2)}) collective-permute-start(bf16[128,768]{1,0:T(8,128)(2,1)S(1)} %get-tuple-element.24), channel_id=1, source_target_pairs={{0,16},{1,17},{2,18},{3,19},{4,20},{5,21},{6,22},{7,23},{8,24},{9,... | collective-permute-start | bytes 589832 | tf_op jit(solution)/shard_map/ppermute | solution.py:402
  14.4 0.7 copy-start.6
  15.1 0.7 copy-start.7
  25.0 2.4 %copy-start.1 = (bf16[2048,128]{1,0:T(8,128)(2,1)S(1)}, bf16[2048,128]{1,0:T(8,128)(2,1)}, u32[]{:S(2)}) copy-start(bf16[2048,128]{1,0:T(8,128)(2,1)} %refs_9_.1) | copy-start | bytes 1572868
  25.0 2.4 %copy-start.3 = (bf16[128,128]{1,0:T(8,128)(2,1)S(1)}, bf16[128,128]{1,0:T(8,128)(2,1)}, u32[]{:S(2)}) copy-start(bf16[128,128]{1,0:T(8,128)(2,1)} %ws_ref.1) | copy-start | bytes 98308
  25.0 2.4 %copy-start.4 = (bf16[128,128]{1,0:T(8,128)(2,1)S(1)}, bf16[128,128]{1,0:T(8,128)(2,1)}, u32[]{:S(2)}) copy-start(bf16[128,128]{1,0:T(8,128)(2,1)} %refs_12_.1) | copy-start | bytes 98308
  25.0 2.4 %copy-start.5 = (s32[2048]{0:T(1024)S(1)}, s32[2048]{0:T(1024)}, u32[]{:S(2)}) copy-start(s32[2048]{0:T(1024)} %param.20) | copy-start | bytes 24580
  25.0 2.4 %copy-start.8 = (f32[128]{0:T(128)S(1)}, f32[128]{0:T(128)}, u32[]{:S(2)}) copy-start(f32[128]{0:T(128)} %param.14) | copy-start | bytes 1540
  33.7 2.1 %collective-permute-start.5 = (f32[128,128]{1,0:T(8,128)S(1)}, f32[128,128]{1,0:T(8,128)S(1)}, u32[]{:S(2)}, u32[]{:S(2)}) collective-permute-start(f32[128,128]{1,0:T(8,128)S(1)} %get-tuple-element.33), channel_id=1, source_target_pairs={{0,1},{1,0},{2,3},{3,2},{4,5},{5,4},{6,7},{7,6},{8,9},{9,8},{10,11... | collective-permute-start | bytes 196616 | tf_op jit(solution)/shard_map/ppermute | solution.py:402
  35.8 3.4 %collective-permute-start.6 = (f32[128,128]{1,0:T(8,128)S(1)}, f32[128,128]{1,0:T(8,128)S(1)}, u32[]{:S(2)}, u32[]{:S(2)}) collective-permute-start(f32[128,128]{1,0:T(8,128)S(1)} %shard_map.143.before_ref.left_ref), channel_id=1, source_target_pairs={{0,32},{1,33},{2,34},{3,35},{4,36},{5,37},{6,38},{7,39},{8,40},{9,... | collective-permute-start | bytes 196616 | tf_op jit(solution)/shard_map/ppermute | solution.py:402
  39.8 5.5 %collective-permute-start.7 = (f32[128,128]{1,0:T(8,128)S(1)}, f32[128,128]{1,0:T(8,128)S(1)}, u32[]{:S(2)}, u32[]{:S(2)}) collective-permute-start(f32[128,128]{1,0:T(8,128)S(1)} %shard_map.146.before_ref.left_ref), channel_id=1, source_target_pairs={{0,64},{1,65},{2,66},{3,67},{4,68},{5,69},{6,70},{7,71},{8,72},{9,... | collective-permute-start | bytes 196616 | tf_op jit(solution)/shard_map/ppermute | solution.py:402
  43.4 12.8 %copy-start.2 = (s32[5,768]{1,0:T(8,128)S(1)}, s32[5,768]{1,0:T(8,128)}, u32[]{:S(2)}) copy-start(s32[5,768]{1,0:T(8,128)} %rows_ref.7) | copy-start | bytes 46084
  43.4 12.8 %collective-permute-start.9 = (bf16[128,768]{1,0:T(8,128)(2,1)S(1)}, bf16[128,768]{1,0:T(8,128)(2,1)S(1)}, u32[]{:S(2)}, u32[]{:S(2)}) collective-permute-start(bf16[128,768]{1,0:T(8,128)(2,1)S(1)} %shard_map.148.before_ref), channel_id=1, source_target_pairs={{0,1},{1,0},{2,3},{3,2},{4,5},{5,4},{6,7},{7,6},{8,9},{9,8},{10,11... | collective-permute-start | bytes 589832 | tf_op jit(solution)/shard_map/ppermute | solution.py:402
  45.2 10.9 %collective-permute-start.10 = (bf16[128,768]{1,0:T(8,128)(2,1)S(1)}, bf16[128,768]{1,0:T(8,128)(2,1)S(1)}, u32[]{:S(2)}, u32[]{:S(2)}) collective-permute-start(bf16[128,768]{1,0:T(8,128)(2,1)S(1)} %shard_map.147.before_ref), channel_id=1, source_target_pairs={{0,8},{1,9},{2,10},{3,11},{4,12},{5,13},{6,14},{7,15},{8,0},{9,1},... | collective-permute-start | bytes 589832 | tf_op jit(solution)/shard_map/ppermute | solution.py:402
  45.3 7.8 %collective-permute-start.8 = (f32[128,128]{1,0:T(8,128)S(1)}, f32[128,128]{1,0:T(8,128)S(1)}, u32[]{:S(2)}, u32[]{:S(2)}) collective-permute-start(f32[128,128]{1,0:T(8,128)S(1)} %shard_map.149.before_ref.left_ref), channel_id=1, source_target_pairs={{0,8},{1,9},{2,10},{3,11},{4,12},{5,13},{6,14},{7,15},{8,0},{9,1},... | collective-permute-start | bytes 196616 | tf_op jit(solution)/shard_map/ppermute | solution.py:402
  46.8 11.2 %collective-permute-start.12 = (bf16[128,768]{1,0:T(8,128)(2,1)S(1)}, bf16[128,768]{1,0:T(8,128)(2,1)S(1)}, u32[]{:S(2)}, u32[]{:S(2)}) collective-permute-start(bf16[128,768]{1,0:T(8,128)(2,1)S(1)} %shard_map.145.before_ref), channel_id=1, source_target_pairs={{0,2},{1,3},{2,0},{3,1},{4,6},{5,7},{6,4},{7,5},{8,10},{9,11},{10,... | collective-permute-start | bytes 589832 | tf_op jit(solution)/shard_map/ppermute | solution.py:402
  53.1 4.7 %collective-permute-start.11 = (f32[128,128]{1,0:T(8,128)S(1)}, f32[128,128]{1,0:T(8,128)S(1)}, u32[]{:S(2)}, u32[]{:S(2)}) collective-permute-start(f32[128,128]{1,0:T(8,128)S(1)} %shard_map.151.before_ref.left_ref), channel_id=1, source_target_pairs={{0,16},{1,17},{2,18},{3,19},{4,20},{5,21},{6,22},{7,23},{8,24},{9,... | collective-permute-start | bytes 196616 | tf_op jit(solution)/shard_map/ppermute | solution.py:402
  53.7 8.1 %collective-permute-start.14 = (bf16[128,768]{1,0:T(8,128)(2,1)S(1)}, bf16[128,768]{1,0:T(8,128)(2,1)S(1)}, u32[]{:S(2)}, u32[]{:S(2)}) collective-permute-start(bf16[128,768]{1,0:T(8,128)(2,1)S(1)} %shard_map.144.before_ref), channel_id=1, source_target_pairs={{0,16},{1,17},{2,18},{3,19},{4,20},{5,21},{6,22},{7,23},{8,24},{9,... | collective-permute-start | bytes 589832 | tf_op jit(solution)/shard_map/ppermute | solution.py:402
  57.8 3.5 %collective-permute-start.13 = (f32[128,128]{1,0:T(8,128)S(1)}, f32[128,128]{1,0:T(8,128)S(1)}, u32[]{:S(2)}, u32[]{:S(2)}) collective-permute-start(f32[128,128]{1,0:T(8,128)S(1)} %shard_map.153.before_ref.left_ref), channel_id=1, source_target_pairs={{0,2},{1,3},{2,0},{3,1},{4,6},{5,7},{6,4},{7,5},{8,10},{9,11},{10,... | collective-permute-start | bytes 196616 | tf_op jit(solution)/shard_map/ppermute | solution.py:402
  57.9 13.2 %collective-permute-start.16 = (bf16[128,768]{1,0:T(8,128)(2,1)S(1)}, bf16[128,768]{1,0:T(8,128)(2,1)S(1)}, u32[]{:S(2)}, u32[]{:S(2)}) collective-permute-start(bf16[128,768]{1,0:T(8,128)(2,1)S(1)} %shard_map.142.before_ref), channel_id=1, source_target_pairs={{0,4},{1,5},{2,6},{3,7},{4,0},{5,1},{6,2},{7,3},{8,12},{9,13},{10,... | collective-permute-start | bytes 589832 | tf_op jit(solution)/shard_map/ppermute | solution.py:402
  61.3 5.7 %collective-permute-start.15 = (f32[128,128]{1,0:T(8,128)S(1)}, f32[128,128]{1,0:T(8,128)S(1)}, u32[]{:S(2)}, u32[]{:S(2)}) collective-permute-start(f32[128,128]{1,0:T(8,128)S(1)} %shard_map.155.before_ref.left_ref), channel_id=1, source_target_pairs={{0,4},{1,5},{2,6},{3,7},{4,0},{5,1},{6,2},{7,3},{8,12},{9,13},{10,... | collective-permute-start | bytes 196616 | tf_op jit(solution)/shard_map/ppermute | solution.py:402
  67.1 5.8 %collective-permute-start.17 = (f32[128,128]{1,0:T(8,128)S(1)}, f32[128,128]{1,0:T(8,128)S(1)}, u32[]{:S(2)}, u32[]{:S(2)}) collective-permute-start(f32[128,128]{1,0:T(8,128)S(1)} %shard_map.157.before_ref.total_ref), channel_id=1, source_target_pairs={{0,1},{1,0},{2,3},{3,2},{4,5},{5,4},{6,7},{7,6},{8,9},{9,8},{10,11... | collective-permute-start | bytes 196616 | tf_op jit(solution)/shard_map/ppermute | solution.py:402

commit v5 on v4

--- a/solution.py
+++ b/solution.py
@@ -89,7 +89,9 @@
     )(in_hbm(send_rows), in_hbm(features))
 
 
-def densify_kernel(lc, hc, lt, ht, dl0, dl1, dh0, dh1, lslots, hslots, zeros, sems, zsems):
+def densify_kernel(
+    lc_hbm, hc_hbm, lt, ht, dl0, dl1, dh0, dh1, lslots, hslots, zeros, lc, hc, sems, zsems, csems
+):
     half = lt.shape[0] // 2
     depth = lslots.shape[0]
     dense = (dl0, dl1, dh0, dh1)
@@ -115,9 +117,17 @@
     for d in range(depth - 1):
         for copy in fetch(d, d):
             copy.start()
+    columns = [
+        pltpu.make_async_copy(lc_hbm, lc, csems.at[0]),
+        pltpu.make_async_copy(hc_hbm, hc, csems.at[1]),
+    ]
+    for copy in columns:
+        copy.start()
     zeros[...] = jnp.zeros_like(zeros)
     for copy in clear(0, 0):
         copy.start()
+    for copy in columns:
+        copy.wait()
 
     def body(i, carry):
         slot, zslot = lax.rem(i, depth), lax.rem(i, 2)
@@ -160,18 +170,21 @@
     return pl.pallas_call(
         densify_kernel,
         out_shape=[VMEM((n, half, TILE), jnp.bfloat16) for n in slabs],
-        in_specs=[sspec(), sspec()] + [pl.BlockSpec(memory_space=pltpu.HBM)] * 2,
+        in_specs=[pl.BlockSpec(memory_space=pltpu.HBM)] * 4,
         out_specs=[vspec()] * 4,
         scratch_shapes=[
             VMEM((depth, 2, local_count, TILE, TILE), jnp.bfloat16),
             VMEM((depth, 2, halo_count, TILE, TILE), jnp.bfloat16),
             VMEM((max(slabs), TILE, TILE), jnp.bfloat16),
+            pltpu.SMEM(local_cols.shape, jnp.int32),
+            pltpu.SMEM(halo_cols.shape, jnp.int32),
             pltpu.SemaphoreType.DMA((depth, 4)),
             pltpu.SemaphoreType.DMA((2, 4)),
+            pltpu.SemaphoreType.DMA((2,)),
         ],
         compiler_params=params(12 * 1024 * 1024),
         cost_estimate=cost(16_000_000, nblocks * (local_count + halo_count) * TILE * TILE * 2),
-    )(local_cols, halo_cols, in_hbm(local_tiles), in_hbm(halo_tiles))
+    )(in_hbm(local_cols), in_hbm(halo_cols), in_hbm(local_tiles), in_hbm(halo_tiles))
 
 
 def local_sums_kernel(d0_ref, d1_ref, x_ref, out_ref):
@@ -322,7 +335,8 @@
 
 
 def place_kernel(rounds, last, rows_ref, acc_ref, before_ref, *refs):
-    returned, (out_ref, listed) = refs[: len(rounds)], refs[len(rounds) :]
+    returned, (out_ref, token_ref, listed) = refs[: len(rounds)], refs[len(rounds) :]
+    token_ref[...] = jnp.zeros_like(token_ref)
     step, boundary = 2 * TILE, rows_ref.shape[1]
     for place, r in enumerate(rounds):
         for k in range(0, boundary, TILE):
@@ -355,9 +369,9 @@
         out = VMEM((width, rows), jnp.float32)
     return pl.pallas_call(
         functools.partial(place_kernel, rounds, last),
-        out_shape=out,
+        out_shape=[out, VMEM((8, TILE), jnp.float32)],
         in_specs=[vspec()] * 2 + [pl.BlockSpec(memory_space=pl.ANY)] + [vspec()] * count,
-        out_specs=vspec(),
+        out_specs=[vspec()] * 2,
         scratch_shapes=[VMEM((count, boundary, TILE), jnp.float32)],
         compiler_params=params(),
         cost_estimate=cost(1, 1),
@@ -446,36 +460,35 @@
 
     def place(rounds, acc, before):
         got = [returned[r] for r in rounds]
-        return place_rows(rounds, 2 in rounds, send_rows, acc, got, before)
+        return place_rows(rounds, 0 in rounds, send_rows, acc, got, before)
 
     other = swapped(give, 1)
     last = send_back(2, scaled_t)
+    last = send_back(4, last)
     total = added(mine, other, last)
     other = swapped(total, 32)
-    last = send_back(4, total)
-    last = send_back(1, last)
+    last = send_back(1, total)
+    last = send_back(3, last)
+    last = send_back(0, last)
     total = added(total, other, last)
     other = swapped(total, 64)
-    last = send_back(3, total)
-    last = send_back(0, last)
-    total = added(total, other, last)
-    other = swapped(total, 8)
     grads_t = own(scaled_t, dl0, dl1, grad_pre, w_self, total)
     total = added(total, other, grads_t)
+    other = swapped(total, 8)
+    grads_t, last = place((2, 4), grads_t, total)
+    total = added(total, other, last)
     other = swapped(total, 16)
-    grads_t = place((0, 3), grads_t, total)
-    total = added(total, other, grads_t)
+    grads_t, last = place((3, 1), grads_t, total)
+    total = added(total, other, last)
     other = swapped(total, 2)
-    grads_t = place((1,), grads_t, total)
-    total = added(total, other, grads_t)
+    grads, last = place((0,), grads_t, total)
+    total = added(total, other, last)
     other = swapped(total, 4)
-    grads_t = place((4,), grads_t, total)
-    total = added(total, other, grads_t)
+    total = added(total, other, total)
     other = swapped(total, 1)
-    grads_t = place((2,), grads_t, total)
     grad_scale = 1.0 / math.sqrt(row_count * lax.axis_size("dom"))
     grad_self, grad_neigh = halves(grad_scale, total, other)
-    return (output, grads_t, grad_self, grad_neigh)
+    return (output, grads, grad_self, grad_neigh)
 
 
 def solution(mesh):

time: 73.8 us -> 67.6 us (0.916)
  waiting for transfers between devices: 13.4 us -> 4.55 us
  starting transfers between devices: 27.1 us -> 32.3 us
  local copies, waits for them, and re-layouts: 1.43 us -> 0.04 us
  Pallas kernels: 30.7 us -> 29.7 us
    ppermute x18, waiting for transfers between devices: 13.4 us -> 4.55 us  [swapped(): lax.ppermute(shard, 'dom', [(i, i ^ mask) for i in range(lax.axis_size('d...]
    ppermute x18, starting transfers between devices: 27.1 us -> 32.3 us  [swapped(): lax.ppermute(shard, 'dom', [(i, i ^ mask) for i in range(lax.axis_size('d...]
    unnamed x18 -> x14, local copies, waits for them, and re-layouts: 1.43 us -> 0.04 us
    pallas_call x4 -> x3, Pallas kernels: 4.29 us -> 4.01 us  [place_rows(): pl.pallas_call(functools.partial(place_kernel, rounds, last), out_shape=[...]
  transfers between devices with their start and end apart: 18 -> 18, of which waited for: 6 -> 4; matrix products, arithmetic and copies ran while one was open for 0% -> 0% of each run, Pallas kernels for 27% -> 28%
where the time goes in v5:
time: 67.6 us; the launch traced here: 67.5 us
  starting transfers between devices  32.3 us (48%)
  Pallas kernels  29.7 us (44%)
  waiting for transfers between devices  4.55 us (7%)
  between operations  0.91 us (1%)
    ppermute x18, starting transfers between devices, swapped(): lax.ppermute(shard, 'dom', [(i, i ^ mask) for i in range(lax.axis_size('d...  32.3 us
    pallas_call x1, Pallas kernels, densify(): pl.pallas_call(densify_kernel, out_shape=[VMEM((n, half, TILE), jnp.bfloa...  8.48 us
    pallas_call x1, Pallas kernels, middle(): pl.pallas_call(functools.partial(middle_kernel, rounds), out_shape=[half,...  6.21 us
    ppermute x18, waiting for transfers between devices, swapped(): lax.ppermute(shard, 'dom', [(i, i ^ mask) for i in range(lax.axis_size('d...  4.55 us
    pallas_call x3, Pallas kernels, place_rows(): pl.pallas_call(functools.partial(place_kernel, rounds, last), out_shape=[...  4.01 us
    pallas_call x1, Pallas kernels, pick_rows(): pl.pallas_call(pick_kernel, out_shape=outs, in_specs=[pl.BlockSpec(memory...  3.58 us
    pallas_call x5, Pallas kernels, back(): pl.pallas_call(functools.partial(back_kernel, first, n), out_shape=jax.Sh...  2.91 us
    pallas_call x1, Pallas kernels, local_sums(): pl.pallas_call(local_sums_kernel, out_shape=VMEM((rows, width), jnp.float...  2.31 us
  transfers between devices with their start and end apart: 18, of which 4 were waited for; matrix products, arithmetic and copies ran while one was open for 0% of the time, Pallas kernels for 28%

profile of v5, /device:TPU:1, one launch (start us, length us, event | category | flops | bytes accessed | tf_op | source)
XLA Modules:
  0.0 67.5 jit_solution(4265014296121093022)
XLA Ops:
  0.6 3.6 %shard_map.138 = (bf16[128,768]{1,0:T(8,128)(2,1)S(1)}, bf16[128,768]{1,0:T(8,128)(2,1)S(1)}, bf16[128,768]{1,0:T(8,128)(2,1)S(1)}, bf16[128,768]{1,0:T(8,128)(2,1)S(1)}, bf16[128,768]{1,0:T(8,128)(2,1)S(1)}) custom-call(s32[5,768]{1,0:T(8,128)} %rows_ref.5, bf16[2048,128]{1,0:T(8,128)(2,1)} %refs_8_.1), custom_call_target="tpu_custom_call" | custom-call | flops 2013265920 | bytes 1000000 | tf_op jit(solution)/shard_map/pallas_call | solution.py:75
  4.2 1.5 %collective-permute-start = (bf16[128,768]{1,0:T(8,128)(2,1)S(1)}, bf16[128,768]{1,0:T(8,128)(2,1)S(1)}, u32[]{:S(2)}, u32[]{:S(2)}) collective-permute-start(bf16[128,768]{1,0:T(8,128)(2,1)S(1)} %get-tuple-element.26), channel_id=1, source_target_pairs={{0,1},{1,0},{2,3},{3,2},{4,5},{5,4},{6,7},{7,6},{8,9},{9,8},{10,11... | collective-permute-start | bytes 589832 | tf_op jit(solution)/shard_map/ppermute | solution.py:416
  5.7 1.7 %collective-permute-start.1 = (bf16[128,768]{1,0:T(8,128)(2,1)S(1)}, bf16[128,768]{1,0:T(8,128)(2,1)S(1)}, u32[]{:S(2)}, u32[]{:S(2)}) collective-permute-start(bf16[128,768]{1,0:T(8,128)(2,1)S(1)} %get-tuple-element.27), channel_id=1, source_target_pairs={{0,2},{1,3},{2,0},{3,1},{4,6},{5,7},{6,4},{7,5},{8,10},{9,11},{10,... | collective-permute-start | bytes 589832 | tf_op jit(solution)/shard_map/ppermute | solution.py:416
  7.5 3.3 %collective-permute-start.2 = (bf16[128,768]{1,0:T(8,128)(2,1)S(1)}, bf16[128,768]{1,0:T(8,128)(2,1)S(1)}, u32[]{:S(2)}, u32[]{:S(2)}) collective-permute-start(bf16[128,768]{1,0:T(8,128)(2,1)S(1)} %get-tuple-element.28), channel_id=1, source_target_pairs={{0,4},{1,5},{2,6},{3,7},{4,0},{5,1},{6,2},{7,3},{8,12},{9,13},{10,... | collective-permute-start | bytes 589832 | tf_op jit(solution)/shard_map/ppermute | solution.py:416
  10.8 1.2 %collective-permute-start.3 = (bf16[128,768]{1,0:T(8,128)(2,1)S(1)}, bf16[128,768]{1,0:T(8,128)(2,1)S(1)}, u32[]{:S(2)}, u32[]{:S(2)}) collective-permute-start(bf16[128,768]{1,0:T(8,128)(2,1)S(1)} %get-tuple-element.29), channel_id=1, source_target_pairs={{0,8},{1,9},{2,10},{3,11},{4,12},{5,13},{6,14},{7,15},{8,0},{9,1},... | collective-permute-start | bytes 589832 | tf_op jit(solution)/shard_map/ppermute | solution.py:416
  12.0 2.5 %collective-permute-start.4 = (bf16[128,768]{1,0:T(8,128)(2,1)S(1)}, bf16[128,768]{1,0:T(8,128)(2,1)S(1)}, u32[]{:S(2)}, u32[]{:S(2)}) collective-permute-start(bf16[128,768]{1,0:T(8,128)(2,1)S(1)} %get-tuple-element.30), channel_id=1, source_target_pairs={{0,16},{1,17},{2,18},{3,19},{4,20},{5,21},{6,22},{7,23},{8,24},{9,... | collective-permute-start | bytes 589832 | tf_op jit(solution)/shard_map/ppermute | solution.py:416
  14.4 8.5 %shard_map.139 = (bf16[16,1024,128]{2,1,0:T(8,128)(2,1)S(1)}, bf16[16,1024,128]{2,1,0:T(8,128)(2,1)S(1)}, bf16[30,1024,128]{2,1,0:T(8,128)(2,1)S(1)}, bf16[30,1024,128]{2,1,0:T(8,128)(2,1)S(1)}) custom-call(s32[16,22]{1,0:T(8,128)} %lc_hbm.1, s32[16,20]{1,0:T(8,128)} %hc_hbm.1, bf16[16,22,128,128]{3,2,1,0:T(8,128)(2,1)} %lt.1, bf16[16,20,128,128]{3,2,1,0:T(8,128)(2,1)} %ht.1), custom_call_target="tpu_custom_call" | custom-call | flops 16000000 | bytes 22020096 | tf_op jit(solution)/shard_map/pallas_call | solution.py:170
  22.9 0.0 copy-start.1
  22.9 0.0 copy-start.3
  22.9 0.0 copy-start.4
  22.9 0.0 copy-start.5
  23.0 0.0 copy-start.6
  23.0 2.3 %shard_map.140.refs_7_ = f32[2048,128]{1,0:T(8,128)S(1)} custom-call(bf16[16,1024,128]{2,1,0:T(8,128)(2,1)S(1)} %get-tuple-element.33.d0_ref, bf16[16,1024,128]{2,1,0:T(8,128)(2,1)S(1)} %get-tuple-element.34.d1_ref, bf16[2048,128]{1,0:T(8,128)(2,1)S(1)} %copy-done), custom_call_target="tpu_custom_call" | custom-call | flops 1073741824 | bytes 1500000 | tf_op jit(solution)/shard_map/pallas_call | solution.py:202
  25.3 0.0 collective-permute-done.refs_0_
  25.3 0.0 collective-permute-done.1.refs_1_
  25.3 0.0 collective-permute-done.2.refs_2_
  25.4 6.2 %shard_map.141 = (bf16[2048,128]{1,0:T(8,128)(2,1)}, bf16[2048,128]{1,0:T(8,128)(2,1)S(1)}, bf16[128,2048]{1,0:T(8,128)(2,1)S(1)}, f32[128,128]{1,0:T(8,128)S(1)}, f32[128,128]{1,0:T(8,128)S(1)}) custom-call(bf16[128,768]{1,0:T(8,128)(2,1)S(1)} %collective-permute-done.refs_0_, bf16[128,768]{1,0:T(8,128)(2,1)S(1)} %collective-permute-done.1.refs_1_, ...), custom_call_target="tpu_custom_call" | custom-call | flops 2013265920 | bytes 5000000 | tf_op jit(solution)/shard_map/pallas_call | solution.py:262
  31.6 1.2 %collective-permute-start.5 = (f32[128,128]{1,0:T(8,128)S(1)}, f32[128,128]{1,0:T(8,128)S(1)}, u32[]{:S(2)}, u32[]{:S(2)}) collective-permute-start(f32[128,128]{1,0:T(8,128)S(1)} %get-tuple-element.39), channel_id=1, source_target_pairs={{0,1},{1,0},{2,3},{3,2},{4,5},{5,4},{6,7},{7,6},{8,9},{9,8},{10,11... | collective-permute-start | bytes 196616 | tf_op jit(solution)/shard_map/ppermute | solution.py:416
  32.8 0.6 shard_map.142.before_ref
  33.4 0.6 shard_map.143.before_ref
  34.0 0.8 %collective-permute-start.9 = (bf16[128,768]{1,0:T(8,128)(2,1)S(1)}, bf16[128,768]{1,0:T(8,128)(2,1)S(1)}, u32[]{:S(2)}, u32[]{:S(2)}) collective-permute-start(bf16[128,768]{1,0:T(8,128)(2,1)S(1)} %shard_map.143.before_ref), channel_id=1, source_target_pairs={{0,16},{1,17},{2,18},{3,19},{4,20},{5,21},{6,22},{7,23},{8,24},{9,... | collective-permute-start | bytes 589832 | tf_op jit(solution)/shard_map/ppermute | solution.py:416
  34.8 0.0 collective-permute-done.5.right_ref
  34.8 1.4 %collective-permute-start.6 = (f32[128,128]{1,0:T(8,128)S(1)}, f32[128,128]{1,0:T(8,128)S(1)}, u32[]{:S(2)}, u32[]{:S(2)}) collective-permute-start(f32[128,128]{1,0:T(8,128)S(1)} %shard_map.144.before_ref.left_ref), channel_id=1, source_target_pairs={{0,32},{1,33},{2,34},{3,35},{4,36},{5,37},{6,38},{7,39},{8,40},{9,... | collective-permute-start | bytes 196616 | tf_op jit(solution)/shard_map/ppermute | solution.py:416
  36.2 0.6 shard_map.145.before_ref
  36.8 0.6 shard_map.146.before_ref
  37.4 0.6 shard_map.147.before_ref
  38.0 0.0 copy-start.2
  38.0 0.0 collective-permute-done.6.right_ref
  38.0 3.0 %collective-permute-start.7 = (f32[128,128]{1,0:T(8,128)S(1)}, f32[128,128]{1,0:T(8,128)S(1)}, u32[]{:S(2)}, u32[]{:S(2)}) collective-permute-start(f32[128,128]{1,0:T(8,128)S(1)} %shard_map.148.before_ref.left_ref), channel_id=1, source_target_pairs={{0,64},{1,65},{2,66},{3,67},{4,68},{5,69},{6,70},{7,71},{8,72},{9,... | collective-permute-start | bytes 196616 | tf_op jit(solution)/shard_map/ppermute | solution.py:416
  41.0 0.3 collective-permute-start.11
  41.3 1.4 %shard_map.149.before_ref.acc_ref = f32[128,2048]{1,0:T(8,128)S(1)} custom-call(bf16[128,2048]{1,0:T(8,128)(2,1)S(1)} %get-tuple-element.36.st_ref.before_ref, bf16[16,1024,128]{2,1,0:T(8,128)(2,1)S(1)} %get-tuple-element.33.d0_ref, bf16[16,1024,128]{2,1,0:T(8,128)(2,1)S(1)} %get-tuple-element.34.d1_ref, bf16[2048,128]{1,0:T(8,128)(2,1)S(1)} %get-tuple-element.37.gp_ref, ...), custom_call_target="tpu_custom_call" | custom-call | flops 1 | bytes 1 | tf_op jit(solution)/shard_map/pallas_call | solution.py:327
  42.7 0.3 collective-permute-done.7.right_ref
  43.0 1.0 %collective-permute-start.10 = (f32[128,128]{1,0:T(8,128)S(1)}, f32[128,128]{1,0:T(8,128)S(1)}, u32[]{:S(2)}, u32[]{:S(2)}) collective-permute-start(f32[128,128]{1,0:T(8,128)S(1)} %shard_map.150.before_ref.left_ref), channel_id=1, source_target_pairs={{0,8},{1,9},{2,10},{3,11},{4,12},{5,13},{6,14},{7,15},{8,0},{9,1},... | collective-permute-start | bytes 196616 | tf_op jit(solution)/shard_map/ppermute | solution.py:416
  44.0 0.0 collective-permute-done.9.refs_1_
  44.0 2.3 %collective-permute-start.14 = (bf16[128,768]{1,0:T(8,128)(2,1)S(1)}, bf16[128,768]{1,0:T(8,128)(2,1)S(1)}, u32[]{:S(2)}, u32[]{:S(2)}) collective-permute-start(bf16[128,768]{1,0:T(8,128)(2,1)S(1)} %shard_map.147.before_ref), channel_id=1, source_target_pairs={{0,1},{1,0},{2,3},{3,2},{4,5},{5,4},{6,7},{7,6},{8,9},{9,8},{10,11... | collective-permute-start | bytes 589832 | tf_op jit(solution)/shard_map/ppermute | solution.py:416
  46.3 1.1 %shard_map.151 = (f32[128,2048]{1,0:T(8,128)S(1)}, f32[8,128]{1,0:T(8,128)S(1)}) custom-call(s32[5,768]{1,0:T(8,128)S(1)} %copy-done.2, f32[128,2048]{1,0:T(8,128)S(1)} %shard_map.149.before_ref.acc_ref, f32[128,128]{1,0:T(8,128)S(1)} %shard_map.150.before_ref.left_ref, bf16[128,768]{1,0:T(8,128)(2,1)S(1)} %collective-permute-done.8.refs_0_, ...), custom_call_target="tpu_custom_call" | custom-call | flops 1 | bytes 1 | tf_op jit(solution)/shard_map/pallas_call | solution.py:370
  47.5 2.8 %collective-permute-start.13 = (f32[128,128]{1,0:T(8,128)S(1)}, f32[128,128]{1,0:T(8,128)S(1)}, u32[]{:S(2)}, u32[]{:S(2)}) collective-permute-start(f32[128,128]{1,0:T(8,128)S(1)} %shard_map.152.before_ref.left_ref), channel_id=1, source_target_pairs={{0,16},{1,17},{2,18},{3,19},{4,20},{5,21},{6,22},{7,23},{8,24},{9,... | collective-permute-start | bytes 196616 | tf_op jit(solution)/shard_map/ppermute | solution.py:416
  50.2 0.0 collective-permute-done.11.refs_0_
  50.2 1.1 %shard_map.153 = (f32[128,2048]{1,0:T(8,128)S(1)}, f32[8,128]{1,0:T(8,128)S(1)}) custom-call(s32[5,768]{1,0:T(8,128)S(1)} %copy-done.2, f32[128,2048]{1,0:T(8,128)S(1)} %get-tuple-element.40.acc_ref, f32[128,128]{1,0:T(8,128)S(1)} %shard_map.152.before_ref.left_ref, bf16[128,768]{1,0:T(8,128)(2,1)S(1)} %collective-permute-done.11.refs_0_, ...), custom_call_target="tpu_custom_call" | custom-call | flops 1 | bytes 1 | tf_op jit(solution)/shard_map/pallas_call | solution.py:370
  51.3 0.8 %collective-permute-done.13.right_ref = f32[128,128]{1,0:T(8,128)S(1)} collective-permute-done((f32[128,128]{1,0:T(8,128)S(1)}, f32[128,128]{1,0:T(8,128)S(1)}, u32[]{:S(2)}, u32[]{:S(2)}) %collective-permute-start.13) | collective-permute-done | bytes 65568 | tf_op jit(solution)/shard_map/ppermute | solution.py:416
  52.2 1.8 %collective-permute-start.15 = (f32[128,128]{1,0:T(8,128)S(1)}, f32[128,128]{1,0:T(8,128)S(1)}, u32[]{:S(2)}, u32[]{:S(2)}) collective-permute-start(f32[128,128]{1,0:T(8,128)S(1)} %shard_map.154.before_ref.left_ref), channel_id=1, source_target_pairs={{0,2},{1,3},{2,0},{3,1},{4,6},{5,7},{6,4},{7,5},{8,10},{9,11},{10,... | collective-permute-start | bytes 196616 | tf_op jit(solution)/shard_map/ppermute | solution.py:416
  54.0 0.0 collective-permute-done.14.refs_0_
  54.0 1.8 %shard_map.155 = (f32[2048,128]{1,0:T(8,128)}, f32[8,128]{1,0:T(8,128)S(1)}) custom-call(s32[5,768]{1,0:T(8,128)S(1)} %copy-done.2, f32[128,2048]{1,0:T(8,128)S(1)} %get-tuple-element.42.acc_ref, f32[128,128]{1,0:T(8,128)S(1)} %shard_map.154.before_ref.left_ref, bf16[128,768]{1,0:T(8,128)(2,1)S(1)} %collective-permute-done.14.refs_0_), custom_call_target="tpu_custom_call" | custom-call | flops 1 | bytes 1 | tf_op jit(solution)/shard_map/pallas_call | solution.py:370
  55.8 2.5 %collective-permute-start.16 = (f32[128,128]{1,0:T(8,128)S(1)}, f32[128,128]{1,0:T(8,128)S(1)}, u32[]{:S(2)}, u32[]{:S(2)}) collective-permute-start(f32[128,128]{1,0:T(8,128)S(1)} %shard_map.156.left_ref.before_ref), channel_id=1, source_target_pairs={{0,4},{1,5},{2,6},{3,7},{4,0},{5,1},{6,2},{7,3},{8,12},{9,13},{10,... | collective-permute-start | bytes 196616 | tf_op jit(solution)/shard_map/ppermute | solution.py:416
  58.3 2.5 %collective-permute-done.16.right_ref = f32[128,128]{1,0:T(8,128)S(1)} collective-permute-done((f32[128,128]{1,0:T(8,128)S(1)}, f32[128,128]{1,0:T(8,128)S(1)}, u32[]{:S(2)}, u32[]{:S(2)}) %collective-permute-start.16) | collective-permute-done | bytes 65568 | tf_op jit(solution)/shard_map/ppermute | solution.py:416
  60.8 5.1 %collective-permute-start.17 = (f32[128,128]{1,0:T(8,128)S(1)}, f32[128,128]{1,0:T(8,128)S(1)}, u32[]{:S(2)}, u32[]{:S(2)}) collective-permute-start(f32[128,128]{1,0:T(8,128)S(1)} %shard_map.157.total_ref), channel_id=1, source_target_pairs={{0,1},{1,0},{2,3},{3,2},{4,5},{5,4},{6,7},{7,6},{8,9},{9,8},{10,11... | collective-permute-start | bytes 196616 | tf_op jit(solution)/shard_map/ppermute | solution.py:416
  65.9 0.9 %collective-permute-done.17.other_ref = f32[128,128]{1,0:T(8,128)S(1)} collective-permute-done((f32[128,128]{1,0:T(8,128)S(1)}, f32[128,128]{1,0:T(8,128)S(1)}, u32[]{:S(2)}, u32[]{:S(2)}) %collective-permute-start.17) | collective-permute-done | bytes 65568 | tf_op jit(solution)/shard_map/ppermute | solution.py:416
  66.8 0.7 shard_map.158
  (23 shorter events, 0.1 us)
Async XLA Ops:
  4.2 21.1 %collective-permute-start = (bf16[128,768]{1,0:T(8,128)(2,1)S(1)}, bf16[128,768]{1,0:T(8,128)(2,1)S(1)}, u32[]{:S(2)}, u32[]{:S(2)}) collective-permute-start(bf16[128,768]{1,0:T(8,128)(2,1)S(1)} %get-tuple-element.26), channel_id=1, source_target_pairs={{0,1},{1,0},{2,3},{3,2},{4,5},{5,4},{6,7},{7,6},{8,9},{9,8},{10,11... | collective-permute-start | bytes 589832 | tf_op jit(solution)/shard_map/ppermute | solution.py:416
  5.7 19.6 %collective-permute-start.1 = (bf16[128,768]{1,0:T(8,128)(2,1)S(1)}, bf16[128,768]{1,0:T(8,128)(2,1)S(1)}, u32[]{:S(2)}, u32[]{:S(2)}) collective-permute-start(bf16[128,768]{1,0:T(8,128)(2,1)S(1)} %get-tuple-element.27), channel_id=1, source_target_pairs={{0,2},{1,3},{2,0},{3,1},{4,6},{5,7},{6,4},{7,5},{8,10},{9,11},{10,... | collective-permute-start | bytes 589832 | tf_op jit(solution)/shard_map/ppermute | solution.py:416
  7.5 17.9 %collective-permute-start.2 = (bf16[128,768]{1,0:T(8,128)(2,1)S(1)}, bf16[128,768]{1,0:T(8,128)(2,1)S(1)}, u32[]{:S(2)}, u32[]{:S(2)}) collective-permute-start(bf16[128,768]{1,0:T(8,128)(2,1)S(1)} %get-tuple-element.28), channel_id=1, source_target_pairs={{0,4},{1,5},{2,6},{3,7},{4,0},{5,1},{6,2},{7,3},{8,12},{9,13},{10,... | collective-permute-start | bytes 589832 | tf_op jit(solution)/shard_map/ppermute | solution.py:416
  10.8 14.6 %collective-permute-start.3 = (bf16[128,768]{1,0:T(8,128)(2,1)S(1)}, bf16[128,768]{1,0:T(8,128)(2,1)S(1)}, u32[]{:S(2)}, u32[]{:S(2)}) collective-permute-start(bf16[128,768]{1,0:T(8,128)(2,1)S(1)} %get-tuple-element.29), channel_id=1, source_target_pairs={{0,8},{1,9},{2,10},{3,11},{4,12},{5,13},{6,14},{7,15},{8,0},{9,1},... | collective-permute-start | bytes 589832 | tf_op jit(solution)/shard_map/ppermute | solution.py:416
  12.0 11.0 %copy-start = (bf16[2048,128]{1,0:T(8,128)(2,1)S(1)}, bf16[2048,128]{1,0:T(8,128)(2,1)}, u32[]{:S(2)}) copy-start(bf16[2048,128]{1,0:T(8,128)(2,1)} %refs_8_.1) | copy-start | bytes 1572868
  12.0 13.4 %collective-permute-start.4 = (bf16[128,768]{1,0:T(8,128)(2,1)S(1)}, bf16[128,768]{1,0:T(8,128)(2,1)S(1)}, u32[]{:S(2)}, u32[]{:S(2)}) collective-permute-start(bf16[128,768]{1,0:T(8,128)(2,1)S(1)} %get-tuple-element.30), channel_id=1, source_target_pairs={{0,16},{1,17},{2,18},{3,19},{4,20},{5,21},{6,22},{7,23},{8,24},{9,... | collective-permute-start | bytes 589832 | tf_op jit(solution)/shard_map/ppermute | solution.py:416
  22.9 2.4 %copy-start.1 = (bf16[2048,128]{1,0:T(8,128)(2,1)S(1)}, bf16[2048,128]{1,0:T(8,128)(2,1)}, u32[]{:S(2)}) copy-start(bf16[2048,128]{1,0:T(8,128)(2,1)} %refs_9_.1) | copy-start | bytes 1572868
  22.9 2.4 %copy-start.3 = (bf16[128,128]{1,0:T(8,128)(2,1)S(1)}, bf16[128,128]{1,0:T(8,128)(2,1)}, u32[]{:S(2)}) copy-start(bf16[128,128]{1,0:T(8,128)(2,1)} %ws_ref.1) | copy-start | bytes 98308
  22.9 2.4 %copy-start.4 = (bf16[128,128]{1,0:T(8,128)(2,1)S(1)}, bf16[128,128]{1,0:T(8,128)(2,1)}, u32[]{:S(2)}) copy-start(bf16[128,128]{1,0:T(8,128)(2,1)} %refs_12_.1) | copy-start | bytes 98308
  22.9 2.4 %copy-start.5 = (s32[2048]{0:T(1024)S(1)}, s32[2048]{0:T(1024)}, u32[]{:S(2)}) copy-start(s32[2048]{0:T(1024)} %param.20) | copy-start | bytes 24580
  23.0 2.4 %copy-start.6 = (f32[128]{0:T(128)S(1)}, f32[128]{0:T(128)}, u32[]{:S(2)}) copy-start(f32[128]{0:T(128)} %param.14) | copy-start | bytes 1540
  31.6 3.2 %collective-permute-start.5 = (f32[128,128]{1,0:T(8,128)S(1)}, f32[128,128]{1,0:T(8,128)S(1)}, u32[]{:S(2)}, u32[]{:S(2)}) collective-permute-start(f32[128,128]{1,0:T(8,128)S(1)} %get-tuple-element.39), channel_id=1, source_target_pairs={{0,1},{1,0},{2,3},{3,2},{4,5},{5,4},{6,7},{7,6},{8,9},{9,8},{10,11... | collective-permute-start | bytes 196616 | tf_op jit(solution)/shard_map/ppermute | solution.py:416
  34.0 10.0 %collective-permute-start.9 = (bf16[128,768]{1,0:T(8,128)(2,1)S(1)}, bf16[128,768]{1,0:T(8,128)(2,1)S(1)}, u32[]{:S(2)}, u32[]{:S(2)}) collective-permute-start(bf16[128,768]{1,0:T(8,128)(2,1)S(1)} %shard_map.143.before_ref), channel_id=1, source_target_pairs={{0,16},{1,17},{2,18},{3,19},{4,20},{5,21},{6,22},{7,23},{8,24},{9,... | collective-permute-start | bytes 589832 | tf_op jit(solution)/shard_map/ppermute | solution.py:416
  34.8 3.2 %collective-permute-start.6 = (f32[128,128]{1,0:T(8,128)S(1)}, f32[128,128]{1,0:T(8,128)S(1)}, u32[]{:S(2)}, u32[]{:S(2)}) collective-permute-start(f32[128,128]{1,0:T(8,128)S(1)} %shard_map.144.before_ref.left_ref), channel_id=1, source_target_pairs={{0,32},{1,33},{2,34},{3,35},{4,36},{5,37},{6,38},{7,39},{8,40},{9,... | collective-permute-start | bytes 196616 | tf_op jit(solution)/shard_map/ppermute | solution.py:416
  36.2 10.1 %collective-permute-start.8 = (bf16[128,768]{1,0:T(8,128)(2,1)S(1)}, bf16[128,768]{1,0:T(8,128)(2,1)S(1)}, u32[]{:S(2)}, u32[]{:S(2)}) collective-permute-start(bf16[128,768]{1,0:T(8,128)(2,1)S(1)} %shard_map.142.before_ref), channel_id=1, source_target_pairs={{0,4},{1,5},{2,6},{3,7},{4,0},{5,1},{6,2},{7,3},{8,12},{9,13},{10,... | collective-permute-start | bytes 589832 | tf_op jit(solution)/shard_map/ppermute | solution.py:416
  38.0 8.4 %copy-start.2 = (s32[5,768]{1,0:T(8,128)S(1)}, s32[5,768]{1,0:T(8,128)}, u32[]{:S(2)}) copy-start(s32[5,768]{1,0:T(8,128)} %rows_ref.5) | copy-start | bytes 46084
  38.0 5.0 %collective-permute-start.7 = (f32[128,128]{1,0:T(8,128)S(1)}, f32[128,128]{1,0:T(8,128)S(1)}, u32[]{:S(2)}, u32[]{:S(2)}) collective-permute-start(f32[128,128]{1,0:T(8,128)S(1)} %shard_map.148.before_ref.left_ref), channel_id=1, source_target_pairs={{0,64},{1,65},{2,66},{3,67},{4,68},{5,69},{6,70},{7,71},{8,72},{9,... | collective-permute-start | bytes 196616 | tf_op jit(solution)/shard_map/ppermute | solution.py:416
  41.0 9.2 %collective-permute-start.11 = (bf16[128,768]{1,0:T(8,128)(2,1)S(1)}, bf16[128,768]{1,0:T(8,128)(2,1)S(1)}, u32[]{:S(2)}, u32[]{:S(2)}) collective-permute-start(bf16[128,768]{1,0:T(8,128)(2,1)S(1)} %shard_map.146.before_ref), channel_id=1, source_target_pairs={{0,8},{1,9},{2,10},{3,11},{4,12},{5,13},{6,14},{7,15},{8,0},{9,1},... | collective-permute-start | bytes 589832 | tf_op jit(solution)/shard_map/ppermute | solution.py:416
  41.3 9.0 %collective-permute-start.12 = (bf16[128,768]{1,0:T(8,128)(2,1)S(1)}, bf16[128,768]{1,0:T(8,128)(2,1)S(1)}, u32[]{:S(2)}, u32[]{:S(2)}) collective-permute-start(bf16[128,768]{1,0:T(8,128)(2,1)S(1)} %shard_map.145.before_ref), channel_id=1, source_target_pairs={{0,2},{1,3},{2,0},{3,1},{4,6},{5,7},{6,4},{7,5},{8,10},{9,11},{10,... | collective-permute-start | bytes 589832 | tf_op jit(solution)/shard_map/ppermute | solution.py:416
  43.0 4.4 %collective-permute-start.10 = (f32[128,128]{1,0:T(8,128)S(1)}, f32[128,128]{1,0:T(8,128)S(1)}, u32[]{:S(2)}, u32[]{:S(2)}) collective-permute-start(f32[128,128]{1,0:T(8,128)S(1)} %shard_map.150.before_ref.left_ref), channel_id=1, source_target_pairs={{0,8},{1,9},{2,10},{3,11},{4,12},{5,13},{6,14},{7,15},{8,0},{9,1},... | collective-permute-start | bytes 196616 | tf_op jit(solution)/shard_map/ppermute | solution.py:416
  44.0 10.0 %collective-permute-start.14 = (bf16[128,768]{1,0:T(8,128)(2,1)S(1)}, bf16[128,768]{1,0:T(8,128)(2,1)S(1)}, u32[]{:S(2)}, u32[]{:S(2)}) collective-permute-start(bf16[128,768]{1,0:T(8,128)(2,1)S(1)} %shard_map.147.before_ref), channel_id=1, source_target_pairs={{0,1},{1,0},{2,3},{3,2},{4,5},{5,4},{6,7},{7,6},{8,9},{9,8},{10,11... | collective-permute-start | bytes 589832 | tf_op jit(solution)/shard_map/ppermute | solution.py:416
  47.5 4.7 %collective-permute-start.13 = (f32[128,128]{1,0:T(8,128)S(1)}, f32[128,128]{1,0:T(8,128)S(1)}, u32[]{:S(2)}, u32[]{:S(2)}) collective-permute-start(f32[128,128]{1,0:T(8,128)S(1)} %shard_map.152.before_ref.left_ref), channel_id=1, source_target_pairs={{0,16},{1,17},{2,18},{3,19},{4,20},{5,21},{6,22},{7,23},{8,24},{9,... | collective-permute-start | bytes 196616 | tf_op jit(solution)/shard_map/ppermute | solution.py:416
  52.2 3.6 %collective-permute-start.15 = (f32[128,128]{1,0:T(8,128)S(1)}, f32[128,128]{1,0:T(8,128)S(1)}, u32[]{:S(2)}, u32[]{:S(2)}) collective-permute-start(f32[128,128]{1,0:T(8,128)S(1)} %shard_map.154.before_ref.left_ref), channel_id=1, source_target_pairs={{0,2},{1,3},{2,0},{3,1},{4,6},{5,7},{6,4},{7,5},{8,10},{9,11},{10,... | collective-permute-start | bytes 196616 | tf_op jit(solution)/shard_map/ppermute | solution.py:416
  55.8 5.0 %collective-permute-start.16 = (f32[128,128]{1,0:T(8,128)S(1)}, f32[128,128]{1,0:T(8,128)S(1)}, u32[]{:S(2)}, u32[]{:S(2)}) collective-permute-start(f32[128,128]{1,0:T(8,128)S(1)} %shard_map.156.left_ref.before_ref), channel_id=1, source_target_pairs={{0,4},{1,5},{2,6},{3,7},{4,0},{5,1},{6,2},{7,3},{8,12},{9,13},{10,... | collective-permute-start | bytes 196616 | tf_op jit(solution)/shard_map/ppermute | solution.py:416
  60.8 6.0 %collective-permute-start.17 = (f32[128,128]{1,0:T(8,128)S(1)}, f32[128,128]{1,0:T(8,128)S(1)}, u32[]{:S(2)}, u32[]{:S(2)}) collective-permute-start(f32[128,128]{1,0:T(8,128)S(1)} %shard_map.157.total_ref), channel_id=1, source_target_pairs={{0,1},{1,0},{2,3},{3,2},{4,5},{5,4},{6,7},{7,6},{8,9},{9,8},{10,11... | collective-permute-start | bytes 196616 | tf_op jit(solution)/shard_map/ppermute | solution.py:416

commit v6 on v5

--- a/solution.py
+++ b/solution.py
@@ -471,19 +471,19 @@
     last = send_back(3, last)
     last = send_back(0, last)
     total = added(total, other, last)
-    other = swapped(total, 64)
+    other = swapped(total, 96)
     grads_t = own(scaled_t, dl0, dl1, grad_pre, w_self, total)
     total = added(total, other, grads_t)
     other = swapped(total, 8)
     grads_t, last = place((2, 4), grads_t, total)
     total = added(total, other, last)
-    other = swapped(total, 16)
+    other = swapped(total, 24)
     grads_t, last = place((3, 1), grads_t, total)
     total = added(total, other, last)
     other = swapped(total, 2)
     grads, last = place((0,), grads_t, total)
     total = added(total, other, last)
-    other = swapped(total, 4)
+    other = swapped(total, 6)
     total = added(total, other, total)
     other = swapped(total, 1)
     grad_scale = 1.0 / math.sqrt(row_count * lax.axis_size("dom"))

time: 67.6 us -> 66.8 us (0.988)
  starting transfers between devices: 32.3 us -> 31.2 us
    ppermute x18, starting transfers between devices: 32.3 us -> 31.2 us  [swapped(): lax.ppermute(shard, 'dom', [(i, i ^ mask) for i in range(lax.axis_size('d...]
  transfers between devices with their start and end apart: 18 -> 18, of which waited for: 4 -> 4; matrix products, arithmetic and copies ran while one was open for 0% -> 0% of each run, Pallas kernels for 28% -> 29%
where the time goes in v6:
time: 66.8 us; the launch traced here: 66.7 us
  starting transfers between devices  31.2 us (47%)
  Pallas kernels  29.7 us (44%)
  waiting for transfers between devices  4.82 us (7%)
  between operations  0.91 us (1%)
    ppermute x18, starting transfers between devices, swapped(): lax.ppermute(shard, 'dom', [(i, i ^ mask) for i in range(lax.axis_size('d...  31.2 us
    pallas_call x1, Pallas kernels, densify(): pl.pallas_call(densify_kernel, out_shape=[VMEM((n, half, TILE), jnp.bfloa...  8.48 us
    pallas_call x1, Pallas kernels, middle(): pl.pallas_call(functools.partial(middle_kernel, rounds), out_shape=[half,...  6.21 us
    ppermute x18, waiting for transfers between devices, swapped(): lax.ppermute(shard, 'dom', [(i, i ^ mask) for i in range(lax.axis_size('d...  4.82 us
    pallas_call x3, Pallas kernels, place_rows(): pl.pallas_call(functools.partial(place_kernel, rounds, last), out_shape=[...  4.02 us
    pallas_call x1, Pallas kernels, pick_rows(): pl.pallas_call(pick_kernel, out_shape=outs, in_specs=[pl.BlockSpec(memory...  3.58 us
    pallas_call x5, Pallas kernels, back(): pl.pallas_call(functools.partial(back_kernel, first, n), out_shape=jax.Sh...  2.91 us
    pallas_call x1, Pallas kernels, local_sums(): pl.pallas_call(local_sums_kernel, out_shape=VMEM((rows, width), jnp.float...  2.31 us
  transfers between devices with their start and end apart: 18, of which 4 were waited for; matrix products, arithmetic and copies ran while one was open for 0% of the time, Pallas kernels for 29%

profile of v6, /device:TPU:1, one launch (start us, length us, event | category | flops | bytes accessed | tf_op | source)
XLA Modules:
  0.0 66.7 jit_solution(15888533886449219014)
XLA Ops:
  0.6 3.6 %shard_map.138 = (bf16[128,768]{1,0:T(8,128)(2,1)S(1)}, bf16[128,768]{1,0:T(8,128)(2,1)S(1)}, bf16[128,768]{1,0:T(8,128)(2,1)S(1)}, bf16[128,768]{1,0:T(8,128)(2,1)S(1)}, bf16[128,768]{1,0:T(8,128)(2,1)S(1)}) custom-call(s32[5,768]{1,0:T(8,128)} %rows_ref.5, bf16[2048,128]{1,0:T(8,128)(2,1)} %refs_8_.1), custom_call_target="tpu_custom_call" | custom-call | flops 2013265920 | bytes 1000000 | tf_op jit(solution)/shard_map/pallas_call | solution.py:75
  4.2 1.5 %collective-permute-start = (bf16[128,768]{1,0:T(8,128)(2,1)S(1)}, bf16[128,768]{1,0:T(8,128)(2,1)S(1)}, u32[]{:S(2)}, u32[]{:S(2)}) collective-permute-start(bf16[128,768]{1,0:T(8,128)(2,1)S(1)} %get-tuple-element.26), channel_id=1, source_target_pairs={{0,1},{1,0},{2,3},{3,2},{4,5},{5,4},{6,7},{7,6},{8,9},{9,8},{10,11... | collective-permute-start | bytes 589832 | tf_op jit(solution)/shard_map/ppermute | solution.py:416
  5.7 1.7 %collective-permute-start.1 = (bf16[128,768]{1,0:T(8,128)(2,1)S(1)}, bf16[128,768]{1,0:T(8,128)(2,1)S(1)}, u32[]{:S(2)}, u32[]{:S(2)}) collective-permute-start(bf16[128,768]{1,0:T(8,128)(2,1)S(1)} %get-tuple-element.27), channel_id=1, source_target_pairs={{0,2},{1,3},{2,0},{3,1},{4,6},{5,7},{6,4},{7,5},{8,10},{9,11},{10,... | collective-permute-start | bytes 589832 | tf_op jit(solution)/shard_map/ppermute | solution.py:416
  7.5 3.3 %collective-permute-start.2 = (bf16[128,768]{1,0:T(8,128)(2,1)S(1)}, bf16[128,768]{1,0:T(8,128)(2,1)S(1)}, u32[]{:S(2)}, u32[]{:S(2)}) collective-permute-start(bf16[128,768]{1,0:T(8,128)(2,1)S(1)} %get-tuple-element.28), channel_id=1, source_target_pairs={{0,4},{1,5},{2,6},{3,7},{4,0},{5,1},{6,2},{7,3},{8,12},{9,13},{10,... | collective-permute-start | bytes 589832 | tf_op jit(solution)/shard_map/ppermute | solution.py:416
  10.8 1.2 %collective-permute-start.3 = (bf16[128,768]{1,0:T(8,128)(2,1)S(1)}, bf16[128,768]{1,0:T(8,128)(2,1)S(1)}, u32[]{:S(2)}, u32[]{:S(2)}) collective-permute-start(bf16[128,768]{1,0:T(8,128)(2,1)S(1)} %get-tuple-element.29), channel_id=1, source_target_pairs={{0,8},{1,9},{2,10},{3,11},{4,12},{5,13},{6,14},{7,15},{8,0},{9,1},... | collective-permute-start | bytes 589832 | tf_op jit(solution)/shard_map/ppermute | solution.py:416
  12.0 2.5 %collective-permute-start.4 = (bf16[128,768]{1,0:T(8,128)(2,1)S(1)}, bf16[128,768]{1,0:T(8,128)(2,1)S(1)}, u32[]{:S(2)}, u32[]{:S(2)}) collective-permute-start(bf16[128,768]{1,0:T(8,128)(2,1)S(1)} %get-tuple-element.30), channel_id=1, source_target_pairs={{0,16},{1,17},{2,18},{3,19},{4,20},{5,21},{6,22},{7,23},{8,24},{9,... | collective-permute-start | bytes 589832 | tf_op jit(solution)/shard_map/ppermute | solution.py:416
  14.4 8.5 %shard_map.139 = (bf16[16,1024,128]{2,1,0:T(8,128)(2,1)S(1)}, bf16[16,1024,128]{2,1,0:T(8,128)(2,1)S(1)}, bf16[30,1024,128]{2,1,0:T(8,128)(2,1)S(1)}, bf16[30,1024,128]{2,1,0:T(8,128)(2,1)S(1)}) custom-call(s32[16,22]{1,0:T(8,128)} %lc_hbm.1, s32[16,20]{1,0:T(8,128)} %hc_hbm.1, bf16[16,22,128,128]{3,2,1,0:T(8,128)(2,1)} %lt.1, bf16[16,20,128,128]{3,2,1,0:T(8,128)(2,1)} %ht.1), custom_call_target="tpu_custom_call" | custom-call | flops 16000000 | bytes 22020096 | tf_op jit(solution)/shard_map/pallas_call | solution.py:170
  22.9 0.0 copy-start.1
  22.9 0.0 copy-start.3
  22.9 0.0 copy-start.4
  22.9 0.0 copy-start.5
  23.0 0.0 copy-start.6
  23.0 2.3 %shard_map.140.refs_7_ = f32[2048,128]{1,0:T(8,128)S(1)} custom-call(bf16[16,1024,128]{2,1,0:T(8,128)(2,1)S(1)} %get-tuple-element.33.d0_ref, bf16[16,1024,128]{2,1,0:T(8,128)(2,1)S(1)} %get-tuple-element.34.d1_ref, bf16[2048,128]{1,0:T(8,128)(2,1)S(1)} %copy-done), custom_call_target="tpu_custom_call" | custom-call | flops 1073741824 | bytes 1500000 | tf_op jit(solution)/shard_map/pallas_call | solution.py:202
  25.3 0.0 collective-permute-done.1.refs_1_
  25.3 0.0 collective-permute-done.2.refs_2_
  25.3 0.0 collective-permute-done.4.refs_4_
  25.4 6.2 %shard_map.141 = (bf16[2048,128]{1,0:T(8,128)(2,1)}, bf16[2048,128]{1,0:T(8,128)(2,1)S(1)}, bf16[128,2048]{1,0:T(8,128)(2,1)S(1)}, f32[128,128]{1,0:T(8,128)S(1)}, f32[128,128]{1,0:T(8,128)S(1)}) custom-call(bf16[128,768]{1,0:T(8,128)(2,1)S(1)} %collective-permute-done.refs_0_, bf16[128,768]{1,0:T(8,128)(2,1)S(1)} %collective-permute-done.1.refs_1_, ...), custom_call_target="tpu_custom_call" | custom-call | flops 2013265920 | bytes 5000000 | tf_op jit(solution)/shard_map/pallas_call | solution.py:262
  31.6 1.2 %collective-permute-start.5 = (f32[128,128]{1,0:T(8,128)S(1)}, f32[128,128]{1,0:T(8,128)S(1)}, u32[]{:S(2)}, u32[]{:S(2)}) collective-permute-start(f32[128,128]{1,0:T(8,128)S(1)} %get-tuple-element.39), channel_id=1, source_target_pairs={{0,1},{1,0},{2,3},{3,2},{4,5},{5,4},{6,7},{7,6},{8,9},{9,8},{10,11... | collective-permute-start | bytes 196616 | tf_op jit(solution)/shard_map/ppermute | solution.py:416
  32.8 0.6 shard_map.142.before_ref
  33.4 0.6 shard_map.143.before_ref
  34.0 0.8 %collective-permute-start.9 = (bf16[128,768]{1,0:T(8,128)(2,1)S(1)}, bf16[128,768]{1,0:T(8,128)(2,1)S(1)}, u32[]{:S(2)}, u32[]{:S(2)}) collective-permute-start(bf16[128,768]{1,0:T(8,128)(2,1)S(1)} %shard_map.143.before_ref), channel_id=1, source_target_pairs={{0,16},{1,17},{2,18},{3,19},{4,20},{5,21},{6,22},{7,23},{8,24},{9,... | collective-permute-start | bytes 589832 | tf_op jit(solution)/shard_map/ppermute | solution.py:416
  34.8 1.4 %collective-permute-start.6 = (f32[128,128]{1,0:T(8,128)S(1)}, f32[128,128]{1,0:T(8,128)S(1)}, u32[]{:S(2)}, u32[]{:S(2)}) collective-permute-start(f32[128,128]{1,0:T(8,128)S(1)} %shard_map.144.before_ref.left_ref), channel_id=1, source_target_pairs={{0,32},{1,33},{2,34},{3,35},{4,36},{5,37},{6,38},{7,39},{8,40},{9,... | collective-permute-start | bytes 196616 | tf_op jit(solution)/shard_map/ppermute | solution.py:416
  36.2 0.0 collective-permute-start.8
  36.2 0.6 shard_map.145.before_ref
  36.8 0.6 shard_map.146.before_ref
  37.4 0.6 shard_map.147.before_ref
  38.0 0.0 copy-start.2
  38.0 0.0 collective-permute-done.6.right_ref
  38.0 2.8 %collective-permute-start.7 = (f32[128,128]{1,0:T(8,128)S(1)}, f32[128,128]{1,0:T(8,128)S(1)}, u32[]{:S(2)}, u32[]{:S(2)}) collective-permute-start(f32[128,128]{1,0:T(8,128)S(1)} %shard_map.148.before_ref.left_ref), channel_id=1, source_target_pairs={{0,96},{1,97},{2,98},{3,99},{4,100},{5,101},{6,102},{7,103},{8,104... | collective-permute-start | bytes 196616 | tf_op jit(solution)/shard_map/ppermute | solution.py:416
  40.8 0.3 collective-permute-start.11
  41.1 0.0 collective-permute-start.12
  41.1 1.4 %shard_map.149.before_ref.acc_ref = f32[128,2048]{1,0:T(8,128)S(1)} custom-call(bf16[128,2048]{1,0:T(8,128)(2,1)S(1)} %get-tuple-element.36.st_ref.before_ref, bf16[16,1024,128]{2,1,0:T(8,128)(2,1)S(1)} %get-tuple-element.33.d0_ref, bf16[16,1024,128]{2,1,0:T(8,128)(2,1)S(1)} %get-tuple-element.34.d1_ref, bf16[2048,128]{1,0:T(8,128)(2,1)S(1)} %get-tuple-element.37.gp_ref, ...), custom_call_target="tpu_custom_call" | custom-call | flops 1 | bytes 1 | tf_op jit(solution)/shard_map/pallas_call | solution.py:327
  42.5 0.2 collective-permute-done.7.right_ref
  42.8 1.1 %collective-permute-start.10 = (f32[128,128]{1,0:T(8,128)S(1)}, f32[128,128]{1,0:T(8,128)S(1)}, u32[]{:S(2)}, u32[]{:S(2)}) collective-permute-start(f32[128,128]{1,0:T(8,128)S(1)} %shard_map.150.before_ref.left_ref), channel_id=1, source_target_pairs={{0,8},{1,9},{2,10},{3,11},{4,12},{5,13},{6,14},{7,15},{8,0},{9,1},... | collective-permute-start | bytes 196616 | tf_op jit(solution)/shard_map/ppermute | solution.py:416
  43.8 0.0 collective-permute-done.9.refs_1_
  43.8 2.3 %collective-permute-start.14 = (bf16[128,768]{1,0:T(8,128)(2,1)S(1)}, bf16[128,768]{1,0:T(8,128)(2,1)S(1)}, u32[]{:S(2)}, u32[]{:S(2)}) collective-permute-start(bf16[128,768]{1,0:T(8,128)(2,1)S(1)} %shard_map.147.before_ref), channel_id=1, source_target_pairs={{0,1},{1,0},{2,3},{3,2},{4,5},{5,4},{6,7},{7,6},{8,9},{9,8},{10,11... | collective-permute-start | bytes 589832 | tf_op jit(solution)/shard_map/ppermute | solution.py:416
  46.1 0.0 collective-permute-done.8.refs_0_
  46.1 1.1 %shard_map.151 = (f32[128,2048]{1,0:T(8,128)S(1)}, f32[8,128]{1,0:T(8,128)S(1)}) custom-call(s32[5,768]{1,0:T(8,128)S(1)} %copy-done.2, f32[128,2048]{1,0:T(8,128)S(1)} %shard_map.149.before_ref.acc_ref, f32[128,128]{1,0:T(8,128)S(1)} %shard_map.150.before_ref.left_ref, bf16[128,768]{1,0:T(8,128)(2,1)S(1)} %collective-permute-done.8.refs_0_, ...), custom_call_target="tpu_custom_call" | custom-call | flops 1 | bytes 1 | tf_op jit(solution)/shard_map/pallas_call | solution.py:370
  47.3 2.3 %collective-permute-start.13 = (f32[128,128]{1,0:T(8,128)S(1)}, f32[128,128]{1,0:T(8,128)S(1)}, u32[]{:S(2)}, u32[]{:S(2)}) collective-permute-start(f32[128,128]{1,0:T(8,128)S(1)} %shard_map.152.before_ref.left_ref), channel_id=1, source_target_pairs={{0,24},{1,25},{2,26},{3,27},{4,28},{5,29},{6,30},{7,31},{8,16},{9,... | collective-permute-start | bytes 196616 | tf_op jit(solution)/shard_map/ppermute | solution.py:416
  49.6 1.1 %shard_map.153 = (f32[128,2048]{1,0:T(8,128)S(1)}, f32[8,128]{1,0:T(8,128)S(1)}) custom-call(s32[5,768]{1,0:T(8,128)S(1)} %copy-done.2, f32[128,2048]{1,0:T(8,128)S(1)} %get-tuple-element.40.acc_ref, f32[128,128]{1,0:T(8,128)S(1)} %shard_map.152.before_ref.left_ref, bf16[128,768]{1,0:T(8,128)(2,1)S(1)} %collective-permute-done.11.refs_0_, ...), custom_call_target="tpu_custom_call" | custom-call | flops 1 | bytes 1 | tf_op jit(solution)/shard_map/pallas_call | solution.py:370
  50.7 1.0 %collective-permute-done.13.right_ref = f32[128,128]{1,0:T(8,128)S(1)} collective-permute-done((f32[128,128]{1,0:T(8,128)S(1)}, f32[128,128]{1,0:T(8,128)S(1)}, u32[]{:S(2)}, u32[]{:S(2)}) %collective-permute-start.13) | collective-permute-done | bytes 65568 | tf_op jit(solution)/shard_map/ppermute | solution.py:416
  51.7 1.8 %collective-permute-start.15 = (f32[128,128]{1,0:T(8,128)S(1)}, f32[128,128]{1,0:T(8,128)S(1)}, u32[]{:S(2)}, u32[]{:S(2)}) collective-permute-start(f32[128,128]{1,0:T(8,128)S(1)} %shard_map.154.before_ref.left_ref), channel_id=1, source_target_pairs={{0,2},{1,3},{2,0},{3,1},{4,6},{5,7},{6,4},{7,5},{8,10},{9,11},{10,... | collective-permute-start | bytes 196616 | tf_op jit(solution)/shard_map/ppermute | solution.py:416
  53.6 1.8 %shard_map.155 = (f32[2048,128]{1,0:T(8,128)}, f32[8,128]{1,0:T(8,128)S(1)}) custom-call(s32[5,768]{1,0:T(8,128)S(1)} %copy-done.2, f32[128,2048]{1,0:T(8,128)S(1)} %get-tuple-element.42.acc_ref, f32[128,128]{1,0:T(8,128)S(1)} %shard_map.154.before_ref.left_ref, bf16[128,768]{1,0:T(8,128)(2,1)S(1)} %collective-permute-done.14.refs_0_), custom_call_target="tpu_custom_call" | custom-call | flops 1 | bytes 1 | tf_op jit(solution)/shard_map/pallas_call | solution.py:370
  55.3 1.8 %collective-permute-start.16 = (f32[128,128]{1,0:T(8,128)S(1)}, f32[128,128]{1,0:T(8,128)S(1)}, u32[]{:S(2)}, u32[]{:S(2)}) collective-permute-start(f32[128,128]{1,0:T(8,128)S(1)} %shard_map.156.left_ref.before_ref), channel_id=1, source_target_pairs={{0,6},{1,7},{2,4},{3,5},{4,2},{5,3},{6,0},{7,1},{8,14},{9,15},{10,... | collective-permute-start | bytes 196616 | tf_op jit(solution)/shard_map/ppermute | solution.py:416
  57.1 2.6 %collective-permute-done.16.right_ref = f32[128,128]{1,0:T(8,128)S(1)} collective-permute-done((f32[128,128]{1,0:T(8,128)S(1)}, f32[128,128]{1,0:T(8,128)S(1)}, u32[]{:S(2)}, u32[]{:S(2)}) %collective-permute-start.16) | collective-permute-done | bytes 65568 | tf_op jit(solution)/shard_map/ppermute | solution.py:416
  59.8 5.4 %collective-permute-start.17 = (f32[128,128]{1,0:T(8,128)S(1)}, f32[128,128]{1,0:T(8,128)S(1)}, u32[]{:S(2)}, u32[]{:S(2)}) collective-permute-start(f32[128,128]{1,0:T(8,128)S(1)} %shard_map.157.total_ref), channel_id=1, source_target_pairs={{0,1},{1,0},{2,3},{3,2},{4,5},{5,4},{6,7},{7,6},{8,9},{9,8},{10,11... | collective-permute-start | bytes 196616 | tf_op jit(solution)/shard_map/ppermute | solution.py:416
  65.1 0.9 %collective-permute-done.17.other_ref = f32[128,128]{1,0:T(8,128)S(1)} collective-permute-done((f32[128,128]{1,0:T(8,128)S(1)}, f32[128,128]{1,0:T(8,128)S(1)}, u32[]{:S(2)}, u32[]{:S(2)}) %collective-permute-start.17) | collective-permute-done | bytes 65568 | tf_op jit(solution)/shard_map/ppermute | solution.py:416
  66.0 0.7 shard_map.158
  (23 shorter events, 0.1 us)
Async XLA Ops:
  4.2 21.1 %collective-permute-start = (bf16[128,768]{1,0:T(8,128)(2,1)S(1)}, bf16[128,768]{1,0:T(8,128)(2,1)S(1)}, u32[]{:S(2)}, u32[]{:S(2)}) collective-permute-start(bf16[128,768]{1,0:T(8,128)(2,1)S(1)} %get-tuple-element.26), channel_id=1, source_target_pairs={{0,1},{1,0},{2,3},{3,2},{4,5},{5,4},{6,7},{7,6},{8,9},{9,8},{10,11... | collective-permute-start | bytes 589832 | tf_op jit(solution)/shard_map/ppermute | solution.py:416
  5.7 19.6 %collective-permute-start.1 = (bf16[128,768]{1,0:T(8,128)(2,1)S(1)}, bf16[128,768]{1,0:T(8,128)(2,1)S(1)}, u32[]{:S(2)}, u32[]{:S(2)}) collective-permute-start(bf16[128,768]{1,0:T(8,128)(2,1)S(1)} %get-tuple-element.27), channel_id=1, source_target_pairs={{0,2},{1,3},{2,0},{3,1},{4,6},{5,7},{6,4},{7,5},{8,10},{9,11},{10,... | collective-permute-start | bytes 589832 | tf_op jit(solution)/shard_map/ppermute | solution.py:416
  7.5 17.9 %collective-permute-start.2 = (bf16[128,768]{1,0:T(8,128)(2,1)S(1)}, bf16[128,768]{1,0:T(8,128)(2,1)S(1)}, u32[]{:S(2)}, u32[]{:S(2)}) collective-permute-start(bf16[128,768]{1,0:T(8,128)(2,1)S(1)} %get-tuple-element.28), channel_id=1, source_target_pairs={{0,4},{1,5},{2,6},{3,7},{4,0},{5,1},{6,2},{7,3},{8,12},{9,13},{10,... | collective-permute-start | bytes 589832 | tf_op jit(solution)/shard_map/ppermute | solution.py:416
  10.8 14.6 %collective-permute-start.3 = (bf16[128,768]{1,0:T(8,128)(2,1)S(1)}, bf16[128,768]{1,0:T(8,128)(2,1)S(1)}, u32[]{:S(2)}, u32[]{:S(2)}) collective-permute-start(bf16[128,768]{1,0:T(8,128)(2,1)S(1)} %get-tuple-element.29), channel_id=1, source_target_pairs={{0,8},{1,9},{2,10},{3,11},{4,12},{5,13},{6,14},{7,15},{8,0},{9,1},... | collective-permute-start | bytes 589832 | tf_op jit(solution)/shard_map/ppermute | solution.py:416
  12.0 11.0 %copy-start = (bf16[2048,128]{1,0:T(8,128)(2,1)S(1)}, bf16[2048,128]{1,0:T(8,128)(2,1)}, u32[]{:S(2)}) copy-start(bf16[2048,128]{1,0:T(8,128)(2,1)} %refs_8_.1) | copy-start | bytes 1572868
  12.0 13.4 %collective-permute-start.4 = (bf16[128,768]{1,0:T(8,128)(2,1)S(1)}, bf16[128,768]{1,0:T(8,128)(2,1)S(1)}, u32[]{:S(2)}, u32[]{:S(2)}) collective-permute-start(bf16[128,768]{1,0:T(8,128)(2,1)S(1)} %get-tuple-element.30), channel_id=1, source_target_pairs={{0,16},{1,17},{2,18},{3,19},{4,20},{5,21},{6,22},{7,23},{8,24},{9,... | collective-permute-start | bytes 589832 | tf_op jit(solution)/shard_map/ppermute | solution.py:416
  22.9 2.4 %copy-start.1 = (bf16[2048,128]{1,0:T(8,128)(2,1)S(1)}, bf16[2048,128]{1,0:T(8,128)(2,1)}, u32[]{:S(2)}) copy-start(bf16[2048,128]{1,0:T(8,128)(2,1)} %refs_9_.1) | copy-start | bytes 1572868
  22.9 2.4 %copy-start.3 = (bf16[128,128]{1,0:T(8,128)(2,1)S(1)}, bf16[128,128]{1,0:T(8,128)(2,1)}, u32[]{:S(2)}) copy-start(bf16[128,128]{1,0:T(8,128)(2,1)} %ws_ref.1) | copy-start | bytes 98308
  22.9 2.4 %copy-start.4 = (bf16[128,128]{1,0:T(8,128)(2,1)S(1)}, bf16[128,128]{1,0:T(8,128)(2,1)}, u32[]{:S(2)}) copy-start(bf16[128,128]{1,0:T(8,128)(2,1)} %refs_12_.1) | copy-start | bytes 98308
  22.9 2.4 %copy-start.5 = (s32[2048]{0:T(1024)S(1)}, s32[2048]{0:T(1024)}, u32[]{:S(2)}) copy-start(s32[2048]{0:T(1024)} %param.20) | copy-start | bytes 24580
  23.0 2.4 %copy-start.6 = (f32[128]{0:T(128)S(1)}, f32[128]{0:T(128)}, u32[]{:S(2)}) copy-start(f32[128]{0:T(128)} %param.14) | copy-start | bytes 1540
  31.6 3.2 %collective-permute-start.5 = (f32[128,128]{1,0:T(8,128)S(1)}, f32[128,128]{1,0:T(8,128)S(1)}, u32[]{:S(2)}, u32[]{:S(2)}) collective-permute-start(f32[128,128]{1,0:T(8,128)S(1)} %get-tuple-element.39), channel_id=1, source_target_pairs={{0,1},{1,0},{2,3},{3,2},{4,5},{5,4},{6,7},{7,6},{8,9},{9,8},{10,11... | collective-permute-start | bytes 196616 | tf_op jit(solution)/shard_map/ppermute | solution.py:416
  34.0 9.8 %collective-permute-start.9 = (bf16[128,768]{1,0:T(8,128)(2,1)S(1)}, bf16[128,768]{1,0:T(8,128)(2,1)S(1)}, u32[]{:S(2)}, u32[]{:S(2)}) collective-permute-start(bf16[128,768]{1,0:T(8,128)(2,1)S(1)} %shard_map.143.before_ref), channel_id=1, source_target_pairs={{0,16},{1,17},{2,18},{3,19},{4,20},{5,21},{6,22},{7,23},{8,24},{9,... | collective-permute-start | bytes 589832 | tf_op jit(solution)/shard_map/ppermute | solution.py:416
  34.8 3.2 %collective-permute-start.6 = (f32[128,128]{1,0:T(8,128)S(1)}, f32[128,128]{1,0:T(8,128)S(1)}, u32[]{:S(2)}, u32[]{:S(2)}) collective-permute-start(f32[128,128]{1,0:T(8,128)S(1)} %shard_map.144.before_ref.left_ref), channel_id=1, source_target_pairs={{0,32},{1,33},{2,34},{3,35},{4,36},{5,37},{6,38},{7,39},{8,40},{9,... | collective-permute-start | bytes 196616 | tf_op jit(solution)/shard_map/ppermute | solution.py:416
  36.2 9.9 %collective-permute-start.8 = (bf16[128,768]{1,0:T(8,128)(2,1)S(1)}, bf16[128,768]{1,0:T(8,128)(2,1)S(1)}, u32[]{:S(2)}, u32[]{:S(2)}) collective-permute-start(bf16[128,768]{1,0:T(8,128)(2,1)S(1)} %shard_map.142.before_ref), channel_id=1, source_target_pairs={{0,4},{1,5},{2,6},{3,7},{4,0},{5,1},{6,2},{7,3},{8,12},{9,13},{10,... | collective-permute-start | bytes 589832 | tf_op jit(solution)/shard_map/ppermute | solution.py:416
  38.0 8.2 %copy-start.2 = (s32[5,768]{1,0:T(8,128)S(1)}, s32[5,768]{1,0:T(8,128)}, u32[]{:S(2)}) copy-start(s32[5,768]{1,0:T(8,128)} %rows_ref.5) | copy-start | bytes 46084
  38.0 4.7 %collective-permute-start.7 = (f32[128,128]{1,0:T(8,128)S(1)}, f32[128,128]{1,0:T(8,128)S(1)}, u32[]{:S(2)}, u32[]{:S(2)}) collective-permute-start(f32[128,128]{1,0:T(8,128)S(1)} %shard_map.148.before_ref.left_ref), channel_id=1, source_target_pairs={{0,96},{1,97},{2,98},{3,99},{4,100},{5,101},{6,102},{7,103},{8,104... | collective-permute-start | bytes 196616 | tf_op jit(solution)/shard_map/ppermute | solution.py:416
  40.8 8.8 %collective-permute-start.11 = (bf16[128,768]{1,0:T(8,128)(2,1)S(1)}, bf16[128,768]{1,0:T(8,128)(2,1)S(1)}, u32[]{:S(2)}, u32[]{:S(2)}) collective-permute-start(bf16[128,768]{1,0:T(8,128)(2,1)S(1)} %shard_map.146.before_ref), channel_id=1, source_target_pairs={{0,8},{1,9},{2,10},{3,11},{4,12},{5,13},{6,14},{7,15},{8,0},{9,1},... | collective-permute-start | bytes 589832 | tf_op jit(solution)/shard_map/ppermute | solution.py:416
  41.1 8.5 %collective-permute-start.12 = (bf16[128,768]{1,0:T(8,128)(2,1)S(1)}, bf16[128,768]{1,0:T(8,128)(2,1)S(1)}, u32[]{:S(2)}, u32[]{:S(2)}) collective-permute-start(bf16[128,768]{1,0:T(8,128)(2,1)S(1)} %shard_map.145.before_ref), channel_id=1, source_target_pairs={{0,2},{1,3},{2,0},{3,1},{4,6},{5,7},{6,4},{7,5},{8,10},{9,11},{10,... | collective-permute-start | bytes 589832 | tf_op jit(solution)/shard_map/ppermute | solution.py:416
  42.8 4.5 %collective-permute-start.10 = (f32[128,128]{1,0:T(8,128)S(1)}, f32[128,128]{1,0:T(8,128)S(1)}, u32[]{:S(2)}, u32[]{:S(2)}) collective-permute-start(f32[128,128]{1,0:T(8,128)S(1)} %shard_map.150.before_ref.left_ref), channel_id=1, source_target_pairs={{0,8},{1,9},{2,10},{3,11},{4,12},{5,13},{6,14},{7,15},{8,0},{9,1},... | collective-permute-start | bytes 196616 | tf_op jit(solution)/shard_map/ppermute | solution.py:416
  43.8 9.7 %collective-permute-start.14 = (bf16[128,768]{1,0:T(8,128)(2,1)S(1)}, bf16[128,768]{1,0:T(8,128)(2,1)S(1)}, u32[]{:S(2)}, u32[]{:S(2)}) collective-permute-start(bf16[128,768]{1,0:T(8,128)(2,1)S(1)} %shard_map.147.before_ref), channel_id=1, source_target_pairs={{0,1},{1,0},{2,3},{3,2},{4,5},{5,4},{6,7},{7,6},{8,9},{9,8},{10,11... | collective-permute-start | bytes 589832 | tf_op jit(solution)/shard_map/ppermute | solution.py:416
  47.3 4.4 %collective-permute-start.13 = (f32[128,128]{1,0:T(8,128)S(1)}, f32[128,128]{1,0:T(8,128)S(1)}, u32[]{:S(2)}, u32[]{:S(2)}) collective-permute-start(f32[128,128]{1,0:T(8,128)S(1)} %shard_map.152.before_ref.left_ref), channel_id=1, source_target_pairs={{0,24},{1,25},{2,26},{3,27},{4,28},{5,29},{6,30},{7,31},{8,16},{9,... | collective-permute-start | bytes 196616 | tf_op jit(solution)/shard_map/ppermute | solution.py:416
  51.7 3.6 %collective-permute-start.15 = (f32[128,128]{1,0:T(8,128)S(1)}, f32[128,128]{1,0:T(8,128)S(1)}, u32[]{:S(2)}, u32[]{:S(2)}) collective-permute-start(f32[128,128]{1,0:T(8,128)S(1)} %shard_map.154.before_ref.left_ref), channel_id=1, source_target_pairs={{0,2},{1,3},{2,0},{3,1},{4,6},{5,7},{6,4},{7,5},{8,10},{9,11},{10,... | collective-permute-start | bytes 196616 | tf_op jit(solution)/shard_map/ppermute | solution.py:416
  55.3 4.4 %collective-permute-start.16 = (f32[128,128]{1,0:T(8,128)S(1)}, f32[128,128]{1,0:T(8,128)S(1)}, u32[]{:S(2)}, u32[]{:S(2)}) collective-permute-start(f32[128,128]{1,0:T(8,128)S(1)} %shard_map.156.left_ref.before_ref), channel_id=1, source_target_pairs={{0,6},{1,7},{2,4},{3,5},{4,2},{5,3},{6,0},{7,1},{8,14},{9,15},{10,... | collective-permute-start | bytes 196616 | tf_op jit(solution)/shard_map/ppermute | solution.py:416
  59.8 6.3 %collective-permute-start.17 = (f32[128,128]{1,0:T(8,128)S(1)}, f32[128,128]{1,0:T(8,128)S(1)}, u32[]{:S(2)}, u32[]{:S(2)}) collective-permute-start(f32[128,128]{1,0:T(8,128)S(1)} %shard_map.157.total_ref), channel_id=1, source_target_pairs={{0,1},{1,0},{2,3},{3,2},{4,5},{5,4},{6,7},{7,6},{8,9},{9,8},{10,11... | collective-permute-start | bytes 196616 | tf_op jit(solution)/shard_map/ppermute | solution.py:416

commit v7 on v6

--- a/solution.py
+++ b/solution.py
@@ -464,27 +464,27 @@
 
     other = swapped(give, 1)
     last = send_back(2, scaled_t)
-    last = send_back(4, last)
     total = added(mine, other, last)
     other = swapped(total, 32)
+    last = send_back(4, total)
+    total = added(total, other, last)
+    other = swapped(total, 96)
     last = send_back(1, total)
     last = send_back(3, last)
-    last = send_back(0, last)
     total = added(total, other, last)
-    other = swapped(total, 96)
-    grads_t = own(scaled_t, dl0, dl1, grad_pre, w_self, total)
+    other = swapped(total, 8)
+    last = send_back(0, total)
+    grads_t = own(scaled_t, dl0, dl1, grad_pre, w_self, last)
     total = added(total, other, grads_t)
-    other = swapped(total, 8)
+    other = swapped(total, 24)
     grads_t, last = place((2, 4), grads_t, total)
     total = added(total, other, last)
-    other = swapped(total, 24)
+    other = swapped(total, 2)
     grads_t, last = place((3, 1), grads_t, total)
     total = added(total, other, last)
-    other = swapped(total, 2)
+    other = swapped(total, 6)
     grads, last = place((0,), grads_t, total)
     total = added(total, other, last)
-    other = swapped(total, 6)
-    total = added(total, other, total)
     other = swapped(total, 1)
     grad_scale = 1.0 / math.sqrt(row_count * lax.axis_size("dom"))
     grad_self, grad_neigh = halves(grad_scale, total, other)

time: 66.8 us -> 66.9 us (level)
  waiting for transfers between devices: 4.82 us -> 7.42 us
  starting transfers between devices: 31.2 us -> 28.7 us
    ppermute x18, waiting for transfers between devices: 4.82 us -> 7.42 us  [swapped(): lax.ppermute(shard, 'dom', [(i, i ^ mask) for i in range(lax.axis_size('d...]
    ppermute x18, starting transfers between devices: 31.2 us -> 28.7 us  [swapped(): lax.ppermute(shard, 'dom', [(i, i ^ mask) for i in range(lax.axis_size('d...]
  transfers between devices with their start and end apart: 18 -> 18, of which waited for: 4 -> 7; matrix products, arithmetic and copies ran while one was open for 0% -> 0% of each run, Pallas kernels for 29% -> 29%
where the time goes in v7:
time: 66.9 us; the launch traced here: 66.8 us
  Pallas kernels  29.7 us (44%)
  starting transfers between devices  28.7 us (43%)
  waiting for transfers between devices  7.42 us (11%)
  between operations  0.94 us (1%)
    ppermute x18, starting transfers between devices, swapped(): lax.ppermute(shard, 'dom', [(i, i ^ mask) for i in range(lax.axis_size('d...  28.7 us
    pallas_call x1, Pallas kernels, densify(): pl.pallas_call(densify_kernel, out_shape=[VMEM((n, half, TILE), jnp.bfloa...  8.48 us
    ppermute x18, waiting for transfers between devices, swapped(): lax.ppermute(shard, 'dom', [(i, i ^ mask) for i in range(lax.axis_size('d...  7.42 us
    pallas_call x1, Pallas kernels, middle(): pl.pallas_call(functools.partial(middle_kernel, rounds), out_shape=[half,...  6.21 us
    pallas_call x3, Pallas kernels, place_rows(): pl.pallas_call(functools.partial(place_kernel, rounds, last), out_shape=[...  4.03 us
    pallas_call x1, Pallas kernels, pick_rows(): pl.pallas_call(pick_kernel, out_shape=outs, in_specs=[pl.BlockSpec(memory...  3.58 us
    pallas_call x5, Pallas kernels, back(): pl.pallas_call(functools.partial(back_kernel, first, n), out_shape=jax.Sh...  2.92 us
    pallas_call x1, Pallas kernels, local_sums(): pl.pallas_call(local_sums_kernel, out_shape=VMEM((rows, width), jnp.float...  2.31 us
  transfers between devices with their start and end apart: 18, of which 7 were waited for; matrix products, arithmetic and copies ran while one was open for 0% of the time, Pallas kernels for 29%

profile of v7, /device:TPU:1, one launch (start us, length us, event | category | flops | bytes accessed | tf_op | source)
XLA Modules:
  0.0 66.8 jit_solution(10755116807229384107)
XLA Ops:
  0.6 3.6 %shard_map.138 = (bf16[128,768]{1,0:T(8,128)(2,1)S(1)}, bf16[128,768]{1,0:T(8,128)(2,1)S(1)}, bf16[128,768]{1,0:T(8,128)(2,1)S(1)}, bf16[128,768]{1,0:T(8,128)(2,1)S(1)}, bf16[128,768]{1,0:T(8,128)(2,1)S(1)}) custom-call(s32[5,768]{1,0:T(8,128)} %rows_ref.5, bf16[2048,128]{1,0:T(8,128)(2,1)} %refs_8_.1), custom_call_target="tpu_custom_call" | custom-call | flops 2013265920 | bytes 1000000 | tf_op jit(solution)/shard_map/pallas_call | solution.py:75
  4.2 1.5 %collective-permute-start = (bf16[128,768]{1,0:T(8,128)(2,1)S(1)}, bf16[128,768]{1,0:T(8,128)(2,1)S(1)}, u32[]{:S(2)}, u32[]{:S(2)}) collective-permute-start(bf16[128,768]{1,0:T(8,128)(2,1)S(1)} %get-tuple-element.26), channel_id=1, source_target_pairs={{0,1},{1,0},{2,3},{3,2},{4,5},{5,4},{6,7},{7,6},{8,9},{9,8},{10,11... | collective-permute-start | bytes 589832 | tf_op jit(solution)/shard_map/ppermute | solution.py:416
  5.7 1.7 %collective-permute-start.1 = (bf16[128,768]{1,0:T(8,128)(2,1)S(1)}, bf16[128,768]{1,0:T(8,128)(2,1)S(1)}, u32[]{:S(2)}, u32[]{:S(2)}) collective-permute-start(bf16[128,768]{1,0:T(8,128)(2,1)S(1)} %get-tuple-element.27), channel_id=1, source_target_pairs={{0,2},{1,3},{2,0},{3,1},{4,6},{5,7},{6,4},{7,5},{8,10},{9,11},{10,... | collective-permute-start | bytes 589832 | tf_op jit(solution)/shard_map/ppermute | solution.py:416
  7.5 3.3 %collective-permute-start.2 = (bf16[128,768]{1,0:T(8,128)(2,1)S(1)}, bf16[128,768]{1,0:T(8,128)(2,1)S(1)}, u32[]{:S(2)}, u32[]{:S(2)}) collective-permute-start(bf16[128,768]{1,0:T(8,128)(2,1)S(1)} %get-tuple-element.28), channel_id=1, source_target_pairs={{0,4},{1,5},{2,6},{3,7},{4,0},{5,1},{6,2},{7,3},{8,12},{9,13},{10,... | collective-permute-start | bytes 589832 | tf_op jit(solution)/shard_map/ppermute | solution.py:416
  10.8 1.2 %collective-permute-start.3 = (bf16[128,768]{1,0:T(8,128)(2,1)S(1)}, bf16[128,768]{1,0:T(8,128)(2,1)S(1)}, u32[]{:S(2)}, u32[]{:S(2)}) collective-permute-start(bf16[128,768]{1,0:T(8,128)(2,1)S(1)} %get-tuple-element.29), channel_id=1, source_target_pairs={{0,8},{1,9},{2,10},{3,11},{4,12},{5,13},{6,14},{7,15},{8,0},{9,1},... | collective-permute-start | bytes 589832 | tf_op jit(solution)/shard_map/ppermute | solution.py:416
  12.0 2.5 %collective-permute-start.4 = (bf16[128,768]{1,0:T(8,128)(2,1)S(1)}, bf16[128,768]{1,0:T(8,128)(2,1)S(1)}, u32[]{:S(2)}, u32[]{:S(2)}) collective-permute-start(bf16[128,768]{1,0:T(8,128)(2,1)S(1)} %get-tuple-element.30), channel_id=1, source_target_pairs={{0,16},{1,17},{2,18},{3,19},{4,20},{5,21},{6,22},{7,23},{8,24},{9,... | collective-permute-start | bytes 589832 | tf_op jit(solution)/shard_map/ppermute | solution.py:416
  14.4 8.5 %shard_map.139 = (bf16[16,1024,128]{2,1,0:T(8,128)(2,1)S(1)}, bf16[16,1024,128]{2,1,0:T(8,128)(2,1)S(1)}, bf16[30,1024,128]{2,1,0:T(8,128)(2,1)S(1)}, bf16[30,1024,128]{2,1,0:T(8,128)(2,1)S(1)}) custom-call(s32[16,22]{1,0:T(8,128)} %lc_hbm.1, s32[16,20]{1,0:T(8,128)} %hc_hbm.1, bf16[16,22,128,128]{3,2,1,0:T(8,128)(2,1)} %lt.1, bf16[16,20,128,128]{3,2,1,0:T(8,128)(2,1)} %ht.1), custom_call_target="tpu_custom_call" | custom-call | flops 16000000 | bytes 22020096 | tf_op jit(solution)/shard_map/pallas_call | solution.py:170
  22.9 0.0 copy-start.1
  22.9 0.0 copy-start.3
  22.9 0.0 copy-start.4
  22.9 0.0 copy-start.5
  23.0 0.0 copy-start.6
  23.0 2.3 %shard_map.140.refs_7_ = f32[2048,128]{1,0:T(8,128)S(1)} custom-call(bf16[16,1024,128]{2,1,0:T(8,128)(2,1)S(1)} %get-tuple-element.33.d0_ref, bf16[16,1024,128]{2,1,0:T(8,128)(2,1)S(1)} %get-tuple-element.34.d1_ref, bf16[2048,128]{1,0:T(8,128)(2,1)S(1)} %copy-done), custom_call_target="tpu_custom_call" | custom-call | flops 1073741824 | bytes 1500000 | tf_op jit(solution)/shard_map/pallas_call | solution.py:202
  25.3 0.0 collective-permute-done.refs_0_
  25.3 0.0 collective-permute-done.1.refs_1_
  25.3 0.0 collective-permute-done.3.refs_3_
  25.3 0.0 collective-permute-done.4.refs_4_
  25.4 6.2 %shard_map.141 = (bf16[2048,128]{1,0:T(8,128)(2,1)}, bf16[2048,128]{1,0:T(8,128)(2,1)S(1)}, bf16[128,2048]{1,0:T(8,128)(2,1)S(1)}, f32[128,128]{1,0:T(8,128)S(1)}, f32[128,128]{1,0:T(8,128)S(1)}) custom-call(bf16[128,768]{1,0:T(8,128)(2,1)S(1)} %collective-permute-done.refs_0_, bf16[128,768]{1,0:T(8,128)(2,1)S(1)} %collective-permute-done.1.refs_1_, ...), custom_call_target="tpu_custom_call" | custom-call | flops 2013265920 | bytes 5000000 | tf_op jit(solution)/shard_map/pallas_call | solution.py:262
  31.6 1.2 %collective-permute-start.5 = (f32[128,128]{1,0:T(8,128)S(1)}, f32[128,128]{1,0:T(8,128)S(1)}, u32[]{:S(2)}, u32[]{:S(2)}) collective-permute-start(f32[128,128]{1,0:T(8,128)S(1)} %get-tuple-element.39), channel_id=1, source_target_pairs={{0,1},{1,0},{2,3},{3,2},{4,5},{5,4},{6,7},{7,6},{8,9},{9,8},{10,11... | collective-permute-start | bytes 196616 | tf_op jit(solution)/shard_map/ppermute | solution.py:416
  32.8 0.6 shard_map.142.before_ref
  33.4 0.3 collective-permute-done.5.right_ref
  33.7 1.4 %collective-permute-start.6 = (f32[128,128]{1,0:T(8,128)S(1)}, f32[128,128]{1,0:T(8,128)S(1)}, u32[]{:S(2)}, u32[]{:S(2)}) collective-permute-start(f32[128,128]{1,0:T(8,128)S(1)} %shard_map.143.before_ref.left_ref), channel_id=1, source_target_pairs={{0,32},{1,33},{2,34},{3,35},{4,36},{5,37},{6,38},{7,39},{8,40},{9,... | collective-permute-start | bytes 196616 | tf_op jit(solution)/shard_map/ppermute | solution.py:416
  35.1 0.0 collective-permute-start.9
  35.1 0.6 shard_map.144.before_ref
  35.7 1.2 %collective-permute-done.6.right_ref = f32[128,128]{1,0:T(8,128)S(1)} collective-permute-done((f32[128,128]{1,0:T(8,128)S(1)}, f32[128,128]{1,0:T(8,128)S(1)}, u32[]{:S(2)}, u32[]{:S(2)}) %collective-permute-start.6) | collective-permute-done | bytes 65568 | tf_op jit(solution)/shard_map/ppermute | solution.py:416
  36.9 2.8 %collective-permute-start.7 = (f32[128,128]{1,0:T(8,128)S(1)}, f32[128,128]{1,0:T(8,128)S(1)}, u32[]{:S(2)}, u32[]{:S(2)}) collective-permute-start(f32[128,128]{1,0:T(8,128)S(1)} %shard_map.145.before_ref.left_ref), channel_id=1, source_target_pairs={{0,96},{1,97},{2,98},{3,99},{4,100},{5,101},{6,102},{7,103},{8,104... | collective-permute-start | bytes 196616 | tf_op jit(solution)/shard_map/ppermute | solution.py:416
  39.7 0.5 collective-permute-start.10
  40.3 0.6 shard_map.146.before_ref
  40.8 0.6 shard_map.147.before_ref
  41.4 0.2 collective-permute-done.7.right_ref
  41.7 0.1 collective-permute-start.8
  41.8 1.4 %collective-permute-start.12 = (bf16[128,768]{1,0:T(8,128)(2,1)S(1)}, bf16[128,768]{1,0:T(8,128)(2,1)S(1)}, u32[]{:S(2)}, u32[]{:S(2)}) collective-permute-start(bf16[128,768]{1,0:T(8,128)(2,1)S(1)} %shard_map.147.before_ref), channel_id=1, source_target_pairs={{0,8},{1,9},{2,10},{3,11},{4,12},{5,13},{6,14},{7,15},{8,0},{9,1},... | collective-permute-start | bytes 589832 | tf_op jit(solution)/shard_map/ppermute | solution.py:416
  43.3 0.6 shard_map.149.before_ref
  43.8 0.0 copy-start.2
  43.9 1.4 %shard_map.150.before_ref.acc_ref = f32[128,2048]{1,0:T(8,128)S(1)} custom-call(bf16[128,2048]{1,0:T(8,128)(2,1)S(1)} %get-tuple-element.36.st_ref.before_ref, bf16[16,1024,128]{2,1,0:T(8,128)(2,1)S(1)} %get-tuple-element.33.d0_ref, bf16[16,1024,128]{2,1,0:T(8,128)(2,1)S(1)} %get-tuple-element.34.d1_ref, bf16[2048,128]{1,0:T(8,128)(2,1)S(1)} %get-tuple-element.37.gp_ref, ...), custom_call_target="tpu_custom_call" | custom-call | flops 1 | bytes 1 | tf_op jit(solution)/shard_map/pallas_call | solution.py:327
  45.3 0.2 collective-permute-done.8.right_ref
  45.5 2.1 %collective-permute-start.11 = (f32[128,128]{1,0:T(8,128)S(1)}, f32[128,128]{1,0:T(8,128)S(1)}, u32[]{:S(2)}, u32[]{:S(2)}) collective-permute-start(f32[128,128]{1,0:T(8,128)S(1)} %shard_map.151.before_ref.left_ref), channel_id=1, source_target_pairs={{0,24},{1,25},{2,26},{3,27},{4,28},{5,29},{6,30},{7,31},{8,16},{9,... | collective-permute-start | bytes 196616 | tf_op jit(solution)/shard_map/ppermute | solution.py:416
  47.6 5.1 %collective-permute-start.15 = (bf16[128,768]{1,0:T(8,128)(2,1)S(1)}, bf16[128,768]{1,0:T(8,128)(2,1)S(1)}, u32[]{:S(2)}, u32[]{:S(2)}) collective-permute-start(bf16[128,768]{1,0:T(8,128)(2,1)S(1)} %shard_map.149.before_ref), channel_id=1, source_target_pairs={{0,1},{1,0},{2,3},{3,2},{4,5},{5,4},{6,7},{7,6},{8,9},{9,8},{10,11... | collective-permute-start | bytes 589832 | tf_op jit(solution)/shard_map/ppermute | solution.py:416
  52.7 1.1 %shard_map.152 = (f32[128,2048]{1,0:T(8,128)S(1)}, f32[8,128]{1,0:T(8,128)S(1)}) custom-call(s32[5,768]{1,0:T(8,128)S(1)} %copy-done.2, f32[128,2048]{1,0:T(8,128)S(1)} %shard_map.150.before_ref.acc_ref, f32[128,128]{1,0:T(8,128)S(1)} %shard_map.151.before_ref.left_ref, bf16[128,768]{1,0:T(8,128)(2,1)S(1)} %collective-permute-done.9.refs_0_, ...), custom_call_target="tpu_custom_call" | custom-call | flops 1 | bytes 1 | tf_op jit(solution)/shard_map/pallas_call | solution.py:370
  53.9 0.1 collective-permute-start.14
  54.0 1.1 %shard_map.154 = (f32[128,2048]{1,0:T(8,128)S(1)}, f32[8,128]{1,0:T(8,128)S(1)}) custom-call(s32[5,768]{1,0:T(8,128)S(1)} %copy-done.2, f32[128,2048]{1,0:T(8,128)S(1)} %get-tuple-element.40.acc_ref, f32[128,128]{1,0:T(8,128)S(1)} %shard_map.153.before_ref.left_ref, bf16[128,768]{1,0:T(8,128)(2,1)S(1)} %collective-permute-done.12.refs_0_, ...), custom_call_target="tpu_custom_call" | custom-call | flops 1 | bytes 1 | tf_op jit(solution)/shard_map/pallas_call | solution.py:370
  55.2 2.0 %collective-permute-done.14.right_ref = f32[128,128]{1,0:T(8,128)S(1)} collective-permute-done((f32[128,128]{1,0:T(8,128)S(1)}, f32[128,128]{1,0:T(8,128)S(1)}, u32[]{:S(2)}, u32[]{:S(2)}) %collective-permute-start.14) | collective-permute-done | bytes 65568 | tf_op jit(solution)/shard_map/ppermute | solution.py:416
  57.1 0.1 collective-permute-start.16
  57.2 1.8 %shard_map.156 = (f32[2048,128]{1,0:T(8,128)}, f32[8,128]{1,0:T(8,128)S(1)}) custom-call(s32[5,768]{1,0:T(8,128)S(1)} %copy-done.2, f32[128,2048]{1,0:T(8,128)S(1)} %get-tuple-element.42.acc_ref, f32[128,128]{1,0:T(8,128)S(1)} %shard_map.155.before_ref.left_ref, bf16[128,768]{1,0:T(8,128)(2,1)S(1)} %collective-permute-done.15.refs_0_), custom_call_target="tpu_custom_call" | custom-call | flops 1 | bytes 1 | tf_op jit(solution)/shard_map/pallas_call | solution.py:370
  59.0 2.5 %collective-permute-done.16.right_ref = f32[128,128]{1,0:T(8,128)S(1)} collective-permute-done((f32[128,128]{1,0:T(8,128)S(1)}, f32[128,128]{1,0:T(8,128)S(1)}, u32[]{:S(2)}, u32[]{:S(2)}) %collective-permute-start.16) | collective-permute-done | bytes 65568 | tf_op jit(solution)/shard_map/ppermute | solution.py:416
  61.5 3.6 %collective-permute-start.17 = (f32[128,128]{1,0:T(8,128)S(1)}, f32[128,128]{1,0:T(8,128)S(1)}, u32[]{:S(2)}, u32[]{:S(2)}) collective-permute-start(f32[128,128]{1,0:T(8,128)S(1)} %shard_map.157.total_ref), channel_id=1, source_target_pairs={{0,1},{1,0},{2,3},{3,2},{4,5},{5,4},{6,7},{7,6},{8,9},{9,8},{10,11... | collective-permute-start | bytes 196616 | tf_op jit(solution)/shard_map/ppermute | solution.py:416
  65.2 0.9 %collective-permute-done.17.other_ref = f32[128,128]{1,0:T(8,128)S(1)} collective-permute-done((f32[128,128]{1,0:T(8,128)S(1)}, f32[128,128]{1,0:T(8,128)S(1)}, u32[]{:S(2)}, u32[]{:S(2)}) %collective-permute-start.17) | collective-permute-done | bytes 65568 | tf_op jit(solution)/shard_map/ppermute | solution.py:416
  66.1 0.7 shard_map.158
  (23 shorter events, 0.1 us)
Async XLA Ops:
  4.2 21.1 %collective-permute-start = (bf16[128,768]{1,0:T(8,128)(2,1)S(1)}, bf16[128,768]{1,0:T(8,128)(2,1)S(1)}, u32[]{:S(2)}, u32[]{:S(2)}) collective-permute-start(bf16[128,768]{1,0:T(8,128)(2,1)S(1)} %get-tuple-element.26), channel_id=1, source_target_pairs={{0,1},{1,0},{2,3},{3,2},{4,5},{5,4},{6,7},{7,6},{8,9},{9,8},{10,11... | collective-permute-start | bytes 589832 | tf_op jit(solution)/shard_map/ppermute | solution.py:416
  5.7 19.6 %collective-permute-start.1 = (bf16[128,768]{1,0:T(8,128)(2,1)S(1)}, bf16[128,768]{1,0:T(8,128)(2,1)S(1)}, u32[]{:S(2)}, u32[]{:S(2)}) collective-permute-start(bf16[128,768]{1,0:T(8,128)(2,1)S(1)} %get-tuple-element.27), channel_id=1, source_target_pairs={{0,2},{1,3},{2,0},{3,1},{4,6},{5,7},{6,4},{7,5},{8,10},{9,11},{10,... | collective-permute-start | bytes 589832 | tf_op jit(solution)/shard_map/ppermute | solution.py:416
  7.5 17.9 %collective-permute-start.2 = (bf16[128,768]{1,0:T(8,128)(2,1)S(1)}, bf16[128,768]{1,0:T(8,128)(2,1)S(1)}, u32[]{:S(2)}, u32[]{:S(2)}) collective-permute-start(bf16[128,768]{1,0:T(8,128)(2,1)S(1)} %get-tuple-element.28), channel_id=1, source_target_pairs={{0,4},{1,5},{2,6},{3,7},{4,0},{5,1},{6,2},{7,3},{8,12},{9,13},{10,... | collective-permute-start | bytes 589832 | tf_op jit(solution)/shard_map/ppermute | solution.py:416
  10.8 14.6 %collective-permute-start.3 = (bf16[128,768]{1,0:T(8,128)(2,1)S(1)}, bf16[128,768]{1,0:T(8,128)(2,1)S(1)}, u32[]{:S(2)}, u32[]{:S(2)}) collective-permute-start(bf16[128,768]{1,0:T(8,128)(2,1)S(1)} %get-tuple-element.29), channel_id=1, source_target_pairs={{0,8},{1,9},{2,10},{3,11},{4,12},{5,13},{6,14},{7,15},{8,0},{9,1},... | collective-permute-start | bytes 589832 | tf_op jit(solution)/shard_map/ppermute | solution.py:416
  12.0 11.0 %copy-start = (bf16[2048,128]{1,0:T(8,128)(2,1)S(1)}, bf16[2048,128]{1,0:T(8,128)(2,1)}, u32[]{:S(2)}) copy-start(bf16[2048,128]{1,0:T(8,128)(2,1)} %refs_8_.1) | copy-start | bytes 1572868
  12.0 13.4 %collective-permute-start.4 = (bf16[128,768]{1,0:T(8,128)(2,1)S(1)}, bf16[128,768]{1,0:T(8,128)(2,1)S(1)}, u32[]{:S(2)}, u32[]{:S(2)}) collective-permute-start(bf16[128,768]{1,0:T(8,128)(2,1)S(1)} %get-tuple-element.30), channel_id=1, source_target_pairs={{0,16},{1,17},{2,18},{3,19},{4,20},{5,21},{6,22},{7,23},{8,24},{9,... | collective-permute-start | bytes 589832 | tf_op jit(solution)/shard_map/ppermute | solution.py:416
  22.9 2.4 %copy-start.1 = (bf16[2048,128]{1,0:T(8,128)(2,1)S(1)}, bf16[2048,128]{1,0:T(8,128)(2,1)}, u32[]{:S(2)}) copy-start(bf16[2048,128]{1,0:T(8,128)(2,1)} %refs_9_.1) | copy-start | bytes 1572868
  22.9 2.4 %copy-start.3 = (bf16[128,128]{1,0:T(8,128)(2,1)S(1)}, bf16[128,128]{1,0:T(8,128)(2,1)}, u32[]{:S(2)}) copy-start(bf16[128,128]{1,0:T(8,128)(2,1)} %ws_ref.1) | copy-start | bytes 98308
  22.9 2.4 %copy-start.4 = (bf16[128,128]{1,0:T(8,128)(2,1)S(1)}, bf16[128,128]{1,0:T(8,128)(2,1)}, u32[]{:S(2)}) copy-start(bf16[128,128]{1,0:T(8,128)(2,1)} %refs_12_.1) | copy-start | bytes 98308
  22.9 2.4 %copy-start.5 = (s32[2048]{0:T(1024)S(1)}, s32[2048]{0:T(1024)}, u32[]{:S(2)}) copy-start(s32[2048]{0:T(1024)} %param.20) | copy-start | bytes 24580
  23.0 2.4 %copy-start.6 = (f32[128]{0:T(128)S(1)}, f32[128]{0:T(128)}, u32[]{:S(2)}) copy-start(f32[128]{0:T(128)} %param.14) | copy-start | bytes 1540
  31.6 2.1 %collective-permute-start.5 = (f32[128,128]{1,0:T(8,128)S(1)}, f32[128,128]{1,0:T(8,128)S(1)}, u32[]{:S(2)}, u32[]{:S(2)}) collective-permute-start(f32[128,128]{1,0:T(8,128)S(1)} %get-tuple-element.39), channel_id=1, source_target_pairs={{0,1},{1,0},{2,3},{3,2},{4,5},{5,4},{6,7},{7,6},{8,9},{9,8},{10,11... | collective-permute-start | bytes 196616 | tf_op jit(solution)/shard_map/ppermute | solution.py:416
  33.7 3.2 %collective-permute-start.6 = (f32[128,128]{1,0:T(8,128)S(1)}, f32[128,128]{1,0:T(8,128)S(1)}, u32[]{:S(2)}, u32[]{:S(2)}) collective-permute-start(f32[128,128]{1,0:T(8,128)S(1)} %shard_map.143.before_ref.left_ref), channel_id=1, source_target_pairs={{0,32},{1,33},{2,34},{3,35},{4,36},{5,37},{6,38},{7,39},{8,40},{9,... | collective-permute-start | bytes 196616 | tf_op jit(solution)/shard_map/ppermute | solution.py:416
  35.1 12.5 %collective-permute-start.9 = (bf16[128,768]{1,0:T(8,128)(2,1)S(1)}, bf16[128,768]{1,0:T(8,128)(2,1)S(1)}, u32[]{:S(2)}, u32[]{:S(2)}) collective-permute-start(bf16[128,768]{1,0:T(8,128)(2,1)S(1)} %shard_map.142.before_ref), channel_id=1, source_target_pairs={{0,4},{1,5},{2,6},{3,7},{4,0},{5,1},{6,2},{7,3},{8,12},{9,13},{10,... | collective-permute-start | bytes 589832 | tf_op jit(solution)/shard_map/ppermute | solution.py:416
  36.9 4.8 %collective-permute-start.7 = (f32[128,128]{1,0:T(8,128)S(1)}, f32[128,128]{1,0:T(8,128)S(1)}, u32[]{:S(2)}, u32[]{:S(2)}) collective-permute-start(f32[128,128]{1,0:T(8,128)S(1)} %shard_map.145.before_ref.left_ref), channel_id=1, source_target_pairs={{0,96},{1,97},{2,98},{3,99},{4,100},{5,101},{6,102},{7,103},{8,104... | collective-permute-start | bytes 196616 | tf_op jit(solution)/shard_map/ppermute | solution.py:416
  39.7 13.0 %collective-permute-start.10 = (bf16[128,768]{1,0:T(8,128)(2,1)S(1)}, bf16[128,768]{1,0:T(8,128)(2,1)S(1)}, u32[]{:S(2)}, u32[]{:S(2)}) collective-permute-start(bf16[128,768]{1,0:T(8,128)(2,1)S(1)} %shard_map.144.before_ref), channel_id=1, source_target_pairs={{0,16},{1,17},{2,18},{3,19},{4,20},{5,21},{6,22},{7,23},{8,24},{9,... | collective-permute-start | bytes 589832 | tf_op jit(solution)/shard_map/ppermute | solution.py:416
  41.7 3.8 %collective-permute-start.8 = (f32[128,128]{1,0:T(8,128)S(1)}, f32[128,128]{1,0:T(8,128)S(1)}, u32[]{:S(2)}, u32[]{:S(2)}) collective-permute-start(f32[128,128]{1,0:T(8,128)S(1)} %shard_map.148.before_ref.left_ref), channel_id=1, source_target_pairs={{0,8},{1,9},{2,10},{3,11},{4,12},{5,13},{6,14},{7,15},{8,0},{9,1},... | collective-permute-start | bytes 196616 | tf_op jit(solution)/shard_map/ppermute | solution.py:416
  41.8 12.2 %collective-permute-start.12 = (bf16[128,768]{1,0:T(8,128)(2,1)S(1)}, bf16[128,768]{1,0:T(8,128)(2,1)S(1)}, u32[]{:S(2)}, u32[]{:S(2)}) collective-permute-start(bf16[128,768]{1,0:T(8,128)(2,1)S(1)} %shard_map.147.before_ref), channel_id=1, source_target_pairs={{0,8},{1,9},{2,10},{3,11},{4,12},{5,13},{6,14},{7,15},{8,0},{9,1},... | collective-permute-start | bytes 589832 | tf_op jit(solution)/shard_map/ppermute | solution.py:416
  43.3 10.8 %collective-permute-start.13 = (bf16[128,768]{1,0:T(8,128)(2,1)S(1)}, bf16[128,768]{1,0:T(8,128)(2,1)S(1)}, u32[]{:S(2)}, u32[]{:S(2)}) collective-permute-start(bf16[128,768]{1,0:T(8,128)(2,1)S(1)} %shard_map.146.before_ref), channel_id=1, source_target_pairs={{0,2},{1,3},{2,0},{3,1},{4,6},{5,7},{6,4},{7,5},{8,10},{9,11},{10,... | collective-permute-start | bytes 589832 | tf_op jit(solution)/shard_map/ppermute | solution.py:416
  43.8 8.9 %copy-start.2 = (s32[5,768]{1,0:T(8,128)S(1)}, s32[5,768]{1,0:T(8,128)}, u32[]{:S(2)}) copy-start(s32[5,768]{1,0:T(8,128)} %rows_ref.5) | copy-start | bytes 46084
  45.5 8.3 %collective-permute-start.11 = (f32[128,128]{1,0:T(8,128)S(1)}, f32[128,128]{1,0:T(8,128)S(1)}, u32[]{:S(2)}, u32[]{:S(2)}) collective-permute-start(f32[128,128]{1,0:T(8,128)S(1)} %shard_map.151.before_ref.left_ref), channel_id=1, source_target_pairs={{0,24},{1,25},{2,26},{3,27},{4,28},{5,29},{6,30},{7,31},{8,16},{9,... | collective-permute-start | bytes 196616 | tf_op jit(solution)/shard_map/ppermute | solution.py:416
  47.6 9.6 %collective-permute-start.15 = (bf16[128,768]{1,0:T(8,128)(2,1)S(1)}, bf16[128,768]{1,0:T(8,128)(2,1)S(1)}, u32[]{:S(2)}, u32[]{:S(2)}) collective-permute-start(bf16[128,768]{1,0:T(8,128)(2,1)S(1)} %shard_map.149.before_ref), channel_id=1, source_target_pairs={{0,1},{1,0},{2,3},{3,2},{4,5},{5,4},{6,7},{7,6},{8,9},{9,8},{10,11... | collective-permute-start | bytes 589832 | tf_op jit(solution)/shard_map/ppermute | solution.py:416
  53.9 3.2 %collective-permute-start.14 = (f32[128,128]{1,0:T(8,128)S(1)}, f32[128,128]{1,0:T(8,128)S(1)}, u32[]{:S(2)}, u32[]{:S(2)}) collective-permute-start(f32[128,128]{1,0:T(8,128)S(1)} %shard_map.153.before_ref.left_ref), channel_id=1, source_target_pairs={{0,2},{1,3},{2,0},{3,1},{4,6},{5,7},{6,4},{7,5},{8,10},{9,11},{10,... | collective-permute-start | bytes 196616 | tf_op jit(solution)/shard_map/ppermute | solution.py:416
  57.1 4.4 %collective-permute-start.16 = (f32[128,128]{1,0:T(8,128)S(1)}, f32[128,128]{1,0:T(8,128)S(1)}, u32[]{:S(2)}, u32[]{:S(2)}) collective-permute-start(f32[128,128]{1,0:T(8,128)S(1)} %shard_map.155.before_ref.left_ref), channel_id=1, source_target_pairs={{0,6},{1,7},{2,4},{3,5},{4,2},{5,3},{6,0},{7,1},{8,14},{9,15},{10,... | collective-permute-start | bytes 196616 | tf_op jit(solution)/shard_map/ppermute | solution.py:416
  61.5 4.5 %collective-permute-start.17 = (f32[128,128]{1,0:T(8,128)S(1)}, f32[128,128]{1,0:T(8,128)S(1)}, u32[]{:S(2)}, u32[]{:S(2)}) collective-permute-start(f32[128,128]{1,0:T(8,128)S(1)} %shard_map.157.total_ref), channel_id=1, source_target_pairs={{0,1},{1,0},{2,3},{3,2},{4,5},{5,4},{6,7},{7,6},{8,9},{9,8},{10,11... | collective-permute-start | bytes 196616 | tf_op jit(solution)/shard_map/ppermute | solution.py:416

commit v8 on v7

--- a/solution.py
+++ b/solution.py
@@ -212,8 +212,7 @@
 def middle_kernel(rounds, *refs):
     got, refs = refs[:rounds], refs[rounds:]
     d0, d1, sum_ref, x_ref, ct_ref, deg_ref, ws_ref, wn_ref, bias_ref = refs[:9]
-    out_ref, gp_ref, st_ref, mine_ref, give_ref, both, halo, sums = refs[9:]
-    core = lax.axis_index("dom") & 1
+    out_ref, gp_ref, st_ref, parts_ref, both, halo, sums = refs[9:]
     half, step = d0.shape[1], 512
     boundary = got[0].shape[1]
     per = boundary // TILE
@@ -247,29 +246,25 @@
             grad = grad.astype(jnp.bfloat16)
             gp_ref[rows, :] = grad
             st_ref[:, rows] = (nt_dot(wn_ref[...], grad) / line).astype(jnp.bfloat16)
-    parts = lax.dot_general(
+    parts_ref[...] = lax.dot_general(
         both[...], gp_ref[...], (((0,), (0,)), ((), ())), preferred_element_type=jnp.float32
     )
-    mine_ref[...] = jnp.where(core == 0, parts[:TILE], parts[TILE:])
-    give_ref[...] = jnp.where(core == 0, parts[TILE:], parts[:TILE])
 
 
 def middle(received, d0, d1, summed, features, cotangent, degree, w_self, w_neigh, bias):
     rows, width = features.shape
     rounds, boundary = len(received), received[0].shape[1]
     half = jax.ShapeDtypeStruct((rows, width), jnp.bfloat16)
-    part = VMEM((width, width), jnp.float32)
     return pl.pallas_call(
         functools.partial(middle_kernel, rounds),
         out_shape=[
             half,
             VMEM((rows, width), jnp.bfloat16),
             VMEM((width, rows), jnp.bfloat16),
-            part,
-            part,
+            VMEM((2 * width, width), jnp.float32),
         ],
         in_specs=[vspec()] * (rounds + 9),
-        out_specs=[vspec()] * 5,
+        out_specs=[vspec()] * 4,
         scratch_shapes=[
             VMEM((rows, 2 * width), jnp.bfloat16),
             VMEM((rounds * boundary, width), jnp.bfloat16),
@@ -393,27 +388,34 @@
     )(pinned(left), right, before)
 
 
-def halves_kernel(scale, total_ref, other_ref, self_ref, neigh_ref):
+def split_kernel(scale, total_ref, other_ref, self_ref, neigh_ref):
     core = lax.axis_index("dom") & 1
-    total, other = total_ref[...], other_ref[...]
-    self_ref[...] = jnp.where(core == 0, total, other) * scale
-    neigh_ref[...] = jnp.where(core == 0, other, total) * scale
-
-
-def halves(scale, total, other):
-    out = jax.ShapeDtypeStruct(total.shape, jnp.float32)
-    return pl.pallas_call(
-        functools.partial(halves_kernel, scale),
+    width = self_ref.shape[0]
+    total = jnp.where(core == 1, total_ref[...], other_ref[...]) * scale
+    self_ref[...] = total[:width]
+    neigh_ref[...] = total[width:]
+
+
+def split(scale, total, other):
+    rows, width = total.shape
+    out = jax.ShapeDtypeStruct((rows // 2, width), jnp.float32)
+    return pl.pallas_call(
+        functools.partial(split_kernel, scale),
         out_shape=[out, out],
         in_specs=[vspec()] * 2,
         out_specs=[vspec()] * 2,
         compiler_params=params(1024 * 1024),
-        cost_estimate=cost(2 * total.size, 4 * total.size * 4),
+        cost_estimate=cost(1, 1),
     )(pinned(total), other)
 
 
 def swapped(shard, mask):
     return lax.ppermute(shard, "dom", [(i, i ^ mask) for i in range(lax.axis_size("dom"))])
+
+
+def swapped_from(core, shard, mask):
+    senders = range(core, lax.axis_size("dom"), 2)
+    return lax.ppermute(shard, "dom", [(i, i ^ mask) for i in senders])
 
 
 def local(
@@ -439,7 +441,7 @@
         local_cols, halo_cols, local_tiles, halo_tiles, round_count * per
     )
     summed = local_sums(dl0, dl1, node_features)
-    output, grad_pre, scaled_t, mine, give = middle(
+    output, grad_pre, scaled_t, parts = middle(
         received,
         dh0,
         dh1,
@@ -462,32 +464,32 @@
         got = [returned[r] for r in rounds]
         return place_rows(rounds, 0 in rounds, send_rows, acc, got, before)
 
-    other = swapped(give, 1)
+    other = swapped_from(0, parts, 1)
     last = send_back(2, scaled_t)
-    total = added(mine, other, last)
-    other = swapped(total, 32)
+    total = added(parts, other, last)
+    other = swapped_from(1, total, 32)
     last = send_back(4, total)
     total = added(total, other, last)
-    other = swapped(total, 96)
+    other = swapped_from(1, total, 96)
     last = send_back(1, total)
     last = send_back(3, last)
     total = added(total, other, last)
-    other = swapped(total, 8)
+    other = swapped_from(1, total, 8)
     last = send_back(0, total)
     grads_t = own(scaled_t, dl0, dl1, grad_pre, w_self, last)
     total = added(total, other, grads_t)
-    other = swapped(total, 24)
+    other = swapped_from(1, total, 24)
     grads_t, last = place((2, 4), grads_t, total)
     total = added(total, other, last)
-    other = swapped(total, 2)
+    other = swapped_from(1, total, 2)
     grads_t, last = place((3, 1), grads_t, total)
     total = added(total, other, last)
-    other = swapped(total, 6)
+    other = swapped_from(1, total, 6)
     grads, last = place((0,), grads_t, total)
     total = added(total, other, last)
-    other = swapped(total, 1)
+    other = swapped_from(1, total, 1)
     grad_scale = 1.0 / math.sqrt(row_count * lax.axis_size("dom"))
-    grad_self, grad_neigh = halves(grad_scale, total, other)
+    grad_self, grad_neigh = split(grad_scale, total, other)
     return (output, grads, grad_self, grad_neigh)
 
 

time: 66.9 us -> 76.3 us (1.14)
  starting transfers between devices: 28.7 us -> 34.9 us
  waiting for transfers between devices: 7.42 us -> 10.3 us
    ppermute x0 -> x8, starting transfers between devices: none -> 22.7 us  [swapped_from(): return lax.ppermute(shard, 'dom', [(i, i ^ mask) for i in senders])]
    ppermute x18 -> x10, starting transfers between devices: 28.7 us -> 12.1 us  [swapped(): lax.ppermute(shard, 'dom', [(i, i ^ mask) for i in range(lax.axis_size('d...]
    ppermute x0 -> x8, waiting for transfers between devices: none -> 10.2 us  [swapped_from(): return lax.ppermute(shard, 'dom', [(i, i ^ mask) for i in senders])]
    ppermute x18 -> x10, waiting for transfers between devices: 7.42 us -> 0.03 us  [swapped(): lax.ppermute(shard, 'dom', [(i, i ^ mask) for i in range(lax.axis_size('d...]
  transfers between devices with their start and end apart: 18 -> 18, of which waited for: 7 -> 8; matrix products, arithmetic and copies ran while one was open for 0% -> 0% of each run, Pallas kernels for 29% -> 25%
where the time goes in v8:
time: 76.3 us; the launch traced here: 76 us
  starting transfers between devices  34.9 us (46%)
  Pallas kernels  29.8 us (39%)
  waiting for transfers between devices  10.3 us (13%)
  between operations  1.01 us (1%)
    ppermute x8, starting transfers between devices, swapped_from(): return lax.ppermute(shard, 'dom', [(i, i ^ mask) for i in senders])  22.7 us
    ppermute x10, starting transfers between devices, swapped(): lax.ppermute(shard, 'dom', [(i, i ^ mask) for i in range(lax.axis_size('d...  12.1 us
    ppermute x8, waiting for transfers between devices, swapped_from(): return lax.ppermute(shard, 'dom', [(i, i ^ mask) for i in senders])  10.2 us
    pallas_call x1, Pallas kernels, densify(): pl.pallas_call(densify_kernel, out_shape=[VMEM((n, half, TILE), jnp.bfloa...  8.48 us
    pallas_call x1, Pallas kernels, middle(): pl.pallas_call(functools.partial(middle_kernel, rounds), out_shape=[half,...  6.21 us
    pallas_call x3, Pallas kernels, place_rows(): pl.pallas_call(functools.partial(place_kernel, rounds, last), out_shape=[...  4.04 us
    pallas_call x1, Pallas kernels, pick_rows(): pl.pallas_call(pick_kernel, out_shape=outs, in_specs=[pl.BlockSpec(memory...  3.58 us
    pallas_call x5, Pallas kernels, back(): pl.pallas_call(functools.partial(back_kernel, first, n), out_shape=jax.Sh...  2.92 us
  transfers between devices with their start and end apart: 18, of which 8 were waited for; matrix products, arithmetic and copies ran while one was open for 0% of the time, Pallas kernels for 25%

profile of v8, /device:TPU:1, one launch (start us, length us, event | category | flops | bytes accessed | tf_op | source)
XLA Modules:
  0.0 76.0 jit_solution(1366640923165034319)
XLA Ops:
  0.6 3.6 %shard_map.138 = (bf16[128,768]{1,0:T(8,128)(2,1)S(1)}, bf16[128,768]{1,0:T(8,128)(2,1)S(1)}, bf16[128,768]{1,0:T(8,128)(2,1)S(1)}, bf16[128,768]{1,0:T(8,128)(2,1)S(1)}, bf16[128,768]{1,0:T(8,128)(2,1)S(1)}) custom-call(s32[5,768]{1,0:T(8,128)} %rows_ref.5, bf16[2048,128]{1,0:T(8,128)(2,1)} %refs_8_.1), custom_call_target="tpu_custom_call" | custom-call | flops 2013265920 | bytes 1000000 | tf_op jit(solution)/shard_map/pallas_call | solution.py:75
  4.2 1.5 %collective-permute-start = (bf16[128,768]{1,0:T(8,128)(2,1)S(1)}, bf16[128,768]{1,0:T(8,128)(2,1)S(1)}, u32[]{:S(2)}, u32[]{:S(2)}) collective-permute-start(bf16[128,768]{1,0:T(8,128)(2,1)S(1)} %get-tuple-element.25), channel_id=1, source_target_pairs={{0,1},{1,0},{2,3},{3,2},{4,5},{5,4},{6,7},{7,6},{8,9},{9,8},{10,11... | collective-permute-start | bytes 589832 | tf_op jit(solution)/shard_map/ppermute | solution.py:413
  5.7 1.7 %collective-permute-start.1 = (bf16[128,768]{1,0:T(8,128)(2,1)S(1)}, bf16[128,768]{1,0:T(8,128)(2,1)S(1)}, u32[]{:S(2)}, u32[]{:S(2)}) collective-permute-start(bf16[128,768]{1,0:T(8,128)(2,1)S(1)} %get-tuple-element.26), channel_id=1, source_target_pairs={{0,2},{1,3},{2,0},{3,1},{4,6},{5,7},{6,4},{7,5},{8,10},{9,11},{10,... | collective-permute-start | bytes 589832 | tf_op jit(solution)/shard_map/ppermute | solution.py:413
  7.5 3.3 %collective-permute-start.2 = (bf16[128,768]{1,0:T(8,128)(2,1)S(1)}, bf16[128,768]{1,0:T(8,128)(2,1)S(1)}, u32[]{:S(2)}, u32[]{:S(2)}) collective-permute-start(bf16[128,768]{1,0:T(8,128)(2,1)S(1)} %get-tuple-element.27), channel_id=1, source_target_pairs={{0,4},{1,5},{2,6},{3,7},{4,0},{5,1},{6,2},{7,3},{8,12},{9,13},{10,... | collective-permute-start | bytes 589832 | tf_op jit(solution)/shard_map/ppermute | solution.py:413
  10.8 1.2 %collective-permute-start.3 = (bf16[128,768]{1,0:T(8,128)(2,1)S(1)}, bf16[128,768]{1,0:T(8,128)(2,1)S(1)}, u32[]{:S(2)}, u32[]{:S(2)}) collective-permute-start(bf16[128,768]{1,0:T(8,128)(2,1)S(1)} %get-tuple-element.28), channel_id=1, source_target_pairs={{0,8},{1,9},{2,10},{3,11},{4,12},{5,13},{6,14},{7,15},{8,0},{9,1},... | collective-permute-start | bytes 589832 | tf_op jit(solution)/shard_map/ppermute | solution.py:413
  12.0 2.5 %collective-permute-start.4 = (bf16[128,768]{1,0:T(8,128)(2,1)S(1)}, bf16[128,768]{1,0:T(8,128)(2,1)S(1)}, u32[]{:S(2)}, u32[]{:S(2)}) collective-permute-start(bf16[128,768]{1,0:T(8,128)(2,1)S(1)} %get-tuple-element.29), channel_id=1, source_target_pairs={{0,16},{1,17},{2,18},{3,19},{4,20},{5,21},{6,22},{7,23},{8,24},{9,... | collective-permute-start | bytes 589832 | tf_op jit(solution)/shard_map/ppermute | solution.py:413
  14.4 8.5 %shard_map.139 = (bf16[16,1024,128]{2,1,0:T(8,128)(2,1)S(1)}, bf16[16,1024,128]{2,1,0:T(8,128)(2,1)S(1)}, bf16[30,1024,128]{2,1,0:T(8,128)(2,1)S(1)}, bf16[30,1024,128]{2,1,0:T(8,128)(2,1)S(1)}) custom-call(s32[16,22]{1,0:T(8,128)} %lc_hbm.1, s32[16,20]{1,0:T(8,128)} %hc_hbm.1, bf16[16,22,128,128]{3,2,1,0:T(8,128)(2,1)} %lt.1, bf16[16,20,128,128]{3,2,1,0:T(8,128)(2,1)} %ht.1), custom_call_target="tpu_custom_call" | custom-call | flops 16000000 | bytes 22020096 | tf_op jit(solution)/shard_map/pallas_call | solution.py:170
  22.9 0.0 copy-start.1
  22.9 0.0 copy-start.3
  22.9 0.0 copy-start.4
  22.9 0.0 copy-start.5
  23.0 0.0 copy-start.6
  23.0 2.3 %shard_map.140.refs_7_ = f32[2048,128]{1,0:T(8,128)S(1)} custom-call(bf16[16,1024,128]{2,1,0:T(8,128)(2,1)S(1)} %get-tuple-element.32.d0_ref, bf16[16,1024,128]{2,1,0:T(8,128)(2,1)S(1)} %get-tuple-element.33.d1_ref, bf16[2048,128]{1,0:T(8,128)(2,1)S(1)} %copy-done), custom_call_target="tpu_custom_call" | custom-call | flops 1073741824 | bytes 1500000 | tf_op jit(solution)/shard_map/pallas_call | solution.py:202
  25.3 0.0 collective-permute-done.refs_0_
  25.3 0.0 collective-permute-done.1.refs_1_
  25.4 6.2 %shard_map.141 = (bf16[2048,128]{1,0:T(8,128)(2,1)}, bf16[2048,128]{1,0:T(8,128)(2,1)S(1)}, bf16[128,2048]{1,0:T(8,128)(2,1)S(1)}, f32[256,128]{1,0:T(8,128)S(1)}) custom-call(bf16[128,768]{1,0:T(8,128)(2,1)S(1)} %collective-permute-done.refs_0_, bf16[128,768]{1,0:T(8,128)(2,1)S(1)} %collective-permute-done.1.refs_1_, ...), custom_call_target="tpu_custom_call" | custom-call | flops 2013265920 | bytes 5000000 | tf_op jit(solution)/shard_map/pallas_call | solution.py:258
  31.6 1.3 %collective-permute-start.5 = (f32[256,128]{1,0:T(8,128)S(1)}, f32[256,128]{1,0:T(8,128)S(1)}, u32[]{:S(2)}, u32[]{:S(2)}) collective-permute-start(f32[256,128]{1,0:T(8,128)S(1)} %get-tuple-element.37.left_ref), channel_id=1, source_target_pairs={{0,1},{2,3},{4,5},{6,7},{8,9},{10,11},{12,13},{14,15},{16,17},{18,... | collective-permute-start | bytes 393224 | tf_op jit(solution)/shard_map/ppermute | solution.py:418
  32.9 0.6 shard_map.142.before_ref
  33.5 1.4 %collective-permute-done.5.right_ref = f32[256,128]{1,0:T(8,128)S(1)} collective-permute-done((f32[256,128]{1,0:T(8,128)S(1)}, f32[256,128]{1,0:T(8,128)S(1)}, u32[]{:S(2)}, u32[]{:S(2)}) %collective-permute-start.5) | collective-permute-done | bytes 131104 | tf_op jit(solution)/shard_map/ppermute | solution.py:418
  34.9 3.2 %collective-permute-start.6 = (f32[256,128]{1,0:T(8,128)S(1)}, f32[256,128]{1,0:T(8,128)S(1)}, u32[]{:S(2)}, u32[]{:S(2)}) collective-permute-start(f32[256,128]{1,0:T(8,128)S(1)} %shard_map.143.before_ref.left_ref), channel_id=1, source_target_pairs={{1,33},{3,35},{5,37},{7,39},{9,41},{11,43},{13,45},{15,47},{17,49}... | collective-permute-start | bytes 393224 | tf_op jit(solution)/shard_map/ppermute | solution.py:418
  38.1 0.6 shard_map.144.before_ref
  38.7 1.9 %collective-permute-done.6.right_ref = f32[256,128]{1,0:T(8,128)S(1)} collective-permute-done((f32[256,128]{1,0:T(8,128)S(1)}, f32[256,128]{1,0:T(8,128)S(1)}, u32[]{:S(2)}, u32[]{:S(2)}) %collective-permute-start.6) | collective-permute-done | bytes 131104 | tf_op jit(solution)/shard_map/ppermute | solution.py:418
  40.7 4.8 %collective-permute-start.7 = (f32[256,128]{1,0:T(8,128)S(1)}, f32[256,128]{1,0:T(8,128)S(1)}, u32[]{:S(2)}, u32[]{:S(2)}) collective-permute-start(f32[256,128]{1,0:T(8,128)S(1)} %shard_map.145.before_ref.left_ref), channel_id=1, source_target_pairs={{1,97},{3,99},{5,101},{7,103},{9,105},{11,107},{13,109},{15,111},{... | collective-permute-start | bytes 393224 | tf_op jit(solution)/shard_map/ppermute | solution.py:418
  45.5 0.6 shard_map.146.before_ref
  46.1 0.6 shard_map.147.before_ref
  46.7 1.0 %collective-permute-done.7.right_ref = f32[256,128]{1,0:T(8,128)S(1)} collective-permute-done((f32[256,128]{1,0:T(8,128)S(1)}, f32[256,128]{1,0:T(8,128)S(1)}, u32[]{:S(2)}, u32[]{:S(2)}) %collective-permute-start.7) | collective-permute-done | bytes 131104 | tf_op jit(solution)/shard_map/ppermute | solution.py:418
  47.7 1.9 %collective-permute-start.8 = (f32[256,128]{1,0:T(8,128)S(1)}, f32[256,128]{1,0:T(8,128)S(1)}, u32[]{:S(2)}, u32[]{:S(2)}) collective-permute-start(f32[256,128]{1,0:T(8,128)S(1)} %shard_map.148.before_ref.left_ref), channel_id=1, source_target_pairs={{1,9},{3,11},{5,13},{7,15},{9,1},{11,3},{13,5},{15,7},{17,25},{19,... | collective-permute-start | bytes 393224 | tf_op jit(solution)/shard_map/ppermute | solution.py:418
  49.6 0.3 collective-permute-start.9
  49.9 1.4 %collective-permute-start.10 = (bf16[128,768]{1,0:T(8,128)(2,1)S(1)}, bf16[128,768]{1,0:T(8,128)(2,1)S(1)}, u32[]{:S(2)}, u32[]{:S(2)}) collective-permute-start(bf16[128,768]{1,0:T(8,128)(2,1)S(1)} %shard_map.144.before_ref), channel_id=1, source_target_pairs={{0,16},{1,17},{2,18},{3,19},{4,20},{5,21},{6,22},{7,23},{8,24},{9,... | collective-permute-start | bytes 589832 | tf_op jit(solution)/shard_map/ppermute | solution.py:413
  51.3 0.6 shard_map.149.before_ref
  51.9 0.0 copy-start.2
  51.9 1.4 %shard_map.150.before_ref.acc_ref = f32[128,2048]{1,0:T(8,128)S(1)} custom-call(bf16[128,2048]{1,0:T(8,128)(2,1)S(1)} %get-tuple-element.35.st_ref.before_ref, bf16[16,1024,128]{2,1,0:T(8,128)(2,1)S(1)} %get-tuple-element.32.d0_ref, bf16[16,1024,128]{2,1,0:T(8,128)(2,1)S(1)} %get-tuple-element.33.d1_ref, bf16[2048,128]{1,0:T(8,128)(2,1)S(1)} %get-tuple-element.36.gp_ref, ...), custom_call_target="tpu_custom_call" | custom-call | flops 1 | bytes 1 | tf_op jit(solution)/shard_map/pallas_call | solution.py:322
  53.3 0.1 collective-permute-done.8.right_ref
  53.4 4.3 %collective-permute-start.11 = (f32[256,128]{1,0:T(8,128)S(1)}, f32[256,128]{1,0:T(8,128)S(1)}, u32[]{:S(2)}, u32[]{:S(2)}) collective-permute-start(f32[256,128]{1,0:T(8,128)S(1)} %shard_map.151.before_ref.left_ref), channel_id=1, source_target_pairs={{1,25},{3,27},{5,29},{7,31},{9,17},{11,19},{13,21},{15,23},{17,9},... | collective-permute-start | bytes 393224 | tf_op jit(solution)/shard_map/ppermute | solution.py:418
  57.8 0.1 collective-permute-start.12
  57.9 0.1 collective-permute-start.13
  58.0 1.1 %shard_map.152 = (f32[128,2048]{1,0:T(8,128)S(1)}, f32[8,128]{1,0:T(8,128)S(1)}) custom-call(s32[5,768]{1,0:T(8,128)S(1)} %copy-done.2, f32[128,2048]{1,0:T(8,128)S(1)} %shard_map.150.before_ref.acc_ref, f32[256,128]{1,0:T(8,128)S(1)} %shard_map.151.before_ref.left_ref, bf16[128,768]{1,0:T(8,128)(2,1)S(1)} %collective-permute-done.9.refs_0_, ...), custom_call_target="tpu_custom_call" | custom-call | flops 1 | bytes 1 | tf_op jit(solution)/shard_map/pallas_call | solution.py:365
  59.1 1.2 %collective-permute-done.11.right_ref = f32[256,128]{1,0:T(8,128)S(1)} collective-permute-done((f32[256,128]{1,0:T(8,128)S(1)}, f32[256,128]{1,0:T(8,128)S(1)}, u32[]{:S(2)}, u32[]{:S(2)}) %collective-permute-start.11) | collective-permute-done | bytes 131104 | tf_op jit(solution)/shard_map/ppermute | solution.py:418
  60.3 2.1 %collective-permute-start.14 = (f32[256,128]{1,0:T(8,128)S(1)}, f32[256,128]{1,0:T(8,128)S(1)}, u32[]{:S(2)}, u32[]{:S(2)}) collective-permute-start(f32[256,128]{1,0:T(8,128)S(1)} %shard_map.153.before_ref.left_ref), channel_id=1, source_target_pairs={{1,3},{3,1},{5,7},{7,5},{9,11},{11,9},{13,15},{15,13},{17,19},{19,... | collective-permute-start | bytes 393224 | tf_op jit(solution)/shard_map/ppermute | solution.py:418
  62.5 0.1 collective-permute-start.15
  62.6 1.1 %shard_map.154 = (f32[128,2048]{1,0:T(8,128)S(1)}, f32[8,128]{1,0:T(8,128)S(1)}) custom-call(s32[5,768]{1,0:T(8,128)S(1)} %copy-done.2, f32[128,2048]{1,0:T(8,128)S(1)} %get-tuple-element.38.acc_ref, f32[256,128]{1,0:T(8,128)S(1)} %shard_map.153.before_ref.left_ref, bf16[128,768]{1,0:T(8,128)(2,1)S(1)} %collective-permute-done.12.refs_0_, ...), custom_call_target="tpu_custom_call" | custom-call | flops 1 | bytes 1 | tf_op jit(solution)/shard_map/pallas_call | solution.py:365
  63.8 2.3 %collective-permute-done.14.right_ref = f32[256,128]{1,0:T(8,128)S(1)} collective-permute-done((f32[256,128]{1,0:T(8,128)S(1)}, f32[256,128]{1,0:T(8,128)S(1)}, u32[]{:S(2)}, u32[]{:S(2)}) %collective-permute-start.14) | collective-permute-done | bytes 131104 | tf_op jit(solution)/shard_map/ppermute | solution.py:418
  66.1 3.7 %collective-permute-start.16 = (f32[256,128]{1,0:T(8,128)S(1)}, f32[256,128]{1,0:T(8,128)S(1)}, u32[]{:S(2)}, u32[]{:S(2)}) collective-permute-start(f32[256,128]{1,0:T(8,128)S(1)} %shard_map.155.before_ref.left_ref), channel_id=1, source_target_pairs={{1,7},{3,5},{5,3},{7,1},{9,15},{11,13},{13,11},{15,9},{17,23},{19,... | collective-permute-start | bytes 393224 | tf_op jit(solution)/shard_map/ppermute | solution.py:418
  69.8 1.8 %shard_map.156 = (f32[2048,128]{1,0:T(8,128)}, f32[8,128]{1,0:T(8,128)S(1)}) custom-call(s32[5,768]{1,0:T(8,128)S(1)} %copy-done.2, f32[128,2048]{1,0:T(8,128)S(1)} %get-tuple-element.40.acc_ref, f32[256,128]{1,0:T(8,128)S(1)} %shard_map.155.before_ref.left_ref, bf16[128,768]{1,0:T(8,128)(2,1)S(1)} %collective-permute-done.15.refs_0_), custom_call_target="tpu_custom_call" | custom-call | flops 1 | bytes 1 | tf_op jit(solution)/shard_map/pallas_call | solution.py:365
  71.6 1.4 %collective-permute-done.16.right_ref = f32[256,128]{1,0:T(8,128)S(1)} collective-permute-done((f32[256,128]{1,0:T(8,128)S(1)}, f32[256,128]{1,0:T(8,128)S(1)}, u32[]{:S(2)}, u32[]{:S(2)}) %collective-permute-start.16) | collective-permute-done | bytes 131104 | tf_op jit(solution)/shard_map/ppermute | solution.py:418
  73.0 1.3 %collective-permute-start.17 = (f32[256,128]{1,0:T(8,128)S(1)}, f32[256,128]{1,0:T(8,128)S(1)}, u32[]{:S(2)}, u32[]{:S(2)}) collective-permute-start(f32[256,128]{1,0:T(8,128)S(1)} %shard_map.157.total_ref), channel_id=1, source_target_pairs={{1,0},{3,2},{5,4},{7,6},{9,8},{11,10},{13,12},{15,14},{17,16},{19,... | collective-permute-start | bytes 393224 | tf_op jit(solution)/shard_map/ppermute | solution.py:418
  74.3 1.0 %collective-permute-done.17.other_ref = f32[256,128]{1,0:T(8,128)S(1)} collective-permute-done((f32[256,128]{1,0:T(8,128)S(1)}, f32[256,128]{1,0:T(8,128)S(1)}, u32[]{:S(2)}, u32[]{:S(2)}) %collective-permute-start.17) | collective-permute-done | bytes 131104 | tf_op jit(solution)/shard_map/ppermute | solution.py:418
  75.3 0.7 shard_map.158
  (23 shorter events, 0.2 us)
Async XLA Ops:
  4.2 21.1 %collective-permute-start = (bf16[128,768]{1,0:T(8,128)(2,1)S(1)}, bf16[128,768]{1,0:T(8,128)(2,1)S(1)}, u32[]{:S(2)}, u32[]{:S(2)}) collective-permute-start(bf16[128,768]{1,0:T(8,128)(2,1)S(1)} %get-tuple-element.25), channel_id=1, source_target_pairs={{0,1},{1,0},{2,3},{3,2},{4,5},{5,4},{6,7},{7,6},{8,9},{9,8},{10,11... | collective-permute-start | bytes 589832 | tf_op jit(solution)/shard_map/ppermute | solution.py:413
  5.7 19.6 %collective-permute-start.1 = (bf16[128,768]{1,0:T(8,128)(2,1)S(1)}, bf16[128,768]{1,0:T(8,128)(2,1)S(1)}, u32[]{:S(2)}, u32[]{:S(2)}) collective-permute-start(bf16[128,768]{1,0:T(8,128)(2,1)S(1)} %get-tuple-element.26), channel_id=1, source_target_pairs={{0,2},{1,3},{2,0},{3,1},{4,6},{5,7},{6,4},{7,5},{8,10},{9,11},{10,... | collective-permute-start | bytes 589832 | tf_op jit(solution)/shard_map/ppermute | solution.py:413
  7.5 17.9 %collective-permute-start.2 = (bf16[128,768]{1,0:T(8,128)(2,1)S(1)}, bf16[128,768]{1,0:T(8,128)(2,1)S(1)}, u32[]{:S(2)}, u32[]{:S(2)}) collective-permute-start(bf16[128,768]{1,0:T(8,128)(2,1)S(1)} %get-tuple-element.27), channel_id=1, source_target_pairs={{0,4},{1,5},{2,6},{3,7},{4,0},{5,1},{6,2},{7,3},{8,12},{9,13},{10,... | collective-permute-start | bytes 589832 | tf_op jit(solution)/shard_map/ppermute | solution.py:413
  10.8 14.6 %collective-permute-start.3 = (bf16[128,768]{1,0:T(8,128)(2,1)S(1)}, bf16[128,768]{1,0:T(8,128)(2,1)S(1)}, u32[]{:S(2)}, u32[]{:S(2)}) collective-permute-start(bf16[128,768]{1,0:T(8,128)(2,1)S(1)} %get-tuple-element.28), channel_id=1, source_target_pairs={{0,8},{1,9},{2,10},{3,11},{4,12},{5,13},{6,14},{7,15},{8,0},{9,1},... | collective-permute-start | bytes 589832 | tf_op jit(solution)/shard_map/ppermute | solution.py:413
  12.0 11.0 %copy-start = (bf16[2048,128]{1,0:T(8,128)(2,1)S(1)}, bf16[2048,128]{1,0:T(8,128)(2,1)}, u32[]{:S(2)}) copy-start(bf16[2048,128]{1,0:T(8,128)(2,1)} %refs_8_.1) | copy-start | bytes 1572868
  12.0 13.4 %collective-permute-start.4 = (bf16[128,768]{1,0:T(8,128)(2,1)S(1)}, bf16[128,768]{1,0:T(8,128)(2,1)S(1)}, u32[]{:S(2)}, u32[]{:S(2)}) collective-permute-start(bf16[128,768]{1,0:T(8,128)(2,1)S(1)} %get-tuple-element.29), channel_id=1, source_target_pairs={{0,16},{1,17},{2,18},{3,19},{4,20},{5,21},{6,22},{7,23},{8,24},{9,... | collective-permute-start | bytes 589832 | tf_op jit(solution)/shard_map/ppermute | solution.py:413
  22.9 2.4 %copy-start.1 = (bf16[2048,128]{1,0:T(8,128)(2,1)S(1)}, bf16[2048,128]{1,0:T(8,128)(2,1)}, u32[]{:S(2)}) copy-start(bf16[2048,128]{1,0:T(8,128)(2,1)} %refs_9_.1) | copy-start | bytes 1572868
  22.9 2.4 %copy-start.3 = (bf16[128,128]{1,0:T(8,128)(2,1)S(1)}, bf16[128,128]{1,0:T(8,128)(2,1)}, u32[]{:S(2)}) copy-start(bf16[128,128]{1,0:T(8,128)(2,1)} %ws_ref.1) | copy-start | bytes 98308
  22.9 2.4 %copy-start.4 = (bf16[128,128]{1,0:T(8,128)(2,1)S(1)}, bf16[128,128]{1,0:T(8,128)(2,1)}, u32[]{:S(2)}) copy-start(bf16[128,128]{1,0:T(8,128)(2,1)} %refs_12_.1) | copy-start | bytes 98308
  22.9 2.4 %copy-start.5 = (s32[2048]{0:T(1024)S(1)}, s32[2048]{0:T(1024)}, u32[]{:S(2)}) copy-start(s32[2048]{0:T(1024)} %param.20) | copy-start | bytes 24580
  23.0 2.4 %copy-start.6 = (f32[128]{0:T(128)S(1)}, f32[128]{0:T(128)}, u32[]{:S(2)}) copy-start(f32[128]{0:T(128)} %param.14) | copy-start | bytes 1540
  31.6 3.3 %collective-permute-start.5 = (f32[256,128]{1,0:T(8,128)S(1)}, f32[256,128]{1,0:T(8,128)S(1)}, u32[]{:S(2)}, u32[]{:S(2)}) collective-permute-start(f32[256,128]{1,0:T(8,128)S(1)} %get-tuple-element.37.left_ref), channel_id=1, source_target_pairs={{0,1},{2,3},{4,5},{6,7},{8,9},{10,11},{12,13},{14,15},{16,17},{18,... | collective-permute-start | bytes 393224 | tf_op jit(solution)/shard_map/ppermute | solution.py:418
  34.9 5.7 %collective-permute-start.6 = (f32[256,128]{1,0:T(8,128)S(1)}, f32[256,128]{1,0:T(8,128)S(1)}, u32[]{:S(2)}, u32[]{:S(2)}) collective-permute-start(f32[256,128]{1,0:T(8,128)S(1)} %shard_map.143.before_ref.left_ref), channel_id=1, source_target_pairs={{1,33},{3,35},{5,37},{7,39},{9,41},{11,43},{13,45},{15,47},{17,49}... | collective-permute-start | bytes 393224 | tf_op jit(solution)/shard_map/ppermute | solution.py:418
  40.7 7.0 %collective-permute-start.7 = (f32[256,128]{1,0:T(8,128)S(1)}, f32[256,128]{1,0:T(8,128)S(1)}, u32[]{:S(2)}, u32[]{:S(2)}) collective-permute-start(f32[256,128]{1,0:T(8,128)S(1)} %shard_map.145.before_ref.left_ref), channel_id=1, source_target_pairs={{1,97},{3,99},{5,101},{7,103},{9,105},{11,107},{13,109},{15,111},{... | collective-permute-start | bytes 393224 | tf_op jit(solution)/shard_map/ppermute | solution.py:418
  47.7 5.7 %collective-permute-start.8 = (f32[256,128]{1,0:T(8,128)S(1)}, f32[256,128]{1,0:T(8,128)S(1)}, u32[]{:S(2)}, u32[]{:S(2)}) collective-permute-start(f32[256,128]{1,0:T(8,128)S(1)} %shard_map.148.before_ref.left_ref), channel_id=1, source_target_pairs={{1,9},{3,11},{5,13},{7,15},{9,1},{11,3},{13,5},{15,7},{17,25},{19,... | collective-permute-start | bytes 393224 | tf_op jit(solution)/shard_map/ppermute | solution.py:418
  49.6 8.3 %collective-permute-start.9 = (bf16[128,768]{1,0:T(8,128)(2,1)S(1)}, bf16[128,768]{1,0:T(8,128)(2,1)S(1)}, u32[]{:S(2)}, u32[]{:S(2)}) collective-permute-start(bf16[128,768]{1,0:T(8,128)(2,1)S(1)} %shard_map.142.before_ref), channel_id=1, source_target_pairs={{0,4},{1,5},{2,6},{3,7},{4,0},{5,1},{6,2},{7,3},{8,12},{9,13},{10,... | collective-permute-start | bytes 589832 | tf_op jit(solution)/shard_map/ppermute | solution.py:413
  49.9 8.1 %collective-permute-start.10 = (bf16[128,768]{1,0:T(8,128)(2,1)S(1)}, bf16[128,768]{1,0:T(8,128)(2,1)S(1)}, u32[]{:S(2)}, u32[]{:S(2)}) collective-permute-start(bf16[128,768]{1,0:T(8,128)(2,1)S(1)} %shard_map.144.before_ref), channel_id=1, source_target_pairs={{0,16},{1,17},{2,18},{3,19},{4,20},{5,21},{6,22},{7,23},{8,24},{9,... | collective-permute-start | bytes 589832 | tf_op jit(solution)/shard_map/ppermute | solution.py:413
  51.9 6.1 %copy-start.2 = (s32[5,768]{1,0:T(8,128)S(1)}, s32[5,768]{1,0:T(8,128)}, u32[]{:S(2)}) copy-start(s32[5,768]{1,0:T(8,128)} %rows_ref.5) | copy-start | bytes 46084
  53.4 6.9 %collective-permute-start.11 = (f32[256,128]{1,0:T(8,128)S(1)}, f32[256,128]{1,0:T(8,128)S(1)}, u32[]{:S(2)}, u32[]{:S(2)}) collective-permute-start(f32[256,128]{1,0:T(8,128)S(1)} %shard_map.151.before_ref.left_ref), channel_id=1, source_target_pairs={{1,25},{3,27},{5,29},{7,31},{9,17},{11,19},{13,21},{15,23},{17,9},... | collective-permute-start | bytes 393224 | tf_op jit(solution)/shard_map/ppermute | solution.py:418
  57.8 4.8 %collective-permute-start.12 = (bf16[128,768]{1,0:T(8,128)(2,1)S(1)}, bf16[128,768]{1,0:T(8,128)(2,1)S(1)}, u32[]{:S(2)}, u32[]{:S(2)}) collective-permute-start(bf16[128,768]{1,0:T(8,128)(2,1)S(1)} %shard_map.147.before_ref), channel_id=1, source_target_pairs={{0,8},{1,9},{2,10},{3,11},{4,12},{5,13},{6,14},{7,15},{8,0},{9,1},... | collective-permute-start | bytes 589832 | tf_op jit(solution)/shard_map/ppermute | solution.py:413
  57.9 4.8 %collective-permute-start.13 = (bf16[128,768]{1,0:T(8,128)(2,1)S(1)}, bf16[128,768]{1,0:T(8,128)(2,1)S(1)}, u32[]{:S(2)}, u32[]{:S(2)}) collective-permute-start(bf16[128,768]{1,0:T(8,128)(2,1)S(1)} %shard_map.146.before_ref), channel_id=1, source_target_pairs={{0,2},{1,3},{2,0},{3,1},{4,6},{5,7},{6,4},{7,5},{8,10},{9,11},{10,... | collective-permute-start | bytes 589832 | tf_op jit(solution)/shard_map/ppermute | solution.py:413
  60.3 5.7 %collective-permute-start.14 = (f32[256,128]{1,0:T(8,128)S(1)}, f32[256,128]{1,0:T(8,128)S(1)}, u32[]{:S(2)}, u32[]{:S(2)}) collective-permute-start(f32[256,128]{1,0:T(8,128)S(1)} %shard_map.153.before_ref.left_ref), channel_id=1, source_target_pairs={{1,3},{3,1},{5,7},{7,5},{9,11},{11,9},{13,15},{15,13},{17,19},{19,... | collective-permute-start | bytes 393224 | tf_op jit(solution)/shard_map/ppermute | solution.py:418
  62.5 7.3 %collective-permute-start.15 = (bf16[128,768]{1,0:T(8,128)(2,1)S(1)}, bf16[128,768]{1,0:T(8,128)(2,1)S(1)}, u32[]{:S(2)}, u32[]{:S(2)}) collective-permute-start(bf16[128,768]{1,0:T(8,128)(2,1)S(1)} %shard_map.149.before_ref), channel_id=1, source_target_pairs={{0,1},{1,0},{2,3},{3,2},{4,5},{5,4},{6,7},{7,6},{8,9},{9,8},{10,11... | collective-permute-start | bytes 589832 | tf_op jit(solution)/shard_map/ppermute | solution.py:413
  66.1 6.9 %collective-permute-start.16 = (f32[256,128]{1,0:T(8,128)S(1)}, f32[256,128]{1,0:T(8,128)S(1)}, u32[]{:S(2)}, u32[]{:S(2)}) collective-permute-start(f32[256,128]{1,0:T(8,128)S(1)} %shard_map.155.before_ref.left_ref), channel_id=1, source_target_pairs={{1,7},{3,5},{5,3},{7,1},{9,15},{11,13},{13,11},{15,9},{17,23},{19,... | collective-permute-start | bytes 393224 | tf_op jit(solution)/shard_map/ppermute | solution.py:418
  73.0 2.3 %collective-permute-start.17 = (f32[256,128]{1,0:T(8,128)S(1)}, f32[256,128]{1,0:T(8,128)S(1)}, u32[]{:S(2)}, u32[]{:S(2)}) collective-permute-start(f32[256,128]{1,0:T(8,128)S(1)} %shard_map.157.total_ref), channel_id=1, source_target_pairs={{1,0},{3,2},{5,4},{7,6},{9,8},{11,10},{13,12},{15,14},{17,16},{19,... | collective-permute-start | bytes 393224 | tf_op jit(solution)/shard_map/ppermute | solution.py:418

commit v9 on v7

--- a/solution.py
+++ b/solution.py
@@ -47,13 +47,15 @@
     return jnp.dot(left, right, preferred_element_type=jnp.float32)
 
 
-def pick_kernel(rows_hbm, x_hbm, *refs):
-    outs, (rows_ref, x_ref, xt_ref, rows_sem, x_sem) = refs[:-5], refs[-5:]
+def pick_kernel(rows_hbm, x_hbm, tiles_hbm, *refs):
+    outs, (tiles_ref, rows_ref, x_ref, xt_ref, rows_sem, x_sem, tiles_sem) = refs[:-7], refs[-7:]
     rounds = len(outs)
+    tiles_copy = pltpu.make_async_copy(tiles_hbm, tiles_ref, tiles_sem)
     rows_copy = pltpu.make_async_copy(rows_hbm, rows_ref, rows_sem)
     x_copy = pltpu.make_async_copy(x_hbm, x_ref, x_sem)
     rows_copy.start()
     x_copy.start()
+    tiles_copy.start()
     rows_copy.wait()
     count, step = x_ref.shape[0], 2 * TILE
     numbers = lax.broadcasted_iota(jnp.int32, (count, step), 0)
@@ -66,16 +68,18 @@
                 for i in range(0, count, TILE):
                     xt_ref[:, i : i + TILE] = x_ref[i : i + TILE, :].T
             outs[r][:, k : k + step] = nn_dot(xt_ref[...], table).astype(jnp.bfloat16)
-
-
-def pick_rows(send_rows, features):
+    tiles_copy.wait()
+
+
+def pick_rows(send_rows, features, tiles):
     rows, width = features.shape
     rounds, boundary = send_rows.shape
     outs = [jax.ShapeDtypeStruct((width, boundary), jnp.bfloat16) for _ in range(rounds)]
+    outs.append(VMEM(tiles.shape, tiles.dtype))
     return pl.pallas_call(
         pick_kernel,
         out_shape=outs,
-        in_specs=[pl.BlockSpec(memory_space=pltpu.HBM)] * 2,
+        in_specs=[pl.BlockSpec(memory_space=pltpu.HBM)] * 3,
         out_specs=[vspec()] * len(outs),
         scratch_shapes=[
             VMEM(send_rows.shape, jnp.int32),
@@ -83,25 +87,23 @@
             VMEM((width, rows), jnp.bfloat16),
             pltpu.SemaphoreType.DMA,
             pltpu.SemaphoreType.DMA,
+            pltpu.SemaphoreType.DMA,
         ],
         compiler_params=params(),
         cost_estimate=cost(2 * rows * boundary * rounds * width, 1_000_000),
-    )(in_hbm(send_rows), in_hbm(features))
+    )(in_hbm(send_rows), in_hbm(features), in_hbm(tiles))
 
 
 def densify_kernel(
-    lc_hbm, hc_hbm, lt, ht, dl0, dl1, dh0, dh1, lslots, hslots, zeros, lc, hc, sems, zsems, csems
+    lc_hbm, hc_hbm, lt, ht, dl0, dl1, dh0, dh1, hslots, zeros, lc, hc, sems, zsems, csems
 ):
     half = lt.shape[0] // 2
-    depth = lslots.shape[0]
+    depth = hslots.shape[0]
     dense = (dl0, dl1, dh0, dh1)
 
     def fetch(i, slot):
         return [
-            pltpu.make_async_copy(
-                src.at[i + p * half], dst.at[slot, p], sems.at[slot, 2 * q + p]
-            )
-            for q, (src, dst) in enumerate(((lt, lslots), (ht, hslots)))
+            pltpu.make_async_copy(ht.at[i + p * half], hslots.at[slot, p], sems.at[slot, p])
             for p in range(2)
         ]
 
@@ -150,11 +152,14 @@
         for t in range(max(lt.shape[1], ht.shape[1])):
             jobs = []
             if t < lt.shape[1]:
-                jobs += [(dl0, lc[i, t], lslots, 0), (dl1, lc[i + half, t], lslots, 1)]
+                jobs += [(dl0, lc[i, t], lt[i, t]), (dl1, lc[i + half, t], lt[i + half, t])]
             if t < ht.shape[1]:
-                jobs += [(dh0, hc[i, t], hslots, 0), (dh1, hc[i + half, t], hslots, 1)]
-            sums = [d[c, rows, :] + s[slot, p, t] for d, c, s, p in jobs]
-            for (d, c, _, _), total in zip(jobs, sums):
+                jobs += [
+                    (dh0, hc[i, t], hslots[slot, 0, t]),
+                    (dh1, hc[i + half, t], hslots[slot, 1, t]),
+                ]
+            sums = [d[c, rows, :] + tile for d, c, tile in jobs]
+            for (d, c, _), total in zip(jobs, sums):
                 d[c, rows, :] = total
         return carry
 
@@ -170,21 +175,21 @@
     return pl.pallas_call(
         densify_kernel,
         out_shape=[VMEM((n, half, TILE), jnp.bfloat16) for n in slabs],
-        in_specs=[pl.BlockSpec(memory_space=pltpu.HBM)] * 4,
+        in_specs=[pl.BlockSpec(memory_space=pltpu.HBM)] * 2
+        + [vspec(), pl.BlockSpec(memory_space=pltpu.HBM)],
         out_specs=[vspec()] * 4,
         scratch_shapes=[
-            VMEM((depth, 2, local_count, TILE, TILE), jnp.bfloat16),
             VMEM((depth, 2, halo_count, TILE, TILE), jnp.bfloat16),
             VMEM((max(slabs), TILE, TILE), jnp.bfloat16),
             pltpu.SMEM(local_cols.shape, jnp.int32),
             pltpu.SMEM(halo_cols.shape, jnp.int32),
-            pltpu.SemaphoreType.DMA((depth, 4)),
+            pltpu.SemaphoreType.DMA((depth, 2)),
             pltpu.SemaphoreType.DMA((2, 4)),
             pltpu.SemaphoreType.DMA((2,)),
         ],
-        compiler_params=params(12 * 1024 * 1024),
+        compiler_params=params(8 * 1024 * 1024),
         cost_estimate=cost(16_000_000, nblocks * (local_count + halo_count) * TILE * TILE * 2),
-    )(in_hbm(local_cols), in_hbm(halo_cols), in_hbm(local_tiles), in_hbm(halo_tiles))
+    )(in_hbm(local_cols), in_hbm(halo_cols), pinned(local_tiles), in_hbm(halo_tiles))
 
 
 def local_sums_kernel(d0_ref, d1_ref, x_ref, out_ref):
@@ -335,7 +340,7 @@
 
 
 def place_kernel(rounds, last, rows_ref, acc_ref, before_ref, *refs):
-    returned, (out_ref, token_ref, listed) = refs[: len(rounds)], refs[len(rounds) :]
+    returned, (out_ref, token_ref, listed, *rest) = refs[: len(rounds)], refs[len(rounds) :]
     token_ref[...] = jnp.zeros_like(token_ref)
     step, boundary = 2 * TILE, rows_ref.shape[1]
     for place, r in enumerate(rounds):
@@ -343,6 +348,7 @@
             line = rows_ref[r : r + 1, k : k + TILE].astype(jnp.float32)
             listed[place, k : k + TILE, :] = jnp.broadcast_to(line, (TILE, TILE)).T
     numbers = lax.broadcasted_iota(jnp.int32, (boundary, TILE), 1).astype(jnp.float32)
+    copies = []
     for j in range(0, acc_ref.shape[1], step):
         total = acc_ref[:, j : j + step]
         for place, got_ref in enumerate(returned):
@@ -355,24 +361,35 @@
             )
             total = total + nn_dot(got_ref[...], table)
         if last:
-            out_ref[j : j + step, :] = total.T
+            ready, sems = rest
+            ready[j : j + step, :] = total.T
+            rows = pl.ds(j, step)
+            copies.append(
+                pltpu.make_async_copy(ready.at[rows], out_ref.at[rows], sems.at[j // step])
+            )
+            copies[-1].start()
         else:
             out_ref[:, j : j + step] = total
+    for copy in copies:
+        copy.wait()
 
 
 def place_rows(rounds, last, send_rows, acc, returned, before):
     width, rows = acc.shape
     count, boundary = len(rounds), send_rows.shape[1]
+    scratch = [VMEM((count, boundary, TILE), jnp.float32)]
     if last:
         out = jax.ShapeDtypeStruct((rows, width), jnp.float32)
+        scratch += [VMEM((rows, width), jnp.float32)]
+        scratch += [pltpu.SemaphoreType.DMA((rows // (2 * TILE),))]
     else:
         out = VMEM((width, rows), jnp.float32)
     return pl.pallas_call(
         functools.partial(place_kernel, rounds, last),
         out_shape=[out, VMEM((8, TILE), jnp.float32)],
         in_specs=[vspec()] * 2 + [pl.BlockSpec(memory_space=pl.ANY)] + [vspec()] * count,
-        out_specs=[vspec()] * 2,
-        scratch_shapes=[VMEM((count, boundary, TILE), jnp.float32)],
+        out_specs=[pl.BlockSpec(memory_space=pltpu.HBM) if last else vspec(), vspec()],
+        scratch_shapes=scratch,
         compiler_params=params(),
         cost_estimate=cost(1, 1),
     )(send_rows, pinned(acc), before, *returned)
@@ -433,10 +450,10 @@
     nblocks = local_tiles.shape[0]
     round_count, boundary = send_rows.shape
     per = boundary // TILE
-    picked = pick_rows(send_rows, node_features)
+    *picked, near_tiles = pick_rows(send_rows, node_features, local_tiles)
     received = [swapped(rows, 1 << r) for r, rows in enumerate(picked)]
     dl0, dl1, dh0, dh1 = densify(
-        local_cols, halo_cols, local_tiles, halo_tiles, round_count * per
+        local_cols, halo_cols, near_tiles, halo_tiles, round_count * per
     )
     summed = local_sums(dl0, dl1, node_features)
     output, grad_pre, scaled_t, mine, give = middle(
@@ -467,25 +484,26 @@
     total = added(mine, other, last)
     other = swapped(total, 32)
     last = send_back(4, total)
+    last = send_back(1, last)
     total = added(total, other, last)
     other = swapped(total, 96)
-    last = send_back(1, total)
-    last = send_back(3, last)
+    last = send_back(3, total)
+    last = send_back(0, last)
     total = added(total, other, last)
     other = swapped(total, 8)
-    last = send_back(0, total)
-    grads_t = own(scaled_t, dl0, dl1, grad_pre, w_self, last)
+    grads_t = own(scaled_t, dl0, dl1, grad_pre, w_self, total)
     total = added(total, other, grads_t)
     other = swapped(total, 24)
-    grads_t, last = place((2, 4), grads_t, total)
+    grads_t, last = place((2,), grads_t, total)
     total = added(total, other, last)
     other = swapped(total, 2)
-    grads_t, last = place((3, 1), grads_t, total)
+    grads_t, last = place((4, 3), grads_t, total)
     total = added(total, other, last)
     other = swapped(total, 6)
-    grads, last = place((0,), grads_t, total)
+    grads_t, last = place((1,), grads_t, total)
     total = added(total, other, last)
     other = swapped(total, 1)
+    grads, last = place((0,), grads_t, total)
     grad_scale = 1.0 / math.sqrt(row_count * lax.axis_size("dom"))
     grad_self, grad_neigh = halves(grad_scale, total, other)
     return (output, grads, grad_self, grad_neigh)

time: 66.9 us -> 68.2 us (1.019)
  starting transfers between devices: 28.7 us -> 31.6 us
  waiting for transfers between devices: 7.42 us -> 4.79 us
  Pallas kernels: 29.7 us -> 30.6 us
    ppermute x18, starting transfers between devices: 28.7 us -> 31.6 us  [swapped(): lax.ppermute(shard, 'dom', [(i, i ^ mask) for i in range(lax.axis_size('d...]
    ppermute x18, waiting for transfers between devices: 7.42 us -> 4.79 us  [swapped(): lax.ppermute(shard, 'dom', [(i, i ^ mask) for i in range(lax.axis_size('d...]
    pallas_call x1, Pallas kernels: 3.58 us -> 4.51 us  [pick_rows(): pl.pallas_call(pick_kernel, out_shape=outs, in_specs=[pl.BlockSpec(memory...]
    pallas_call x3 -> x4, Pallas kernels: 4.03 us -> 4.67 us  [place_rows(): pl.pallas_call(functools.partial(place_kernel, rounds, last), out_shape=[...]
  transfers between devices with their start and end apart: 18 -> 18, of which waited for: 7 -> 6; matrix products, arithmetic and copies ran while one was open for 0% -> 0% of each run, Pallas kernels for 29% -> 28%
where the time goes in v9:
time: 68.2 us; the launch traced here: 68 us
  starting transfers between devices  31.6 us (46%)
  Pallas kernels  30.6 us (45%)
  waiting for transfers between devices  4.79 us (7%)
  between operations  0.95 us (1%)
    ppermute x18, starting transfers between devices, swapped(): lax.ppermute(shard, 'dom', [(i, i ^ mask) for i in range(lax.axis_size('d...  31.6 us
    pallas_call x1, Pallas kernels, densify(): pl.pallas_call(densify_kernel, out_shape=[VMEM((n, half, TILE), jnp.bfloa...  7.86 us
    pallas_call x1, Pallas kernels, middle(): pl.pallas_call(functools.partial(middle_kernel, rounds), out_shape=[half,...  6.2 us
    ppermute x18, waiting for transfers between devices, swapped(): lax.ppermute(shard, 'dom', [(i, i ^ mask) for i in range(lax.axis_size('d...  4.79 us
    pallas_call x4, Pallas kernels, place_rows(): pl.pallas_call(functools.partial(place_kernel, rounds, last), out_shape=[...  4.67 us
    pallas_call x1, Pallas kernels, pick_rows(): pl.pallas_call(pick_kernel, out_shape=outs, in_specs=[pl.BlockSpec(memory...  4.51 us
    pallas_call x5, Pallas kernels, back(): pl.pallas_call(functools.partial(back_kernel, first, n), out_shape=jax.Sh...  2.93 us
    pallas_call x1, Pallas kernels, local_sums(): pl.pallas_call(local_sums_kernel, out_shape=VMEM((rows, width), jnp.float...  2.31 us
  transfers between devices with their start and end apart: 18, of which 6 were waited for; matrix products, arithmetic and copies ran while one was open for 0% of the time, Pallas kernels for 28%

profile of v9, /device:TPU:1, one launch (start us, length us, event | category | flops | bytes accessed | tf_op | source)
XLA Modules:
  0.0 68.0 jit_solution(8715337607148662831)
XLA Ops:
  0.6 4.5 %shard_map.138 = (bf16[128,768]{1,0:T(8,128)(2,1)S(1)}, bf16[128,768]{1,0:T(8,128)(2,1)S(1)}, bf16[128,768]{1,0:T(8,128)(2,1)S(1)}, bf16[128,768]{1,0:T(8,128)(2...) custom-call(s32[5,768]{1,0:T(8,128)} %rows_ref.7, bf16[2048,128]{1,0:T(8,128)(2,1)} %refs_8_.1, ...), custom_call_target="tpu_custom_call" | custom-call | flops 2013265920 | bytes 1000000 | tf_op jit(solution)/shard_map/pallas_call | solution.py:79
  5.1 1.5 %collective-permute-start = (bf16[128,768]{1,0:T(8,128)(2,1)S(1)}, bf16[128,768]{1,0:T(8,128)(2,1)S(1)}, u32[]{:S(2)}, u32[]{:S(2)}) collective-permute-start(bf16[128,768]{1,0:T(8,128)(2,1)S(1)} %get-tuple-element.28), channel_id=1, source_target_pairs={{0,1},{1,0},{2,3},{3,2},{4,5},{5,4},{6,7},{7,6},{8,9},{9,8},{10,11... | collective-permute-start | bytes 589832 | tf_op jit(solution)/shard_map/ppermute | solution.py:433
  6.6 1.7 %collective-permute-start.1 = (bf16[128,768]{1,0:T(8,128)(2,1)S(1)}, bf16[128,768]{1,0:T(8,128)(2,1)S(1)}, u32[]{:S(2)}, u32[]{:S(2)}) collective-permute-start(bf16[128,768]{1,0:T(8,128)(2,1)S(1)} %get-tuple-element.29), channel_id=1, source_target_pairs={{0,2},{1,3},{2,0},{3,1},{4,6},{5,7},{6,4},{7,5},{8,10},{9,11},{10,... | collective-permute-start | bytes 589832 | tf_op jit(solution)/shard_map/ppermute | solution.py:433
  8.4 3.3 %collective-permute-start.2 = (bf16[128,768]{1,0:T(8,128)(2,1)S(1)}, bf16[128,768]{1,0:T(8,128)(2,1)S(1)}, u32[]{:S(2)}, u32[]{:S(2)}) collective-permute-start(bf16[128,768]{1,0:T(8,128)(2,1)S(1)} %get-tuple-element.30), channel_id=1, source_target_pairs={{0,4},{1,5},{2,6},{3,7},{4,0},{5,1},{6,2},{7,3},{8,12},{9,13},{10,... | collective-permute-start | bytes 589832 | tf_op jit(solution)/shard_map/ppermute | solution.py:433
  11.7 1.2 %collective-permute-start.3 = (bf16[128,768]{1,0:T(8,128)(2,1)S(1)}, bf16[128,768]{1,0:T(8,128)(2,1)S(1)}, u32[]{:S(2)}, u32[]{:S(2)}) collective-permute-start(bf16[128,768]{1,0:T(8,128)(2,1)S(1)} %get-tuple-element.31), channel_id=1, source_target_pairs={{0,8},{1,9},{2,10},{3,11},{4,12},{5,13},{6,14},{7,15},{8,0},{9,1},... | collective-permute-start | bytes 589832 | tf_op jit(solution)/shard_map/ppermute | solution.py:433
  12.9 2.5 %collective-permute-start.4 = (bf16[128,768]{1,0:T(8,128)(2,1)S(1)}, bf16[128,768]{1,0:T(8,128)(2,1)S(1)}, u32[]{:S(2)}, u32[]{:S(2)}) collective-permute-start(bf16[128,768]{1,0:T(8,128)(2,1)S(1)} %get-tuple-element.32), channel_id=1, source_target_pairs={{0,16},{1,17},{2,18},{3,19},{4,20},{5,21},{6,22},{7,23},{8,24},{9,... | collective-permute-start | bytes 589832 | tf_op jit(solution)/shard_map/ppermute | solution.py:433
  15.3 7.9 %shard_map.139 = (bf16[16,1024,128]{2,1,0:T(8,128)(2,1)S(1)}, bf16[16,1024,128]{2,1,0:T(8,128)(2,1)S(1)}, bf16[30,1024,128]{2,1,0:T(8,128)(2,1)S(1)}, bf16[30,1024,128]{2,1,0:T(8,128)(2,1)S(1)}) custom-call(s32[16,22]{1,0:T(8,128)} %lc_hbm.1, s32[16,20]{1,0:T(8,128)} %hc_hbm.1, bf16[16,22,128,128]{3,2,1,0:T(8,128)(2,1)S(1)} %get-tuple-element.33.lt, ...), custom_call_target="tpu_custom_call" | custom-call | flops 16000000 | bytes 22020096 | tf_op jit(solution)/shard_map/pallas_call | solution.py:175
  23.2 0.0 copy-start.2
  23.2 0.0 copy-start.3
  23.2 0.0 copy-start.4
  23.3 0.0 copy-start.5
  23.3 0.0 copy-start.6
  23.3 2.3 %shard_map.140.refs_7_ = f32[2048,128]{1,0:T(8,128)S(1)} custom-call(bf16[16,1024,128]{2,1,0:T(8,128)(2,1)S(1)} %get-tuple-element.36.d0_ref, bf16[16,1024,128]{2,1,0:T(8,128)(2,1)S(1)} %get-tuple-element.37.d1_ref, bf16[2048,128]{1,0:T(8,128)(2,1)S(1)} %copy-done), custom_call_target="tpu_custom_call" | custom-call | flops 1073741824 | bytes 1500000 | tf_op jit(solution)/shard_map/pallas_call | solution.py:207
  25.6 0.0 collective-permute-done.refs_0_
  25.6 0.0 collective-permute-done.2.refs_2_
  25.6 0.0 collective-permute-done.3.refs_3_
  25.7 6.2 %shard_map.141 = (bf16[2048,128]{1,0:T(8,128)(2,1)}, bf16[2048,128]{1,0:T(8,128)(2,1)S(1)}, bf16[128,2048]{1,0:T(8,128)(2,1)S(1)}, f32[128,128]{1,0:T(8,128)S(1)}, f32[128,128]{1,0:T(8,128)S(1)}) custom-call(bf16[128,768]{1,0:T(8,128)(2,1)S(1)} %collective-permute-done.refs_0_, bf16[128,768]{1,0:T(8,128)(2,1)S(1)} %collective-permute-done.1.refs_1_, ...), custom_call_target="tpu_custom_call" | custom-call | flops 2013265920 | bytes 5000000 | tf_op jit(solution)/shard_map/pallas_call | solution.py:267
  31.9 1.2 %collective-permute-start.5 = (f32[128,128]{1,0:T(8,128)S(1)}, f32[128,128]{1,0:T(8,128)S(1)}, u32[]{:S(2)}, u32[]{:S(2)}) collective-permute-start(f32[128,128]{1,0:T(8,128)S(1)} %get-tuple-element.42), channel_id=1, source_target_pairs={{0,1},{1,0},{2,3},{3,2},{4,5},{5,4},{6,7},{7,6},{8,9},{9,8},{10,11... | collective-permute-start | bytes 196616 | tf_op jit(solution)/shard_map/ppermute | solution.py:433
  33.1 0.6 shard_map.142.before_ref
  33.7 0.3 collective-permute-done.5.right_ref
  34.0 1.6 %collective-permute-start.6 = (f32[128,128]{1,0:T(8,128)S(1)}, f32[128,128]{1,0:T(8,128)S(1)}, u32[]{:S(2)}, u32[]{:S(2)}) collective-permute-start(f32[128,128]{1,0:T(8,128)S(1)} %shard_map.143.before_ref.left_ref), channel_id=1, source_target_pairs={{0,32},{1,33},{2,34},{3,35},{4,36},{5,37},{6,38},{7,39},{8,40},{9,... | collective-permute-start | bytes 196616 | tf_op jit(solution)/shard_map/ppermute | solution.py:433
  35.6 0.6 shard_map.144.before_ref
  36.2 0.6 shard_map.145.before_ref
  36.8 0.6 collective-permute-done.6.right_ref
  37.4 2.8 %collective-permute-start.7 = (f32[128,128]{1,0:T(8,128)S(1)}, f32[128,128]{1,0:T(8,128)S(1)}, u32[]{:S(2)}, u32[]{:S(2)}) collective-permute-start(f32[128,128]{1,0:T(8,128)S(1)} %shard_map.146.before_ref.left_ref), channel_id=1, source_target_pairs={{0,96},{1,97},{2,98},{3,99},{4,100},{5,101},{6,102},{7,103},{8,104... | collective-permute-start | bytes 196616 | tf_op jit(solution)/shard_map/ppermute | solution.py:433
  40.2 0.0 collective-permute-start.9
  40.2 0.6 shard_map.147.before_ref
  40.8 0.6 shard_map.148.before_ref
  41.4 0.0 copy-start.1
  41.4 0.4 collective-permute-done.7.right_ref
  41.9 0.1 collective-permute-start.8
  42.0 1.4 %collective-permute-start.11 = (bf16[128,768]{1,0:T(8,128)(2,1)S(1)}, bf16[128,768]{1,0:T(8,128)(2,1)S(1)}, u32[]{:S(2)}, u32[]{:S(2)}) collective-permute-start(bf16[128,768]{1,0:T(8,128)(2,1)S(1)} %shard_map.144.before_ref), channel_id=1, source_target_pairs={{0,16},{1,17},{2,18},{3,19},{4,20},{5,21},{6,22},{7,23},{8,24},{9,... | collective-permute-start | bytes 589832 | tf_op jit(solution)/shard_map/ppermute | solution.py:433
  43.4 0.1 collective-permute-start.12
  43.5 1.4 %shard_map.150.before_ref.acc_ref = f32[128,2048]{1,0:T(8,128)S(1)} custom-call(bf16[128,2048]{1,0:T(8,128)(2,1)S(1)} %get-tuple-element.39.st_ref.before_ref, bf16[16,1024,128]{2,1,0:T(8,128)(2,1)S(1)} %get-tuple-element.36.d0_ref, bf16[16,1024,128]{2,1,0:T(8,128)(2,1)S(1)} %get-tuple-element.37.d1_ref, bf16[2048,128]{1,0:T(8,128)(2,1)S(1)} %get-tuple-element.40.gp_ref, ...), custom_call_target="tpu_custom_call" | custom-call | flops 1 | bytes 1 | tf_op jit(solution)/shard_map/pallas_call | solution.py:332
  44.9 0.2 collective-permute-done.8.right_ref
  45.1 2.3 %collective-permute-start.10 = (f32[128,128]{1,0:T(8,128)S(1)}, f32[128,128]{1,0:T(8,128)S(1)}, u32[]{:S(2)}, u32[]{:S(2)}) collective-permute-start(f32[128,128]{1,0:T(8,128)S(1)} %shard_map.151.before_ref.left_ref), channel_id=1, source_target_pairs={{0,24},{1,25},{2,26},{3,27},{4,28},{5,29},{6,30},{7,31},{8,16},{9,... | collective-permute-start | bytes 196616 | tf_op jit(solution)/shard_map/ppermute | solution.py:433
  47.4 0.0 collective-permute-done.9.refs_0_
  47.4 0.7 %shard_map.152 = (f32[128,2048]{1,0:T(8,128)S(1)}, f32[8,128]{1,0:T(8,128)S(1)}) custom-call(s32[5,768]{1,0:T(8,128)S(1)} %copy-done.1, f32[128,2048]{1,0:T(8,128)S(1)} %shard_map.150.before_ref.acc_ref, f32[128,128]{1,0:T(8,128)S(1)} %shard_map.151.before_ref.left_ref, bf16[128,768]{1,0:T(8,128)(2,1)S(1)} %collective-permute-done.9.refs_0_), custom_call_target="tpu_custom_call" | custom-call | flops 1 | bytes 1 | tf_op jit(solution)/shard_map/pallas_call | solution.py:387
  48.1 2.0 %collective-permute-done.10.right_ref = f32[128,128]{1,0:T(8,128)S(1)} collective-permute-done((f32[128,128]{1,0:T(8,128)S(1)}, f32[128,128]{1,0:T(8,128)S(1)}, u32[]{:S(2)}, u32[]{:S(2)}) %collective-permute-start.10) | collective-permute-done | bytes 65568 | tf_op jit(solution)/shard_map/ppermute | solution.py:433
  50.1 0.1 collective-permute-start.13
  50.2 5.2 %collective-permute-start.16 = (bf16[128,768]{1,0:T(8,128)(2,1)S(1)}, bf16[128,768]{1,0:T(8,128)(2,1)S(1)}, u32[]{:S(2)}, u32[]{:S(2)}) collective-permute-start(bf16[128,768]{1,0:T(8,128)(2,1)S(1)} %shard_map.148.before_ref), channel_id=1, source_target_pairs={{0,1},{1,0},{2,3},{3,2},{4,5},{5,4},{6,7},{7,6},{8,9},{9,8},{10,11... | collective-permute-start | bytes 589832 | tf_op jit(solution)/shard_map/ppermute | solution.py:433
  55.4 1.1 %shard_map.154 = (f32[128,2048]{1,0:T(8,128)S(1)}, f32[8,128]{1,0:T(8,128)S(1)}) custom-call(s32[5,768]{1,0:T(8,128)S(1)} %copy-done.1, f32[128,2048]{1,0:T(8,128)S(1)} %get-tuple-element.43.acc_ref, f32[128,128]{1,0:T(8,128)S(1)} %shard_map.153.before_ref.left_ref, bf16[128,768]{1,0:T(8,128)(2,1)S(1)} %collective-permute-done.11.refs_0_, ...), custom_call_target="tpu_custom_call" | custom-call | flops 1 | bytes 1 | tf_op jit(solution)/shard_map/pallas_call | solution.py:387
  56.5 2.5 %collective-permute-start.15 = (f32[128,128]{1,0:T(8,128)S(1)}, f32[128,128]{1,0:T(8,128)S(1)}, u32[]{:S(2)}, u32[]{:S(2)}) collective-permute-start(f32[128,128]{1,0:T(8,128)S(1)} %shard_map.155.before_ref.left_ref), channel_id=1, source_target_pairs={{0,6},{1,7},{2,4},{3,5},{4,2},{5,3},{6,0},{7,1},{8,14},{9,15},{10,... | collective-permute-start | bytes 196616 | tf_op jit(solution)/shard_map/ppermute | solution.py:433
  59.1 0.7 %shard_map.156 = (f32[128,2048]{1,0:T(8,128)S(1)}, f32[8,128]{1,0:T(8,128)S(1)}) custom-call(s32[5,768]{1,0:T(8,128)S(1)} %copy-done.1, f32[128,2048]{1,0:T(8,128)S(1)} %get-tuple-element.45.acc_ref, f32[128,128]{1,0:T(8,128)S(1)} %shard_map.155.before_ref.left_ref, bf16[128,768]{1,0:T(8,128)(2,1)S(1)} %collective-permute-done.14.refs_0_), custom_call_target="tpu_custom_call" | custom-call | flops 1 | bytes 1 | tf_op jit(solution)/shard_map/pallas_call | solution.py:387
  59.8 1.2 %collective-permute-done.15.right_ref = f32[128,128]{1,0:T(8,128)S(1)} collective-permute-done((f32[128,128]{1,0:T(8,128)S(1)}, f32[128,128]{1,0:T(8,128)S(1)}, u32[]{:S(2)}, u32[]{:S(2)}) %collective-permute-start.15) | collective-permute-done | bytes 65568 | tf_op jit(solution)/shard_map/ppermute | solution.py:433
  61.0 4.2 %collective-permute-start.17 = (f32[128,128]{1,0:T(8,128)S(1)}, f32[128,128]{1,0:T(8,128)S(1)}, u32[]{:S(2)}, u32[]{:S(2)}) collective-permute-start(f32[128,128]{1,0:T(8,128)S(1)} %shard_map.157.before_ref.total_ref), channel_id=1, source_target_pairs={{0,1},{1,0},{2,3},{3,2},{4,5},{5,4},{6,7},{7,6},{8,9},{9,8},{10,11... | collective-permute-start | bytes 196616 | tf_op jit(solution)/shard_map/ppermute | solution.py:433
  65.2 2.1 %shard_map.158 = (f32[2048,128]{1,0:T(8,128)}, f32[8,128]{1,0:T(8,128)}) custom-call(s32[5,768]{1,0:T(8,128)S(1)} %copy-done.1, f32[128,2048]{1,0:T(8,128)S(1)} %get-tuple-element.47.acc_ref, f32[128,128]{1,0:T(8,128)S(1)} %shard_map.157.before_ref.total_ref, bf16[128,768]{1,0:T(8,128)(2,1)S(1)} %collective-permute-done.16.refs_0_), custom_call_target="tpu_custom_call" | custom-call | flops 1 | bytes 1 | tf_op jit(solution)/shard_map/pallas_call | solution.py:387
  67.4 0.7 shard_map.159
  (24 shorter events, 0.1 us)
Async XLA Ops:
  5.1 20.5 %collective-permute-start = (bf16[128,768]{1,0:T(8,128)(2,1)S(1)}, bf16[128,768]{1,0:T(8,128)(2,1)S(1)}, u32[]{:S(2)}, u32[]{:S(2)}) collective-permute-start(bf16[128,768]{1,0:T(8,128)(2,1)S(1)} %get-tuple-element.28), channel_id=1, source_target_pairs={{0,1},{1,0},{2,3},{3,2},{4,5},{5,4},{6,7},{7,6},{8,9},{9,8},{10,11... | collective-permute-start | bytes 589832 | tf_op jit(solution)/shard_map/ppermute | solution.py:433
  6.6 19.0 %collective-permute-start.1 = (bf16[128,768]{1,0:T(8,128)(2,1)S(1)}, bf16[128,768]{1,0:T(8,128)(2,1)S(1)}, u32[]{:S(2)}, u32[]{:S(2)}) collective-permute-start(bf16[128,768]{1,0:T(8,128)(2,1)S(1)} %get-tuple-element.29), channel_id=1, source_target_pairs={{0,2},{1,3},{2,0},{3,1},{4,6},{5,7},{6,4},{7,5},{8,10},{9,11},{10,... | collective-permute-start | bytes 589832 | tf_op jit(solution)/shard_map/ppermute | solution.py:433
  8.4 17.3 %collective-permute-start.2 = (bf16[128,768]{1,0:T(8,128)(2,1)S(1)}, bf16[128,768]{1,0:T(8,128)(2,1)S(1)}, u32[]{:S(2)}, u32[]{:S(2)}) collective-permute-start(bf16[128,768]{1,0:T(8,128)(2,1)S(1)} %get-tuple-element.30), channel_id=1, source_target_pairs={{0,4},{1,5},{2,6},{3,7},{4,0},{5,1},{6,2},{7,3},{8,12},{9,13},{10,... | collective-permute-start | bytes 589832 | tf_op jit(solution)/shard_map/ppermute | solution.py:433
  11.7 14.0 %collective-permute-start.3 = (bf16[128,768]{1,0:T(8,128)(2,1)S(1)}, bf16[128,768]{1,0:T(8,128)(2,1)S(1)}, u32[]{:S(2)}, u32[]{:S(2)}) collective-permute-start(bf16[128,768]{1,0:T(8,128)(2,1)S(1)} %get-tuple-element.31), channel_id=1, source_target_pairs={{0,8},{1,9},{2,10},{3,11},{4,12},{5,13},{6,14},{7,15},{8,0},{9,1},... | collective-permute-start | bytes 589832 | tf_op jit(solution)/shard_map/ppermute | solution.py:433
  12.9 12.8 %collective-permute-start.4 = (bf16[128,768]{1,0:T(8,128)(2,1)S(1)}, bf16[128,768]{1,0:T(8,128)(2,1)S(1)}, u32[]{:S(2)}, u32[]{:S(2)}) collective-permute-start(bf16[128,768]{1,0:T(8,128)(2,1)S(1)} %get-tuple-element.32), channel_id=1, source_target_pairs={{0,16},{1,17},{2,18},{3,19},{4,20},{5,21},{6,22},{7,23},{8,24},{9,... | collective-permute-start | bytes 589832 | tf_op jit(solution)/shard_map/ppermute | solution.py:433
  15.3 7.9 %copy-start = (bf16[2048,128]{1,0:T(8,128)(2,1)S(1)}, bf16[2048,128]{1,0:T(8,128)(2,1)}, u32[]{:S(2)}) copy-start(bf16[2048,128]{1,0:T(8,128)(2,1)} %refs_8_.1) | copy-start | bytes 1572868
  23.2 2.4 %copy-start.2 = (bf16[2048,128]{1,0:T(8,128)(2,1)S(1)}, bf16[2048,128]{1,0:T(8,128)(2,1)}, u32[]{:S(2)}) copy-start(bf16[2048,128]{1,0:T(8,128)(2,1)} %refs_9_.1) | copy-start | bytes 1572868
  23.2 2.4 %copy-start.3 = (bf16[128,128]{1,0:T(8,128)(2,1)S(1)}, bf16[128,128]{1,0:T(8,128)(2,1)}, u32[]{:S(2)}) copy-start(bf16[128,128]{1,0:T(8,128)(2,1)} %ws_ref.1) | copy-start | bytes 98308
  23.2 2.4 %copy-start.4 = (bf16[128,128]{1,0:T(8,128)(2,1)S(1)}, bf16[128,128]{1,0:T(8,128)(2,1)}, u32[]{:S(2)}) copy-start(bf16[128,128]{1,0:T(8,128)(2,1)} %refs_12_.1) | copy-start | bytes 98308
  23.3 2.4 %copy-start.5 = (s32[2048]{0:T(1024)S(1)}, s32[2048]{0:T(1024)}, u32[]{:S(2)}) copy-start(s32[2048]{0:T(1024)} %param.20) | copy-start | bytes 24580
  23.3 2.4 %copy-start.6 = (f32[128]{0:T(128)S(1)}, f32[128]{0:T(128)}, u32[]{:S(2)}) copy-start(f32[128]{0:T(128)} %param.14) | copy-start | bytes 1540
  31.9 2.1 %collective-permute-start.5 = (f32[128,128]{1,0:T(8,128)S(1)}, f32[128,128]{1,0:T(8,128)S(1)}, u32[]{:S(2)}, u32[]{:S(2)}) collective-permute-start(f32[128,128]{1,0:T(8,128)S(1)} %get-tuple-element.42), channel_id=1, source_target_pairs={{0,1},{1,0},{2,3},{3,2},{4,5},{5,4},{6,7},{7,6},{8,9},{9,8},{10,11... | collective-permute-start | bytes 196616 | tf_op jit(solution)/shard_map/ppermute | solution.py:433
  34.0 3.4 %collective-permute-start.6 = (f32[128,128]{1,0:T(8,128)S(1)}, f32[128,128]{1,0:T(8,128)S(1)}, u32[]{:S(2)}, u32[]{:S(2)}) collective-permute-start(f32[128,128]{1,0:T(8,128)S(1)} %shard_map.143.before_ref.left_ref), channel_id=1, source_target_pairs={{0,32},{1,33},{2,34},{3,35},{4,36},{5,37},{6,38},{7,39},{8,40},{9,... | collective-permute-start | bytes 196616 | tf_op jit(solution)/shard_map/ppermute | solution.py:433
  37.4 4.5 %collective-permute-start.7 = (f32[128,128]{1,0:T(8,128)S(1)}, f32[128,128]{1,0:T(8,128)S(1)}, u32[]{:S(2)}, u32[]{:S(2)}) collective-permute-start(f32[128,128]{1,0:T(8,128)S(1)} %shard_map.146.before_ref.left_ref), channel_id=1, source_target_pairs={{0,96},{1,97},{2,98},{3,99},{4,100},{5,101},{6,102},{7,103},{8,104... | collective-permute-start | bytes 196616 | tf_op jit(solution)/shard_map/ppermute | solution.py:433
  40.2 7.2 %collective-permute-start.9 = (bf16[128,768]{1,0:T(8,128)(2,1)S(1)}, bf16[128,768]{1,0:T(8,128)(2,1)S(1)}, u32[]{:S(2)}, u32[]{:S(2)}) collective-permute-start(bf16[128,768]{1,0:T(8,128)(2,1)S(1)} %shard_map.142.before_ref), channel_id=1, source_target_pairs={{0,4},{1,5},{2,6},{3,7},{4,0},{5,1},{6,2},{7,3},{8,12},{9,13},{10,... | collective-permute-start | bytes 589832 | tf_op jit(solution)/shard_map/ppermute | solution.py:433
  41.4 6.0 %copy-start.1 = (s32[5,768]{1,0:T(8,128)S(1)}, s32[5,768]{1,0:T(8,128)}, u32[]{:S(2)}) copy-start(s32[5,768]{1,0:T(8,128)} %rows_ref.7) | copy-start | bytes 46084
  41.9 3.2 %collective-permute-start.8 = (f32[128,128]{1,0:T(8,128)S(1)}, f32[128,128]{1,0:T(8,128)S(1)}, u32[]{:S(2)}, u32[]{:S(2)}) collective-permute-start(f32[128,128]{1,0:T(8,128)S(1)} %shard_map.149.before_ref.left_ref), channel_id=1, source_target_pairs={{0,8},{1,9},{2,10},{3,11},{4,12},{5,13},{6,14},{7,15},{8,0},{9,1},... | collective-permute-start | bytes 196616 | tf_op jit(solution)/shard_map/ppermute | solution.py:433
  42.0 13.4 %collective-permute-start.11 = (bf16[128,768]{1,0:T(8,128)(2,1)S(1)}, bf16[128,768]{1,0:T(8,128)(2,1)S(1)}, u32[]{:S(2)}, u32[]{:S(2)}) collective-permute-start(bf16[128,768]{1,0:T(8,128)(2,1)S(1)} %shard_map.144.before_ref), channel_id=1, source_target_pairs={{0,16},{1,17},{2,18},{3,19},{4,20},{5,21},{6,22},{7,23},{8,24},{9,... | collective-permute-start | bytes 589832 | tf_op jit(solution)/shard_map/ppermute | solution.py:433
  43.4 12.0 %collective-permute-start.12 = (bf16[128,768]{1,0:T(8,128)(2,1)S(1)}, bf16[128,768]{1,0:T(8,128)(2,1)S(1)}, u32[]{:S(2)}, u32[]{:S(2)}) collective-permute-start(bf16[128,768]{1,0:T(8,128)(2,1)S(1)} %shard_map.147.before_ref), channel_id=1, source_target_pairs={{0,8},{1,9},{2,10},{3,11},{4,12},{5,13},{6,14},{7,15},{8,0},{9,1},... | collective-permute-start | bytes 589832 | tf_op jit(solution)/shard_map/ppermute | solution.py:433
  45.1 5.0 %collective-permute-start.10 = (f32[128,128]{1,0:T(8,128)S(1)}, f32[128,128]{1,0:T(8,128)S(1)}, u32[]{:S(2)}, u32[]{:S(2)}) collective-permute-start(f32[128,128]{1,0:T(8,128)S(1)} %shard_map.151.before_ref.left_ref), channel_id=1, source_target_pairs={{0,24},{1,25},{2,26},{3,27},{4,28},{5,29},{6,30},{7,31},{8,16},{9,... | collective-permute-start | bytes 196616 | tf_op jit(solution)/shard_map/ppermute | solution.py:433
  47.4 11.7 %collective-permute-start.14 = (bf16[128,768]{1,0:T(8,128)(2,1)S(1)}, bf16[128,768]{1,0:T(8,128)(2,1)S(1)}, u32[]{:S(2)}, u32[]{:S(2)}) collective-permute-start(bf16[128,768]{1,0:T(8,128)(2,1)S(1)} %shard_map.145.before_ref), channel_id=1, source_target_pairs={{0,2},{1,3},{2,0},{3,1},{4,6},{5,7},{6,4},{7,5},{8,10},{9,11},{10,... | collective-permute-start | bytes 589832 | tf_op jit(solution)/shard_map/ppermute | solution.py:433
  50.1 6.4 %collective-permute-start.13 = (f32[128,128]{1,0:T(8,128)S(1)}, f32[128,128]{1,0:T(8,128)S(1)}, u32[]{:S(2)}, u32[]{:S(2)}) collective-permute-start(f32[128,128]{1,0:T(8,128)S(1)} %shard_map.153.before_ref.left_ref), channel_id=1, source_target_pairs={{0,2},{1,3},{2,0},{3,1},{4,6},{5,7},{6,4},{7,5},{8,10},{9,11},{10,... | collective-permute-start | bytes 196616 | tf_op jit(solution)/shard_map/ppermute | solution.py:433
  50.2 15.0 %collective-permute-start.16 = (bf16[128,768]{1,0:T(8,128)(2,1)S(1)}, bf16[128,768]{1,0:T(8,128)(2,1)S(1)}, u32[]{:S(2)}, u32[]{:S(2)}) collective-permute-start(bf16[128,768]{1,0:T(8,128)(2,1)S(1)} %shard_map.148.before_ref), channel_id=1, source_target_pairs={{0,1},{1,0},{2,3},{3,2},{4,5},{5,4},{6,7},{7,6},{8,9},{9,8},{10,11... | collective-permute-start | bytes 589832 | tf_op jit(solution)/shard_map/ppermute | solution.py:433
  56.5 4.4 %collective-permute-start.15 = (f32[128,128]{1,0:T(8,128)S(1)}, f32[128,128]{1,0:T(8,128)S(1)}, u32[]{:S(2)}, u32[]{:S(2)}) collective-permute-start(f32[128,128]{1,0:T(8,128)S(1)} %shard_map.155.before_ref.left_ref), channel_id=1, source_target_pairs={{0,6},{1,7},{2,4},{3,5},{4,2},{5,3},{6,0},{7,1},{8,14},{9,15},{10,... | collective-permute-start | bytes 196616 | tf_op jit(solution)/shard_map/ppermute | solution.py:433
  61.0 6.4 %collective-permute-start.17 = (f32[128,128]{1,0:T(8,128)S(1)}, f32[128,128]{1,0:T(8,128)S(1)}, u32[]{:S(2)}, u32[]{:S(2)}) collective-permute-start(f32[128,128]{1,0:T(8,128)S(1)} %shard_map.157.before_ref.total_ref), channel_id=1, source_target_pairs={{0,1},{1,0},{2,3},{3,2},{4,5},{5,4},{6,7},{7,6},{8,9},{9,8},{10,11... | collective-permute-start | bytes 196616 | tf_op jit(solution)/shard_map/ppermute | solution.py:433

commit v10 on v7

--- a/solution.py
+++ b/solution.py
@@ -378,38 +378,42 @@
     )(send_rows, pinned(acc), before, *returned)
 
 
-def add_kernel(left_ref, right_ref, before_ref, out_ref):
-    out_ref[...] = left_ref[...] + right_ref[...]
-
-
-def added(left, right, before):
+def add_kernel(left_ref, before_ref, *refs):
+    others, out_ref = refs[:-1], refs[-1]
+    total = left_ref[...] + others[0][...]
+    if len(others) == 3:
+        total = total + (others[1][...] + others[2][...])
+    out_ref[...] = total
+
+
+def added(left, others, before):
     return pl.pallas_call(
         add_kernel,
         out_shape=VMEM(left.shape, jnp.float32),
-        in_specs=[vspec()] * 2 + [pl.BlockSpec(memory_space=pl.ANY)],
+        in_specs=[vspec(), pl.BlockSpec(memory_space=pl.ANY)] + [vspec()] * len(others),
         out_specs=vspec(),
         compiler_params=params(1024 * 1024),
         cost_estimate=cost(1, 1),
-    )(pinned(left), right, before)
-
-
-def halves_kernel(scale, total_ref, other_ref, self_ref, neigh_ref):
+    )(pinned(left), before, *others)
+
+
+def halves_kernel(scale, total_ref, other_ref, before_ref, self_ref, neigh_ref):
     core = lax.axis_index("dom") & 1
     total, other = total_ref[...], other_ref[...]
     self_ref[...] = jnp.where(core == 0, total, other) * scale
     neigh_ref[...] = jnp.where(core == 0, other, total) * scale
 
 
-def halves(scale, total, other):
+def halves(scale, total, other, before):
     out = jax.ShapeDtypeStruct(total.shape, jnp.float32)
     return pl.pallas_call(
         functools.partial(halves_kernel, scale),
         out_shape=[out, out],
-        in_specs=[vspec()] * 2,
+        in_specs=[vspec()] * 2 + [pl.BlockSpec(memory_space=pl.ANY)],
         out_specs=[vspec()] * 2,
         compiler_params=params(1024 * 1024),
         cost_estimate=cost(2 * total.size, 4 * total.size * 4),
-    )(pinned(total), other)
+    )(pinned(total), other, before)
 
 
 def swapped(shard, mask):
@@ -462,32 +466,29 @@
         got = [returned[r] for r in rounds]
         return place_rows(rounds, 0 in rounds, send_rows, acc, got, before)
 
-    other = swapped(give, 1)
+    others = [swapped(give, 1)]
     last = send_back(2, scaled_t)
-    total = added(mine, other, last)
-    other = swapped(total, 32)
+    total = added(mine, others, last)
+    others = [swapped(total, mask) for mask in (32, 64, 96)]
     last = send_back(4, total)
-    total = added(total, other, last)
-    other = swapped(total, 96)
-    last = send_back(1, total)
-    last = send_back(3, last)
-    total = added(total, other, last)
-    other = swapped(total, 8)
-    last = send_back(0, total)
-    grads_t = own(scaled_t, dl0, dl1, grad_pre, w_self, last)
-    total = added(total, other, grads_t)
-    other = swapped(total, 24)
-    grads_t, last = place((2, 4), grads_t, total)
-    total = added(total, other, last)
-    other = swapped(total, 2)
-    grads_t, last = place((3, 1), grads_t, total)
-    total = added(total, other, last)
-    other = swapped(total, 6)
+    last = send_back(1, last)
+    total = added(total, others, last)
+    others = [swapped(total, 8)]
+    last = send_back(3, total)
+    total = added(total, others, last)
+    others = [swapped(total, 24)]
+    grads_t = own(scaled_t, dl0, dl1, grad_pre, w_self, total)
+    last = send_back(0, grads_t)
+    total = added(total, others, last)
+    others = [swapped(total, mask) for mask in (2, 4, 6)]
+    grads_t, last = place((2,), grads_t, total)
+    grads_t, last = place((4,), grads_t, last)
+    grads_t, last = place((3, 1), grads_t, last)
+    total = added(total, others, last)
+    other = swapped(total, 1)
     grads, last = place((0,), grads_t, total)
-    total = added(total, other, last)
-    other = swapped(total, 1)
     grad_scale = 1.0 / math.sqrt(row_count * lax.axis_size("dom"))
-    grad_self, grad_neigh = halves(grad_scale, total, other)
+    grad_self, grad_neigh = halves(grad_scale, total, other, last)
     return (output, grads, grad_self, grad_neigh)
 
 

time: 66.9 us -> 64.5 us (0.964)
  starting transfers between devices: 28.7 us -> 26.3 us
    ppermute x18 -> x20, starting transfers between devices: 28.7 us -> 26.3 us  [swapped(): lax.ppermute(shard, 'dom', [(i, i ^ mask) for i in range(lax.axis_size('d...]
    ppermute x18 -> x20, waiting for transfers between devices: 7.42 us -> 7.1 us  [swapped(): lax.ppermute(shard, 'dom', [(i, i ^ mask) for i in range(lax.axis_size('d...]
    pallas_call x3 -> x4, Pallas kernels: 4.03 us -> 4.28 us  [place_rows(): pl.pallas_call(functools.partial(place_kernel, rounds, last), out_shape=[...]
  transfers between devices with their start and end apart: 18 -> 20, of which waited for: 7 -> 6; matrix products, arithmetic and copies ran while one was open for 0% -> 0% of each run, Pallas kernels for 29% -> 30%
where the time goes in v10:
time: 64.5 us; the launch traced here: 64.3 us
  Pallas kernels  29.9 us (46%)
  starting transfers between devices  26.3 us (41%)
  waiting for transfers between devices  7.1 us (11%)
  between operations  0.94 us (1%)
    ppermute x20, starting transfers between devices, swapped(): lax.ppermute(shard, 'dom', [(i, i ^ mask) for i in range(lax.axis_size('d...  26.3 us
    pallas_call x1, Pallas kernels, densify(): pl.pallas_call(densify_kernel, out_shape=[VMEM((n, half, TILE), jnp.bfloa...  8.48 us
    ppermute x20, waiting for transfers between devices, swapped(): lax.ppermute(shard, 'dom', [(i, i ^ mask) for i in range(lax.axis_size('d...  7.1 us
    pallas_call x1, Pallas kernels, middle(): pl.pallas_call(functools.partial(middle_kernel, rounds), out_shape=[half,...  6.21 us
    pallas_call x4, Pallas kernels, place_rows(): pl.pallas_call(functools.partial(place_kernel, rounds, last), out_shape=[...  4.28 us
    pallas_call x1, Pallas kernels, pick_rows(): pl.pallas_call(pick_kernel, out_shape=outs, in_specs=[pl.BlockSpec(memory...  3.58 us
    pallas_call x5, Pallas kernels, back(): pl.pallas_call(functools.partial(back_kernel, first, n), out_shape=jax.Sh...  2.91 us
    pallas_call x1, Pallas kernels, local_sums(): pl.pallas_call(local_sums_kernel, out_shape=VMEM((rows, width), jnp.float...  2.31 us
  transfers between devices with their start and end apart: 20, of which 6 were waited for; matrix products, arithmetic and copies ran while one was open for 0% of the time, Pallas kernels for 30%

profile of v10, /device:TPU:1, one launch (start us, length us, event | category | flops | bytes accessed | tf_op | source)
XLA Modules:
  0.0 64.3 jit_solution(8189384195842556760)
XLA Ops:
  0.6 3.6 %shard_map.138 = (bf16[128,768]{1,0:T(8,128)(2,1)S(1)}, bf16[128,768]{1,0:T(8,128)(2,1)S(1)}, bf16[128,768]{1,0:T(8,128)(2,1)S(1)}, bf16[128,768]{1,0:T(8,128)(2,1)S(1)}, bf16[128,768]{1,0:T(8,128)(2,1)S(1)}) custom-call(s32[5,768]{1,0:T(8,128)} %rows_ref.7, bf16[2048,128]{1,0:T(8,128)(2,1)} %refs_8_.1), custom_call_target="tpu_custom_call" | custom-call | flops 2013265920 | bytes 1000000 | tf_op jit(solution)/shard_map/pallas_call | solution.py:75
  4.2 1.5 %collective-permute-start = (bf16[128,768]{1,0:T(8,128)(2,1)S(1)}, bf16[128,768]{1,0:T(8,128)(2,1)S(1)}, u32[]{:S(2)}, u32[]{:S(2)}) collective-permute-start(bf16[128,768]{1,0:T(8,128)(2,1)S(1)} %get-tuple-element.28), channel_id=1, source_target_pairs={{0,1},{1,0},{2,3},{3,2},{4,5},{5,4},{6,7},{7,6},{8,9},{9,8},{10,11... | collective-permute-start | bytes 589832 | tf_op jit(solution)/shard_map/ppermute | solution.py:420
  5.7 1.7 %collective-permute-start.1 = (bf16[128,768]{1,0:T(8,128)(2,1)S(1)}, bf16[128,768]{1,0:T(8,128)(2,1)S(1)}, u32[]{:S(2)}, u32[]{:S(2)}) collective-permute-start(bf16[128,768]{1,0:T(8,128)(2,1)S(1)} %get-tuple-element.29), channel_id=1, source_target_pairs={{0,2},{1,3},{2,0},{3,1},{4,6},{5,7},{6,4},{7,5},{8,10},{9,11},{10,... | collective-permute-start | bytes 589832 | tf_op jit(solution)/shard_map/ppermute | solution.py:420
  7.5 3.3 %collective-permute-start.2 = (bf16[128,768]{1,0:T(8,128)(2,1)S(1)}, bf16[128,768]{1,0:T(8,128)(2,1)S(1)}, u32[]{:S(2)}, u32[]{:S(2)}) collective-permute-start(bf16[128,768]{1,0:T(8,128)(2,1)S(1)} %get-tuple-element.30), channel_id=1, source_target_pairs={{0,4},{1,5},{2,6},{3,7},{4,0},{5,1},{6,2},{7,3},{8,12},{9,13},{10,... | collective-permute-start | bytes 589832 | tf_op jit(solution)/shard_map/ppermute | solution.py:420
  10.8 1.2 %collective-permute-start.3 = (bf16[128,768]{1,0:T(8,128)(2,1)S(1)}, bf16[128,768]{1,0:T(8,128)(2,1)S(1)}, u32[]{:S(2)}, u32[]{:S(2)}) collective-permute-start(bf16[128,768]{1,0:T(8,128)(2,1)S(1)} %get-tuple-element.31), channel_id=1, source_target_pairs={{0,8},{1,9},{2,10},{3,11},{4,12},{5,13},{6,14},{7,15},{8,0},{9,1},... | collective-permute-start | bytes 589832 | tf_op jit(solution)/shard_map/ppermute | solution.py:420
  12.0 2.5 %collective-permute-start.4 = (bf16[128,768]{1,0:T(8,128)(2,1)S(1)}, bf16[128,768]{1,0:T(8,128)(2,1)S(1)}, u32[]{:S(2)}, u32[]{:S(2)}) collective-permute-start(bf16[128,768]{1,0:T(8,128)(2,1)S(1)} %get-tuple-element.32), channel_id=1, source_target_pairs={{0,16},{1,17},{2,18},{3,19},{4,20},{5,21},{6,22},{7,23},{8,24},{9,... | collective-permute-start | bytes 589832 | tf_op jit(solution)/shard_map/ppermute | solution.py:420
  14.4 8.5 %shard_map.139 = (bf16[16,1024,128]{2,1,0:T(8,128)(2,1)S(1)}, bf16[16,1024,128]{2,1,0:T(8,128)(2,1)S(1)}, bf16[30,1024,128]{2,1,0:T(8,128)(2,1)S(1)}, bf16[30,1024,128]{2,1,0:T(8,128)(2,1)S(1)}) custom-call(s32[16,22]{1,0:T(8,128)} %lc_hbm.1, s32[16,20]{1,0:T(8,128)} %hc_hbm.1, bf16[16,22,128,128]{3,2,1,0:T(8,128)(2,1)} %lt.1, bf16[16,20,128,128]{3,2,1,0:T(8,128)(2,1)} %ht.1), custom_call_target="tpu_custom_call" | custom-call | flops 16000000 | bytes 22020096 | tf_op jit(solution)/shard_map/pallas_call | solution.py:170
  22.9 0.0 copy-start.1
  22.9 0.0 copy-start.3
  22.9 0.0 copy-start.4
  22.9 0.0 copy-start.5
  23.0 0.0 copy-start.6
  23.0 2.3 %shard_map.140.refs_7_ = f32[2048,128]{1,0:T(8,128)S(1)} custom-call(bf16[16,1024,128]{2,1,0:T(8,128)(2,1)S(1)} %get-tuple-element.35.d0_ref, bf16[16,1024,128]{2,1,0:T(8,128)(2,1)S(1)} %get-tuple-element.36.d1_ref, bf16[2048,128]{1,0:T(8,128)(2,1)S(1)} %copy-done), custom_call_target="tpu_custom_call" | custom-call | flops 1073741824 | bytes 1500000 | tf_op jit(solution)/shard_map/pallas_call | solution.py:202
  25.3 0.0 collective-permute-done.refs_0_
  25.4 6.2 %shard_map.141 = (bf16[2048,128]{1,0:T(8,128)(2,1)}, bf16[2048,128]{1,0:T(8,128)(2,1)S(1)}, bf16[128,2048]{1,0:T(8,128)(2,1)S(1)}, f32[128,128]{1,0:T(8,128)S(1)}, f32[128,128]{1,0:T(8,128)S(1)}) custom-call(bf16[128,768]{1,0:T(8,128)(2,1)S(1)} %collective-permute-done.refs_0_, bf16[128,768]{1,0:T(8,128)(2,1)S(1)} %collective-permute-done.1.refs_1_, ...), custom_call_target="tpu_custom_call" | custom-call | flops 2013265920 | bytes 5000000 | tf_op jit(solution)/shard_map/pallas_call | solution.py:262
  31.6 1.2 %collective-permute-start.5 = (f32[128,128]{1,0:T(8,128)S(1)}, f32[128,128]{1,0:T(8,128)S(1)}, u32[]{:S(2)}, u32[]{:S(2)}) collective-permute-start(f32[128,128]{1,0:T(8,128)S(1)} %get-tuple-element.41), channel_id=1, source_target_pairs={{0,1},{1,0},{2,3},{3,2},{4,5},{5,4},{6,7},{7,6},{8,9},{9,8},{10,11... | collective-permute-start | bytes 196616 | tf_op jit(solution)/shard_map/ppermute | solution.py:420
  32.8 0.6 shard_map.142.before_ref
  33.4 0.3 collective-permute-done.5.refs_0_
  33.7 2.8 %collective-permute-start.8 = (f32[128,128]{1,0:T(8,128)S(1)}, f32[128,128]{1,0:T(8,128)S(1)}, u32[]{:S(2)}, u32[]{:S(2)}) collective-permute-start(f32[128,128]{1,0:T(8,128)S(1)} %shard_map.143.before_ref.left_ref), channel_id=1, source_target_pairs={{0,96},{1,97},{2,98},{3,99},{4,100},{5,101},{6,102},{7,103},{8,104... | collective-permute-start | bytes 196616 | tf_op jit(solution)/shard_map/ppermute | solution.py:420
  36.5 0.3 collective-permute-start.7
  36.9 0.3 collective-permute-start.6
  37.2 0.6 shard_map.144.before_ref
  37.8 0.1 collective-permute-start.11
  37.9 0.6 shard_map.145.before_ref
  38.5 0.1 collective-permute-start.14
  38.6 2.6 %collective-permute-done.7.refs_1_ = f32[128,128]{1,0:T(8,128)S(1)} collective-permute-done((f32[128,128]{1,0:T(8,128)S(1)}, f32[128,128]{1,0:T(8,128)S(1)}, u32[]{:S(2)}, u32[]{:S(2)}) %collective-permute-start.7) | collective-permute-done | bytes 65568 | tf_op jit(solution)/shard_map/ppermute | solution.py:420
  41.2 0.1 collective-permute-start.9
  41.3 1.4 %collective-permute-start.12 = (bf16[128,768]{1,0:T(8,128)(2,1)S(1)}, bf16[128,768]{1,0:T(8,128)(2,1)S(1)}, u32[]{:S(2)}, u32[]{:S(2)}) collective-permute-start(bf16[128,768]{1,0:T(8,128)(2,1)S(1)} %shard_map.144.before_ref), channel_id=1, source_target_pairs={{0,16},{1,17},{2,18},{3,19},{4,20},{5,21},{6,22},{7,23},{8,24},{9,... | collective-permute-start | bytes 589832 | tf_op jit(solution)/shard_map/ppermute | solution.py:420
  42.6 0.6 shard_map.147.before_ref
  43.2 0.2 collective-permute-start.13
  43.4 1.3 %collective-permute-done.9.refs_0_ = f32[128,128]{1,0:T(8,128)S(1)} collective-permute-done((f32[128,128]{1,0:T(8,128)S(1)}, f32[128,128]{1,0:T(8,128)S(1)}, u32[]{:S(2)}, u32[]{:S(2)}) %collective-permute-start.9) | collective-permute-done | bytes 65568 | tf_op jit(solution)/shard_map/ppermute | solution.py:420
  44.7 1.2 %collective-permute-start.10 = (f32[128,128]{1,0:T(8,128)S(1)}, f32[128,128]{1,0:T(8,128)S(1)}, u32[]{:S(2)}, u32[]{:S(2)}) collective-permute-start(f32[128,128]{1,0:T(8,128)S(1)} %shard_map.148.before_ref.left_ref), channel_id=1, source_target_pairs={{0,24},{1,25},{2,26},{3,27},{4,28},{5,29},{6,30},{7,31},{8,16},{9,... | collective-permute-start | bytes 196616 | tf_op jit(solution)/shard_map/ppermute | solution.py:420
  45.9 1.4 %shard_map.149.before_ref.acc_ref = f32[128,2048]{1,0:T(8,128)S(1)} custom-call(bf16[128,2048]{1,0:T(8,128)(2,1)S(1)} %get-tuple-element.38.st_ref.before_ref, bf16[16,1024,128]{2,1,0:T(8,128)(2,1)S(1)} %get-tuple-element.35.d0_ref, bf16[16,1024,128]{2,1,0:T(8,128)(2,1)S(1)} %get-tuple-element.36.d1_ref, bf16[2048,128]{1,0:T(8,128)(2,1)S(1)} %get-tuple-element.39.gp_ref, ...), custom_call_target="tpu_custom_call" | custom-call | flops 1 | bytes 1 | tf_op jit(solution)/shard_map/pallas_call | solution.py:327
  47.4 0.0 copy-start.2
  47.4 0.6 shard_map.150.before_ref
  48.0 2.1 %collective-permute-done.10.refs_0_ = f32[128,128]{1,0:T(8,128)S(1)} collective-permute-done((f32[128,128]{1,0:T(8,128)S(1)}, f32[128,128]{1,0:T(8,128)S(1)}, u32[]{:S(2)}, u32[]{:S(2)}) %collective-permute-start.10) | collective-permute-done | bytes 65568 | tf_op jit(solution)/shard_map/ppermute | solution.py:420
  50.1 3.9 %collective-permute-start.18 = (bf16[128,768]{1,0:T(8,128)(2,1)S(1)}, bf16[128,768]{1,0:T(8,128)(2,1)S(1)}, u32[]{:S(2)}, u32[]{:S(2)}) collective-permute-start(bf16[128,768]{1,0:T(8,128)(2,1)S(1)} %shard_map.150.before_ref), channel_id=1, source_target_pairs={{0,1},{1,0},{2,3},{3,2},{4,5},{5,4},{6,7},{7,6},{8,9},{9,8},{10,11... | collective-permute-start | bytes 589832 | tf_op jit(solution)/shard_map/ppermute | solution.py:420
  54.0 0.2 collective-permute-start.17
  54.2 1.1 %collective-permute-start.16 = (f32[128,128]{1,0:T(8,128)S(1)}, f32[128,128]{1,0:T(8,128)S(1)}, u32[]{:S(2)}, u32[]{:S(2)}) collective-permute-start(f32[128,128]{1,0:T(8,128)S(1)} %shard_map.151.before_ref.left_ref), channel_id=1, source_target_pairs={{0,4},{1,5},{2,6},{3,7},{4,0},{5,1},{6,2},{7,3},{8,12},{9,13},{10,... | collective-permute-start | bytes 196616 | tf_op jit(solution)/shard_map/ppermute | solution.py:420
  55.4 2.0 %collective-permute-start.15 = (f32[128,128]{1,0:T(8,128)S(1)}, f32[128,128]{1,0:T(8,128)S(1)}, u32[]{:S(2)}, u32[]{:S(2)}) collective-permute-start(f32[128,128]{1,0:T(8,128)S(1)} %shard_map.151.before_ref.left_ref), channel_id=1, source_target_pairs={{0,2},{1,3},{2,0},{3,1},{4,6},{5,7},{6,4},{7,5},{8,10},{9,11},{10,... | collective-permute-start | bytes 196616 | tf_op jit(solution)/shard_map/ppermute | solution.py:420
  57.3 0.7 %shard_map.152 = (f32[128,2048]{1,0:T(8,128)S(1)}, f32[8,128]{1,0:T(8,128)S(1)}) custom-call(s32[5,768]{1,0:T(8,128)S(1)} %copy-done.2, f32[128,2048]{1,0:T(8,128)S(1)} %shard_map.149.before_ref.acc_ref, f32[128,128]{1,0:T(8,128)S(1)} %shard_map.151.before_ref.left_ref, bf16[128,768]{1,0:T(8,128)(2,1)S(1)} %collective-permute-done.11.refs_0_), custom_call_target="tpu_custom_call" | custom-call | flops 1 | bytes 1 | tf_op jit(solution)/shard_map/pallas_call | solution.py:370
  58.0 0.7 %shard_map.153 = (f32[128,2048]{1,0:T(8,128)S(1)}, f32[8,128]{1,0:T(8,128)S(1)}) custom-call(s32[5,768]{1,0:T(8,128)S(1)} %copy-done.2, f32[128,2048]{1,0:T(8,128)S(1)} %get-tuple-element.42.acc_ref, f32[8,128]{1,0:T(8,128)S(1)} %get-tuple-element.43.before_ref, bf16[128,768]{1,0:T(8,128)(2,1)S(1)} %collective-permute-done.12.refs_0_), custom_call_target="tpu_custom_call" | custom-call | flops 1 | bytes 1 | tf_op jit(solution)/shard_map/pallas_call | solution.py:370
  58.7 1.1 %shard_map.154 = (f32[128,2048]{1,0:T(8,128)S(1)}, f32[8,128]{1,0:T(8,128)S(1)}) custom-call(s32[5,768]{1,0:T(8,128)S(1)} %copy-done.2, f32[128,2048]{1,0:T(8,128)S(1)} %get-tuple-element.44.acc_ref, f32[8,128]{1,0:T(8,128)S(1)} %get-tuple-element.45.before_ref, bf16[128,768]{1,0:T(8,128)(2,1)S(1)} %collective-permute-done.13.refs_0_, ...), custom_call_target="tpu_custom_call" | custom-call | flops 1 | bytes 1 | tf_op jit(solution)/shard_map/pallas_call | solution.py:370
  59.9 0.4 collective-permute-done.17.refs_2_
  60.3 0.4 collective-permute-done.15.refs_0_
  60.7 1.2 %collective-permute-start.19 = (f32[128,128]{1,0:T(8,128)S(1)}, f32[128,128]{1,0:T(8,128)S(1)}, u32[]{:S(2)}, u32[]{:S(2)}) collective-permute-start(f32[128,128]{1,0:T(8,128)S(1)} %shard_map.155.before_ref.total_ref), channel_id=1, source_target_pairs={{0,1},{1,0},{2,3},{3,2},{4,5},{5,4},{6,7},{7,6},{8,9},{9,8},{10,11... | collective-permute-start | bytes 196616 | tf_op jit(solution)/shard_map/ppermute | solution.py:420
  61.9 1.8 %shard_map.156 = (f32[2048,128]{1,0:T(8,128)}, f32[8,128]{1,0:T(8,128)S(1)}) custom-call(s32[5,768]{1,0:T(8,128)S(1)} %copy-done.2, f32[128,2048]{1,0:T(8,128)S(1)} %get-tuple-element.46.acc_ref, f32[128,128]{1,0:T(8,128)S(1)} %shard_map.155.before_ref.total_ref, bf16[128,768]{1,0:T(8,128)(2,1)S(1)} %collective-permute-done.18.refs_0_), custom_call_target="tpu_custom_call" | custom-call | flops 1 | bytes 1 | tf_op jit(solution)/shard_map/pallas_call | solution.py:370
  63.6 0.7 %shard_map.157 = (f32[128,128]{1,0:T(8,128)}, f32[128,128]{1,0:T(8,128)}) custom-call(f32[128,128]{1,0:T(8,128)S(1)} %shard_map.155.before_ref.total_ref, f32[128,128]{1,0:T(8,128)S(1)} %collective-permute-done.19.other_ref, f32[8,128]{1,0:T(8,128)S(1)} %get-tuple-element.49.before_ref), custom_call_target="tpu_custom_call" | custom-call | flops 32768 | bytes 262144 | tf_op jit(solution)/shard_map/pallas_call | solution.py:409
  (26 shorter events, 0.1 us)
Async XLA Ops:
  4.2 21.1 %collective-permute-start = (bf16[128,768]{1,0:T(8,128)(2,1)S(1)}, bf16[128,768]{1,0:T(8,128)(2,1)S(1)}, u32[]{:S(2)}, u32[]{:S(2)}) collective-permute-start(bf16[128,768]{1,0:T(8,128)(2,1)S(1)} %get-tuple-element.28), channel_id=1, source_target_pairs={{0,1},{1,0},{2,3},{3,2},{4,5},{5,4},{6,7},{7,6},{8,9},{9,8},{10,11... | collective-permute-start | bytes 589832 | tf_op jit(solution)/shard_map/ppermute | solution.py:420
  5.7 19.6 %collective-permute-start.1 = (bf16[128,768]{1,0:T(8,128)(2,1)S(1)}, bf16[128,768]{1,0:T(8,128)(2,1)S(1)}, u32[]{:S(2)}, u32[]{:S(2)}) collective-permute-start(bf16[128,768]{1,0:T(8,128)(2,1)S(1)} %get-tuple-element.29), channel_id=1, source_target_pairs={{0,2},{1,3},{2,0},{3,1},{4,6},{5,7},{6,4},{7,5},{8,10},{9,11},{10,... | collective-permute-start | bytes 589832 | tf_op jit(solution)/shard_map/ppermute | solution.py:420
  7.5 17.9 %collective-permute-start.2 = (bf16[128,768]{1,0:T(8,128)(2,1)S(1)}, bf16[128,768]{1,0:T(8,128)(2,1)S(1)}, u32[]{:S(2)}, u32[]{:S(2)}) collective-permute-start(bf16[128,768]{1,0:T(8,128)(2,1)S(1)} %get-tuple-element.30), channel_id=1, source_target_pairs={{0,4},{1,5},{2,6},{3,7},{4,0},{5,1},{6,2},{7,3},{8,12},{9,13},{10,... | collective-permute-start | bytes 589832 | tf_op jit(solution)/shard_map/ppermute | solution.py:420
  10.8 14.6 %collective-permute-start.3 = (bf16[128,768]{1,0:T(8,128)(2,1)S(1)}, bf16[128,768]{1,0:T(8,128)(2,1)S(1)}, u32[]{:S(2)}, u32[]{:S(2)}) collective-permute-start(bf16[128,768]{1,0:T(8,128)(2,1)S(1)} %get-tuple-element.31), channel_id=1, source_target_pairs={{0,8},{1,9},{2,10},{3,11},{4,12},{5,13},{6,14},{7,15},{8,0},{9,1},... | collective-permute-start | bytes 589832 | tf_op jit(solution)/shard_map/ppermute | solution.py:420
  12.0 11.0 %copy-start = (bf16[2048,128]{1,0:T(8,128)(2,1)S(1)}, bf16[2048,128]{1,0:T(8,128)(2,1)}, u32[]{:S(2)}) copy-start(bf16[2048,128]{1,0:T(8,128)(2,1)} %refs_8_.1) | copy-start | bytes 1572868
  12.0 13.4 %collective-permute-start.4 = (bf16[128,768]{1,0:T(8,128)(2,1)S(1)}, bf16[128,768]{1,0:T(8,128)(2,1)S(1)}, u32[]{:S(2)}, u32[]{:S(2)}) collective-permute-start(bf16[128,768]{1,0:T(8,128)(2,1)S(1)} %get-tuple-element.32), channel_id=1, source_target_pairs={{0,16},{1,17},{2,18},{3,19},{4,20},{5,21},{6,22},{7,23},{8,24},{9,... | collective-permute-start | bytes 589832 | tf_op jit(solution)/shard_map/ppermute | solution.py:420
  22.9 2.4 %copy-start.1 = (bf16[2048,128]{1,0:T(8,128)(2,1)S(1)}, bf16[2048,128]{1,0:T(8,128)(2,1)}, u32[]{:S(2)}) copy-start(bf16[2048,128]{1,0:T(8,128)(2,1)} %refs_9_.1) | copy-start | bytes 1572868
  22.9 2.4 %copy-start.3 = (bf16[128,128]{1,0:T(8,128)(2,1)S(1)}, bf16[128,128]{1,0:T(8,128)(2,1)}, u32[]{:S(2)}) copy-start(bf16[128,128]{1,0:T(8,128)(2,1)} %ws_ref.1) | copy-start | bytes 98308
  22.9 2.4 %copy-start.4 = (bf16[128,128]{1,0:T(8,128)(2,1)S(1)}, bf16[128,128]{1,0:T(8,128)(2,1)}, u32[]{:S(2)}) copy-start(bf16[128,128]{1,0:T(8,128)(2,1)} %refs_12_.1) | copy-start | bytes 98308
  22.9 2.4 %copy-start.5 = (s32[2048]{0:T(1024)S(1)}, s32[2048]{0:T(1024)}, u32[]{:S(2)}) copy-start(s32[2048]{0:T(1024)} %param.20) | copy-start | bytes 24580
  23.0 2.4 %copy-start.6 = (f32[128]{0:T(128)S(1)}, f32[128]{0:T(128)}, u32[]{:S(2)}) copy-start(f32[128]{0:T(128)} %param.14) | copy-start | bytes 1540
  31.6 2.1 %collective-permute-start.5 = (f32[128,128]{1,0:T(8,128)S(1)}, f32[128,128]{1,0:T(8,128)S(1)}, u32[]{:S(2)}, u32[]{:S(2)}) collective-permute-start(f32[128,128]{1,0:T(8,128)S(1)} %get-tuple-element.41), channel_id=1, source_target_pairs={{0,1},{1,0},{2,3},{3,2},{4,5},{5,4},{6,7},{7,6},{8,9},{9,8},{10,11... | collective-permute-start | bytes 196616 | tf_op jit(solution)/shard_map/ppermute | solution.py:420
  33.7 4.9 %collective-permute-start.8 = (f32[128,128]{1,0:T(8,128)S(1)}, f32[128,128]{1,0:T(8,128)S(1)}, u32[]{:S(2)}, u32[]{:S(2)}) collective-permute-start(f32[128,128]{1,0:T(8,128)S(1)} %shard_map.143.before_ref.left_ref), channel_id=1, source_target_pairs={{0,96},{1,97},{2,98},{3,99},{4,100},{5,101},{6,102},{7,103},{8,104... | collective-permute-start | bytes 196616 | tf_op jit(solution)/shard_map/ppermute | solution.py:420
  36.5 4.6 %collective-permute-start.7 = (f32[128,128]{1,0:T(8,128)S(1)}, f32[128,128]{1,0:T(8,128)S(1)}, u32[]{:S(2)}, u32[]{:S(2)}) collective-permute-start(f32[128,128]{1,0:T(8,128)S(1)} %shard_map.143.before_ref.left_ref), channel_id=1, source_target_pairs={{0,64},{1,65},{2,66},{3,67},{4,68},{5,69},{6,70},{7,71},{8,72},{9,... | collective-permute-start | bytes 196616 | tf_op jit(solution)/shard_map/ppermute | solution.py:420
  36.9 4.3 %collective-permute-start.6 = (f32[128,128]{1,0:T(8,128)S(1)}, f32[128,128]{1,0:T(8,128)S(1)}, u32[]{:S(2)}, u32[]{:S(2)}) collective-permute-start(f32[128,128]{1,0:T(8,128)S(1)} %shard_map.143.before_ref.left_ref), channel_id=1, source_target_pairs={{0,32},{1,33},{2,34},{3,35},{4,36},{5,37},{6,38},{7,39},{8,40},{9,... | collective-permute-start | bytes 196616 | tf_op jit(solution)/shard_map/ppermute | solution.py:420
  37.8 16.2 %collective-permute-start.11 = (bf16[128,768]{1,0:T(8,128)(2,1)S(1)}, bf16[128,768]{1,0:T(8,128)(2,1)S(1)}, u32[]{:S(2)}, u32[]{:S(2)}) collective-permute-start(bf16[128,768]{1,0:T(8,128)(2,1)S(1)} %shard_map.142.before_ref), channel_id=1, source_target_pairs={{0,4},{1,5},{2,6},{3,7},{4,0},{5,1},{6,2},{7,3},{8,12},{9,13},{10,... | collective-permute-start | bytes 589832 | tf_op jit(solution)/shard_map/ppermute | solution.py:420
  38.5 15.7 %collective-permute-start.14 = (bf16[128,768]{1,0:T(8,128)(2,1)S(1)}, bf16[128,768]{1,0:T(8,128)(2,1)S(1)}, u32[]{:S(2)}, u32[]{:S(2)}) collective-permute-start(bf16[128,768]{1,0:T(8,128)(2,1)S(1)} %shard_map.145.before_ref), channel_id=1, source_target_pairs={{0,2},{1,3},{2,0},{3,1},{4,6},{5,7},{6,4},{7,5},{8,10},{9,11},{10,... | collective-permute-start | bytes 589832 | tf_op jit(solution)/shard_map/ppermute | solution.py:420
  41.2 3.5 %collective-permute-start.9 = (f32[128,128]{1,0:T(8,128)S(1)}, f32[128,128]{1,0:T(8,128)S(1)}, u32[]{:S(2)}, u32[]{:S(2)}) collective-permute-start(f32[128,128]{1,0:T(8,128)S(1)} %shard_map.146.before_ref.left_ref), channel_id=1, source_target_pairs={{0,8},{1,9},{2,10},{3,11},{4,12},{5,13},{6,14},{7,15},{8,0},{9,1},... | collective-permute-start | bytes 196616 | tf_op jit(solution)/shard_map/ppermute | solution.py:420
  41.3 14.1 %collective-permute-start.12 = (bf16[128,768]{1,0:T(8,128)(2,1)S(1)}, bf16[128,768]{1,0:T(8,128)(2,1)S(1)}, u32[]{:S(2)}, u32[]{:S(2)}) collective-permute-start(bf16[128,768]{1,0:T(8,128)(2,1)S(1)} %shard_map.144.before_ref), channel_id=1, source_target_pairs={{0,16},{1,17},{2,18},{3,19},{4,20},{5,21},{6,22},{7,23},{8,24},{9,... | collective-permute-start | bytes 589832 | tf_op jit(solution)/shard_map/ppermute | solution.py:420
  43.2 15.5 %collective-permute-start.13 = (bf16[128,768]{1,0:T(8,128)(2,1)S(1)}, bf16[128,768]{1,0:T(8,128)(2,1)S(1)}, u32[]{:S(2)}, u32[]{:S(2)}) collective-permute-start(bf16[128,768]{1,0:T(8,128)(2,1)S(1)} %shard_map.147.before_ref), channel_id=1, source_target_pairs={{0,8},{1,9},{2,10},{3,11},{4,12},{5,13},{6,14},{7,15},{8,0},{9,1},... | collective-permute-start | bytes 589832 | tf_op jit(solution)/shard_map/ppermute | solution.py:420
  44.7 5.4 %collective-permute-start.10 = (f32[128,128]{1,0:T(8,128)S(1)}, f32[128,128]{1,0:T(8,128)S(1)}, u32[]{:S(2)}, u32[]{:S(2)}) collective-permute-start(f32[128,128]{1,0:T(8,128)S(1)} %shard_map.148.before_ref.left_ref), channel_id=1, source_target_pairs={{0,24},{1,25},{2,26},{3,27},{4,28},{5,29},{6,30},{7,31},{8,16},{9,... | collective-permute-start | bytes 196616 | tf_op jit(solution)/shard_map/ppermute | solution.py:420
  47.4 10.0 %copy-start.2 = (s32[5,768]{1,0:T(8,128)S(1)}, s32[5,768]{1,0:T(8,128)}, u32[]{:S(2)}) copy-start(s32[5,768]{1,0:T(8,128)} %rows_ref.7) | copy-start | bytes 46084
  50.1 11.8 %collective-permute-start.18 = (bf16[128,768]{1,0:T(8,128)(2,1)S(1)}, bf16[128,768]{1,0:T(8,128)(2,1)S(1)}, u32[]{:S(2)}, u32[]{:S(2)}) collective-permute-start(bf16[128,768]{1,0:T(8,128)(2,1)S(1)} %shard_map.150.before_ref), channel_id=1, source_target_pairs={{0,1},{1,0},{2,3},{3,2},{4,5},{5,4},{6,7},{7,6},{8,9},{9,8},{10,11... | collective-permute-start | bytes 589832 | tf_op jit(solution)/shard_map/ppermute | solution.py:420
  54.0 6.3 %collective-permute-start.17 = (f32[128,128]{1,0:T(8,128)S(1)}, f32[128,128]{1,0:T(8,128)S(1)}, u32[]{:S(2)}, u32[]{:S(2)}) collective-permute-start(f32[128,128]{1,0:T(8,128)S(1)} %shard_map.151.before_ref.left_ref), channel_id=1, source_target_pairs={{0,6},{1,7},{2,4},{3,5},{4,2},{5,3},{6,0},{7,1},{8,14},{9,15},{10,... | collective-permute-start | bytes 196616 | tf_op jit(solution)/shard_map/ppermute | solution.py:420
  54.2 6.0 %collective-permute-start.16 = (f32[128,128]{1,0:T(8,128)S(1)}, f32[128,128]{1,0:T(8,128)S(1)}, u32[]{:S(2)}, u32[]{:S(2)}) collective-permute-start(f32[128,128]{1,0:T(8,128)S(1)} %shard_map.151.before_ref.left_ref), channel_id=1, source_target_pairs={{0,4},{1,5},{2,6},{3,7},{4,0},{5,1},{6,2},{7,3},{8,12},{9,13},{10,... | collective-permute-start | bytes 196616 | tf_op jit(solution)/shard_map/ppermute | solution.py:420
  55.4 5.3 %collective-permute-start.15 = (f32[128,128]{1,0:T(8,128)S(1)}, f32[128,128]{1,0:T(8,128)S(1)}, u32[]{:S(2)}, u32[]{:S(2)}) collective-permute-start(f32[128,128]{1,0:T(8,128)S(1)} %shard_map.151.before_ref.left_ref), channel_id=1, source_target_pairs={{0,2},{1,3},{2,0},{3,1},{4,6},{5,7},{6,4},{7,5},{8,10},{9,11},{10,... | collective-permute-start | bytes 196616 | tf_op jit(solution)/shard_map/ppermute | solution.py:420
  60.7 3.0 %collective-permute-start.19 = (f32[128,128]{1,0:T(8,128)S(1)}, f32[128,128]{1,0:T(8,128)S(1)}, u32[]{:S(2)}, u32[]{:S(2)}) collective-permute-start(f32[128,128]{1,0:T(8,128)S(1)} %shard_map.155.before_ref.total_ref), channel_id=1, source_target_pairs={{0,1},{1,0},{2,3},{3,2},{4,5},{5,4},{6,7},{7,6},{8,9},{9,8},{10,11... | collective-permute-start | bytes 196616 | tf_op jit(solution)/shard_map/ppermute | solution.py:420

commit v11 on v10

--- a/solution.py
+++ b/solution.py
@@ -468,22 +468,22 @@
 
     others = [swapped(give, 1)]
     last = send_back(2, scaled_t)
+    last = send_back(4, last)
     total = added(mine, others, last)
     others = [swapped(total, mask) for mask in (32, 64, 96)]
-    last = send_back(4, total)
-    last = send_back(1, last)
+    last = send_back(1, total)
     total = added(total, others, last)
-    others = [swapped(total, 8)]
+    others = [swapped(total, mask) for mask in (8,)]
     last = send_back(3, total)
     total = added(total, others, last)
-    others = [swapped(total, 24)]
+    others = [swapped(total, mask) for mask in (24,)]
     grads_t = own(scaled_t, dl0, dl1, grad_pre, w_self, total)
     last = send_back(0, grads_t)
     total = added(total, others, last)
     others = [swapped(total, mask) for mask in (2, 4, 6)]
     grads_t, last = place((2,), grads_t, total)
     grads_t, last = place((4,), grads_t, last)
-    grads_t, last = place((3, 1), grads_t, last)
+    grads_t, last = place((3,1,), grads_t, last)
     total = added(total, others, last)
     other = swapped(total, 1)
     grads, last = place((0,), grads_t, total)

time: 64.5 us -> 64.5 us (level)
  starting transfers between devices: 26.3 us -> 27.6 us
  waiting for transfers between devices: 7.1 us -> 5.8 us
    ppermute x20, starting transfers between devices: 26.3 us -> 27.6 us  [swapped(): lax.ppermute(shard, 'dom', [(i, i ^ mask) for i in range(lax.axis_size('d...]
    ppermute x20, waiting for transfers between devices: 7.1 us -> 5.8 us  [swapped(): lax.ppermute(shard, 'dom', [(i, i ^ mask) for i in range(lax.axis_size('d...]
where the time goes in v11:
time: 64.5 us; the launch traced here: 64.4 us
  Pallas kernels  29.9 us (46%)
  starting transfers between devices  27.6 us (43%)
  waiting for transfers between devices  5.8 us (9%)
  between operations  0.95 us (1%)
    ppermute x20, starting transfers between devices, swapped(): lax.ppermute(shard, 'dom', [(i, i ^ mask) for i in range(lax.axis_size('d...  27.6 us
    pallas_call x1, Pallas kernels, densify(): pl.pallas_call(densify_kernel, out_shape=[VMEM((n, half, TILE), jnp.bfloa...  8.48 us
    pallas_call x1, Pallas kernels, middle(): pl.pallas_call(functools.partial(middle_kernel, rounds), out_shape=[half,...  6.21 us
    ppermute x20, waiting for transfers between devices, swapped(): lax.ppermute(shard, 'dom', [(i, i ^ mask) for i in range(lax.axis_size('d...  5.8 us
    pallas_call x4, Pallas kernels, place_rows(): pl.pallas_call(functools.partial(place_kernel, rounds, last), out_shape=[...  4.28 us
    pallas_call x1, Pallas kernels, pick_rows(): pl.pallas_call(pick_kernel, out_shape=outs, in_specs=[pl.BlockSpec(memory...  3.58 us
    pallas_call x5, Pallas kernels, back(): pl.pallas_call(functools.partial(back_kernel, first, n), out_shape=jax.Sh...  2.92 us
    pallas_call x1, Pallas kernels, local_sums(): pl.pallas_call(local_sums_kernel, out_shape=VMEM((rows, width), jnp.float...  2.31 us
  transfers between devices with their start and end apart: 20, of which 6 were waited for; matrix products, arithmetic and copies ran while one was open for 0% of the time, Pallas kernels for 30%

profile of v11, /device:TPU:1, one launch (start us, length us, event | category | flops | bytes accessed | tf_op | source)
XLA Modules:
  0.0 64.4 jit_solution(1727481967042028884)
XLA Ops:
  0.6 3.6 %shard_map.138 = (bf16[128,768]{1,0:T(8,128)(2,1)S(1)}, bf16[128,768]{1,0:T(8,128)(2,1)S(1)}, bf16[128,768]{1,0:T(8,128)(2,1)S(1)}, bf16[128,768]{1,0:T(8,128)(2,1)S(1)}, bf16[128,768]{1,0:T(8,128)(2,1)S(1)}) custom-call(s32[5,768]{1,0:T(8,128)} %rows_ref.7, bf16[2048,128]{1,0:T(8,128)(2,1)} %refs_8_.1), custom_call_target="tpu_custom_call" | custom-call | flops 2013265920 | bytes 1000000 | tf_op jit(solution)/shard_map/pallas_call | solution.py:75
  4.2 1.5 %collective-permute-start = (bf16[128,768]{1,0:T(8,128)(2,1)S(1)}, bf16[128,768]{1,0:T(8,128)(2,1)S(1)}, u32[]{:S(2)}, u32[]{:S(2)}) collective-permute-start(bf16[128,768]{1,0:T(8,128)(2,1)S(1)} %get-tuple-element.28), channel_id=1, source_target_pairs={{0,1},{1,0},{2,3},{3,2},{4,5},{5,4},{6,7},{7,6},{8,9},{9,8},{10,11... | collective-permute-start | bytes 589832 | tf_op jit(solution)/shard_map/ppermute | solution.py:420
  5.7 1.7 %collective-permute-start.1 = (bf16[128,768]{1,0:T(8,128)(2,1)S(1)}, bf16[128,768]{1,0:T(8,128)(2,1)S(1)}, u32[]{:S(2)}, u32[]{:S(2)}) collective-permute-start(bf16[128,768]{1,0:T(8,128)(2,1)S(1)} %get-tuple-element.29), channel_id=1, source_target_pairs={{0,2},{1,3},{2,0},{3,1},{4,6},{5,7},{6,4},{7,5},{8,10},{9,11},{10,... | collective-permute-start | bytes 589832 | tf_op jit(solution)/shard_map/ppermute | solution.py:420
  7.5 3.3 %collective-permute-start.2 = (bf16[128,768]{1,0:T(8,128)(2,1)S(1)}, bf16[128,768]{1,0:T(8,128)(2,1)S(1)}, u32[]{:S(2)}, u32[]{:S(2)}) collective-permute-start(bf16[128,768]{1,0:T(8,128)(2,1)S(1)} %get-tuple-element.30), channel_id=1, source_target_pairs={{0,4},{1,5},{2,6},{3,7},{4,0},{5,1},{6,2},{7,3},{8,12},{9,13},{10,... | collective-permute-start | bytes 589832 | tf_op jit(solution)/shard_map/ppermute | solution.py:420
  10.8 1.2 %collective-permute-start.3 = (bf16[128,768]{1,0:T(8,128)(2,1)S(1)}, bf16[128,768]{1,0:T(8,128)(2,1)S(1)}, u32[]{:S(2)}, u32[]{:S(2)}) collective-permute-start(bf16[128,768]{1,0:T(8,128)(2,1)S(1)} %get-tuple-element.31), channel_id=1, source_target_pairs={{0,8},{1,9},{2,10},{3,11},{4,12},{5,13},{6,14},{7,15},{8,0},{9,1},... | collective-permute-start | bytes 589832 | tf_op jit(solution)/shard_map/ppermute | solution.py:420
  12.0 2.5 %collective-permute-start.4 = (bf16[128,768]{1,0:T(8,128)(2,1)S(1)}, bf16[128,768]{1,0:T(8,128)(2,1)S(1)}, u32[]{:S(2)}, u32[]{:S(2)}) collective-permute-start(bf16[128,768]{1,0:T(8,128)(2,1)S(1)} %get-tuple-element.32), channel_id=1, source_target_pairs={{0,16},{1,17},{2,18},{3,19},{4,20},{5,21},{6,22},{7,23},{8,24},{9,... | collective-permute-start | bytes 589832 | tf_op jit(solution)/shard_map/ppermute | solution.py:420
  14.4 8.5 %shard_map.139 = (bf16[16,1024,128]{2,1,0:T(8,128)(2,1)S(1)}, bf16[16,1024,128]{2,1,0:T(8,128)(2,1)S(1)}, bf16[30,1024,128]{2,1,0:T(8,128)(2,1)S(1)}, bf16[30,1024,128]{2,1,0:T(8,128)(2,1)S(1)}) custom-call(s32[16,22]{1,0:T(8,128)} %lc_hbm.1, s32[16,20]{1,0:T(8,128)} %hc_hbm.1, bf16[16,22,128,128]{3,2,1,0:T(8,128)(2,1)} %lt.1, bf16[16,20,128,128]{3,2,1,0:T(8,128)(2,1)} %ht.1), custom_call_target="tpu_custom_call" | custom-call | flops 16000000 | bytes 22020096 | tf_op jit(solution)/shard_map/pallas_call | solution.py:170
  22.9 0.0 copy-start.1
  22.9 0.0 copy-start.3
  22.9 0.0 copy-start.4
  22.9 0.0 copy-start.5
  23.0 0.0 copy-start.6
  23.0 2.3 %shard_map.140.refs_7_ = f32[2048,128]{1,0:T(8,128)S(1)} custom-call(bf16[16,1024,128]{2,1,0:T(8,128)(2,1)S(1)} %get-tuple-element.35.d0_ref, bf16[16,1024,128]{2,1,0:T(8,128)(2,1)S(1)} %get-tuple-element.36.d1_ref, bf16[2048,128]{1,0:T(8,128)(2,1)S(1)} %copy-done), custom_call_target="tpu_custom_call" | custom-call | flops 1073741824 | bytes 1500000 | tf_op jit(solution)/shard_map/pallas_call | solution.py:202
  25.3 0.0 collective-permute-done.refs_0_
  25.3 0.0 collective-permute-done.1.refs_1_
  25.4 6.2 %shard_map.141 = (bf16[2048,128]{1,0:T(8,128)(2,1)}, bf16[2048,128]{1,0:T(8,128)(2,1)S(1)}, bf16[128,2048]{1,0:T(8,128)(2,1)S(1)}, f32[128,128]{1,0:T(8,128)S(1)}, f32[128,128]{1,0:T(8,128)S(1)}) custom-call(bf16[128,768]{1,0:T(8,128)(2,1)S(1)} %collective-permute-done.refs_0_, bf16[128,768]{1,0:T(8,128)(2,1)S(1)} %collective-permute-done.1.refs_1_, ...), custom_call_target="tpu_custom_call" | custom-call | flops 2013265920 | bytes 5000000 | tf_op jit(solution)/shard_map/pallas_call | solution.py:262
  31.6 1.2 %collective-permute-start.5 = (f32[128,128]{1,0:T(8,128)S(1)}, f32[128,128]{1,0:T(8,128)S(1)}, u32[]{:S(2)}, u32[]{:S(2)}) collective-permute-start(f32[128,128]{1,0:T(8,128)S(1)} %get-tuple-element.41), channel_id=1, source_target_pairs={{0,1},{1,0},{2,3},{3,2},{4,5},{5,4},{6,7},{7,6},{8,9},{9,8},{10,11... | collective-permute-start | bytes 196616 | tf_op jit(solution)/shard_map/ppermute | solution.py:420
  32.8 0.6 shard_map.142.before_ref
  33.4 0.6 shard_map.143.before_ref
  34.0 3.0 %collective-permute-start.8 = (f32[128,128]{1,0:T(8,128)S(1)}, f32[128,128]{1,0:T(8,128)S(1)}, u32[]{:S(2)}, u32[]{:S(2)}) collective-permute-start(f32[128,128]{1,0:T(8,128)S(1)} %shard_map.144.before_ref.left_ref), channel_id=1, source_target_pairs={{0,96},{1,97},{2,98},{3,99},{4,100},{5,101},{6,102},{7,103},{8,104... | collective-permute-start | bytes 196616 | tf_op jit(solution)/shard_map/ppermute | solution.py:420
  37.0 0.3 collective-permute-start.7
  37.4 0.3 collective-permute-start.6
  37.7 0.5 collective-permute-start.12
  38.2 0.6 shard_map.145.before_ref
  38.8 0.8 %collective-permute-done.8.refs_2_ = f32[128,128]{1,0:T(8,128)S(1)} collective-permute-done((f32[128,128]{1,0:T(8,128)S(1)}, f32[128,128]{1,0:T(8,128)S(1)}, u32[]{:S(2)}, u32[]{:S(2)}) %collective-permute-start.8) | collective-permute-done | bytes 65568 | tf_op jit(solution)/shard_map/ppermute | solution.py:420
  39.6 2.0 %collective-permute-done.7.refs_1_ = f32[128,128]{1,0:T(8,128)S(1)} collective-permute-done((f32[128,128]{1,0:T(8,128)S(1)}, f32[128,128]{1,0:T(8,128)S(1)}, u32[]{:S(2)}, u32[]{:S(2)}) %collective-permute-start.7) | collective-permute-done | bytes 65568 | tf_op jit(solution)/shard_map/ppermute | solution.py:420
  41.7 0.1 collective-permute-start.9
  41.8 0.1 collective-permute-start.14
  41.9 0.6 shard_map.147.before_ref
  42.4 1.4 %collective-permute-start.13 = (bf16[128,768]{1,0:T(8,128)(2,1)S(1)}, bf16[128,768]{1,0:T(8,128)(2,1)S(1)}, u32[]{:S(2)}, u32[]{:S(2)}) collective-permute-start(bf16[128,768]{1,0:T(8,128)(2,1)S(1)} %shard_map.147.before_ref), channel_id=1, source_target_pairs={{0,8},{1,9},{2,10},{3,11},{4,12},{5,13},{6,14},{7,15},{8,0},{9,1},... | collective-permute-start | bytes 589832 | tf_op jit(solution)/shard_map/ppermute | solution.py:420
  43.9 1.3 %collective-permute-done.9.refs_0_ = f32[128,128]{1,0:T(8,128)S(1)} collective-permute-done((f32[128,128]{1,0:T(8,128)S(1)}, f32[128,128]{1,0:T(8,128)S(1)}, u32[]{:S(2)}, u32[]{:S(2)}) %collective-permute-start.9) | collective-permute-done | bytes 65568 | tf_op jit(solution)/shard_map/ppermute | solution.py:420
  45.2 1.5 %collective-permute-start.10 = (f32[128,128]{1,0:T(8,128)S(1)}, f32[128,128]{1,0:T(8,128)S(1)}, u32[]{:S(2)}, u32[]{:S(2)}) collective-permute-start(f32[128,128]{1,0:T(8,128)S(1)} %shard_map.148.before_ref.left_ref), channel_id=1, source_target_pairs={{0,24},{1,25},{2,26},{3,27},{4,28},{5,29},{6,30},{7,31},{8,16},{9,... | collective-permute-start | bytes 196616 | tf_op jit(solution)/shard_map/ppermute | solution.py:420
  46.7 1.4 %shard_map.149.before_ref.acc_ref = f32[128,2048]{1,0:T(8,128)S(1)} custom-call(bf16[128,2048]{1,0:T(8,128)(2,1)S(1)} %get-tuple-element.38.st_ref.before_ref, bf16[16,1024,128]{2,1,0:T(8,128)(2,1)S(1)} %get-tuple-element.35.d0_ref, bf16[16,1024,128]{2,1,0:T(8,128)(2,1)S(1)} %get-tuple-element.36.d1_ref, bf16[2048,128]{1,0:T(8,128)(2,1)S(1)} %get-tuple-element.39.gp_ref, ...), custom_call_target="tpu_custom_call" | custom-call | flops 1 | bytes 1 | tf_op jit(solution)/shard_map/pallas_call | solution.py:327
  48.1 0.0 copy-start.2
  48.1 0.6 shard_map.150.before_ref
  48.7 0.8 %collective-permute-done.10.refs_0_ = f32[128,128]{1,0:T(8,128)S(1)} collective-permute-done((f32[128,128]{1,0:T(8,128)S(1)}, f32[128,128]{1,0:T(8,128)S(1)}, u32[]{:S(2)}, u32[]{:S(2)}) %collective-permute-start.10) | collective-permute-done | bytes 65568 | tf_op jit(solution)/shard_map/ppermute | solution.py:420
  49.6 4.4 %collective-permute-start.18 = (bf16[128,768]{1,0:T(8,128)(2,1)S(1)}, bf16[128,768]{1,0:T(8,128)(2,1)S(1)}, u32[]{:S(2)}, u32[]{:S(2)}) collective-permute-start(bf16[128,768]{1,0:T(8,128)(2,1)S(1)} %shard_map.150.before_ref), channel_id=1, source_target_pairs={{0,1},{1,0},{2,3},{3,2},{4,5},{5,4},{6,7},{7,6},{8,9},{9,8},{10,11... | collective-permute-start | bytes 589832 | tf_op jit(solution)/shard_map/ppermute | solution.py:420
  54.0 0.1 collective-permute-start.17
  54.1 1.6 %collective-permute-start.16 = (f32[128,128]{1,0:T(8,128)S(1)}, f32[128,128]{1,0:T(8,128)S(1)}, u32[]{:S(2)}, u32[]{:S(2)}) collective-permute-start(f32[128,128]{1,0:T(8,128)S(1)} %shard_map.151.before_ref.left_ref), channel_id=1, source_target_pairs={{0,4},{1,5},{2,6},{3,7},{4,0},{5,1},{6,2},{7,3},{8,12},{9,13},{10,... | collective-permute-start | bytes 196616 | tf_op jit(solution)/shard_map/ppermute | solution.py:420
  55.8 1.6 %collective-permute-start.15 = (f32[128,128]{1,0:T(8,128)S(1)}, f32[128,128]{1,0:T(8,128)S(1)}, u32[]{:S(2)}, u32[]{:S(2)}) collective-permute-start(f32[128,128]{1,0:T(8,128)S(1)} %shard_map.151.before_ref.left_ref), channel_id=1, source_target_pairs={{0,2},{1,3},{2,0},{3,1},{4,6},{5,7},{6,4},{7,5},{8,10},{9,11},{10,... | collective-permute-start | bytes 196616 | tf_op jit(solution)/shard_map/ppermute | solution.py:420
  57.4 0.7 %shard_map.152 = (f32[128,2048]{1,0:T(8,128)S(1)}, f32[8,128]{1,0:T(8,128)S(1)}) custom-call(s32[5,768]{1,0:T(8,128)S(1)} %copy-done.2, f32[128,2048]{1,0:T(8,128)S(1)} %shard_map.149.before_ref.acc_ref, f32[128,128]{1,0:T(8,128)S(1)} %shard_map.151.before_ref.left_ref, bf16[128,768]{1,0:T(8,128)(2,1)S(1)} %collective-permute-done.11.refs_0_), custom_call_target="tpu_custom_call" | custom-call | flops 1 | bytes 1 | tf_op jit(solution)/shard_map/pallas_call | solution.py:370
  58.1 0.7 %shard_map.153 = (f32[128,2048]{1,0:T(8,128)S(1)}, f32[8,128]{1,0:T(8,128)S(1)}) custom-call(s32[5,768]{1,0:T(8,128)S(1)} %copy-done.2, f32[128,2048]{1,0:T(8,128)S(1)} %get-tuple-element.42.acc_ref, f32[8,128]{1,0:T(8,128)S(1)} %get-tuple-element.43.before_ref, bf16[128,768]{1,0:T(8,128)(2,1)S(1)} %collective-permute-done.12.refs_0_), custom_call_target="tpu_custom_call" | custom-call | flops 1 | bytes 1 | tf_op jit(solution)/shard_map/pallas_call | solution.py:370
  58.8 1.1 %shard_map.154 = (f32[128,2048]{1,0:T(8,128)S(1)}, f32[8,128]{1,0:T(8,128)S(1)}) custom-call(s32[5,768]{1,0:T(8,128)S(1)} %copy-done.2, f32[128,2048]{1,0:T(8,128)S(1)} %get-tuple-element.44.acc_ref, f32[8,128]{1,0:T(8,128)S(1)} %get-tuple-element.45.before_ref, bf16[128,768]{1,0:T(8,128)(2,1)S(1)} %collective-permute-done.13.refs_0_, ...), custom_call_target="tpu_custom_call" | custom-call | flops 1 | bytes 1 | tf_op jit(solution)/shard_map/pallas_call | solution.py:370
  59.9 0.5 collective-permute-done.17.refs_2_
  60.5 0.2 collective-permute-done.15.refs_0_
  60.7 1.2 %collective-permute-start.19 = (f32[128,128]{1,0:T(8,128)S(1)}, f32[128,128]{1,0:T(8,128)S(1)}, u32[]{:S(2)}, u32[]{:S(2)}) collective-permute-start(f32[128,128]{1,0:T(8,128)S(1)} %shard_map.155.before_ref.total_ref), channel_id=1, source_target_pairs={{0,1},{1,0},{2,3},{3,2},{4,5},{5,4},{6,7},{7,6},{8,9},{9,8},{10,11... | collective-permute-start | bytes 196616 | tf_op jit(solution)/shard_map/ppermute | solution.py:420
  61.9 1.8 %shard_map.156 = (f32[2048,128]{1,0:T(8,128)}, f32[8,128]{1,0:T(8,128)S(1)}) custom-call(s32[5,768]{1,0:T(8,128)S(1)} %copy-done.2, f32[128,2048]{1,0:T(8,128)S(1)} %get-tuple-element.46.acc_ref, f32[128,128]{1,0:T(8,128)S(1)} %shard_map.155.before_ref.total_ref, bf16[128,768]{1,0:T(8,128)(2,1)S(1)} %collective-permute-done.18.refs_0_), custom_call_target="tpu_custom_call" | custom-call | flops 1 | bytes 1 | tf_op jit(solution)/shard_map/pallas_call | solution.py:370
  63.7 0.7 %shard_map.157 = (f32[128,128]{1,0:T(8,128)}, f32[128,128]{1,0:T(8,128)}) custom-call(f32[128,128]{1,0:T(8,128)S(1)} %shard_map.155.before_ref.total_ref, f32[128,128]{1,0:T(8,128)S(1)} %collective-permute-done.19.other_ref, f32[8,128]{1,0:T(8,128)S(1)} %get-tuple-element.49.before_ref), custom_call_target="tpu_custom_call" | custom-call | flops 32768 | bytes 262144 | tf_op jit(solution)/shard_map/pallas_call | solution.py:409
  (26 shorter events, 0.1 us)
Async XLA Ops:
  4.2 21.1 %collective-permute-start = (bf16[128,768]{1,0:T(8,128)(2,1)S(1)}, bf16[128,768]{1,0:T(8,128)(2,1)S(1)}, u32[]{:S(2)}, u32[]{:S(2)}) collective-permute-start(bf16[128,768]{1,0:T(8,128)(2,1)S(1)} %get-tuple-element.28), channel_id=1, source_target_pairs={{0,1},{1,0},{2,3},{3,2},{4,5},{5,4},{6,7},{7,6},{8,9},{9,8},{10,11... | collective-permute-start | bytes 589832 | tf_op jit(solution)/shard_map/ppermute | solution.py:420
  5.7 19.6 %collective-permute-start.1 = (bf16[128,768]{1,0:T(8,128)(2,1)S(1)}, bf16[128,768]{1,0:T(8,128)(2,1)S(1)}, u32[]{:S(2)}, u32[]{:S(2)}) collective-permute-start(bf16[128,768]{1,0:T(8,128)(2,1)S(1)} %get-tuple-element.29), channel_id=1, source_target_pairs={{0,2},{1,3},{2,0},{3,1},{4,6},{5,7},{6,4},{7,5},{8,10},{9,11},{10,... | collective-permute-start | bytes 589832 | tf_op jit(solution)/shard_map/ppermute | solution.py:420
  7.5 17.9 %collective-permute-start.2 = (bf16[128,768]{1,0:T(8,128)(2,1)S(1)}, bf16[128,768]{1,0:T(8,128)(2,1)S(1)}, u32[]{:S(2)}, u32[]{:S(2)}) collective-permute-start(bf16[128,768]{1,0:T(8,128)(2,1)S(1)} %get-tuple-element.30), channel_id=1, source_target_pairs={{0,4},{1,5},{2,6},{3,7},{4,0},{5,1},{6,2},{7,3},{8,12},{9,13},{10,... | collective-permute-start | bytes 589832 | tf_op jit(solution)/shard_map/ppermute | solution.py:420
  10.8 14.6 %collective-permute-start.3 = (bf16[128,768]{1,0:T(8,128)(2,1)S(1)}, bf16[128,768]{1,0:T(8,128)(2,1)S(1)}, u32[]{:S(2)}, u32[]{:S(2)}) collective-permute-start(bf16[128,768]{1,0:T(8,128)(2,1)S(1)} %get-tuple-element.31), channel_id=1, source_target_pairs={{0,8},{1,9},{2,10},{3,11},{4,12},{5,13},{6,14},{7,15},{8,0},{9,1},... | collective-permute-start | bytes 589832 | tf_op jit(solution)/shard_map/ppermute | solution.py:420
  12.0 11.0 %copy-start = (bf16[2048,128]{1,0:T(8,128)(2,1)S(1)}, bf16[2048,128]{1,0:T(8,128)(2,1)}, u32[]{:S(2)}) copy-start(bf16[2048,128]{1,0:T(8,128)(2,1)} %refs_8_.1) | copy-start | bytes 1572868
  12.0 13.4 %collective-permute-start.4 = (bf16[128,768]{1,0:T(8,128)(2,1)S(1)}, bf16[128,768]{1,0:T(8,128)(2,1)S(1)}, u32[]{:S(2)}, u32[]{:S(2)}) collective-permute-start(bf16[128,768]{1,0:T(8,128)(2,1)S(1)} %get-tuple-element.32), channel_id=1, source_target_pairs={{0,16},{1,17},{2,18},{3,19},{4,20},{5,21},{6,22},{7,23},{8,24},{9,... | collective-permute-start | bytes 589832 | tf_op jit(solution)/shard_map/ppermute | solution.py:420
  22.9 2.4 %copy-start.1 = (bf16[2048,128]{1,0:T(8,128)(2,1)S(1)}, bf16[2048,128]{1,0:T(8,128)(2,1)}, u32[]{:S(2)}) copy-start(bf16[2048,128]{1,0:T(8,128)(2,1)} %refs_9_.1) | copy-start | bytes 1572868
  22.9 2.4 %copy-start.3 = (bf16[128,128]{1,0:T(8,128)(2,1)S(1)}, bf16[128,128]{1,0:T(8,128)(2,1)}, u32[]{:S(2)}) copy-start(bf16[128,128]{1,0:T(8,128)(2,1)} %ws_ref.1) | copy-start | bytes 98308
  22.9 2.4 %copy-start.4 = (bf16[128,128]{1,0:T(8,128)(2,1)S(1)}, bf16[128,128]{1,0:T(8,128)(2,1)}, u32[]{:S(2)}) copy-start(bf16[128,128]{1,0:T(8,128)(2,1)} %refs_12_.1) | copy-start | bytes 98308
  22.9 2.4 %copy-start.5 = (s32[2048]{0:T(1024)S(1)}, s32[2048]{0:T(1024)}, u32[]{:S(2)}) copy-start(s32[2048]{0:T(1024)} %param.20) | copy-start | bytes 24580
  23.0 2.4 %copy-start.6 = (f32[128]{0:T(128)S(1)}, f32[128]{0:T(128)}, u32[]{:S(2)}) copy-start(f32[128]{0:T(128)} %param.14) | copy-start | bytes 1540
  31.6 2.4 %collective-permute-start.5 = (f32[128,128]{1,0:T(8,128)S(1)}, f32[128,128]{1,0:T(8,128)S(1)}, u32[]{:S(2)}, u32[]{:S(2)}) collective-permute-start(f32[128,128]{1,0:T(8,128)S(1)} %get-tuple-element.41), channel_id=1, source_target_pairs={{0,1},{1,0},{2,3},{3,2},{4,5},{5,4},{6,7},{7,6},{8,9},{9,8},{10,11... | collective-permute-start | bytes 196616 | tf_op jit(solution)/shard_map/ppermute | solution.py:420
  34.0 5.6 %collective-permute-start.8 = (f32[128,128]{1,0:T(8,128)S(1)}, f32[128,128]{1,0:T(8,128)S(1)}, u32[]{:S(2)}, u32[]{:S(2)}) collective-permute-start(f32[128,128]{1,0:T(8,128)S(1)} %shard_map.144.before_ref.left_ref), channel_id=1, source_target_pairs={{0,96},{1,97},{2,98},{3,99},{4,100},{5,101},{6,102},{7,103},{8,104... | collective-permute-start | bytes 196616 | tf_op jit(solution)/shard_map/ppermute | solution.py:420
  37.0 4.6 %collective-permute-start.7 = (f32[128,128]{1,0:T(8,128)S(1)}, f32[128,128]{1,0:T(8,128)S(1)}, u32[]{:S(2)}, u32[]{:S(2)}) collective-permute-start(f32[128,128]{1,0:T(8,128)S(1)} %shard_map.144.before_ref.left_ref), channel_id=1, source_target_pairs={{0,64},{1,65},{2,66},{3,67},{4,68},{5,69},{6,70},{7,71},{8,72},{9,... | collective-permute-start | bytes 196616 | tf_op jit(solution)/shard_map/ppermute | solution.py:420
  37.4 4.3 %collective-permute-start.6 = (f32[128,128]{1,0:T(8,128)S(1)}, f32[128,128]{1,0:T(8,128)S(1)}, u32[]{:S(2)}, u32[]{:S(2)}) collective-permute-start(f32[128,128]{1,0:T(8,128)S(1)} %shard_map.144.before_ref.left_ref), channel_id=1, source_target_pairs={{0,32},{1,33},{2,34},{3,35},{4,36},{5,37},{6,38},{7,39},{8,40},{9,... | collective-permute-start | bytes 196616 | tf_op jit(solution)/shard_map/ppermute | solution.py:420
  37.7 16.3 %collective-permute-start.12 = (bf16[128,768]{1,0:T(8,128)(2,1)S(1)}, bf16[128,768]{1,0:T(8,128)(2,1)S(1)}, u32[]{:S(2)}, u32[]{:S(2)}) collective-permute-start(bf16[128,768]{1,0:T(8,128)(2,1)S(1)} %shard_map.143.before_ref), channel_id=1, source_target_pairs={{0,16},{1,17},{2,18},{3,19},{4,20},{5,21},{6,22},{7,23},{8,24},{9,... | collective-permute-start | bytes 589832 | tf_op jit(solution)/shard_map/ppermute | solution.py:420
  38.2 15.9 %collective-permute-start.11 = (bf16[128,768]{1,0:T(8,128)(2,1)S(1)}, bf16[128,768]{1,0:T(8,128)(2,1)S(1)}, u32[]{:S(2)}, u32[]{:S(2)}) collective-permute-start(bf16[128,768]{1,0:T(8,128)(2,1)S(1)} %shard_map.142.before_ref), channel_id=1, source_target_pairs={{0,4},{1,5},{2,6},{3,7},{4,0},{5,1},{6,2},{7,3},{8,12},{9,13},{10,... | collective-permute-start | bytes 589832 | tf_op jit(solution)/shard_map/ppermute | solution.py:420
  41.7 3.5 %collective-permute-start.9 = (f32[128,128]{1,0:T(8,128)S(1)}, f32[128,128]{1,0:T(8,128)S(1)}, u32[]{:S(2)}, u32[]{:S(2)}) collective-permute-start(f32[128,128]{1,0:T(8,128)S(1)} %shard_map.146.before_ref.left_ref), channel_id=1, source_target_pairs={{0,8},{1,9},{2,10},{3,11},{4,12},{5,13},{6,14},{7,15},{8,0},{9,1},... | collective-permute-start | bytes 196616 | tf_op jit(solution)/shard_map/ppermute | solution.py:420
  41.8 14.0 %collective-permute-start.14 = (bf16[128,768]{1,0:T(8,128)(2,1)S(1)}, bf16[128,768]{1,0:T(8,128)(2,1)S(1)}, u32[]{:S(2)}, u32[]{:S(2)}) collective-permute-start(bf16[128,768]{1,0:T(8,128)(2,1)S(1)} %shard_map.145.before_ref), channel_id=1, source_target_pairs={{0,2},{1,3},{2,0},{3,1},{4,6},{5,7},{6,4},{7,5},{8,10},{9,11},{10,... | collective-permute-start | bytes 589832 | tf_op jit(solution)/shard_map/ppermute | solution.py:420
  42.4 16.3 %collective-permute-start.13 = (bf16[128,768]{1,0:T(8,128)(2,1)S(1)}, bf16[128,768]{1,0:T(8,128)(2,1)S(1)}, u32[]{:S(2)}, u32[]{:S(2)}) collective-permute-start(bf16[128,768]{1,0:T(8,128)(2,1)S(1)} %shard_map.147.before_ref), channel_id=1, source_target_pairs={{0,8},{1,9},{2,10},{3,11},{4,12},{5,13},{6,14},{7,15},{8,0},{9,1},... | collective-permute-start | bytes 589832 | tf_op jit(solution)/shard_map/ppermute | solution.py:420
  45.2 4.4 %collective-permute-start.10 = (f32[128,128]{1,0:T(8,128)S(1)}, f32[128,128]{1,0:T(8,128)S(1)}, u32[]{:S(2)}, u32[]{:S(2)}) collective-permute-start(f32[128,128]{1,0:T(8,128)S(1)} %shard_map.148.before_ref.left_ref), channel_id=1, source_target_pairs={{0,24},{1,25},{2,26},{3,27},{4,28},{5,29},{6,30},{7,31},{8,16},{9,... | collective-permute-start | bytes 196616 | tf_op jit(solution)/shard_map/ppermute | solution.py:420
  48.1 9.2 %copy-start.2 = (s32[5,768]{1,0:T(8,128)S(1)}, s32[5,768]{1,0:T(8,128)}, u32[]{:S(2)}) copy-start(s32[5,768]{1,0:T(8,128)} %rows_ref.7) | copy-start | bytes 46084
  49.6 12.3 %collective-permute-start.18 = (bf16[128,768]{1,0:T(8,128)(2,1)S(1)}, bf16[128,768]{1,0:T(8,128)(2,1)S(1)}, u32[]{:S(2)}, u32[]{:S(2)}) collective-permute-start(bf16[128,768]{1,0:T(8,128)(2,1)S(1)} %shard_map.150.before_ref), channel_id=1, source_target_pairs={{0,1},{1,0},{2,3},{3,2},{4,5},{5,4},{6,7},{7,6},{8,9},{9,8},{10,11... | collective-permute-start | bytes 589832 | tf_op jit(solution)/shard_map/ppermute | solution.py:420
  54.0 6.4 %collective-permute-start.17 = (f32[128,128]{1,0:T(8,128)S(1)}, f32[128,128]{1,0:T(8,128)S(1)}, u32[]{:S(2)}, u32[]{:S(2)}) collective-permute-start(f32[128,128]{1,0:T(8,128)S(1)} %shard_map.151.before_ref.left_ref), channel_id=1, source_target_pairs={{0,6},{1,7},{2,4},{3,5},{4,2},{5,3},{6,0},{7,1},{8,14},{9,15},{10,... | collective-permute-start | bytes 196616 | tf_op jit(solution)/shard_map/ppermute | solution.py:420
  54.1 6.3 %collective-permute-start.16 = (f32[128,128]{1,0:T(8,128)S(1)}, f32[128,128]{1,0:T(8,128)S(1)}, u32[]{:S(2)}, u32[]{:S(2)}) collective-permute-start(f32[128,128]{1,0:T(8,128)S(1)} %shard_map.151.before_ref.left_ref), channel_id=1, source_target_pairs={{0,4},{1,5},{2,6},{3,7},{4,0},{5,1},{6,2},{7,3},{8,12},{9,13},{10,... | collective-permute-start | bytes 196616 | tf_op jit(solution)/shard_map/ppermute | solution.py:420
  55.8 5.0 %collective-permute-start.15 = (f32[128,128]{1,0:T(8,128)S(1)}, f32[128,128]{1,0:T(8,128)S(1)}, u32[]{:S(2)}, u32[]{:S(2)}) collective-permute-start(f32[128,128]{1,0:T(8,128)S(1)} %shard_map.151.before_ref.left_ref), channel_id=1, source_target_pairs={{0,2},{1,3},{2,0},{3,1},{4,6},{5,7},{6,4},{7,5},{8,10},{9,11},{10,... | collective-permute-start | bytes 196616 | tf_op jit(solution)/shard_map/ppermute | solution.py:420
  60.7 3.0 %collective-permute-start.19 = (f32[128,128]{1,0:T(8,128)S(1)}, f32[128,128]{1,0:T(8,128)S(1)}, u32[]{:S(2)}, u32[]{:S(2)}) collective-permute-start(f32[128,128]{1,0:T(8,128)S(1)} %shard_map.155.before_ref.total_ref), channel_id=1, source_target_pairs={{0,1},{1,0},{2,3},{3,2},{4,5},{5,4},{6,7},{7,6},{8,9},{9,8},{10,11... | collective-permute-start | bytes 196616 | tf_op jit(solution)/shard_map/ppermute | solution.py:420

commit v12 on v11

--- a/solution.py
+++ b/solution.py
@@ -475,14 +475,14 @@
     total = added(total, others, last)
     others = [swapped(total, mask) for mask in (8,)]
     last = send_back(3, total)
+    last = send_back(0, last)
     total = added(total, others, last)
     others = [swapped(total, mask) for mask in (24,)]
     grads_t = own(scaled_t, dl0, dl1, grad_pre, w_self, total)
-    last = send_back(0, grads_t)
+    grads_t, last = place((2,), grads_t, grads_t)
     total = added(total, others, last)
     others = [swapped(total, mask) for mask in (2, 4, 6)]
-    grads_t, last = place((2,), grads_t, total)
-    grads_t, last = place((4,), grads_t, last)
+    grads_t, last = place((4,), grads_t, total)
     grads_t, last = place((3,1,), grads_t, last)
     total = added(total, others, last)
     other = swapped(total, 1)

time: 64.5 us -> 65 us (level)
  starting transfers between devices: 27.6 us -> 28.9 us
  waiting for transfers between devices: 5.8 us -> 5.01 us
    ppermute x20, starting transfers between devices: 27.6 us -> 28.9 us  [swapped(): lax.ppermute(shard, 'dom', [(i, i ^ mask) for i in range(lax.axis_size('d...]
    ppermute x20, waiting for transfers between devices: 5.8 us -> 5.01 us  [swapped(): lax.ppermute(shard, 'dom', [(i, i ^ mask) for i in range(lax.axis_size('d...]
  transfers between devices with their start and end apart: 20 -> 20, of which waited for: 6 -> 5; matrix products, arithmetic and copies ran while one was open for 0% -> 0% of each run, Pallas kernels for 30% -> 30%
where the time goes in v12:
time: 65 us; the launch traced here: 64.8 us
  Pallas kernels  29.9 us (46%)
  starting transfers between devices  28.9 us (44%)
  waiting for transfers between devices  5.01 us (8%)
  between operations  0.95 us (1%)
    ppermute x20, starting transfers between devices, swapped(): lax.ppermute(shard, 'dom', [(i, i ^ mask) for i in range(lax.axis_size('d...  28.9 us
    pallas_call x1, Pallas kernels, densify(): pl.pallas_call(densify_kernel, out_shape=[VMEM((n, half, TILE), jnp.bfloa...  8.48 us
    pallas_call x1, Pallas kernels, middle(): pl.pallas_call(functools.partial(middle_kernel, rounds), out_shape=[half,...  6.21 us
    ppermute x20, waiting for transfers between devices, swapped(): lax.ppermute(shard, 'dom', [(i, i ^ mask) for i in range(lax.axis_size('d...  5.01 us
    pallas_call x4, Pallas kernels, place_rows(): pl.pallas_call(functools.partial(place_kernel, rounds, last), out_shape=[...  4.28 us
    pallas_call x1, Pallas kernels, pick_rows(): pl.pallas_call(pick_kernel, out_shape=outs, in_specs=[pl.BlockSpec(memory...  3.58 us
    pallas_call x5, Pallas kernels, back(): pl.pallas_call(functools.partial(back_kernel, first, n), out_shape=jax.Sh...  2.91 us
    pallas_call x1, Pallas kernels, local_sums(): pl.pallas_call(local_sums_kernel, out_shape=VMEM((rows, width), jnp.float...  2.31 us
  transfers between devices with their start and end apart: 20, of which 5 were waited for; matrix products, arithmetic and copies ran while one was open for 0% of the time, Pallas kernels for 30%

profile of v12, /device:TPU:1, one launch (start us, length us, event | category | flops | bytes accessed | tf_op | source)
XLA Modules:
  0.0 64.8 jit_solution(38985468763670336)
XLA Ops:
  0.6 3.6 %shard_map.138 = (bf16[128,768]{1,0:T(8,128)(2,1)S(1)}, bf16[128,768]{1,0:T(8,128)(2,1)S(1)}, bf16[128,768]{1,0:T(8,128)(2,1)S(1)}, bf16[128,768]{1,0:T(8,128)(2,1)S(1)}, bf16[128,768]{1,0:T(8,128)(2,1)S(1)}) custom-call(s32[5,768]{1,0:T(8,128)} %rows_ref.7, bf16[2048,128]{1,0:T(8,128)(2,1)} %refs_8_.1), custom_call_target="tpu_custom_call" | custom-call | flops 2013265920 | bytes 1000000 | tf_op jit(solution)/shard_map/pallas_call | solution.py:75
  4.2 1.5 %collective-permute-start = (bf16[128,768]{1,0:T(8,128)(2,1)S(1)}, bf16[128,768]{1,0:T(8,128)(2,1)S(1)}, u32[]{:S(2)}, u32[]{:S(2)}) collective-permute-start(bf16[128,768]{1,0:T(8,128)(2,1)S(1)} %get-tuple-element.28), channel_id=1, source_target_pairs={{0,1},{1,0},{2,3},{3,2},{4,5},{5,4},{6,7},{7,6},{8,9},{9,8},{10,11... | collective-permute-start | bytes 589832 | tf_op jit(solution)/shard_map/ppermute | solution.py:420
  5.7 1.7 %collective-permute-start.1 = (bf16[128,768]{1,0:T(8,128)(2,1)S(1)}, bf16[128,768]{1,0:T(8,128)(2,1)S(1)}, u32[]{:S(2)}, u32[]{:S(2)}) collective-permute-start(bf16[128,768]{1,0:T(8,128)(2,1)S(1)} %get-tuple-element.29), channel_id=1, source_target_pairs={{0,2},{1,3},{2,0},{3,1},{4,6},{5,7},{6,4},{7,5},{8,10},{9,11},{10,... | collective-permute-start | bytes 589832 | tf_op jit(solution)/shard_map/ppermute | solution.py:420
  7.5 3.3 %collective-permute-start.2 = (bf16[128,768]{1,0:T(8,128)(2,1)S(1)}, bf16[128,768]{1,0:T(8,128)(2,1)S(1)}, u32[]{:S(2)}, u32[]{:S(2)}) collective-permute-start(bf16[128,768]{1,0:T(8,128)(2,1)S(1)} %get-tuple-element.30), channel_id=1, source_target_pairs={{0,4},{1,5},{2,6},{3,7},{4,0},{5,1},{6,2},{7,3},{8,12},{9,13},{10,... | collective-permute-start | bytes 589832 | tf_op jit(solution)/shard_map/ppermute | solution.py:420
  10.8 1.2 %collective-permute-start.3 = (bf16[128,768]{1,0:T(8,128)(2,1)S(1)}, bf16[128,768]{1,0:T(8,128)(2,1)S(1)}, u32[]{:S(2)}, u32[]{:S(2)}) collective-permute-start(bf16[128,768]{1,0:T(8,128)(2,1)S(1)} %get-tuple-element.31), channel_id=1, source_target_pairs={{0,8},{1,9},{2,10},{3,11},{4,12},{5,13},{6,14},{7,15},{8,0},{9,1},... | collective-permute-start | bytes 589832 | tf_op jit(solution)/shard_map/ppermute | solution.py:420
  12.0 2.5 %collective-permute-start.4 = (bf16[128,768]{1,0:T(8,128)(2,1)S(1)}, bf16[128,768]{1,0:T(8,128)(2,1)S(1)}, u32[]{:S(2)}, u32[]{:S(2)}) collective-permute-start(bf16[128,768]{1,0:T(8,128)(2,1)S(1)} %get-tuple-element.32), channel_id=1, source_target_pairs={{0,16},{1,17},{2,18},{3,19},{4,20},{5,21},{6,22},{7,23},{8,24},{9,... | collective-permute-start | bytes 589832 | tf_op jit(solution)/shard_map/ppermute | solution.py:420
  14.4 8.5 %shard_map.139 = (bf16[16,1024,128]{2,1,0:T(8,128)(2,1)S(1)}, bf16[16,1024,128]{2,1,0:T(8,128)(2,1)S(1)}, bf16[30,1024,128]{2,1,0:T(8,128)(2,1)S(1)}, bf16[30,1024,128]{2,1,0:T(8,128)(2,1)S(1)}) custom-call(s32[16,22]{1,0:T(8,128)} %lc_hbm.1, s32[16,20]{1,0:T(8,128)} %hc_hbm.1, bf16[16,22,128,128]{3,2,1,0:T(8,128)(2,1)} %lt.1, bf16[16,20,128,128]{3,2,1,0:T(8,128)(2,1)} %ht.1), custom_call_target="tpu_custom_call" | custom-call | flops 16000000 | bytes 22020096 | tf_op jit(solution)/shard_map/pallas_call | solution.py:170
  22.9 0.0 copy-start.1
  22.9 0.0 copy-start.3
  22.9 0.0 copy-start.4
  22.9 0.0 copy-start.5
  23.0 0.0 copy-start.6
  23.0 2.3 %shard_map.140.refs_7_ = f32[2048,128]{1,0:T(8,128)S(1)} custom-call(bf16[16,1024,128]{2,1,0:T(8,128)(2,1)S(1)} %get-tuple-element.35.d0_ref, bf16[16,1024,128]{2,1,0:T(8,128)(2,1)S(1)} %get-tuple-element.36.d1_ref, bf16[2048,128]{1,0:T(8,128)(2,1)S(1)} %copy-done), custom_call_target="tpu_custom_call" | custom-call | flops 1073741824 | bytes 1500000 | tf_op jit(solution)/shard_map/pallas_call | solution.py:202
  25.3 0.0 collective-permute-done.refs_0_
  25.3 0.0 collective-permute-done.1.refs_1_
  25.3 0.0 collective-permute-done.4.refs_4_
  25.4 6.2 %shard_map.141 = (bf16[2048,128]{1,0:T(8,128)(2,1)}, bf16[2048,128]{1,0:T(8,128)(2,1)S(1)}, bf16[128,2048]{1,0:T(8,128)(2,1)S(1)}, f32[128,128]{1,0:T(8,128)S(1)}, f32[128,128]{1,0:T(8,128)S(1)}) custom-call(bf16[128,768]{1,0:T(8,128)(2,1)S(1)} %collective-permute-done.refs_0_, bf16[128,768]{1,0:T(8,128)(2,1)S(1)} %collective-permute-done.1.refs_1_, ...), custom_call_target="tpu_custom_call" | custom-call | flops 2013265920 | bytes 5000000 | tf_op jit(solution)/shard_map/pallas_call | solution.py:262
  31.6 1.2 %collective-permute-start.5 = (f32[128,128]{1,0:T(8,128)S(1)}, f32[128,128]{1,0:T(8,128)S(1)}, u32[]{:S(2)}, u32[]{:S(2)}) collective-permute-start(f32[128,128]{1,0:T(8,128)S(1)} %get-tuple-element.41), channel_id=1, source_target_pairs={{0,1},{1,0},{2,3},{3,2},{4,5},{5,4},{6,7},{7,6},{8,9},{9,8},{10,11... | collective-permute-start | bytes 196616 | tf_op jit(solution)/shard_map/ppermute | solution.py:420
  32.8 0.6 shard_map.142.before_ref
  33.4 0.6 shard_map.143.before_ref
  34.0 3.0 %collective-permute-start.8 = (f32[128,128]{1,0:T(8,128)S(1)}, f32[128,128]{1,0:T(8,128)S(1)}, u32[]{:S(2)}, u32[]{:S(2)}) collective-permute-start(f32[128,128]{1,0:T(8,128)S(1)} %shard_map.144.before_ref.left_ref), channel_id=1, source_target_pairs={{0,96},{1,97},{2,98},{3,99},{4,100},{5,101},{6,102},{7,103},{8,104... | collective-permute-start | bytes 196616 | tf_op jit(solution)/shard_map/ppermute | solution.py:420
  37.0 0.0 collective-permute-start.10
  37.0 0.4 collective-permute-start.7
  37.4 0.4 collective-permute-start.6
  37.8 0.5 collective-permute-start.12
  38.3 0.6 shard_map.145.before_ref
  38.9 0.4 collective-permute-done.8.refs_2_
  39.3 0.0 collective-permute-start.14
  39.3 2.3 %collective-permute-done.7.refs_1_ = f32[128,128]{1,0:T(8,128)S(1)} collective-permute-done((f32[128,128]{1,0:T(8,128)S(1)}, f32[128,128]{1,0:T(8,128)S(1)}, u32[]{:S(2)}, u32[]{:S(2)}) %collective-permute-start.7) | collective-permute-done | bytes 65568 | tf_op jit(solution)/shard_map/ppermute | solution.py:420
  41.7 0.1 collective-permute-start.9
  41.8 0.6 shard_map.147.before_ref
  42.4 1.5 %collective-permute-start.13 = (bf16[128,768]{1,0:T(8,128)(2,1)S(1)}, bf16[128,768]{1,0:T(8,128)(2,1)S(1)}, u32[]{:S(2)}, u32[]{:S(2)}) collective-permute-start(bf16[128,768]{1,0:T(8,128)(2,1)S(1)} %shard_map.147.before_ref), channel_id=1, source_target_pairs={{0,8},{1,9},{2,10},{3,11},{4,12},{5,13},{6,14},{7,15},{8,0},{9,1},... | collective-permute-start | bytes 589832 | tf_op jit(solution)/shard_map/ppermute | solution.py:420
  43.9 0.6 shard_map.148.before_ref
  44.5 0.0 copy-start.2
  44.5 0.7 %collective-permute-done.9.refs_0_ = f32[128,128]{1,0:T(8,128)S(1)} collective-permute-done((f32[128,128]{1,0:T(8,128)S(1)}, f32[128,128]{1,0:T(8,128)S(1)}, u32[]{:S(2)}, u32[]{:S(2)}) %collective-permute-start.9) | collective-permute-done | bytes 65568 | tf_op jit(solution)/shard_map/ppermute | solution.py:420
  45.2 1.7 %collective-permute-start.11 = (f32[128,128]{1,0:T(8,128)S(1)}, f32[128,128]{1,0:T(8,128)S(1)}, u32[]{:S(2)}, u32[]{:S(2)}) collective-permute-start(f32[128,128]{1,0:T(8,128)S(1)} %shard_map.149.before_ref.left_ref), channel_id=1, source_target_pairs={{0,24},{1,25},{2,26},{3,27},{4,28},{5,29},{6,30},{7,31},{8,16},{9,... | collective-permute-start | bytes 196616 | tf_op jit(solution)/shard_map/ppermute | solution.py:420
  46.9 2.9 %collective-permute-start.18 = (bf16[128,768]{1,0:T(8,128)(2,1)S(1)}, bf16[128,768]{1,0:T(8,128)(2,1)S(1)}, u32[]{:S(2)}, u32[]{:S(2)}) collective-permute-start(bf16[128,768]{1,0:T(8,128)(2,1)S(1)} %shard_map.148.before_ref), channel_id=1, source_target_pairs={{0,1},{1,0},{2,3},{3,2},{4,5},{5,4},{6,7},{7,6},{8,9},{9,8},{10,11... | collective-permute-start | bytes 589832 | tf_op jit(solution)/shard_map/ppermute | solution.py:420
  49.8 1.4 %shard_map.150.acc_ref.before_ref = f32[128,2048]{1,0:T(8,128)S(1)} custom-call(bf16[128,2048]{1,0:T(8,128)(2,1)S(1)} %get-tuple-element.38.st_ref.before_ref, bf16[16,1024,128]{2,1,0:T(8,128)(2,1)S(1)} %get-tuple-element.35.d0_ref, bf16[16,1024,128]{2,1,0:T(8,128)(2,1)S(1)} %get-tuple-element.36.d1_ref, bf16[2048,128]{1,0:T(8,128)(2,1)S(1)} %get-tuple-element.39.gp_ref, ...), custom_call_target="tpu_custom_call" | custom-call | flops 1 | bytes 1 | tf_op jit(solution)/shard_map/pallas_call | solution.py:327
  51.2 0.7 %shard_map.151 = (f32[128,2048]{1,0:T(8,128)S(1)}, f32[8,128]{1,0:T(8,128)S(1)}) custom-call(s32[5,768]{1,0:T(8,128)S(1)} %copy-done.2, f32[128,2048]{1,0:T(8,128)S(1)} %shard_map.150.acc_ref.before_ref, f32[128,2048]{1,0:T(8,128)S(1)} %shard_map.150.acc_ref.before_ref, bf16[128,768]{1,0:T(8,128)(2,1)S(1)} %collective-permute-done.10.refs_0_), custom_call_target="tpu_custom_call" | custom-call | flops 1 | bytes 1 | tf_op jit(solution)/shard_map/pallas_call | solution.py:370
  52.0 2.1 %collective-permute-start.17 = (f32[128,128]{1,0:T(8,128)S(1)}, f32[128,128]{1,0:T(8,128)S(1)}, u32[]{:S(2)}, u32[]{:S(2)}) collective-permute-start(f32[128,128]{1,0:T(8,128)S(1)} %shard_map.152.before_ref.left_ref), channel_id=1, source_target_pairs={{0,6},{1,7},{2,4},{3,5},{4,2},{5,3},{6,0},{7,1},{8,14},{9,15},{10,... | collective-permute-start | bytes 196616 | tf_op jit(solution)/shard_map/ppermute | solution.py:420
  54.0 1.4 %collective-permute-start.16 = (f32[128,128]{1,0:T(8,128)S(1)}, f32[128,128]{1,0:T(8,128)S(1)}, u32[]{:S(2)}, u32[]{:S(2)}) collective-permute-start(f32[128,128]{1,0:T(8,128)S(1)} %shard_map.152.before_ref.left_ref), channel_id=1, source_target_pairs={{0,4},{1,5},{2,6},{3,7},{4,0},{5,1},{6,2},{7,3},{8,12},{9,13},{10,... | collective-permute-start | bytes 196616 | tf_op jit(solution)/shard_map/ppermute | solution.py:420
  55.5 0.7 %shard_map.153 = (f32[128,2048]{1,0:T(8,128)S(1)}, f32[8,128]{1,0:T(8,128)S(1)}) custom-call(s32[5,768]{1,0:T(8,128)S(1)} %copy-done.2, f32[128,2048]{1,0:T(8,128)S(1)} %get-tuple-element.42.acc_ref, f32[128,128]{1,0:T(8,128)S(1)} %shard_map.152.before_ref.left_ref, bf16[128,768]{1,0:T(8,128)(2,1)S(1)} %collective-permute-done.12.refs_0_), custom_call_target="tpu_custom_call" | custom-call | flops 1 | bytes 1 | tf_op jit(solution)/shard_map/pallas_call | solution.py:370
  56.2 1.1 %shard_map.154 = (f32[128,2048]{1,0:T(8,128)S(1)}, f32[8,128]{1,0:T(8,128)S(1)}) custom-call(s32[5,768]{1,0:T(8,128)S(1)} %copy-done.2, f32[128,2048]{1,0:T(8,128)S(1)} %get-tuple-element.44.acc_ref, f32[8,128]{1,0:T(8,128)S(1)} %get-tuple-element.45.before_ref, bf16[128,768]{1,0:T(8,128)(2,1)S(1)} %collective-permute-done.13.refs_0_, ...), custom_call_target="tpu_custom_call" | custom-call | flops 1 | bytes 1 | tf_op jit(solution)/shard_map/pallas_call | solution.py:370
  57.3 1.4 %collective-permute-done.16.refs_1_ = f32[128,128]{1,0:T(8,128)S(1)} collective-permute-done((f32[128,128]{1,0:T(8,128)S(1)}, f32[128,128]{1,0:T(8,128)S(1)}, u32[]{:S(2)}, u32[]{:S(2)}) %collective-permute-start.16) | collective-permute-done | bytes 65568 | tf_op jit(solution)/shard_map/ppermute | solution.py:420
  58.7 0.2 collective-permute-done.15.refs_0_
  58.9 3.5 %collective-permute-start.19 = (f32[128,128]{1,0:T(8,128)S(1)}, f32[128,128]{1,0:T(8,128)S(1)}, u32[]{:S(2)}, u32[]{:S(2)}) collective-permute-start(f32[128,128]{1,0:T(8,128)S(1)} %shard_map.155.before_ref.total_ref), channel_id=1, source_target_pairs={{0,1},{1,0},{2,3},{3,2},{4,5},{5,4},{6,7},{7,6},{8,9},{9,8},{10,11... | collective-permute-start | bytes 196616 | tf_op jit(solution)/shard_map/ppermute | solution.py:420
  62.4 1.8 %shard_map.156 = (f32[2048,128]{1,0:T(8,128)}, f32[8,128]{1,0:T(8,128)S(1)}) custom-call(s32[5,768]{1,0:T(8,128)S(1)} %copy-done.2, f32[128,2048]{1,0:T(8,128)S(1)} %get-tuple-element.46.acc_ref, f32[128,128]{1,0:T(8,128)S(1)} %shard_map.155.before_ref.total_ref, bf16[128,768]{1,0:T(8,128)(2,1)S(1)} %collective-permute-done.18.refs_0_), custom_call_target="tpu_custom_call" | custom-call | flops 1 | bytes 1 | tf_op jit(solution)/shard_map/pallas_call | solution.py:370
  64.2 0.7 %shard_map.157 = (f32[128,128]{1,0:T(8,128)}, f32[128,128]{1,0:T(8,128)}) custom-call(f32[128,128]{1,0:T(8,128)S(1)} %shard_map.155.before_ref.total_ref, f32[128,128]{1,0:T(8,128)S(1)} %collective-permute-done.19.other_ref, f32[8,128]{1,0:T(8,128)S(1)} %get-tuple-element.49.before_ref), custom_call_target="tpu_custom_call" | custom-call | flops 32768 | bytes 262144 | tf_op jit(solution)/shard_map/pallas_call | solution.py:409
  (26 shorter events, 0.1 us)
Async XLA Ops:
  4.2 21.1 %collective-permute-start = (bf16[128,768]{1,0:T(8,128)(2,1)S(1)}, bf16[128,768]{1,0:T(8,128)(2,1)S(1)}, u32[]{:S(2)}, u32[]{:S(2)}) collective-permute-start(bf16[128,768]{1,0:T(8,128)(2,1)S(1)} %get-tuple-element.28), channel_id=1, source_target_pairs={{0,1},{1,0},{2,3},{3,2},{4,5},{5,4},{6,7},{7,6},{8,9},{9,8},{10,11... | collective-permute-start | bytes 589832 | tf_op jit(solution)/shard_map/ppermute | solution.py:420
  5.7 19.6 %collective-permute-start.1 = (bf16[128,768]{1,0:T(8,128)(2,1)S(1)}, bf16[128,768]{1,0:T(8,128)(2,1)S(1)}, u32[]{:S(2)}, u32[]{:S(2)}) collective-permute-start(bf16[128,768]{1,0:T(8,128)(2,1)S(1)} %get-tuple-element.29), channel_id=1, source_target_pairs={{0,2},{1,3},{2,0},{3,1},{4,6},{5,7},{6,4},{7,5},{8,10},{9,11},{10,... | collective-permute-start | bytes 589832 | tf_op jit(solution)/shard_map/ppermute | solution.py:420
  7.5 17.9 %collective-permute-start.2 = (bf16[128,768]{1,0:T(8,128)(2,1)S(1)}, bf16[128,768]{1,0:T(8,128)(2,1)S(1)}, u32[]{:S(2)}, u32[]{:S(2)}) collective-permute-start(bf16[128,768]{1,0:T(8,128)(2,1)S(1)} %get-tuple-element.30), channel_id=1, source_target_pairs={{0,4},{1,5},{2,6},{3,7},{4,0},{5,1},{6,2},{7,3},{8,12},{9,13},{10,... | collective-permute-start | bytes 589832 | tf_op jit(solution)/shard_map/ppermute | solution.py:420
  10.8 14.6 %collective-permute-start.3 = (bf16[128,768]{1,0:T(8,128)(2,1)S(1)}, bf16[128,768]{1,0:T(8,128)(2,1)S(1)}, u32[]{:S(2)}, u32[]{:S(2)}) collective-permute-start(bf16[128,768]{1,0:T(8,128)(2,1)S(1)} %get-tuple-element.31), channel_id=1, source_target_pairs={{0,8},{1,9},{2,10},{3,11},{4,12},{5,13},{6,14},{7,15},{8,0},{9,1},... | collective-permute-start | bytes 589832 | tf_op jit(solution)/shard_map/ppermute | solution.py:420
  12.0 11.0 %copy-start = (bf16[2048,128]{1,0:T(8,128)(2,1)S(1)}, bf16[2048,128]{1,0:T(8,128)(2,1)}, u32[]{:S(2)}) copy-start(bf16[2048,128]{1,0:T(8,128)(2,1)} %refs_8_.1) | copy-start | bytes 1572868
  12.0 13.4 %collective-permute-start.4 = (bf16[128,768]{1,0:T(8,128)(2,1)S(1)}, bf16[128,768]{1,0:T(8,128)(2,1)S(1)}, u32[]{:S(2)}, u32[]{:S(2)}) collective-permute-start(bf16[128,768]{1,0:T(8,128)(2,1)S(1)} %get-tuple-element.32), channel_id=1, source_target_pairs={{0,16},{1,17},{2,18},{3,19},{4,20},{5,21},{6,22},{7,23},{8,24},{9,... | collective-permute-start | bytes 589832 | tf_op jit(solution)/shard_map/ppermute | solution.py:420
  22.9 2.4 %copy-start.1 = (bf16[2048,128]{1,0:T(8,128)(2,1)S(1)}, bf16[2048,128]{1,0:T(8,128)(2,1)}, u32[]{:S(2)}) copy-start(bf16[2048,128]{1,0:T(8,128)(2,1)} %refs_9_.1) | copy-start | bytes 1572868
  22.9 2.4 %copy-start.3 = (bf16[128,128]{1,0:T(8,128)(2,1)S(1)}, bf16[128,128]{1,0:T(8,128)(2,1)}, u32[]{:S(2)}) copy-start(bf16[128,128]{1,0:T(8,128)(2,1)} %ws_ref.1) | copy-start | bytes 98308
  22.9 2.4 %copy-start.4 = (bf16[128,128]{1,0:T(8,128)(2,1)S(1)}, bf16[128,128]{1,0:T(8,128)(2,1)}, u32[]{:S(2)}) copy-start(bf16[128,128]{1,0:T(8,128)(2,1)} %refs_12_.1) | copy-start | bytes 98308
  22.9 2.4 %copy-start.5 = (s32[2048]{0:T(1024)S(1)}, s32[2048]{0:T(1024)}, u32[]{:S(2)}) copy-start(s32[2048]{0:T(1024)} %param.20) | copy-start | bytes 24580
  23.0 2.4 %copy-start.6 = (f32[128]{0:T(128)S(1)}, f32[128]{0:T(128)}, u32[]{:S(2)}) copy-start(f32[128]{0:T(128)} %param.14) | copy-start | bytes 1540
  31.6 2.4 %collective-permute-start.5 = (f32[128,128]{1,0:T(8,128)S(1)}, f32[128,128]{1,0:T(8,128)S(1)}, u32[]{:S(2)}, u32[]{:S(2)}) collective-permute-start(f32[128,128]{1,0:T(8,128)S(1)} %get-tuple-element.41), channel_id=1, source_target_pairs={{0,1},{1,0},{2,3},{3,2},{4,5},{5,4},{6,7},{7,6},{8,9},{9,8},{10,11... | collective-permute-start | bytes 196616 | tf_op jit(solution)/shard_map/ppermute | solution.py:420
  34.0 5.3 %collective-permute-start.8 = (f32[128,128]{1,0:T(8,128)S(1)}, f32[128,128]{1,0:T(8,128)S(1)}, u32[]{:S(2)}, u32[]{:S(2)}) collective-permute-start(f32[128,128]{1,0:T(8,128)S(1)} %shard_map.144.before_ref.left_ref), channel_id=1, source_target_pairs={{0,96},{1,97},{2,98},{3,99},{4,100},{5,101},{6,102},{7,103},{8,104... | collective-permute-start | bytes 196616 | tf_op jit(solution)/shard_map/ppermute | solution.py:420
  37.0 9.9 %collective-permute-start.10 = (bf16[128,768]{1,0:T(8,128)(2,1)S(1)}, bf16[128,768]{1,0:T(8,128)(2,1)S(1)}, u32[]{:S(2)}, u32[]{:S(2)}) collective-permute-start(bf16[128,768]{1,0:T(8,128)(2,1)S(1)} %shard_map.142.before_ref), channel_id=1, source_target_pairs={{0,4},{1,5},{2,6},{3,7},{4,0},{5,1},{6,2},{7,3},{8,12},{9,13},{10,... | collective-permute-start | bytes 589832 | tf_op jit(solution)/shard_map/ppermute | solution.py:420
  37.0 4.6 %collective-permute-start.7 = (f32[128,128]{1,0:T(8,128)S(1)}, f32[128,128]{1,0:T(8,128)S(1)}, u32[]{:S(2)}, u32[]{:S(2)}) collective-permute-start(f32[128,128]{1,0:T(8,128)S(1)} %shard_map.144.before_ref.left_ref), channel_id=1, source_target_pairs={{0,64},{1,65},{2,66},{3,67},{4,68},{5,69},{6,70},{7,71},{8,72},{9,... | collective-permute-start | bytes 196616 | tf_op jit(solution)/shard_map/ppermute | solution.py:420
  37.4 4.3 %collective-permute-start.6 = (f32[128,128]{1,0:T(8,128)S(1)}, f32[128,128]{1,0:T(8,128)S(1)}, u32[]{:S(2)}, u32[]{:S(2)}) collective-permute-start(f32[128,128]{1,0:T(8,128)S(1)} %shard_map.144.before_ref.left_ref), channel_id=1, source_target_pairs={{0,32},{1,33},{2,34},{3,35},{4,36},{5,37},{6,38},{7,39},{8,40},{9,... | collective-permute-start | bytes 196616 | tf_op jit(solution)/shard_map/ppermute | solution.py:420
  37.8 16.2 %collective-permute-start.12 = (bf16[128,768]{1,0:T(8,128)(2,1)S(1)}, bf16[128,768]{1,0:T(8,128)(2,1)S(1)}, u32[]{:S(2)}, u32[]{:S(2)}) collective-permute-start(bf16[128,768]{1,0:T(8,128)(2,1)S(1)} %shard_map.143.before_ref), channel_id=1, source_target_pairs={{0,16},{1,17},{2,18},{3,19},{4,20},{5,21},{6,22},{7,23},{8,24},{9,... | collective-permute-start | bytes 589832 | tf_op jit(solution)/shard_map/ppermute | solution.py:420
  39.3 16.1 %collective-permute-start.14 = (bf16[128,768]{1,0:T(8,128)(2,1)S(1)}, bf16[128,768]{1,0:T(8,128)(2,1)S(1)}, u32[]{:S(2)}, u32[]{:S(2)}) collective-permute-start(bf16[128,768]{1,0:T(8,128)(2,1)S(1)} %shard_map.145.before_ref), channel_id=1, source_target_pairs={{0,2},{1,3},{2,0},{3,1},{4,6},{5,7},{6,4},{7,5},{8,10},{9,11},{10,... | collective-permute-start | bytes 589832 | tf_op jit(solution)/shard_map/ppermute | solution.py:420
  41.7 3.5 %collective-permute-start.9 = (f32[128,128]{1,0:T(8,128)S(1)}, f32[128,128]{1,0:T(8,128)S(1)}, u32[]{:S(2)}, u32[]{:S(2)}) collective-permute-start(f32[128,128]{1,0:T(8,128)S(1)} %shard_map.146.before_ref.left_ref), channel_id=1, source_target_pairs={{0,8},{1,9},{2,10},{3,11},{4,12},{5,13},{6,14},{7,15},{8,0},{9,1},... | collective-permute-start | bytes 196616 | tf_op jit(solution)/shard_map/ppermute | solution.py:420
  42.4 13.8 %collective-permute-start.13 = (bf16[128,768]{1,0:T(8,128)(2,1)S(1)}, bf16[128,768]{1,0:T(8,128)(2,1)S(1)}, u32[]{:S(2)}, u32[]{:S(2)}) collective-permute-start(bf16[128,768]{1,0:T(8,128)(2,1)S(1)} %shard_map.147.before_ref), channel_id=1, source_target_pairs={{0,8},{1,9},{2,10},{3,11},{4,12},{5,13},{6,14},{7,15},{8,0},{9,1},... | collective-permute-start | bytes 589832 | tf_op jit(solution)/shard_map/ppermute | solution.py:420
  44.5 6.8 %copy-start.2 = (s32[5,768]{1,0:T(8,128)S(1)}, s32[5,768]{1,0:T(8,128)}, u32[]{:S(2)}) copy-start(s32[5,768]{1,0:T(8,128)} %rows_ref.7) | copy-start | bytes 46084
  45.2 6.8 %collective-permute-start.11 = (f32[128,128]{1,0:T(8,128)S(1)}, f32[128,128]{1,0:T(8,128)S(1)}, u32[]{:S(2)}, u32[]{:S(2)}) collective-permute-start(f32[128,128]{1,0:T(8,128)S(1)} %shard_map.149.before_ref.left_ref), channel_id=1, source_target_pairs={{0,24},{1,25},{2,26},{3,27},{4,28},{5,29},{6,30},{7,31},{8,16},{9,... | collective-permute-start | bytes 196616 | tf_op jit(solution)/shard_map/ppermute | solution.py:420
  46.9 15.5 %collective-permute-start.18 = (bf16[128,768]{1,0:T(8,128)(2,1)S(1)}, bf16[128,768]{1,0:T(8,128)(2,1)S(1)}, u32[]{:S(2)}, u32[]{:S(2)}) collective-permute-start(bf16[128,768]{1,0:T(8,128)(2,1)S(1)} %shard_map.148.before_ref), channel_id=1, source_target_pairs={{0,1},{1,0},{2,3},{3,2},{4,5},{5,4},{6,7},{7,6},{8,9},{9,8},{10,11... | collective-permute-start | bytes 589832 | tf_op jit(solution)/shard_map/ppermute | solution.py:420
  52.0 5.3 %collective-permute-start.17 = (f32[128,128]{1,0:T(8,128)S(1)}, f32[128,128]{1,0:T(8,128)S(1)}, u32[]{:S(2)}, u32[]{:S(2)}) collective-permute-start(f32[128,128]{1,0:T(8,128)S(1)} %shard_map.152.before_ref.left_ref), channel_id=1, source_target_pairs={{0,6},{1,7},{2,4},{3,5},{4,2},{5,3},{6,0},{7,1},{8,14},{9,15},{10,... | collective-permute-start | bytes 196616 | tf_op jit(solution)/shard_map/ppermute | solution.py:420
  54.0 4.7 %collective-permute-start.16 = (f32[128,128]{1,0:T(8,128)S(1)}, f32[128,128]{1,0:T(8,128)S(1)}, u32[]{:S(2)}, u32[]{:S(2)}) collective-permute-start(f32[128,128]{1,0:T(8,128)S(1)} %shard_map.152.before_ref.left_ref), channel_id=1, source_target_pairs={{0,4},{1,5},{2,6},{3,7},{4,0},{5,1},{6,2},{7,3},{8,12},{9,13},{10,... | collective-permute-start | bytes 196616 | tf_op jit(solution)/shard_map/ppermute | solution.py:420
  55.5 3.4 %collective-permute-start.15 = (f32[128,128]{1,0:T(8,128)S(1)}, f32[128,128]{1,0:T(8,128)S(1)}, u32[]{:S(2)}, u32[]{:S(2)}) collective-permute-start(f32[128,128]{1,0:T(8,128)S(1)} %shard_map.152.before_ref.left_ref), channel_id=1, source_target_pairs={{0,2},{1,3},{2,0},{3,1},{4,6},{5,7},{6,4},{7,5},{8,10},{9,11},{10,... | collective-permute-start | bytes 196616 | tf_op jit(solution)/shard_map/ppermute | solution.py:420
  58.9 5.3 %collective-permute-start.19 = (f32[128,128]{1,0:T(8,128)S(1)}, f32[128,128]{1,0:T(8,128)S(1)}, u32[]{:S(2)}, u32[]{:S(2)}) collective-permute-start(f32[128,128]{1,0:T(8,128)S(1)} %shard_map.155.before_ref.total_ref), channel_id=1, source_target_pairs={{0,1},{1,0},{2,3},{3,2},{4,5},{5,4},{6,7},{7,6},{8,9},{9,8},{10,11... | collective-permute-start | bytes 196616 | tf_op jit(solution)/shard_map/ppermute | solution.py:420
